TPU v7x, 32 devices: a whole 2x2x4 slice. The times are simulated.
32 devices in a mesh: gx: 4 (over x, core), gy: 8 (over z, y).
Axes of the slice: x: 2, y: 2, z: 4, core: 2. Of those that a mesh axis runs over, the one named last changes fastest.
Arguments:
- theta: float32 [4, 64, 1024], P(None, 'gy', 'gx'), may hold values from -3.140625 to 3.140625
- phi: float32 [4, 64, 1024], P(None, 'gy', 'gx'), may hold values from -3.140625 to 3.140625
- labels: int32 [4, 64, 1024], P(None, 'gy', 'gx'), may hold values from 0 to 15
- ms_region: float32 [16], replicated, may hold values from 0.4 to 1
- aex_region: float32 [16], replicated, may hold values from 0.5 to 2
- kernel: bfloat16 [6, 8, 2048, 128], P(None, None, ('gx', 'gy')), may hold values from -0.5 to 1.5
Outputs:
- field: float32 [3, 4, 64, 1024], P(None, None, 'gy', 'gx')
- predicted: float32 [3, 4, 64, 1024], P(None, None, 'gy', 'gx')
All inputs are finite; a program needn't handle non-finite values.
Results may differ from a plain program's by a relative error of at most 0.0003.
Values sent between devices are 32-bit elements; how exact they have to be, the bound alone decides.
No kernel may reach another device: no remote copies, remote signals or barrier semaphores. Data moves between devices by JAX's collectives and lax.ppermute only.
A program may use at most 64 MiB of HBM per device.

v0:
```python
import functools
import math

import jax
import jax.numpy as jnp
import ml_dtypes
import numpy as np
from jax import lax
from jax.experimental import pallas as pl
from jax.experimental.pallas import tpu as pltpu
from jax.sharding import PartitionSpec as P

damping = 0.5
time_step = 0.2
side_weight = 0.25
layer_weight = 0.5
root_half = math.sqrt(0.5)
constant_limit = 20 << 20


def split_high(value):
    high = value.astype(jnp.bfloat16)
    low = (value - high.astype(jnp.float32)).astype(jnp.bfloat16)
    return high, low


def split_table(table):
    high = table.astype(np.float32).astype(ml_dtypes.bfloat16)
    low = (table - high.astype(np.float64)).astype(np.float32).astype(ml_dtypes.bfloat16)
    return high, low


def dot(left, right, contract=((1,), (0,))):
    return lax.dot_general(left, right, (contract, ((), ())), preferred_element_type=jnp.float32)


def line_table(count_x, count_y, width, rows):
    cells = count_x * width
    if count_x * 2 * cells * count_y * 2 * rows * 2 > constant_limit:
        return None
    place = np.arange(cells)[None, :, None, None]
    wave = (
        np.arange(count_x)[:, None, None, None] * (count_y * rows)
        + np.arange(count_y)[None, None, :, None] * rows
        + np.arange(rows)[None, None, None, :]
    )
    angle = (place * wave % (2 * cells)) * (2.0 * math.pi / (2 * cells))
    table = np.stack([np.cos(angle), -np.sin(angle)], 3)
    table = table.reshape(count_x, cells, count_y * 2 * rows)
    high, low = split_table(table)
    return np.stack([high, low], 1)


def line_table_here(count_x, count_y, width, rows):
    cells = count_x * width
    place = jnp.arange(cells, dtype=jnp.int32)[:, None, None]
    wave = (
        lax.axis_index("gx") * (count_y * rows)
        + jnp.arange(count_y, dtype=jnp.int32)[None, :, None] * rows
        + jnp.arange(rows, dtype=jnp.int32)[None, None, :]
    )
    angle = (place * wave % (2 * cells)).astype(jnp.float32) * (math.pi / cells)
    table = jnp.stack([jnp.cos(angle), -jnp.sin(angle)], 2).reshape(cells, count_y * 2 * rows)
    return jnp.stack(split_high(table))


def column_tables(height):
    angle = (np.arange(2 * height)[:, None] * np.arange(height)[None, :] % (2 * height)) * (
        math.pi / height
    )
    high, low = split_table(np.concatenate([np.cos(angle), np.sin(angle)], 1))
    forward = np.concatenate([high, high, low], 1)
    high, low = split_table(np.concatenate([np.cos(angle.T), np.sin(angle.T)], 0))
    inverse = np.concatenate([high, high, low], 1)
    return forward, inverse


def sine_cosine(angle):
    turns = jnp.floor(angle * (2.0 / math.pi) + 0.5)
    rest = angle - turns * 1.5703125
    rest = rest - turns * 4.8351287841796875e-4
    rest = rest - turns * 3.1385570764541626e-7
    square = rest * rest
    sine = rest + rest * square * (
        -1.6666654611e-1 + square * (8.3321608736e-3 - square * 1.9515295891e-4)
    )
    cosine = (
        1.0
        - 0.5 * square
        + square * square * (4.166664568298827e-2 + square * (-1.388731625493765e-3 + square * 2.443315711809948e-5))
    )
    quarter = turns.astype(jnp.int32)
    odd = (quarter & 1) == 1
    out_sine = jnp.where(odd, cosine, sine)
    out_cosine = jnp.where(odd, sine, cosine)
    out_sine = jnp.where((quarter & 2) == 2, -out_sine, out_sine)
    out_cosine = jnp.where(((quarter + 1) & 2) == 2, -out_cosine, out_cosine)
    return out_sine, out_cosine


def directions(theta, phi):
    lateral, axial = sine_cosine(theta)
    sine, cosine = sine_cosine(phi)
    return [lateral * cosine, lateral * sine, axial]


def looked_up(labels, region):
    result = jnp.zeros_like(labels) + region[0]
    for index in range(1, region.shape[0]):
        result = jnp.where(labels == float(index), region[index], result)
    return result


def lines_body(raw, region, table_high, table_low):
    blocks = []
    for theta, phi, labels in raw:
        unit = directions(theta, phi)
        saturation = looked_up(labels, region)
        rows = theta.shape[0] * theta.shape[1]
        blocks.append(
            jnp.concatenate([(part * saturation).reshape(rows, -1) for part in unit], 0)
        )
    moment = jnp.concatenate(blocks, 1)
    high, low = split_high(moment)
    both = dot(jnp.concatenate([high, low], 0), table_high)
    lines = moment.shape[0]
    return both[:lines] + both[lines:] + dot(high, table_low)


def lines_kernel(raw_ref, region_ref, table_ref, out_ref):
    raw = [[raw_ref[g, f] for f in range(3)] for g in range(raw_ref.shape[0])]
    result = lines_body(raw, region_ref, table_ref[0], table_ref[1])
    lanes = out_ref.shape[2]
    for index in range(out_ref.shape[0]):
        out_ref[index] = result[:, index * lanes : (index + 1) * lanes]


def back_lines_body(spectrum, table_high, table_low, groups):
    high, low = split_high(spectrum)
    both = jnp.concatenate([high, low], 0)
    lines = spectrum.shape[0]
    width = table_high.shape[0] // groups
    result = []
    for index in range(groups):
        rows = slice(index * width, (index + 1) * width)
        wide = dot(both, table_high[rows], ((1,), (1,)))
        result.append(
            wide[:lines] + wide[lines:] + dot(high, table_low[rows], ((1,), (1,)))
        )
    return result


def back_lines_kernel(spectrum_ref, table_ref, out_ref):
    spectrum = jnp.concatenate([spectrum_ref[g] for g in range(spectrum_ref.shape[0])], 1)
    parts = back_lines_body(spectrum, table_ref[0], table_ref[1], out_ref.shape[0])
    for index, part in enumerate(parts):
        out_ref[index] = part


def tensor_kernel(kernel_ref, twice_ref, out_ref):
    twice = twice_ref[...]

    def step(index, carry):
        turned = dot(kernel_ref[index], twice, ((0,), (0,)))
        out_ref[index] = turned.astype(jnp.bfloat16)
        return carry

    lax.fori_loop(0, kernel_ref.shape[0], step, 0)


def turn(value, sign):
    lanes = value.shape[-1]
    if lanes == 128:
        return pltpu.roll(value, lanes // 2, value.ndim - 1) * sign
    return jnp.concatenate([value[..., lanes // 2 :], value[..., : lanes // 2]], -1) * sign


def layers_forward(layer, sign):
    d0, d1, d2, d3 = layer
    r2 = turn(d2, sign)
    near, far = d1 + d3, d1 - d3
    far_turned = turn(far, sign)
    near_turned = turn(near, sign)
    even, odd = d0 + d2, d0 - d2
    out = [None] * 8
    out[0], out[4] = even + near, even - near
    out[2], out[6] = odd + far_turned, odd - far_turned
    plus, minus = d0 + r2, d0 - r2
    first = (far + near_turned) * root_half
    second = (near_turned - far) * root_half
    out[1], out[5] = plus + first, plus - first
    out[3], out[7] = minus + second, minus - second
    return out


def layers_inverse(wave, sign):
    a, b = wave[0] + wave[4], wave[0] - wave[4]
    e, f = wave[2] + wave[6], turn(wave[2] - wave[6], sign)
    p, q = wave[1] + wave[5], wave[1] - wave[5]
    s, t = wave[3] + wave[7], turn(wave[3] - wave[7], sign)
    o0, o1, o2, o3 = p + s, q - t, p - s, q + t
    return [
        a + e + o0,
        b - f + (o1 - turn(o1, sign)) * root_half,
        a - e - turn(o2, sign),
        b + f - (o3 + turn(o3, sign)) * root_half,
    ]


def apply_tensor(tensor, wave):
    out = [[], [], []]
    for level in range(8):
        xx, yy, zz, xy, xz, yz = [tensor[part][level] for part in range(6)]
        x, y, z = wave[0][level], wave[1][level], wave[2][level]
        out[0].append(xx * x + xy * y + xz * z)
        out[1].append(xy * x + yy * y + yz * z)
        out[2].append(xz * x + yz * y + zz * z)
    return out


def waves_kernel(scale, spec_ref, tensor_ref, forward_ref, inverse_ref, out_ref, wave_ref, back_ref):
    count_y, lines, lanes = spec_ref.shape
    local = 8
    planes = lines // local
    height = count_y * local
    sign = jnp.where(
        lax.broadcasted_iota(jnp.int32, (1, lanes), 1) < lanes // 2, 1.0, -1.0
    ).astype(jnp.float32)
    columns = []
    for plane in range(planes):
        value = spec_ref[:, plane * local : (plane + 1) * local, :].reshape(height, lanes)
        value = jnp.concatenate([value, turn(value, sign)], 0)
        high, low = split_high(value)
        columns.append(jnp.concatenate([high, low, high], 0))
    wave_ref[...] = dot(forward_ref[...], jnp.concatenate(columns, 1))

    chunk = 16
    depth = planes // 3
    double = 2 * height

    def step(index, carry):
        rows = pl.ds(pl.multiple_of(index * chunk, chunk), chunk)
        wave = []
        for part in range(3):
            layer = [
                wave_ref[rows, (part * depth + z) * lanes : (part * depth + z + 1) * lanes]
                for z in range(depth)
            ]
            wave.append(layers_forward(layer, sign))
        tensor = [
            [tensor_ref[part * 8 + level, rows, :].astype(jnp.float32) for level in range(8)]
            for part in range(6)
        ]
        image = apply_tensor(tensor, wave)
        for part in range(3):
            layer = layers_inverse(image[part], sign)
            for z in range(depth):
                place = slice((part * depth + z) * lanes, (part * depth + z + 1) * lanes)
                high, low = split_high(layer[z] * scale)
                back_ref[rows, place] = high
                back_ref[pl.ds(pl.multiple_of(double + index * chunk, chunk), chunk), place] = low
                back_ref[pl.ds(pl.multiple_of(2 * double + index * chunk, chunk), chunk), place] = high
        return carry

    lax.fori_loop(0, double // chunk, step, 0)
    back = dot(inverse_ref[...], back_ref[...])
    for plane in range(planes):
        place = slice(plane * lanes, (plane + 1) * lanes)
        value = back[:height, place] - turn(back[height:, place], sign)
        out_ref[:, plane * local : (plane + 1) * local, :] = value.reshape(count_y, local, lanes)


def exchange_kernel(raw_ref, rows_ref, place_ref, ms_ref, aex_ref, exchange_ref, unit_ref):
    count_x = raw_ref.shape[0]
    depth, height, width = raw_ref.shape[2:]
    gx, gy, count_y = place_ref[0], place_ref[1], place_ref[2]
    left, right = jnp.maximum(gx - 1, 0), jnp.minimum(gx + 1, count_x - 1)
    shape = (depth, height, width)
    lane = lax.broadcasted_iota(jnp.int32, shape, 2)
    row = lax.broadcasted_iota(jnp.int32, shape, 1)

    def quantities(values):
        return directions(values[0], values[1]) + [looked_up(values[2], aex_ref)]

    raw = [raw_ref[gx, f] for f in range(3)]
    here = quantities(raw)
    side = quantities([jnp.where(lane == 0, raw_ref[right, f], raw_ref[left, f]) for f in range(3)])
    above = quantities(
        [
            jnp.where(
                row == 0,
                jnp.broadcast_to(rows_ref[1, f][:, None, :], shape),
                jnp.broadcast_to(rows_ref[0, f][:, None, :], shape),
            )
            for f in range(3)
        ]
    )
    saturation = looked_up(raw[2], ms_ref)
    total = [jnp.zeros(shape, jnp.float32) for _ in range(3)]

    def add(total, beside, weight):
        coupling = 2.0 * here[3] * beside[3] / (here[3] + beside[3]) * weight
        return [total[c] + coupling * (beside[c] - here[c]) for c in range(3)]

    one = jnp.float32(1.0)
    zero = jnp.float32(0.0)
    for shift, edge, there in ((1, 0, gx > 0), (width - 1, width - 1, gx < count_x - 1)):
        beside = [
            jnp.where(lane == edge, pltpu.roll(s, shift, 2), pltpu.roll(h, shift, 2))
            for s, h in zip(side, here)
        ]
        weight = jnp.where(lane == edge, jnp.where(there, one, zero), one) * side_weight
        total = add(total, beside, weight)
    for shift, edge, there in ((1, 0, gy > 0), (height - 1, height - 1, gy < count_y - 1)):
        beside = [
            jnp.where(row == edge, pltpu.roll(s, shift, 1), pltpu.roll(h, shift, 1))
            for s, h in zip(above, here)
        ]
        weight = jnp.where(row == edge, jnp.where(there, one, zero), one) * side_weight
        total = add(total, beside, weight)
    for part in range(3):
        unit_ref[part] = here[part]
    for z in range(depth):
        out = [total[c][z] for c in range(3)]
        for other in (z - 1, z + 1):
            if 0 <= other < depth:
                a, b = here[3][z], here[3][other]
                coupling = 2.0 * a * b / (a + b) * layer_weight
                out = [out[c] + coupling * (here[c][other] - here[c][z]) for c in range(3)]
        for c in range(3):
            exchange_ref[c, z] = out[c] / saturation[z]


def cross(first, second):
    return [
        first[1] * second[2] - first[2] * second[1],
        first[2] * second[0] - first[0] * second[2],
        first[0] * second[1] - first[1] * second[0],
    ]


def final_kernel(parts_ref, exchange_ref, unit_ref, field_ref, predicted_ref):
    depth, height, width = unit_ref.shape[1:]
    rows = depth * height
    unit, field = [], []
    for c in range(3):
        place = slice(c * rows, (c + 1) * rows)
        total = parts_ref[0, place]
        for index in range(1, parts_ref.shape[0]):
            total = total + parts_ref[index, place]
        field.append(exchange_ref[c] + total.reshape(depth, height, width))
        unit.append(unit_ref[c])
        field_ref[c] = field[c]
    twist = cross(unit, field)
    second = cross(unit, twist)
    moved = [
        unit[c] - (time_step / (1.0 + damping * damping)) * (twist[c] + damping * second[c])
        for c in range(3)
    ]
    length = jnp.sqrt(moved[0] * moved[0] + moved[1] * moved[1] + moved[2] * moved[2])
    for c in range(3):
        predicted_ref[c] = moved[c] / length


vmem = pl.BlockSpec(memory_space=pltpu.VMEM)
smem = pl.BlockSpec(memory_space=pltpu.SMEM)


def call(body, out, ins, operands, scratch=(), flops=0, name=None):
    size = sum(math.prod(o.shape) * o.dtype.itemsize for o in operands)
    outs = out if isinstance(out, (list, tuple)) else [out]
    size += sum(math.prod(o.shape) * o.dtype.itemsize for o in outs)
    return pl.pallas_call(
        body,
        out_shape=out,
        in_specs=ins,
        out_specs=jax.tree.map(lambda _: vmem, out),
        scratch_shapes=list(scratch),
        compiler_params=pltpu.CompilerParams(vmem_limit_bytes=40 << 20),
        cost_estimate=pl.CostEstimate(flops=flops, bytes_accessed=size, transcendentals=0),
        name=name,
    )(*operands)


def f32(*shape):
    return jax.ShapeDtypeStruct(shape, jnp.float32)


def per_device(theta, phi, labels, ms_region, aex_region, kernel):
    count_x, count_y = lax.axis_size("gx"), lax.axis_size("gy")
    gx, gy = lax.axis_index("gx"), lax.axis_index("gy")
    depth, height, width = theta.shape
    rows = kernel.shape[2]
    lanes = 2 * rows
    lines = 3 * depth * height
    whole_y = count_y * height

    raw = jnp.stack([theta, phi, labels.astype(jnp.float32)])
    gathered = lax.all_gather(raw, "gx")
    up = [(i, i + 1) for i in range(count_y - 1)]
    down = [(j, i) for i, j in up]
    before = lax.ppermute(raw[:, :, height - 1], "gy", up)
    after = lax.ppermute(raw[:, :, 0], "gy", down)

    table = line_table(count_x, count_y, width, rows)
    if table is None:
        table = line_table_here(count_x, count_y, width, rows)
    else:
        table = lax.dynamic_index_in_dim(jnp.asarray(table), gx, 0, keepdims=False)
    forward, inverse = column_tables(whole_y)

    twice = np.concatenate([np.eye(rows), np.eye(rows)], 1).astype(ml_dtypes.bfloat16)
    tensor = call(
        tensor_kernel,
        jax.ShapeDtypeStruct((48, 2 * whole_y, lanes), jnp.bfloat16),
        [vmem, vmem],
        (kernel.reshape(48, rows, 2 * whole_y), jnp.asarray(twice)),
        flops=48 * 2 * rows * lanes * 2 * whole_y,
        name="tensor",
    )
    spectrum = call(
        lines_kernel,
        f32(count_y, lines, lanes),
        [vmem, smem, vmem],
        (gathered, ms_region, table),
        flops=6 * lines * count_x * width * count_y * lanes,
        name="lines",
    )
    columns = lax.all_to_all(spectrum, "gy", split_axis=0, concat_axis=0, tiled=True)
    scale = -1.0 / (8.0 * depth * 0 + 2 * depth * 2 * whole_y * 2 * count_x * width)
    waves = call(
        functools.partial(waves_kernel, scale),
        f32(count_y, lines, lanes),
        [vmem] * 4,
        (columns, tensor, jnp.asarray(forward), jnp.asarray(inverse)),
        scratch=(
            pltpu.VMEM((2 * whole_y, 3 * depth * lanes), jnp.float32),
            pltpu.VMEM((6 * whole_y, 3 * depth * lanes), jnp.bfloat16),
        ),
        flops=20 * whole_y * whole_y * 3 * depth * lanes,
        name="waves",
    )
    returned = lax.all_to_all(waves, "gy", split_axis=0, concat_axis=0, tiled=True)
    partial = call(
        back_lines_kernel,
        f32(count_x, lines, width),
        [vmem, vmem],
        (returned, table),
        flops=6 * lines * count_x * width * count_y * lanes,
        name="back_lines",
    )
    parts = lax.all_to_all(partial, "gx", split_axis=0, concat_axis=0, tiled=True)
    place = jnp.stack([gx, gy, jnp.int32(count_y)]).astype(jnp.int32)
    exchange, unit = call(
        exchange_kernel,
        [f32(3, depth, height, width), f32(3, depth, height, width)],
        [vmem, vmem, smem, smem, smem],
        (gathered, jnp.stack([before, after]), place, ms_region, aex_region),
        flops=300 * depth * height * width,
        name="exchange",
    )
    field, predicted = call(
        final_kernel,
        [f32(3, depth, height, width), f32(3, depth, height, width)],
        [vmem] * 3,
        (parts, exchange, unit),
        flops=60 * depth * height * width,
        name="predict",
    )
    return field, predicted


def solution(mesh):
    in_specs = (
        P(None, "gy", "gx"),
        P(None, "gy", "gx"),
        P(None, "gy", "gx"),
        P(),
        P(),
        P(None, None, ("gx", "gy"), None),
    )
    out_specs = (P(None, None, "gy", "gx"), P(None, None, "gy", "gx"))
    return jax.shard_map(
        per_device, mesh=mesh, in_specs=in_specs, out_specs=out_specs, check_vma=False
    )
```

profile of v0, /device:TPU:0, one launch (start us, length us, event | category | flops | bytes accessed | tf_op | source)
XLA Modules:
  0.0 73.7 jit_solution(17295492521606196110)
XLA Ops:
  0.6 0.8 %copy.21 = f32[4,8,256]{2,0,1:T(4,128)S(1)} copy(f32[4,8,256]{2,1,0:T(8,128)} %param.10) | data formatting | bytes 65536 | tf_op args[0]
  1.4 0.8 %convert_element_type.4 = f32[4,8,256]{2,1,0:T(8,128)S(1)} convert(s32[4,8,256]{2,1,0:T(8,128)} %param.12) | non-fusion elementwise | flops 8192 | bytes 65536 | tf_op jit(solution)/shard_map/convert_element_type | solution.py:398
  2.2 0.8 %copy_bitcast_fusion = (f32[1,4,8,256]{3,1,0,2:T(4,128)S(1)}, f32[1,4,8,256]{3,1,0,2:T(4,128)S(1)}) fusion(f32[4,8,256]{2,1,0:T(8,128)S(1)} %convert_element_type.4, f32[4,8,256]{2,1,0:T(8,128)} %param.11), kind=kLoop, calls=%fused_computation.2 | loop fusion | bytes 131072 | tf_op jit(solution)/shard_map/stack | solution.py:398
  3.0 7.9 %all-gather = f32[12,4,8,256]{3,1,0,2:T(4,128)S(1)} all-gather(f32[3,4,8,256]{3,1,0,2:T(4,128)S(1)} %pad_maximum_fusion), channel_id=2, replica_groups=mesh['gx'=4,'gy'=8] {'gx'}, dimensions={0}, use_global_device_ids=true | all-gather | bytes 491520 | tf_op jit(solution)/shard_map/all_gather | solution.py:399
  10.9 0.2 copy.15.raw_ref
  11.1 0.0 copy-start.6
  11.1 2.6 %dynamic-slice_bitcast_fusion.table_ref = bf16[2,1024,1024]{2,1,0:T(8,128)(2,1)S(1)} fusion(bf16[4,2,1024,1024]{3,2,1,0:T(8,128)(2,1)} %constant.24.clone, s32[]{:T(128)S(6)} %select_n.4), kind=kLoop, calls=%fused_computation | loop fusion | bytes 8388612 | tf_op jit(solution)/shard_map/jit(dynamic_index_in_dim)/squeeze | solution.py:409
  13.8 0.0 copy-done.6
  13.8 0.0 copy-start.2
  13.8 0.0 copy-start.5
  13.8 0.0 copy-start.3
  13.8 0.0 copy-start.4
  13.8 2.7 %lines.1 = f32[8,96,128]{2,1,0:T(8,128)} custom-call(f32[4,3,4,8,256]{4,3,2,1,0:T(8,128)S(1)} %copy.15.raw_ref, f32[16]{0:T(128)S(1)} %copy-done.6, bf16[2,1024,1024]{2,1,0:T(8,128)(2,1)S(1)} %dynamic-slice_bitcast_fusion.table_ref), custom_call_target="tpu_custom_call" | custom-call | flops 603979776 | bytes 4980800 | tf_op jit(solution)/shard_map/lines/pallas_call | solution.py:373
  16.5 2.0 %copy-done = bf16[2,1024,1024]{2,1,0:T(8,128)(2,1)} copy-done((bf16[2,1024,1024]{2,1,0:T(8,128)(2,1)}, bf16[2,1024,1024]{2,1,0:T(8,128)(2,1)S(1)}, u32[]{:S(2)}) %copy-start) | copy-done | bytes 4194328
  18.5 5.8 %all-to-all-start = ((f32[8,96,128]{2,1,0:T(8,128)}), f32[8,96,128]{2,1,0:T(8,128)S(1)}, u32[]{:S(2)}, u32[]{:S(2)}) async-start(f32[8,96,128]{2,1,0:T(8,128)} %lines.1), calls=%async_computation | async-start | bytes 786432 | tf_op jit(solution)/shard_map/all_to_all | solution.py:429
  24.3 0.0 copy-done.5
  24.3 9.0 %tensor.1.tensor_ref = bf16[48,128,128]{2,1,0:T(8,128)(2,1)S(1)} custom-call(bf16[48,64,128]{2,1,0:T(8,128)(2,1)S(1)} %bitcast.19, bf16[64,128]{1,0:T(8,128)(2,1)S(1)} %copy-done.5), custom_call_target="tpu_custom_call" | custom-call | flops 100663296 | bytes 2375680 | tf_op jit(solution)/shard_map/tensor/pallas_call | solution.py:373
  33.3 0.0 copy-start.7
  33.3 3.1 %all-to-all-done.spec_ref = f32[8,96,128]{2,1,0:T(8,128)S(1)} async-done(((f32[8,96,128]{2,1,0:T(8,128)}), f32[8,96,128]{2,1,0:T(8,128)S(1)}, u32[]{:S(2)}, u32[]{:S(2)}) %all-to-all-start) | async-done | bytes 393248 | tf_op jit(solution)/shard_map/all_to_all | solution.py:429
  36.5 3.1 %waves.1 = f32[8,96,128]{2,1,0:T(8,128)S(1)} custom-call(f32[8,96,128]{2,1,0:T(8,128)S(1)} %all-to-all-done.spec_ref, bf16[48,128,128]{2,1,0:T(8,128)(2,1)S(1)} %tensor.1.tensor_ref, bf16[128,384]{1,0:T(8,128)(2,1)S(1)} %copy-done.4, bf16[128,384]{1,0:T(8,128)(2,1)S(1)} %copy-done.3), custom_call_target="tpu_custom_call" | custom-call | flops 125829120 | bytes 2555904 | tf_op jit(solution)/shard_map/waves/pallas_call | solution.py:373
  39.6 15.7 %all_to_all.15.spectrum_ref = f32[8,96,128]{2,1,0:T(8,128)S(1)} all-to-all(f32[8,96,128]{2,1,0:T(8,128)S(1)} %waves.1), channel_id=1, replica_groups=mesh['gx'=4,'gy'=8] {'gy'}, dimensions={0} | all-to-all | bytes 786432 | tf_op jit(solution)/shard_map/all_to_all | solution.py:443
  55.3 2.2 %copy-done.1 = bf16[2,1024,1024]{2,1,0:T(8,128)(2,1)S(1)} copy-done((bf16[2,1024,1024]{2,1,0:T(8,128)(2,1)S(1)}, bf16[2,1024,1024]{2,1,0:T(8,128)(2,1)}, u32[]{:S(2)}) %copy-start.1) | copy-done | bytes 4194328
  57.5 2.2 %back_lines.1 = f32[4,96,256]{2,1,0:T(8,128)} custom-call(f32[8,96,128]{2,1,0:T(8,128)S(1)} %all_to_all.15.spectrum_ref, bf16[2,1024,1024]{2,1,0:T(8,128)(2,1)S(1)} %copy-done.1), custom_call_target="tpu_custom_call" | custom-call | flops 603979776 | bytes 4980736 | tf_op jit(solution)/shard_map/back_lines/pallas_call | solution.py:373
  59.7 3.5 %all-to-all-start.2 = ((f32[4,96,256]{2,1,0:T(8,128)}), f32[4,96,256]{2,1,0:T(8,128)S(1)}, u32[]{:S(2)}, u32[]{:S(2)}) async-start(f32[4,96,256]{2,1,0:T(8,128)} %back_lines.1), calls=%async_computation.2 | async-start | bytes 786432 | tf_op jit(solution)/shard_map/all_to_all | solution.py:452
  63.2 3.0 %collective-permute-start = (f32[3,4,256]{2,1,0:T(4,128)S(1)}, f32[3,4,256]{2,1,0:T(4,128)S(1)}, u32[]{:S(2)}, u32[]{:S(2)}) collective-permute-start(f32[3,4,256]{2,1,0:T(4,128)S(1)} %get-tuple-element.6), channel_id=1, source_target_pairs={{0,1},{1,2},{2,3},{3,4},{4,5},{5,6},{6,7},{8,9},{9,10},{10,11},{11... | collective-permute-start | bytes 36872 | tf_op jit(solution)/shard_map/ppermute | solution.py:402
  66.2 1.3 %collective-permute-start.1 = (f32[3,4,256]{2,1,0:T(4,128)S(1)}, f32[3,4,256]{2,1,0:T(4,128)S(1)}, u32[]{:S(2)}, u32[]{:S(2)}) collective-permute-start(f32[3,4,256]{2,1,0:T(4,128)S(1)} %get-tuple-element.7), channel_id=1, source_target_pairs={{1,0},{2,1},{3,2},{4,3},{5,4},{6,5},{7,6},{9,8},{10,9},{11,10},{12... | collective-permute-start | bytes 36872 | tf_op jit(solution)/shard_map/ppermute | solution.py:403
  67.5 0.1 pad_add_fusion.place_ref
  67.6 0.0 collective-permute-done
  67.6 4.2 %collective-permute-done.1 = f32[3,4,256]{2,1,0:T(4,128)S(1)} collective-permute-done((f32[3,4,256]{2,1,0:T(4,128)S(1)}, f32[3,4,256]{2,1,0:T(4,128)S(1)}, u32[]{:S(2)}, u32[]{:S(2)}) %collective-permute-start.1) | collective-permute-done | bytes 12320 | tf_op jit(solution)/shard_map/ppermute | solution.py:403
  71.8 1.1 %exchange.1 = (f32[3,4,8,256]{3,2,1,0:T(8,128)S(1)}, f32[3,4,8,256]{3,2,1,0:T(8,128)S(1)}) custom-call(f32[4,3,4,8,256]{4,3,2,1,0:T(8,128)S(1)} %copy.15.raw_ref, f32[2,3,4,256]{3,2,1,0:T(4,128)S(1)} %pad_maximum_fusion.1.rows_ref, s32[3]{0:T(128)S(1)} %pad_add_fusion.place_ref, f32[16]{0:T(128)S(1)} %copy-done.6, f32[16]{0:T(128)S(1)} %copy-done.7), custom_call_target="tpu_custom_call" | custom-call | flops 2457600 | bytes 614540 | tf_op jit(solution)/shard_map/exchange/pallas_call | solution.py:373
  72.9 0.0 all-to-all-done.2.parts_ref
  72.9 0.7 predict.1
  (9 shorter events, 0.0 us)
Async XLA Ops:
  11.1 2.7 %copy-start.6 = (f32[16]{0:T(128)S(1)}, f32[16]{0:T(128)}, u32[]{:S(2)}) copy-start(f32[16]{0:T(128)} %ms_ref.1) | copy-start | bytes 196
  13.8 10.5 %copy-start.2 = (bf16[6,8,64,128]{3,2,1,0:T(8,128)(2,1)S(1)}, bf16[6,8,64,128]{3,2,1,0:T(8,128)(2,1)}, u32[]{:S(2)}) copy-start(bf16[6,8,64,128]{3,2,1,0:T(8,128)(2,1)} %param.15) | copy-start | bytes 2359300
  13.8 10.5 %copy-start.5 = (bf16[64,128]{1,0:T(8,128)(2,1)S(1)}, bf16[64,128]{1,0:T(8,128)(2,1)}, u32[]{:S(2)}) copy-start(bf16[64,128]{1,0:T(8,128)(2,1)} %constant.25.clone.twice_ref) | copy-start | bytes 49156
  13.8 22.7 %copy-start.3 = (bf16[128,384]{1,0:T(8,128)(2,1)S(1)}, bf16[128,384]{1,0:T(8,128)(2,1)}, u32[]{:S(2)}) copy-start(bf16[128,384]{1,0:T(8,128)(2,1)} %constant.27.clone.inverse_ref) | copy-start | bytes 294916
  13.8 22.7 %copy-start.4 = (bf16[128,384]{1,0:T(8,128)(2,1)S(1)}, bf16[128,384]{1,0:T(8,128)(2,1)}, u32[]{:S(2)}) copy-start(bf16[128,384]{1,0:T(8,128)(2,1)} %constant.26.clone.forward_ref) | copy-start | bytes 294916
  16.5 2.0 %copy-start = (bf16[2,1024,1024]{2,1,0:T(8,128)(2,1)}, bf16[2,1024,1024]{2,1,0:T(8,128)(2,1)S(1)}, u32[]{:S(2)}) copy-start(bf16[2,1024,1024]{2,1,0:T(8,128)(2,1)S(1)} %dynamic-slice_bitcast_fusion.table_ref) | copy-start | bytes 12582916
  18.5 18.0 %all-to-all-start = ((f32[8,96,128]{2,1,0:T(8,128)}), f32[8,96,128]{2,1,0:T(8,128)S(1)}, u32[]{:S(2)}, u32[]{:S(2)}) async-start(f32[8,96,128]{2,1,0:T(8,128)} %lines.1), calls=%async_computation | async-start | bytes 786432 | tf_op jit(solution)/shard_map/all_to_all | solution.py:429
  33.3 38.5 %copy-start.7 = (f32[16]{0:T(128)S(1)}, f32[16]{0:T(128)}, u32[]{:S(2)}) copy-start(f32[16]{0:T(128)} %aex_ref.1) | copy-start | bytes 196
  55.3 2.2 %copy-start.1 = (bf16[2,1024,1024]{2,1,0:T(8,128)(2,1)S(1)}, bf16[2,1024,1024]{2,1,0:T(8,128)(2,1)}, u32[]{:S(2)}) copy-start(bf16[2,1024,1024]{2,1,0:T(8,128)(2,1)} %copy-done) | copy-start | bytes 12582916
  59.7 13.2 %all-to-all-start.2 = ((f32[4,96,256]{2,1,0:T(8,128)}), f32[4,96,256]{2,1,0:T(8,128)S(1)}, u32[]{:S(2)}, u32[]{:S(2)}) async-start(f32[4,96,256]{2,1,0:T(8,128)} %back_lines.1), calls=%async_computation.2 | async-start | bytes 786432 | tf_op jit(solution)/shard_map/all_to_all | solution.py:452
  63.2 4.4 %collective-permute-start = (f32[3,4,256]{2,1,0:T(4,128)S(1)}, f32[3,4,256]{2,1,0:T(4,128)S(1)}, u32[]{:S(2)}, u32[]{:S(2)}) collective-permute-start(f32[3,4,256]{2,1,0:T(4,128)S(1)} %get-tuple-element.6), channel_id=1, source_target_pairs={{0,1},{1,2},{2,3},{3,4},{4,5},{5,6},{6,7},{8,9},{9,10},{10,11},{11... | collective-permute-start | bytes 36872 | tf_op jit(solution)/shard_map/ppermute | solution.py:402
  66.2 5.6 %collective-permute-start.1 = (f32[3,4,256]{2,1,0:T(4,128)S(1)}, f32[3,4,256]{2,1,0:T(4,128)S(1)}, u32[]{:S(2)}, u32[]{:S(2)}) collective-permute-start(f32[3,4,256]{2,1,0:T(4,128)S(1)} %get-tuple-element.7), channel_id=1, source_target_pairs={{1,0},{2,1},{3,2},{4,3},{5,4},{6,5},{7,6},{9,8},{10,9},{11,10},{12... | collective-permute-start | bytes 36872 | tf_op jit(solution)/shard_map/ppermute | solution.py:403
where the time goes:
time: 74.3 us; the launch traced here: 73.7 us
  blocking collectives  23.6 us (32%)
  Pallas kernels  18.9 us (25%)
  starting transfers between devices  13.6 us (18%)
  local copies, waits for them, and re-layouts  8.62 us (12%)
  waiting for transfers between devices  7.36 us (10%)
  other arithmetic  0.87 us (1%)
  between operations  0.79 us (1%)
    pallas_call x6, Pallas kernels, call(): pl.pallas_call(body, out_shape=out, in_specs=ins, out_specs=jax.tree.map(...  18.9 us
    all_to_all x1, blocking collectives, per_device(): lax.all_to_all(waves, 'gy', split_axis=0, concat_axis=0, tiled=True)  15.7 us
    all_gather x1, blocking collectives, per_device(): gathered = lax.all_gather(raw, 'gx')  7.91 us
    all_to_all x1, starting transfers between devices, per_device(): lax.all_to_all(spectrum, 'gy', split_axis=0, concat_axis=0, tiled=True)  5.84 us
    unnamed x17, local copies, waits for them, and re-layouts  4.97 us
    ppermute x1, waiting for transfers between devices, per_device(): after = lax.ppermute(raw[:, :, 0], 'gy', down)  4.2 us
    all_to_all x1, starting transfers between devices, per_device(): lax.all_to_all(partial, 'gx', split_axis=0, concat_axis=0, tiled=True)  3.46 us
    all_to_all x1, waiting for transfers between devices, per_device(): lax.all_to_all(spectrum, 'gy', split_axis=0, concat_axis=0, tiled=True)  3.15 us
  transfers between devices with their start and end apart: 4, of which 2 were waited for; matrix products, arithmetic and copies ran while one was open for 0% of the time, Pallas kernels for 14%

commit v1 on v0

--- a/solution.py
+++ b/solution.py
@@ -109,6 +109,16 @@
     for index in range(1, region.shape[0]):
         result = jnp.where(labels == float(index), region[index], result)
     return result
+
+
+def pack_kernel(theta_ref, phi_ref, labels_ref, raw_ref, first_ref, last_ref):
+    height = theta_ref.shape[1]
+    values = [theta_ref[...], phi_ref[...], labels_ref[...].astype(jnp.float32)]
+    for index, value in enumerate(values):
+        for copy in range(raw_ref.shape[0]):
+            raw_ref[copy, index] = value
+        first_ref[index] = value[:, 0]
+        last_ref[index] = value[:, height - 1]
 
 
 def lines_body(raw, region, table_high, table_low):
@@ -160,12 +170,15 @@
 def tensor_kernel(kernel_ref, twice_ref, out_ref):
     twice = twice_ref[...]
 
+    unroll = 8
+
     def step(index, carry):
-        turned = dot(kernel_ref[index], twice, ((0,), (0,)))
-        out_ref[index] = turned.astype(jnp.bfloat16)
+        for offset in range(unroll):
+            turned = dot(kernel_ref[index * unroll + offset], twice, ((0,), (0,)))
+            out_ref[index * unroll + offset] = turned.astype(jnp.bfloat16)
         return carry
 
-    lax.fori_loop(0, kernel_ref.shape[0], step, 0)
+    lax.fori_loop(0, kernel_ref.shape[0] // unroll, step, 0)
 
 
 def turn(value, sign):
@@ -270,7 +283,7 @@
         out_ref[:, plane * local : (plane + 1) * local, :] = value.reshape(count_y, local, lanes)
 
 
-def exchange_kernel(raw_ref, rows_ref, place_ref, ms_ref, aex_ref, exchange_ref, unit_ref):
+def exchange_kernel(raw_ref, before_ref, after_ref, place_ref, ms_ref, aex_ref, exchange_ref, unit_ref):
     count_x = raw_ref.shape[0]
     depth, height, width = raw_ref.shape[2:]
     gx, gy, count_y = place_ref[0], place_ref[1], place_ref[2]
@@ -289,8 +302,8 @@
         [
             jnp.where(
                 row == 0,
-                jnp.broadcast_to(rows_ref[1, f][:, None, :], shape),
-                jnp.broadcast_to(rows_ref[0, f][:, None, :], shape),
+                jnp.broadcast_to(after_ref[f][:, None, :], shape),
+                jnp.broadcast_to(before_ref[f][:, None, :], shape),
             )
             for f in range(3)
         ]
@@ -376,7 +389,7 @@
         in_specs=ins,
         out_specs=jax.tree.map(lambda _: vmem, out),
         scratch_shapes=list(scratch),
-        compiler_params=pltpu.CompilerParams(vmem_limit_bytes=40 << 20),
+        compiler_params=pltpu.CompilerParams(vmem_limit_bytes=16 << 20),
         cost_estimate=pl.CostEstimate(flops=flops, bytes_accessed=size, transcendentals=0),
         name=name,
     )(*operands)
@@ -395,12 +408,18 @@
     lines = 3 * depth * height
     whole_y = count_y * height
 
-    raw = jnp.stack([theta, phi, labels.astype(jnp.float32)])
-    gathered = lax.all_gather(raw, "gx")
+    packed, first, last = call(
+        pack_kernel,
+        [f32(count_x, 3, depth, height, width), f32(3, depth, width), f32(3, depth, width)],
+        [vmem] * 3,
+        (theta, phi, labels),
+        name="pack",
+    )
+    gathered = lax.all_to_all(packed, "gx", split_axis=0, concat_axis=0, tiled=True)
     up = [(i, i + 1) for i in range(count_y - 1)]
     down = [(j, i) for i, j in up]
-    before = lax.ppermute(raw[:, :, height - 1], "gy", up)
-    after = lax.ppermute(raw[:, :, 0], "gy", down)
+    before = lax.ppermute(last, "gy", up)
+    after = lax.ppermute(first, "gy", down)
 
     table = line_table(count_x, count_y, width, rows)
     if table is None:
@@ -427,7 +446,7 @@
         name="lines",
     )
     columns = lax.all_to_all(spectrum, "gy", split_axis=0, concat_axis=0, tiled=True)
-    scale = -1.0 / (8.0 * depth * 0 + 2 * depth * 2 * whole_y * 2 * count_x * width)
+    scale = -1.0 / (2 * depth * 2 * whole_y * 2 * count_x * width)
     waves = call(
         functools.partial(waves_kernel, scale),
         f32(count_y, lines, lanes),
@@ -441,6 +460,16 @@
         name="waves",
     )
     returned = lax.all_to_all(waves, "gy", split_axis=0, concat_axis=0, tiled=True)
+    place = jnp.stack([gx, gy, jnp.int32(count_y)]).astype(jnp.int32)
+    exchange, unit = call(
+        exchange_kernel,
+        [f32(3, depth, height, width), f32(3, depth, height, width)],
+        [vmem, vmem, vmem, smem, smem, smem],
+        (gathered, before, after, place, ms_region, aex_region),
+        flops=300 * depth * height * width,
+        name="exchange",
+    )
+    returned, exchange, unit = lax.optimization_barrier((returned, exchange, unit))
     partial = call(
         back_lines_kernel,
         f32(count_x, lines, width),
@@ -450,15 +479,6 @@
         name="back_lines",
     )
     parts = lax.all_to_all(partial, "gx", split_axis=0, concat_axis=0, tiled=True)
-    place = jnp.stack([gx, gy, jnp.int32(count_y)]).astype(jnp.int32)
-    exchange, unit = call(
-        exchange_kernel,
-        [f32(3, depth, height, width), f32(3, depth, height, width)],
-        [vmem, vmem, smem, smem, smem],
-        (gathered, jnp.stack([before, after]), place, ms_region, aex_region),
-        flops=300 * depth * height * width,
-        name="exchange",
-    )
     field, predicted = call(
         final_kernel,
         [f32(3, depth, height, width), f32(3, depth, height, width)],

time: 74.3 us -> 72.2 us (0.972)
  blocking collectives: 23.6 us -> 9.84 us
  waiting for transfers between devices: 7.36 us -> 17.7 us
  Pallas kernels: 18.9 us -> 12.2 us
  starting transfers between devices: 13.6 us -> 19.7 us
  local copies, waits for them, and re-layouts: 8.62 us -> 11.3 us
  other arithmetic: 0.87 us -> 0.08 us
    all_gather x1 -> x0, blocking collectives: 7.91 us -> none  [per_device(): gathered = lax.all_gather(raw, 'gx')]
    all_to_all x1, waiting for transfers between devices: 3.15 us -> 9.95 us  [per_device(): lax.all_to_all(spectrum, 'gy', split_axis=0, concat_axis=0, tiled=True)]
    pallas_call x6 -> x7, Pallas kernels: 18.9 us -> 12.2 us  [call(): pl.pallas_call(body, out_shape=out, in_specs=ins, out_specs=jax.tree.map(...]
    all_to_all x1, blocking collectives: 15.7 us -> 9.84 us  [per_device(): lax.all_to_all(partial, 'gx', split_axis=0, concat_axis=0, tiled=True)]
    all_to_all x1 -> x2, starting transfers between devices: 3.46 us -> 7.84 us  [the longest x1 4.21 us: per_device(): lax.all_to_all(packed, 'gx', split_axis=0, concat_axis=0, tiled=True)]
    all_to_all x1 -> x2, waiting for transfers between devices: 0.01 us -> 3.55 us  [the longest x1 2.85 us: per_device(): lax.all_to_all(packed, 'gx', split_axis=0, concat_axis=0, tiled=True)]
    squeeze x1, local copies, waits for them, and re-layouts: 2.64 us -> 4.59 us  [per_device(): table = lax.dynamic_index_in_dim(jnp.asarray(table), gx, 0, keepdims=False)]
    unnamed x17 -> x22, local copies, waits for them, and re-layouts: 4.97 us -> 6.66 us
  transfers between devices with their start and end apart: 4 -> 5, of which waited for: 2 -> 4; matrix products, arithmetic and copies ran while one was open for 0% -> 7% of each run, Pallas kernels for 14% -> 4%
where the time goes in v1:
time: 72.2 us; the launch traced here: 71.5 us
  starting transfers between devices  19.7 us (27%)
  waiting for transfers between devices  17.7 us (25%)
  Pallas kernels  12.2 us (17%)
  local copies, waits for them, and re-layouts  11.3 us (16%)
  blocking collectives  9.84 us (14%)
    pallas_call x7, Pallas kernels, call(): pl.pallas_call(body, out_shape=out, in_specs=ins, out_specs=jax.tree.map(...  12.2 us
    all_to_all x1, waiting for transfers between devices, per_device(): lax.all_to_all(spectrum, 'gy', split_axis=0, concat_axis=0, tiled=True)  9.95 us
    all_to_all x1, blocking collectives, per_device(): lax.all_to_all(partial, 'gx', split_axis=0, concat_axis=0, tiled=True)  9.84 us
    unnamed x22, local copies, waits for them, and re-layouts  6.66 us
    all_to_all x1, starting transfers between devices, per_device(): lax.all_to_all(spectrum, 'gy', split_axis=0, concat_axis=0, tiled=True)  6.64 us
    squeeze x1, local copies, waits for them, and re-layouts, per_device(): table = lax.dynamic_index_in_dim(jnp.asarray(table), gx, 0, keepdims=False)  4.59 us
    all_to_all x1, starting transfers between devices, per_device(): lax.all_to_all(packed, 'gx', split_axis=0, concat_axis=0, tiled=True)  4.21 us
    ppermute x1, waiting for transfers between devices, per_device(): after = lax.ppermute(first, 'gy', down)  4.2 us
  transfers between devices with their start and end apart: 5, of which 4 were waited for; matrix products, arithmetic and copies ran while one was open for 7% of the time, Pallas kernels for 4%

profile of v1, /device:TPU:0, one launch (start us, length us, event | category | flops | bytes accessed | tf_op | source)
XLA Modules:
  0.0 71.5 jit_solution(3844154643837303465)
XLA Ops:
  0.6 0.0 copy-start.5
  0.6 0.7 %copy-done.5 = f32[4,8,256]{2,1,0:T(8,128)S(1)} copy-done((f32[4,8,256]{2,1,0:T(8,128)S(1)}, f32[4,8,256]{2,1,0:T(8,128)}, u32[]{:S(2)}) %copy-start.5) | copy-done | bytes 32792
  1.4 0.8 %copy-done.6 = f32[4,8,256]{2,1,0:T(8,128)S(1)} copy-done((f32[4,8,256]{2,1,0:T(8,128)S(1)}, f32[4,8,256]{2,1,0:T(8,128)}, u32[]{:S(2)}) %copy-start.6) | copy-done | bytes 32792
  2.1 0.8 %copy-done.7 = s32[4,8,256]{2,1,0:T(8,128)S(1)} copy-done((s32[4,8,256]{2,1,0:T(8,128)S(1)}, s32[4,8,256]{2,1,0:T(8,128)}, u32[]{:S(2)}) %copy-start.7) | copy-done | bytes 32792
  2.9 0.8 %pack.1 = (f32[4,3,4,8,256]{4,3,2,1,0:T(8,128)}, f32[3,4,256]{2,1,0:T(4,128)S(1)}, f32[3,4,256]{2,1,0:T(4,128)S(1)}) custom-call(f32[4,8,256]{2,1,0:T(8,128)S(1)} %copy-done.5, f32[4,8,256]{2,1,0:T(8,128)S(1)} %copy-done.6, s32[4,8,256]{2,1,0:T(8,128)S(1)} %copy-done.7), custom_call_target="tpu_custom_call" | custom-call | bytes 516096 | tf_op jit(solution)/shard_map/pack/pallas_call | solution.py:386
  3.7 4.2 %all-to-all-start = ((f32[4,3,4,8,256]{4,3,2,1,0:T(8,128)}), f32[4,3,4,8,256]{4,3,2,1,0:T(8,128)S(1)}, u32[]{:S(2)}, u32[]{:S(2)}) async-start(f32[4,3,4,8,256]{4,3,2,1,0:T(8,128)} %get-tuple-element.10), calls=%async_computation | async-start | bytes 786432 | tf_op jit(solution)/shard_map/all_to_all | solution.py:418
  7.9 4.6 %dynamic-slice_bitcast_fusion.table_ref = bf16[2,1024,1024]{2,1,0:T(8,128)(2,1)} fusion(bf16[4,2,1024,1024]{3,2,1,0:T(8,128)(2,1)} %constant.24.clone, s32[]{:T(128)S(6)} %select_n.4), kind=kLoop, calls=%fused_computation | loop fusion | bytes 8388612 | tf_op jit(solution)/shard_map/jit(dynamic_index_in_dim)/squeeze | solution.py:428
  12.5 2.9 %all-to-all-done.raw_ref = f32[4,3,4,8,256]{4,3,2,1,0:T(8,128)S(1)} async-done(((f32[4,3,4,8,256]{4,3,2,1,0:T(8,128)}), f32[4,3,4,8,256]{4,3,2,1,0:T(8,128)S(1)}, u32[]{:S(2)}, u32[]{:S(2)}) %all-to-all-start) | async-done | bytes 393248 | tf_op jit(solution)/shard_map/all_to_all | solution.py:418
  15.3 0.0 copy-done.9
  15.3 2.2 %copy-done = bf16[2,1024,1024]{2,1,0:T(8,128)(2,1)S(1)} copy-done((bf16[2,1024,1024]{2,1,0:T(8,128)(2,1)S(1)}, bf16[2,1024,1024]{2,1,0:T(8,128)(2,1)}, u32[]{:S(2)}) %copy-start) | copy-done | bytes 4194328
  17.5 2.6 %lines.1 = f32[8,96,128]{2,1,0:T(8,128)} custom-call(f32[4,3,4,8,256]{4,3,2,1,0:T(8,128)S(1)} %all-to-all-done.raw_ref, f32[16]{0:T(128)S(1)} %copy-done.9, bf16[2,1024,1024]{2,1,0:T(8,128)(2,1)S(1)} %copy-done), custom_call_target="tpu_custom_call" | custom-call | flops 603979776 | bytes 4980800 | tf_op jit(solution)/shard_map/lines/pallas_call | solution.py:386
  20.2 6.6 %all-to-all-start.1 = ((f32[8,96,128]{2,1,0:T(8,128)}), f32[8,96,128]{2,1,0:T(8,128)S(1)}, u32[]{:S(2)}, u32[]{:S(2)}) async-start(f32[8,96,128]{2,1,0:T(8,128)} %lines.1), calls=%async_computation.1 | async-start | bytes 786432 | tf_op jit(solution)/shard_map/all_to_all | solution.py:448
  26.8 0.0 copy-done.2
  26.8 0.0 copy-done.8
  26.8 1.6 %tensor.1.tensor_ref = bf16[48,128,128]{2,1,0:T(8,128)(2,1)S(1)} custom-call(bf16[48,64,128]{2,1,0:T(8,128)(2,1)S(1)} %bitcast.5, bf16[64,128]{1,0:T(8,128)(2,1)S(1)} %copy-done.8), custom_call_target="tpu_custom_call" | custom-call | flops 100663296 | bytes 2375680 | tf_op jit(solution)/shard_map/tensor/pallas_call | solution.py:386
  28.4 10.0 %all-to-all-done.1.spec_ref = f32[8,96,128]{2,1,0:T(8,128)S(1)} async-done(((f32[8,96,128]{2,1,0:T(8,128)}), f32[8,96,128]{2,1,0:T(8,128)S(1)}, u32[]{:S(2)}, u32[]{:S(2)}) %all-to-all-start.1) | async-done | bytes 393248 | tf_op jit(solution)/shard_map/all_to_all | solution.py:448
  38.4 0.0 copy-done.3
  38.4 0.0 copy-done.4
  38.4 3.9 %waves.1 = f32[8,96,128]{2,1,0:T(8,128)} custom-call(f32[8,96,128]{2,1,0:T(8,128)S(1)} %all-to-all-done.1.spec_ref, bf16[48,128,128]{2,1,0:T(8,128)(2,1)S(1)} %tensor.1.tensor_ref, bf16[128,384]{1,0:T(8,128)(2,1)S(1)} %copy-done.4, bf16[128,384]{1,0:T(8,128)(2,1)S(1)} %copy-done.3), custom_call_target="tpu_custom_call" | custom-call | flops 125829120 | bytes 2555904 | tf_op jit(solution)/shard_map/waves/pallas_call | solution.py:386
  42.3 3.6 %all-to-all-start.2 = ((f32[8,96,128]{2,1,0:T(8,128)}), f32[8,96,128]{2,1,0:T(8,128)S(1)}, u32[]{:S(2)}, u32[]{:S(2)}) async-start(f32[8,96,128]{2,1,0:T(8,128)} %waves.1), calls=%async_computation.2 | async-start | bytes 786432 | tf_op jit(solution)/shard_map/all_to_all | solution.py:462
  45.9 3.9 %collective-permute-start = (f32[3,4,256]{2,1,0:T(4,128)S(1)}, f32[3,4,256]{2,1,0:T(4,128)S(1)}, u32[]{:S(2)}, u32[]{:S(2)}) collective-permute-start(f32[3,4,256]{2,1,0:T(4,128)S(1)} %get-tuple-element.11), channel_id=1, source_target_pairs={{0,1},{1,2},{2,3},{3,4},{4,5},{5,6},{6,7},{8,9},{9,10},{10,11},{11... | collective-permute-start | bytes 36872 | tf_op jit(solution)/shard_map/ppermute | solution.py:421
  49.8 1.3 %collective-permute-start.1 = (f32[3,4,256]{2,1,0:T(4,128)S(1)}, f32[3,4,256]{2,1,0:T(4,128)S(1)}, u32[]{:S(2)}, u32[]{:S(2)}) collective-permute-start(f32[3,4,256]{2,1,0:T(4,128)S(1)} %get-tuple-element.12), channel_id=1, source_target_pairs={{1,0},{2,1},{3,2},{4,3},{5,4},{6,5},{7,6},{9,8},{10,9},{11,10},{12... | collective-permute-start | bytes 36872 | tf_op jit(solution)/shard_map/ppermute | solution.py:422
  51.1 0.1 pad_add_fusion.place_ref
  51.2 0.0 collective-permute-done.before_ref
  51.2 4.2 %collective-permute-done.1.after_ref = f32[3,4,256]{2,1,0:T(4,128)S(1)} collective-permute-done((f32[3,4,256]{2,1,0:T(4,128)S(1)}, f32[3,4,256]{2,1,0:T(4,128)S(1)}, u32[]{:S(2)}, u32[]{:S(2)}) %collective-permute-start.1) | collective-permute-done | bytes 12320 | tf_op jit(solution)/shard_map/ppermute | solution.py:422
  55.4 0.0 copy-done.10
  55.4 1.1 %exchange.1 = (f32[3,4,8,256]{3,2,1,0:T(8,128)S(1)}, f32[3,4,8,256]{3,2,1,0:T(8,128)S(1)}) custom-call(f32[4,3,4,8,256]{4,3,2,1,0:T(8,128)S(1)} %all-to-all-done.raw_ref, f32[3,4,256]{2,1,0:T(4,128)S(1)} %collective-permute-done.before_ref, f32[3,4,256]{2,1,0:T(4,128)S(1)} %collective-permute-done.1.after_ref, s32[3]{0:T(128)S(1)} %pad_add_fusion.place_ref, ...), custom_call_target="tpu_custom_call" | custom-call | flops 2457600 | bytes 614540 | tf_op jit(solution)/shard_map/exchange/pallas_call | solution.py:386
  56.5 0.7 all-to-all-done.2.spectrum_ref
  57.2 2.2 %copy-done.1 = bf16[2,1024,1024]{2,1,0:T(8,128)(2,1)S(1)} copy-done((bf16[2,1024,1024]{2,1,0:T(8,128)(2,1)S(1)}, bf16[2,1024,1024]{2,1,0:T(8,128)(2,1)}, u32[]{:S(2)}) %copy-start.1) | copy-done | bytes 4194328
  59.4 1.5 %back_lines.1 = f32[4,96,256]{2,1,0:T(8,128)S(1)} custom-call(f32[8,96,128]{2,1,0:T(8,128)S(1)} %all-to-all-done.2.spectrum_ref, bf16[2,1024,1024]{2,1,0:T(8,128)(2,1)S(1)} %copy-done.1), custom_call_target="tpu_custom_call" | custom-call | flops 603979776 | bytes 4980736 | tf_op jit(solution)/shard_map/back_lines/pallas_call | solution.py:386
  60.9 9.8 %all_to_all.20.parts_ref = f32[4,96,256]{2,1,0:T(8,128)S(1)} all-to-all(f32[4,96,256]{2,1,0:T(8,128)S(1)} %back_lines.1), channel_id=1, replica_groups=mesh['gx'=4,'gy'=8] {'gx'}, dimensions={0} | all-to-all | bytes 786432 | tf_op jit(solution)/shard_map/all_to_all | solution.py:481
  70.7 0.7 %predict.1 = (f32[3,4,8,256]{3,2,1,0:T(8,128)}, f32[3,4,8,256]{3,2,1,0:T(8,128)}) custom-call(f32[4,96,256]{2,1,0:T(8,128)S(1)} %all_to_all.20.parts_ref, f32[3,4,8,256]{3,2,1,0:T(8,128)S(1)} %get-tuple-element.16.exchange_ref, f32[3,4,8,256]{3,2,1,0:T(8,128)S(1)} %get-tuple-element.17.unit_ref), custom_call_target="tpu_custom_call" | custom-call | flops 491520 | bytes 786432 | tf_op jit(solution)/shard_map/predict/pallas_call | solution.py:386
  (10 shorter events, 0.0 us)
Async XLA Ops:
  0.6 0.8 %copy-start.5 = (f32[4,8,256]{2,1,0:T(8,128)S(1)}, f32[4,8,256]{2,1,0:T(8,128)}, u32[]{:S(2)}) copy-start(f32[4,8,256]{2,1,0:T(8,128)} %theta_ref.1) | copy-start | bytes 98308
  1.4 0.8 %copy-start.6 = (f32[4,8,256]{2,1,0:T(8,128)S(1)}, f32[4,8,256]{2,1,0:T(8,128)}, u32[]{:S(2)}) copy-start(f32[4,8,256]{2,1,0:T(8,128)} %phi_ref.1) | copy-start | bytes 98308
  2.1 0.8 %copy-start.7 = (s32[4,8,256]{2,1,0:T(8,128)S(1)}, s32[4,8,256]{2,1,0:T(8,128)}, u32[]{:S(2)}) copy-start(s32[4,8,256]{2,1,0:T(8,128)} %labels_ref.1) | copy-start | bytes 98308
  3.7 11.7 %all-to-all-start = ((f32[4,3,4,8,256]{4,3,2,1,0:T(8,128)}), f32[4,3,4,8,256]{4,3,2,1,0:T(8,128)S(1)}, u32[]{:S(2)}, u32[]{:S(2)}) async-start(f32[4,3,4,8,256]{4,3,2,1,0:T(8,128)} %get-tuple-element.10), calls=%async_computation | async-start | bytes 786432 | tf_op jit(solution)/shard_map/all_to_all | solution.py:418
  7.9 7.4 %copy-start.9 = (f32[16]{0:T(128)S(1)}, f32[16]{0:T(128)}, u32[]{:S(2)}) copy-start(f32[16]{0:T(128)} %ms_ref.1) | copy-start | bytes 196
  15.3 2.2 %copy-start = (bf16[2,1024,1024]{2,1,0:T(8,128)(2,1)S(1)}, bf16[2,1024,1024]{2,1,0:T(8,128)(2,1)}, u32[]{:S(2)}) copy-start(bf16[2,1024,1024]{2,1,0:T(8,128)(2,1)} %dynamic-slice_bitcast_fusion.table_ref) | copy-start | bytes 12582916
  17.5 9.3 %copy-start.2 = (bf16[6,8,64,128]{3,2,1,0:T(8,128)(2,1)S(1)}, bf16[6,8,64,128]{3,2,1,0:T(8,128)(2,1)}, u32[]{:S(2)}) copy-start(bf16[6,8,64,128]{3,2,1,0:T(8,128)(2,1)} %param.15) | copy-start | bytes 2359300
  17.5 9.3 %copy-start.8 = (bf16[64,128]{1,0:T(8,128)(2,1)S(1)}, bf16[64,128]{1,0:T(8,128)(2,1)}, u32[]{:S(2)}) copy-start(bf16[64,128]{1,0:T(8,128)(2,1)} %constant.25.clone.twice_ref) | copy-start | bytes 49156
  17.5 20.8 %copy-start.3 = (bf16[128,384]{1,0:T(8,128)(2,1)S(1)}, bf16[128,384]{1,0:T(8,128)(2,1)}, u32[]{:S(2)}) copy-start(bf16[128,384]{1,0:T(8,128)(2,1)} %constant.27.clone.inverse_ref) | copy-start | bytes 294916
  17.5 20.8 %copy-start.4 = (bf16[128,384]{1,0:T(8,128)(2,1)S(1)}, bf16[128,384]{1,0:T(8,128)(2,1)}, u32[]{:S(2)}) copy-start(bf16[128,384]{1,0:T(8,128)(2,1)} %constant.26.clone.forward_ref) | copy-start | bytes 294916
  20.2 35.2 %copy-start.10 = (f32[16]{0:T(128)S(1)}, f32[16]{0:T(128)}, u32[]{:S(2)}) copy-start(f32[16]{0:T(128)} %aex_ref.1) | copy-start | bytes 196
  20.2 18.2 %all-to-all-start.1 = ((f32[8,96,128]{2,1,0:T(8,128)}), f32[8,96,128]{2,1,0:T(8,128)S(1)}, u32[]{:S(2)}, u32[]{:S(2)}) async-start(f32[8,96,128]{2,1,0:T(8,128)} %lines.1), calls=%async_computation.1 | async-start | bytes 786432 | tf_op jit(solution)/shard_map/all_to_all | solution.py:448
  42.3 15.0 %all-to-all-start.2 = ((f32[8,96,128]{2,1,0:T(8,128)}), f32[8,96,128]{2,1,0:T(8,128)S(1)}, u32[]{:S(2)}, u32[]{:S(2)}) async-start(f32[8,96,128]{2,1,0:T(8,128)} %waves.1), calls=%async_computation.2 | async-start | bytes 786432 | tf_op jit(solution)/shard_map/all_to_all | solution.py:462
  45.9 5.3 %collective-permute-start = (f32[3,4,256]{2,1,0:T(4,128)S(1)}, f32[3,4,256]{2,1,0:T(4,128)S(1)}, u32[]{:S(2)}, u32[]{:S(2)}) collective-permute-start(f32[3,4,256]{2,1,0:T(4,128)S(1)} %get-tuple-element.11), channel_id=1, source_target_pairs={{0,1},{1,2},{2,3},{3,4},{4,5},{5,6},{6,7},{8,9},{9,10},{10,11},{11... | collective-permute-start | bytes 36872 | tf_op jit(solution)/shard_map/ppermute | solution.py:421
  49.8 5.6 %collective-permute-start.1 = (f32[3,4,256]{2,1,0:T(4,128)S(1)}, f32[3,4,256]{2,1,0:T(4,128)S(1)}, u32[]{:S(2)}, u32[]{:S(2)}) collective-permute-start(f32[3,4,256]{2,1,0:T(4,128)S(1)} %get-tuple-element.12), channel_id=1, source_target_pairs={{1,0},{2,1},{3,2},{4,3},{5,4},{6,5},{7,6},{9,8},{10,9},{11,10},{12... | collective-permute-start | bytes 36872 | tf_op jit(solution)/shard_map/ppermute | solution.py:422
  57.2 2.2 %copy-start.1 = (bf16[2,1024,1024]{2,1,0:T(8,128)(2,1)S(1)}, bf16[2,1024,1024]{2,1,0:T(8,128)(2,1)}, u32[]{:S(2)}) copy-start(bf16[2,1024,1024]{2,1,0:T(8,128)(2,1)} %dynamic-slice_bitcast_fusion.table_ref) | copy-start | bytes 12582916

commit v2 on v1

--- a/solution.py
+++ b/solution.py
@@ -46,7 +46,7 @@
     )
     angle = (place * wave % (2 * cells)) * (2.0 * math.pi / (2 * cells))
     table = np.stack([np.cos(angle), -np.sin(angle)], 3)
-    table = table.reshape(count_x, cells, count_y * 2 * rows)
+    table = table.reshape(count_x, count_x, width, count_y * 2 * rows)
     high, low = split_table(table)
     return np.stack([high, low], 1)
 
@@ -61,7 +61,7 @@
     )
     angle = (place * wave % (2 * cells)).astype(jnp.float32) * (math.pi / cells)
     table = jnp.stack([jnp.cos(angle), -jnp.sin(angle)], 2).reshape(cells, count_y * 2 * rows)
-    return jnp.stack(split_high(table))
+    return jnp.stack(split_high(table)).reshape(1, 2, count_x, width, count_y * 2 * rows)
 
 
 def column_tables(height):
@@ -111,60 +111,80 @@
     return result
 
 
-def pack_kernel(theta_ref, phi_ref, labels_ref, raw_ref, first_ref, last_ref):
+def pack_kernel(theta_ref, phi_ref, labels_ref, raw_ref, first_ref, last_ref, angle, label, sems):
     height = theta_ref.shape[1]
-    values = [theta_ref[...], phi_ref[...], labels_ref[...].astype(jnp.float32)]
-    for index, value in enumerate(values):
-        for copy in range(raw_ref.shape[0]):
-            raw_ref[copy, index] = value
+    copies = [
+        pltpu.make_async_copy(theta_ref, angle.at[0], sems.at[0]),
+        pltpu.make_async_copy(phi_ref, angle.at[1], sems.at[1]),
+        pltpu.make_async_copy(labels_ref, label, sems.at[2]),
+    ]
+    for copy in copies:
+        copy.start()
+    for copy in copies:
+        copy.wait()
+    for index, value in enumerate((angle[0], angle[1], label[...].astype(jnp.float32))):
+        raw_ref[index] = value
         first_ref[index] = value[:, 0]
         last_ref[index] = value[:, height - 1]
 
 
-def lines_body(raw, region, table_high, table_low):
-    blocks = []
-    for theta, phi, labels in raw:
-        unit = directions(theta, phi)
-        saturation = looked_up(labels, region)
-        rows = theta.shape[0] * theta.shape[1]
-        blocks.append(
-            jnp.concatenate([(part * saturation).reshape(rows, -1) for part in unit], 0)
+def table_copies(table_ref, table, sems, gx):
+    mine = gx if table_ref.shape[0] > 1 else 0
+    copies = []
+    for number in range(table_ref.shape[2]):
+        block = lax.bitwise_xor(gx, number)
+        copies.append(
+            pltpu.make_async_copy(table_ref.at[mine, :, block], table.at[number], sems.at[number])
         )
-    moment = jnp.concatenate(blocks, 1)
-    high, low = split_high(moment)
-    both = dot(jnp.concatenate([high, low], 0), table_high)
-    lines = moment.shape[0]
-    return both[:lines] + both[lines:] + dot(high, table_low)
-
-
-def lines_kernel(raw_ref, region_ref, table_ref, out_ref):
-    raw = [[raw_ref[g, f] for f in range(3)] for g in range(raw_ref.shape[0])]
-    result = lines_body(raw, region_ref, table_ref[0], table_ref[1])
-    lanes = out_ref.shape[2]
-    for index in range(out_ref.shape[0]):
-        out_ref[index] = result[:, index * lanes : (index + 1) * lanes]
-
-
-def back_lines_body(spectrum, table_high, table_low, groups):
-    high, low = split_high(spectrum)
+    for copy in copies:
+        copy.start()
+    return copies
+
+
+def lines_kernel(count_x, count_y, *refs):
+    raw_refs, (region, place, table_ref) = refs[:count_x], refs[count_x : count_x + 3]
+    out_refs = refs[count_x + 3 : count_x + 3 + count_y]
+    table, ordered, sems = refs[count_x + 3 + count_y :]
+    gx, gy = place[0], place[1]
+    copies = table_copies(table_ref, table, sems, gx)
+    halves = []
+    for raw_ref in raw_refs:
+        unit = directions(raw_ref[0], raw_ref[1])
+        saturation = looked_up(raw_ref[2], region)
+        rows = saturation.shape[0] * saturation.shape[1]
+        block = jnp.concatenate([(part * saturation).reshape(rows, -1) for part in unit], 0)
+        halves.append(split_high(block))
+    lines = 3 * rows
+    total = None
+    for (high, low), copy, number in zip(halves, copies, range(count_x)):
+        copy.wait()
+        both = dot(jnp.concatenate([high, low], 0), table[number, 0])
+        part = both[:lines] + both[lines:] + dot(high, table[number, 1])
+        total = part if total is None else total + part
+    lanes = ordered.shape[2]
+    for index in range(count_y):
+        ordered[index] = total[:, index * lanes : (index + 1) * lanes]
+    for number in range(count_y):
+        out_refs[number][...] = ordered[lax.bitwise_xor(gy, number)]
+
+
+def back_lines_kernel(count_x, count_y, *refs):
+    in_refs, (place, table_ref) = refs[:count_y], refs[count_y : count_y + 2]
+    out_refs = refs[count_y + 2 : count_y + 2 + count_x]
+    table, ordered, sems = refs[count_y + 2 + count_x :]
+    gx, gy = place[0], place[1]
+    copies = table_copies(table_ref, table, sems, gx)
+    for number in range(count_y):
+        ordered[lax.bitwise_xor(gy, number)] = in_refs[number][...]
+    high, low = split_high(jnp.concatenate([ordered[g] for g in range(count_y)], 1))
     both = jnp.concatenate([high, low], 0)
-    lines = spectrum.shape[0]
-    width = table_high.shape[0] // groups
-    result = []
-    for index in range(groups):
-        rows = slice(index * width, (index + 1) * width)
-        wide = dot(both, table_high[rows], ((1,), (1,)))
-        result.append(
-            wide[:lines] + wide[lines:] + dot(high, table_low[rows], ((1,), (1,)))
+    lines = high.shape[0]
+    for number in range(count_x):
+        copies[number].wait()
+        wide = dot(both, table[number, 0], ((1,), (1,)))
+        out_refs[number][...] = (
+            wide[:lines] + wide[lines:] + dot(high, table[number, 1], ((1,), (1,)))
         )
-    return result
-
-
-def back_lines_kernel(spectrum_ref, table_ref, out_ref):
-    spectrum = jnp.concatenate([spectrum_ref[g] for g in range(spectrum_ref.shape[0])], 1)
-    parts = back_lines_body(spectrum, table_ref[0], table_ref[1], out_ref.shape[0])
-    for index, part in enumerate(parts):
-        out_ref[index] = part
 
 
 def tensor_kernel(kernel_ref, twice_ref, out_ref):
@@ -231,8 +251,14 @@
     return out
 
 
-def waves_kernel(scale, spec_ref, tensor_ref, forward_ref, inverse_ref, out_ref, wave_ref, back_ref):
-    count_y, lines, lanes = spec_ref.shape
+def waves_kernel(scale, count_y, *refs):
+    spec_refs, (place, tensor_ref, forward_ref, inverse_ref) = refs[:count_y], refs[count_y : count_y + 4]
+    out_refs = refs[count_y + 4 : 2 * count_y + 4]
+    ordered, wave_ref, back_ref = refs[2 * count_y + 4 :]
+    gy = place[1]
+    lines, lanes = spec_refs[0].shape
+    for number in range(count_y):
+        ordered[lax.bitwise_xor(gy, number)] = spec_refs[number][...]
     local = 8
     planes = lines // local
     height = count_y * local
@@ -241,7 +267,7 @@
     ).astype(jnp.float32)
     columns = []
     for plane in range(planes):
-        value = spec_ref[:, plane * local : (plane + 1) * local, :].reshape(height, lanes)
+        value = ordered[:, plane * local : (plane + 1) * local, :].reshape(height, lanes)
         value = jnp.concatenate([value, turn(value, sign)], 0)
         high, low = split_high(value)
         columns.append(jnp.concatenate([high, low, high], 0))
@@ -268,25 +294,30 @@
         for part in range(3):
             layer = layers_inverse(image[part], sign)
             for z in range(depth):
-                place = slice((part * depth + z) * lanes, (part * depth + z + 1) * lanes)
+                spot = slice((part * depth + z) * lanes, (part * depth + z + 1) * lanes)
                 high, low = split_high(layer[z] * scale)
-                back_ref[rows, place] = high
-                back_ref[pl.ds(pl.multiple_of(double + index * chunk, chunk), chunk), place] = low
-                back_ref[pl.ds(pl.multiple_of(2 * double + index * chunk, chunk), chunk), place] = high
+                back_ref[rows, spot] = high
+                back_ref[pl.ds(pl.multiple_of(double + index * chunk, chunk), chunk), spot] = low
+                back_ref[pl.ds(pl.multiple_of(2 * double + index * chunk, chunk), chunk), spot] = high
         return carry
 
     lax.fori_loop(0, double // chunk, step, 0)
     back = dot(inverse_ref[...], back_ref[...])
     for plane in range(planes):
-        place = slice(plane * lanes, (plane + 1) * lanes)
-        value = back[:height, place] - turn(back[height:, place], sign)
-        out_ref[:, plane * local : (plane + 1) * local, :] = value.reshape(count_y, local, lanes)
-
-
-def exchange_kernel(raw_ref, before_ref, after_ref, place_ref, ms_ref, aex_ref, exchange_ref, unit_ref):
-    count_x = raw_ref.shape[0]
+        part = slice(plane * lanes, (plane + 1) * lanes)
+        value = back[:height, part] - turn(back[height:, part], sign)
+        ordered[:, plane * local : (plane + 1) * local, :] = value.reshape(count_y, local, lanes)
+    for number in range(count_y):
+        out_refs[number][...] = ordered[lax.bitwise_xor(gy, number)]
+
+
+def exchange_kernel(count_x, count_y, *refs):
+    raw_refs, (before_ref, after_ref, place, ms_ref, aex_ref) = refs[:count_x], refs[count_x : count_x + 5]
+    exchange_ref, unit_ref, raw_ref = refs[count_x + 5 :]
     depth, height, width = raw_ref.shape[2:]
-    gx, gy, count_y = place_ref[0], place_ref[1], place_ref[2]
+    gx, gy = place[0], place[1]
+    for number in range(count_x):
+        raw_ref[lax.bitwise_xor(gx, number)] = raw_refs[number][...]
     left, right = jnp.maximum(gx - 1, 0), jnp.minimum(gx + 1, count_x - 1)
     shape = (depth, height, width)
     lane = lax.broadcasted_iota(jnp.int32, shape, 2)
@@ -295,7 +326,7 @@
     def quantities(values):
         return directions(values[0], values[1]) + [looked_up(values[2], aex_ref)]
 
-    raw = [raw_ref[gx, f] for f in range(3)]
+    raw = [raw_refs[0][f] for f in range(3)]
     here = quantities(raw)
     side = quantities([jnp.where(lane == 0, raw_ref[right, f], raw_ref[left, f]) for f in range(3)])
     above = quantities(
@@ -352,15 +383,16 @@
     ]
 
 
-def final_kernel(parts_ref, exchange_ref, unit_ref, field_ref, predicted_ref):
+def final_kernel(count_x, *refs):
+    part_refs, (exchange_ref, unit_ref, field_ref, predicted_ref) = refs[:count_x], refs[count_x:]
     depth, height, width = unit_ref.shape[1:]
     rows = depth * height
     unit, field = [], []
     for c in range(3):
         place = slice(c * rows, (c + 1) * rows)
-        total = parts_ref[0, place]
-        for index in range(1, parts_ref.shape[0]):
-            total = total + parts_ref[index, place]
+        total = part_refs[0][place]
+        for part_ref in part_refs[1:]:
+            total = total + part_ref[place]
         field.append(exchange_ref[c] + total.reshape(depth, height, width))
         unit.append(unit_ref[c])
         field_ref[c] = field[c]
@@ -377,9 +409,14 @@
 
 vmem = pl.BlockSpec(memory_space=pltpu.VMEM)
 smem = pl.BlockSpec(memory_space=pltpu.SMEM)
-
-
-def call(body, out, ins, operands, scratch=(), flops=0, name=None):
+hbm = pl.BlockSpec(memory_space=pltpu.HBM)
+
+
+def call(body, out, ins, operands, scratch=(), flops=0, name=None, grant=16 << 20):
+    operands = [
+        pltpu.with_memory_space_constraint(o, pltpu.HBM) if i is hbm else o
+        for i, o in zip(ins, operands)
+    ]
     size = sum(math.prod(o.shape) * o.dtype.itemsize for o in operands)
     outs = out if isinstance(out, (list, tuple)) else [out]
     size += sum(math.prod(o.shape) * o.dtype.itemsize for o in outs)
@@ -389,7 +426,7 @@
         in_specs=ins,
         out_specs=jax.tree.map(lambda _: vmem, out),
         scratch_shapes=list(scratch),
-        compiler_params=pltpu.CompilerParams(vmem_limit_bytes=16 << 20),
+        compiler_params=pltpu.CompilerParams(vmem_limit_bytes=grant),
         cost_estimate=pl.CostEstimate(flops=flops, bytes_accessed=size, transcendentals=0),
         name=name,
     )(*operands)
@@ -397,6 +434,15 @@
 
 def f32(*shape):
     return jax.ShapeDtypeStruct(shape, jnp.float32)
+
+
+def exchanged(chunks, axis):
+    devices = lax.axis_size(axis)
+    out = [chunks[0]] + [None] * (devices - 1)
+    for number in reversed(range(1, devices)):
+        pairs = [(i, i ^ number) for i in range(devices)]
+        out[number] = lax.ppermute(chunks[number], axis, pairs)
+    return out
 
 
 def per_device(theta, phi, labels, ms_region, aex_region, kernel):
@@ -408,27 +454,38 @@
     lines = 3 * depth * height
     whole_y = count_y * height
 
+    place = jnp.stack([gx, gy]).astype(jnp.int32)
+    cells = f32(3, depth, height, width)
+    table = line_table(count_x, count_y, width, rows)
+    if table is None:
+        table = line_table_here(count_x, count_y, width, rows)
+    table = jnp.asarray(table)
+    forward, inverse = column_tables(whole_y)
+    twice = np.concatenate([np.eye(rows), np.eye(rows)], 1).astype(ml_dtypes.bfloat16)
+    table_scratch = pltpu.VMEM((count_x, 2, width, count_y * lanes), jnp.bfloat16)
+    ordered = pltpu.VMEM((count_y, lines, lanes), jnp.float32)
+    table_grant = (12 << 20) + 5 * math.prod(table_scratch.shape)
+    table_sems = pltpu.SemaphoreType.DMA((count_x,))
+    transform_flops = 6 * lines * count_x * width * count_y * lanes
+
     packed, first, last = call(
         pack_kernel,
-        [f32(count_x, 3, depth, height, width), f32(3, depth, width), f32(3, depth, width)],
-        [vmem] * 3,
+        [cells, f32(3, depth, width), f32(3, depth, width)],
+        [hbm] * 3,
         (theta, phi, labels),
+        scratch=(
+            pltpu.VMEM((2, depth, height, width), jnp.float32),
+            pltpu.VMEM((depth, height, width), jnp.int32),
+            pltpu.SemaphoreType.DMA((3,)),
+        ),
         name="pack",
     )
-    gathered = lax.all_to_all(packed, "gx", split_axis=0, concat_axis=0, tiled=True)
+    gathered = exchanged([packed] * count_x, "gx")
     up = [(i, i + 1) for i in range(count_y - 1)]
     down = [(j, i) for i, j in up]
     before = lax.ppermute(last, "gy", up)
     after = lax.ppermute(first, "gy", down)
 
-    table = line_table(count_x, count_y, width, rows)
-    if table is None:
-        table = line_table_here(count_x, count_y, width, rows)
-    else:
-        table = lax.dynamic_index_in_dim(jnp.asarray(table), gx, 0, keepdims=False)
-    forward, inverse = column_tables(whole_y)
-
-    twice = np.concatenate([np.eye(rows), np.eye(rows)], 1).astype(ml_dtypes.bfloat16)
     tensor = call(
         tensor_kernel,
         jax.ShapeDtypeStruct((48, 2 * whole_y, lanes), jnp.bfloat16),
@@ -438,52 +495,57 @@
         name="tensor",
     )
     spectrum = call(
-        lines_kernel,
-        f32(count_y, lines, lanes),
-        [vmem, smem, vmem],
-        (gathered, ms_region, table),
-        flops=6 * lines * count_x * width * count_y * lanes,
+        functools.partial(lines_kernel, count_x, count_y),
+        [f32(lines, lanes)] * count_y,
+        [vmem] * count_x + [smem, smem, hbm],
+        (*gathered, ms_region, place, table),
+        scratch=(table_scratch, ordered, table_sems),
+        grant=table_grant,
+        flops=transform_flops,
         name="lines",
     )
-    columns = lax.all_to_all(spectrum, "gy", split_axis=0, concat_axis=0, tiled=True)
+    columns = exchanged(spectrum, "gy")
+    exchange, unit = call(
+        functools.partial(exchange_kernel, count_x, count_y),
+        [cells, cells],
+        [vmem] * (count_x + 2) + [smem] * 3,
+        (*gathered, before, after, place, ms_region, aex_region),
+        scratch=(pltpu.VMEM((count_x, 3, depth, height, width), jnp.float32),),
+        flops=300 * depth * height * width,
+        name="exchange",
+    )
+    columns, exchange, unit = lax.optimization_barrier((columns, exchange, unit))
     scale = -1.0 / (2 * depth * 2 * whole_y * 2 * count_x * width)
     waves = call(
-        functools.partial(waves_kernel, scale),
-        f32(count_y, lines, lanes),
-        [vmem] * 4,
-        (columns, tensor, jnp.asarray(forward), jnp.asarray(inverse)),
+        functools.partial(waves_kernel, scale, count_y),
+        [f32(lines, lanes)] * count_y,
+        [vmem] * count_y + [smem] + [vmem] * 3,
+        (*columns, place, tensor, jnp.asarray(forward), jnp.asarray(inverse)),
         scratch=(
+            ordered,
             pltpu.VMEM((2 * whole_y, 3 * depth * lanes), jnp.float32),
             pltpu.VMEM((6 * whole_y, 3 * depth * lanes), jnp.bfloat16),
         ),
         flops=20 * whole_y * whole_y * 3 * depth * lanes,
         name="waves",
     )
-    returned = lax.all_to_all(waves, "gy", split_axis=0, concat_axis=0, tiled=True)
-    place = jnp.stack([gx, gy, jnp.int32(count_y)]).astype(jnp.int32)
-    exchange, unit = call(
-        exchange_kernel,
-        [f32(3, depth, height, width), f32(3, depth, height, width)],
-        [vmem, vmem, vmem, smem, smem, smem],
-        (gathered, before, after, place, ms_region, aex_region),
-        flops=300 * depth * height * width,
-        name="exchange",
-    )
-    returned, exchange, unit = lax.optimization_barrier((returned, exchange, unit))
+    returned = exchanged(waves, "gy")
     partial = call(
-        back_lines_kernel,
-        f32(count_x, lines, width),
-        [vmem, vmem],
-        (returned, table),
-        flops=6 * lines * count_x * width * count_y * lanes,
+        functools.partial(back_lines_kernel, count_x, count_y),
+        [f32(lines, width)] * count_x,
+        [vmem] * count_y + [smem, hbm],
+        (*returned, place, table),
+        scratch=(table_scratch, ordered, table_sems),
+        grant=table_grant,
+        flops=transform_flops,
         name="back_lines",
     )
-    parts = lax.all_to_all(partial, "gx", split_axis=0, concat_axis=0, tiled=True)
+    parts = exchanged(partial, "gx")
     field, predicted = call(
-        final_kernel,
-        [f32(3, depth, height, width), f32(3, depth, height, width)],
-        [vmem] * 3,
-        (parts, exchange, unit),
+        functools.partial(final_kernel, count_x),
+        [cells, cells],
+        [vmem] * (count_x + 2),
+        (*parts, exchange, unit),
         flops=60 * depth * height * width,
         name="predict",
     )

time: 72.2 us -> 69.2 us (0.958)
  starting transfers between devices: 19.7 us -> 35.8 us
  local copies, waits for them, and re-layouts: 11.3 us -> 0.68 us
  blocking collectives: 9.84 us -> 0 us
  Pallas kernels: 12.2 us -> 15.8 us
  waiting for transfers between devices: 17.7 us -> 15.9 us
    ppermute x0 -> x20, starting transfers between devices: none -> 32.1 us  [exchanged(): out[number] = lax.ppermute(chunks[number], axis, pairs)]
    ppermute x0 -> x20, waiting for transfers between devices: none -> 15.9 us  [exchanged(): out[number] = lax.ppermute(chunks[number], axis, pairs)]
    all_to_all x3 -> x0, starting transfers between devices: 14.5 us -> none  [the longest x1 6.64 us: per_device(): lax.all_to_all(spectrum, 'gy', split_axis=0, concat_axis=0, tiled=True)]
    all_to_all x3 -> x0, waiting for transfers between devices: 13.5 us -> none  [the longest x1 9.95 us: per_device(): lax.all_to_all(spectrum, 'gy', split_axis=0, concat_axis=0, tiled=True)]
    all_to_all x1 -> x0, blocking collectives: 9.84 us -> none  [per_device(): lax.all_to_all(partial, 'gx', split_axis=0, concat_axis=0, tiled=True)]
    unnamed x22 -> x12, local copies, waits for them, and re-layouts: 6.66 us -> 0.68 us
    squeeze x1 -> x0, local copies, waits for them, and re-layouts: 4.59 us -> none  [per_device(): table = lax.dynamic_index_in_dim(jnp.asarray(table), gx, 0, keepdims=False)]
    ppermute x1, waiting for transfers between devices: 4.2 us -> 0.01 us  [per_device(): after = lax.ppermute(first, 'gy', down)]
  transfers between devices with their start and end apart: 5 -> 22, of which waited for: 4 -> 7; matrix products, arithmetic and copies ran while one was open for 7% -> 0% of each run, Pallas kernels for 4% -> 4%
where the time goes in v2:
time: 69.2 us; the launch traced here: 69.1 us
  starting transfers between devices  35.8 us (52%)
  waiting for transfers between devices  15.9 us (23%)
  Pallas kernels  15.8 us (23%)
  between operations  0.81 us (1%)
    ppermute x20, starting transfers between devices, exchanged(): out[number] = lax.ppermute(chunks[number], axis, pairs)  32.1 us
    ppermute x20, waiting for transfers between devices, exchanged(): out[number] = lax.ppermute(chunks[number], axis, pairs)  15.9 us
    pallas_call x7, Pallas kernels, call(): pl.pallas_call(body, out_shape=out, in_specs=ins, out_specs=jax.tree.map(...  15.8 us
    ppermute x1, starting transfers between devices, per_device(): before = lax.ppermute(last, 'gy', up)  2.4 us
  transfers between devices with their start and end apart: 22, of which 7 were waited for; matrix products, arithmetic and copies ran while one was open for 0% of the time, Pallas kernels for 4%

profile of v2, /device:TPU:0, one launch (start us, length us, event | category | flops | bytes accessed | tf_op | source)
XLA Modules:
  0.0 69.1 jit_solution(3812002318525753207)
XLA Ops:
  0.7 0.9 %pack.1 = (f32[3,4,8,256]{3,2,1,0:T(8,128)S(1)}, f32[3,4,256]{2,1,0:T(4,128)S(1)}, f32[3,4,256]{2,1,0:T(4,128)S(1)}) custom-call(f32[4,8,256]{2,1,0:T(8,128)} %theta_ref.1, f32[4,8,256]{2,1,0:T(8,128)} %phi_ref.1, s32[4,8,256]{2,1,0:T(8,128)} %labels_ref.1), custom_call_target="tpu_custom_call" | custom-call | bytes 221184 | tf_op jit(solution)/shard_map/pack/pallas_call | solution.py:423
  1.6 2.4 %collective-permute-start.2 = (f32[3,4,8,256]{3,2,1,0:T(8,128)S(1)}, f32[3,4,8,256]{3,2,1,0:T(8,128)S(1)}, u32[]{:S(2)}, u32[]{:S(2)}) collective-permute-start(f32[3,4,8,256]{3,2,1,0:T(8,128)S(1)} %get-tuple-element.37.refs_0_), channel_id=1, source_target_pairs={{0,24},{8,16},{16,8},{24,0},{1,25},{9,17},{17,9},{25,1},{2,26},{10... | collective-permute-start | bytes 294920 | tf_op jit(solution)/shard_map/ppermute | solution.py:444
  4.0 0.6 collective-permute-start.1
  4.8 2.4 %collective-permute-done.2.refs_3_ = f32[3,4,8,256]{3,2,1,0:T(8,128)S(1)} collective-permute-done((f32[3,4,8,256]{3,2,1,0:T(8,128)S(1)}, f32[3,4,8,256]{3,2,1,0:T(8,128)S(1)}, u32[]{:S(2)}, u32[]{:S(2)}) %collective-permute-start.2) | collective-permute-done | bytes 98336 | tf_op jit(solution)/shard_map/ppermute | solution.py:444
  7.2 2.3 %collective-permute-done.1.refs_2_ = f32[3,4,8,256]{3,2,1,0:T(8,128)S(1)} collective-permute-done((f32[3,4,8,256]{3,2,1,0:T(8,128)S(1)}, f32[3,4,8,256]{3,2,1,0:T(8,128)S(1)}, u32[]{:S(2)}, u32[]{:S(2)}) %collective-permute-start.1) | collective-permute-done | bytes 98336 | tf_op jit(solution)/shard_map/ppermute | solution.py:444
  9.5 0.7 copy-done.4
  10.2 3.1 %lines.1 = (f32[96,128]{1,0:T(8,128)S(1)}, f32[96,128]{1,0:T(8,128)S(1)}, f32[96,128]{1,0:T(8,128)S(1)}, f32[96,128]{1,0:T(8,128)S(1)}, f32[96,128]{1,0:T(8,128)...) custom-call(f32[3,4,8,256]{3,2,1,0:T(8,128)S(1)} %get-tuple-element.37.refs_0_, ...), custom_call_target="tpu_custom_call" | custom-call | flops 603979776 | bytes 17563720 | tf_op jit(solution)/shard_map/lines/pallas_call | solution.py:423
  13.3 2.4 %collective-permute-start.3 = (f32[96,128]{1,0:T(8,128)S(1)}, f32[96,128]{1,0:T(8,128)S(1)}, u32[]{:S(2)}, u32[]{:S(2)}) collective-permute-start(f32[96,128]{1,0:T(8,128)S(1)} %get-tuple-element.39), channel_id=1, source_target_pairs={{0,1},{1,0},{2,3},{3,2},{4,5},{5,4},{6,7},{7,6},{8,9},{9,8},{10,11... | collective-permute-start | bytes 147464 | tf_op jit(solution)/shard_map/ppermute | solution.py:444
  15.7 1.6 %collective-permute-start.4 = (f32[96,128]{1,0:T(8,128)S(1)}, f32[96,128]{1,0:T(8,128)S(1)}, u32[]{:S(2)}, u32[]{:S(2)}) collective-permute-start(f32[96,128]{1,0:T(8,128)S(1)} %get-tuple-element.40), channel_id=1, source_target_pairs={{0,2},{1,3},{2,0},{3,1},{4,6},{5,7},{6,4},{7,5},{8,10},{9,11},{10,... | collective-permute-start | bytes 147464 | tf_op jit(solution)/shard_map/ppermute | solution.py:444
  17.3 2.4 %collective-permute-start.10 = (f32[3,4,256]{2,1,0:T(4,128)S(1)}, f32[3,4,256]{2,1,0:T(4,128)S(1)}, u32[]{:S(2)}, u32[]{:S(2)}) collective-permute-start(f32[3,4,256]{2,1,0:T(4,128)S(1)} %get-tuple-element.46), channel_id=1, source_target_pairs={{0,1},{1,2},{2,3},{3,4},{4,5},{5,6},{6,7},{8,9},{9,10},{10,11},{11... | collective-permute-start | bytes 36872 | tf_op jit(solution)/shard_map/ppermute | solution.py:486
  19.7 1.3 %collective-permute-start.11 = (f32[3,4,256]{2,1,0:T(4,128)S(1)}, f32[3,4,256]{2,1,0:T(4,128)S(1)}, u32[]{:S(2)}, u32[]{:S(2)}) collective-permute-start(f32[3,4,256]{2,1,0:T(4,128)S(1)} %get-tuple-element.47), channel_id=1, source_target_pairs={{1,0},{2,1},{3,2},{4,3},{5,4},{6,5},{7,6},{9,8},{10,9},{11,10},{12... | collective-permute-start | bytes 36872 | tf_op jit(solution)/shard_map/ppermute | solution.py:487
  21.0 4.2 %collective-permute-start.5 = (f32[96,128]{1,0:T(8,128)S(1)}, f32[96,128]{1,0:T(8,128)S(1)}, u32[]{:S(2)}, u32[]{:S(2)}) collective-permute-start(f32[96,128]{1,0:T(8,128)S(1)} %get-tuple-element.41), channel_id=1, source_target_pairs={{0,3},{1,2},{2,1},{3,0},{4,7},{5,6},{6,5},{7,4},{8,11},{9,10},{10,... | collective-permute-start | bytes 147464 | tf_op jit(solution)/shard_map/ppermute | solution.py:444
  25.2 1.5 %collective-permute-start.6 = (f32[96,128]{1,0:T(8,128)S(1)}, f32[96,128]{1,0:T(8,128)S(1)}, u32[]{:S(2)}, u32[]{:S(2)}) collective-permute-start(f32[96,128]{1,0:T(8,128)S(1)} %get-tuple-element.42), channel_id=1, source_target_pairs={{0,4},{1,5},{2,6},{3,7},{4,0},{5,1},{6,2},{7,3},{8,12},{9,13},{10,... | collective-permute-start | bytes 147464 | tf_op jit(solution)/shard_map/ppermute | solution.py:444
  26.8 2.8 %collective-permute-start.7 = (f32[96,128]{1,0:T(8,128)S(1)}, f32[96,128]{1,0:T(8,128)S(1)}, u32[]{:S(2)}, u32[]{:S(2)}) collective-permute-start(f32[96,128]{1,0:T(8,128)S(1)} %get-tuple-element.43), channel_id=1, source_target_pairs={{0,5},{1,4},{2,7},{3,6},{4,1},{5,0},{6,3},{7,2},{8,13},{9,12},{10,... | collective-permute-start | bytes 147464 | tf_op jit(solution)/shard_map/ppermute | solution.py:444
  29.6 2.6 %collective-permute-start.8 = (f32[96,128]{1,0:T(8,128)S(1)}, f32[96,128]{1,0:T(8,128)S(1)}, u32[]{:S(2)}, u32[]{:S(2)}) collective-permute-start(f32[96,128]{1,0:T(8,128)S(1)} %get-tuple-element.44), channel_id=1, source_target_pairs={{0,6},{1,7},{2,4},{3,5},{4,2},{5,3},{6,0},{7,1},{8,14},{9,15},{10,... | collective-permute-start | bytes 147464 | tf_op jit(solution)/shard_map/ppermute | solution.py:444
  32.2 0.7 %collective-permute-start.9 = (f32[96,128]{1,0:T(8,128)S(1)}, f32[96,128]{1,0:T(8,128)S(1)}, u32[]{:S(2)}, u32[]{:S(2)}) collective-permute-start(f32[96,128]{1,0:T(8,128)S(1)} %get-tuple-element.45), channel_id=1, source_target_pairs={{0,7},{1,6},{2,5},{3,4},{4,3},{5,2},{6,1},{7,0},{8,15},{9,14},{10,... | collective-permute-start | bytes 147464 | tf_op jit(solution)/shard_map/ppermute | solution.py:444
  32.9 1.6 %tensor.1.refs_9_ = bf16[48,128,128]{2,1,0:T(8,128)(2,1)S(1)} custom-call(bf16[48,64,128]{2,1,0:T(8,128)(2,1)S(1)} %bitcast.3, bf16[64,128]{1,0:T(8,128)(2,1)S(1)} %copy-done.3), custom_call_target="tpu_custom_call" | custom-call | flops 100663296 | bytes 2375680 | tf_op jit(solution)/shard_map/tensor/pallas_call | solution.py:423
  34.5 1.1 %exchange.1 = (f32[3,4,8,256]{3,2,1,0:T(8,128)S(1)}, f32[3,4,8,256]{3,2,1,0:T(8,128)S(1)}) custom-call(f32[3,4,8,256]{3,2,1,0:T(8,128)S(1)} %get-tuple-element.37.refs_0_, f32[3,4,8,256]{3,2,1,0:T(8,128)S(1)} %collective-permute-done.refs_1_, f32[3,4,8,256]{3,2,1,0:T(8,128)S(1)} %collective-permute-done.1.refs_2_, ...), custom_call_target="tpu_custom_call" | custom-call | flops 2457600 | bytes 614536 | tf_op jit(solution)/shard_map/exchange/pallas_call | solution.py:423
  35.7 3.3 %collective-permute-done.9.refs_7_ = f32[96,128]{1,0:T(8,128)S(1)} collective-permute-done((f32[96,128]{1,0:T(8,128)S(1)}, f32[96,128]{1,0:T(8,128)S(1)}, u32[]{:S(2)}, u32[]{:S(2)}) %collective-permute-start.9) | collective-permute-done | bytes 49184 | tf_op jit(solution)/shard_map/ppermute | solution.py:444
  39.0 3.7 %waves.1 = (f32[96,128]{1,0:T(8,128)S(1)}, f32[96,128]{1,0:T(8,128)S(1)}, f32[96,128]{1,0:T(8,128)S(1)}, f32[96,128]{1,0:T(8,128)S(1)}, f32[96,128]{1,0:T(8,128)...) custom-call(f32[96,128]{1,0:T(8,128)S(1)} %get-tuple-element.50.refs_0_, ...), custom_call_target="tpu_custom_call" | custom-call | flops 125829120 | bytes 2555912 | tf_op jit(solution)/shard_map/waves/pallas_call | solution.py:423
  42.9 3.4 %collective-permute-start.14 = (f32[96,128]{1,0:T(8,128)S(1)}, f32[96,128]{1,0:T(8,128)S(1)}, u32[]{:S(2)}, u32[]{:S(2)}) collective-permute-start(f32[96,128]{1,0:T(8,128)S(1)} %get-tuple-element.61), channel_id=1, source_target_pairs={{0,3},{1,2},{2,1},{3,0},{4,7},{5,6},{6,5},{7,4},{8,11},{9,10},{10,... | collective-permute-start | bytes 147464 | tf_op jit(solution)/shard_map/ppermute | solution.py:444
  46.3 2.4 %collective-permute-start.16 = (f32[96,128]{1,0:T(8,128)S(1)}, f32[96,128]{1,0:T(8,128)S(1)}, u32[]{:S(2)}, u32[]{:S(2)}) collective-permute-start(f32[96,128]{1,0:T(8,128)S(1)} %get-tuple-element.63), channel_id=1, source_target_pairs={{0,5},{1,4},{2,7},{3,6},{4,1},{5,0},{6,3},{7,2},{8,13},{9,12},{10,... | collective-permute-start | bytes 147464 | tf_op jit(solution)/shard_map/ppermute | solution.py:444
  48.7 1.3 %collective-permute-start.17 = (f32[96,128]{1,0:T(8,128)S(1)}, f32[96,128]{1,0:T(8,128)S(1)}, u32[]{:S(2)}, u32[]{:S(2)}) collective-permute-start(f32[96,128]{1,0:T(8,128)S(1)} %get-tuple-element.64), channel_id=1, source_target_pairs={{0,6},{1,7},{2,4},{3,5},{4,2},{5,3},{6,0},{7,1},{8,14},{9,15},{10,... | collective-permute-start | bytes 147464 | tf_op jit(solution)/shard_map/ppermute | solution.py:444
  50.0 4.0 %collective-permute-start.18 = (f32[96,128]{1,0:T(8,128)S(1)}, f32[96,128]{1,0:T(8,128)S(1)}, u32[]{:S(2)}, u32[]{:S(2)}) collective-permute-start(f32[96,128]{1,0:T(8,128)S(1)} %get-tuple-element.65), channel_id=1, source_target_pairs={{0,7},{1,6},{2,5},{3,4},{4,3},{5,2},{6,1},{7,0},{8,15},{9,14},{10,... | collective-permute-start | bytes 147464 | tf_op jit(solution)/shard_map/ppermute | solution.py:444
  53.9 0.8 %collective-permute-done.17.refs_6_ = f32[96,128]{1,0:T(8,128)S(1)} collective-permute-done((f32[96,128]{1,0:T(8,128)S(1)}, f32[96,128]{1,0:T(8,128)S(1)}, u32[]{:S(2)}, u32[]{:S(2)}) %collective-permute-start.17) | collective-permute-done | bytes 49184 | tf_op jit(solution)/shard_map/ppermute | solution.py:444
  54.7 2.1 %collective-permute-done.18.refs_7_ = f32[96,128]{1,0:T(8,128)S(1)} collective-permute-done((f32[96,128]{1,0:T(8,128)S(1)}, f32[96,128]{1,0:T(8,128)S(1)}, u32[]{:S(2)}, u32[]{:S(2)}) %collective-permute-start.18) | collective-permute-done | bytes 49184 | tf_op jit(solution)/shard_map/ppermute | solution.py:444
  56.8 4.6 %back_lines.1 = (f32[96,256]{1,0:T(8,128)S(1)}, f32[96,256]{1,0:T(8,128)S(1)}, f32[96,256]{1,0:T(8,128)S(1)}, f32[96,256]{1,0:T(8,128)S(1)}) custom-call(f32[96,128]{1,0:T(8,128)S(1)} %get-tuple-element.58.refs_0_, f32[96,128]{1,0:T(8,128)S(1)} %collective-permute-done.12.refs_1_, f32[96,128]{1,0:T(8,128)S(1)} %collective-permute-done.13.refs_2_, ...), custom_call_target="tpu_custom_call" | custom-call | flops 603979776 | bytes 17563656 | tf_op jit(solution)/shard_map/back_lines/pallas_call | solution.py:423
  61.5 1.6 %collective-permute-start.20 = (f32[96,256]{1,0:T(8,128)S(1)}, f32[96,256]{1,0:T(8,128)S(1)}, u32[]{:S(2)}, u32[]{:S(2)}) collective-permute-start(f32[96,256]{1,0:T(8,128)S(1)} %get-tuple-element.68), channel_id=1, source_target_pairs={{0,16},{8,24},{16,0},{24,8},{1,17},{9,25},{17,1},{25,9},{2,18},{10... | collective-permute-start | bytes 294920 | tf_op jit(solution)/shard_map/ppermute | solution.py:444
  63.0 0.3 collective-permute-start.21
  63.3 3.8 %collective-permute-done.20.refs_2_ = f32[96,256]{1,0:T(8,128)S(1)} collective-permute-done((f32[96,256]{1,0:T(8,128)S(1)}, f32[96,256]{1,0:T(8,128)S(1)}, u32[]{:S(2)}, u32[]{:S(2)}) %collective-permute-start.20) | collective-permute-done | bytes 98336 | tf_op jit(solution)/shard_map/ppermute | solution.py:444
  67.1 1.2 %collective-permute-done.21.refs_3_ = f32[96,256]{1,0:T(8,128)S(1)} collective-permute-done((f32[96,256]{1,0:T(8,128)S(1)}, f32[96,256]{1,0:T(8,128)S(1)}, u32[]{:S(2)}, u32[]{:S(2)}) %collective-permute-start.21) | collective-permute-done | bytes 98336 | tf_op jit(solution)/shard_map/ppermute | solution.py:444
  68.3 0.7 %predict.1 = (f32[3,4,8,256]{3,2,1,0:T(8,128)}, f32[3,4,8,256]{3,2,1,0:T(8,128)}) custom-call(f32[96,256]{1,0:T(8,128)S(1)} %get-tuple-element.66.refs_0_, f32[96,256]{1,0:T(8,128)S(1)} %collective-permute-done.19.refs_1_, f32[96,256]{1,0:T(8,128)S(1)} %collective-permute-done.20.refs_2_, f32[96,256]{1,0:T(8,128)S(1)} %collective-permute-done.21.refs_3_, ...), custom_call_target="tpu_custom_call" | custom-call | flops 491520 | bytes 786432 | tf_op jit(solution)/shard_map/predict/pallas_call | solution.py:423
  (32 shorter events, 0.4 us)
Async XLA Ops:
  0.6 32.3 %copy-start.3 = (bf16[64,128]{1,0:T(8,128)(2,1)S(1)}, bf16[64,128]{1,0:T(8,128)(2,1)}, u32[]{:S(2)}) copy-start(bf16[64,128]{1,0:T(8,128)(2,1)} %constant.17.clone.twice_ref) | copy-start | bytes 49156
  0.6 38.3 %copy-start.1 = (bf16[128,384]{1,0:T(8,128)(2,1)S(1)}, bf16[128,384]{1,0:T(8,128)(2,1)}, u32[]{:S(2)}) copy-start(bf16[128,384]{1,0:T(8,128)(2,1)} %constant.19.clone.refs_11_) | copy-start | bytes 294916
  0.7 38.3 %copy-start.2 = (bf16[128,384]{1,0:T(8,128)(2,1)S(1)}, bf16[128,384]{1,0:T(8,128)(2,1)}, u32[]{:S(2)}) copy-start(bf16[128,384]{1,0:T(8,128)(2,1)} %constant.18.clone.refs_10_) | copy-start | bytes 294916
  0.7 32.2 %copy-start = (bf16[6,8,64,128]{3,2,1,0:T(8,128)(2,1)S(1)}, bf16[6,8,64,128]{3,2,1,0:T(8,128)(2,1)}, u32[]{:S(2)}) copy-start(bf16[6,8,64,128]{3,2,1,0:T(8,128)(2,1)} %param.15) | copy-start | bytes 2359300
  1.6 5.6 %collective-permute-start.2 = (f32[3,4,8,256]{3,2,1,0:T(8,128)S(1)}, f32[3,4,8,256]{3,2,1,0:T(8,128)S(1)}, u32[]{:S(2)}, u32[]{:S(2)}) collective-permute-start(f32[3,4,8,256]{3,2,1,0:T(8,128)S(1)} %get-tuple-element.37.refs_0_), channel_id=1, source_target_pairs={{0,24},{8,16},{16,8},{24,0},{1,25},{9,17},{17,9},{25,1},{2,26},{10... | collective-permute-start | bytes 294920 | tf_op jit(solution)/shard_map/ppermute | solution.py:444
  4.0 5.5 %collective-permute-start.1 = (f32[3,4,8,256]{3,2,1,0:T(8,128)S(1)}, f32[3,4,8,256]{3,2,1,0:T(8,128)S(1)}, u32[]{:S(2)}, u32[]{:S(2)}) collective-permute-start(f32[3,4,8,256]{3,2,1,0:T(8,128)S(1)} %get-tuple-element.37.refs_0_), channel_id=1, source_target_pairs={{0,16},{8,24},{16,0},{24,8},{1,17},{9,25},{17,1},{25,9},{2,18},{10... | collective-permute-start | bytes 294920 | tf_op jit(solution)/shard_map/ppermute | solution.py:444
  4.7 4.8 %collective-permute-start = (f32[3,4,8,256]{3,2,1,0:T(8,128)S(1)}, f32[3,4,8,256]{3,2,1,0:T(8,128)S(1)}, u32[]{:S(2)}, u32[]{:S(2)}) collective-permute-start(f32[3,4,8,256]{3,2,1,0:T(8,128)S(1)} %get-tuple-element.37.refs_0_), channel_id=1, source_target_pairs={{0,8},{8,0},{16,24},{24,16},{1,9},{9,1},{17,25},{25,17},{2,10},{10... | collective-permute-start | bytes 294920 | tf_op jit(solution)/shard_map/ppermute | solution.py:444
  9.5 0.7 copy-start.4
  10.2 24.3 %copy-start.5 = (f32[16]{0:T(128)S(1)}, f32[16]{0:T(128)}, u32[]{:S(2)}) copy-start(f32[16]{0:T(128)} %refs_8_.1) | copy-start | bytes 196
  13.3 16.3 %collective-permute-start.3 = (f32[96,128]{1,0:T(8,128)S(1)}, f32[96,128]{1,0:T(8,128)S(1)}, u32[]{:S(2)}, u32[]{:S(2)}) collective-permute-start(f32[96,128]{1,0:T(8,128)S(1)} %get-tuple-element.39), channel_id=1, source_target_pairs={{0,1},{1,0},{2,3},{3,2},{4,5},{5,4},{6,7},{7,6},{8,9},{9,8},{10,11... | collective-permute-start | bytes 147464 | tf_op jit(solution)/shard_map/ppermute | solution.py:444
  15.7 16.5 %collective-permute-start.4 = (f32[96,128]{1,0:T(8,128)S(1)}, f32[96,128]{1,0:T(8,128)S(1)}, u32[]{:S(2)}, u32[]{:S(2)}) collective-permute-start(f32[96,128]{1,0:T(8,128)S(1)} %get-tuple-element.40), channel_id=1, source_target_pairs={{0,2},{1,3},{2,0},{3,1},{4,6},{5,7},{6,4},{7,5},{8,10},{9,11},{10,... | collective-permute-start | bytes 147464 | tf_op jit(solution)/shard_map/ppermute | solution.py:444
  17.3 8.0 %collective-permute-start.10 = (f32[3,4,256]{2,1,0:T(4,128)S(1)}, f32[3,4,256]{2,1,0:T(4,128)S(1)}, u32[]{:S(2)}, u32[]{:S(2)}) collective-permute-start(f32[3,4,256]{2,1,0:T(4,128)S(1)} %get-tuple-element.46), channel_id=1, source_target_pairs={{0,1},{1,2},{2,3},{3,4},{4,5},{5,6},{6,7},{8,9},{9,10},{10,11},{11... | collective-permute-start | bytes 36872 | tf_op jit(solution)/shard_map/ppermute | solution.py:486
  19.7 7.1 %collective-permute-start.11 = (f32[3,4,256]{2,1,0:T(4,128)S(1)}, f32[3,4,256]{2,1,0:T(4,128)S(1)}, u32[]{:S(2)}, u32[]{:S(2)}) collective-permute-start(f32[3,4,256]{2,1,0:T(4,128)S(1)} %get-tuple-element.47), channel_id=1, source_target_pairs={{1,0},{2,1},{3,2},{4,3},{5,4},{6,5},{7,6},{9,8},{10,9},{11,10},{12... | collective-permute-start | bytes 36872 | tf_op jit(solution)/shard_map/ppermute | solution.py:487
  21.0 14.7 %collective-permute-start.5 = (f32[96,128]{1,0:T(8,128)S(1)}, f32[96,128]{1,0:T(8,128)S(1)}, u32[]{:S(2)}, u32[]{:S(2)}) collective-permute-start(f32[96,128]{1,0:T(8,128)S(1)} %get-tuple-element.41), channel_id=1, source_target_pairs={{0,3},{1,2},{2,1},{3,0},{4,7},{5,6},{6,5},{7,4},{8,11},{9,10},{10,... | collective-permute-start | bytes 147464 | tf_op jit(solution)/shard_map/ppermute | solution.py:444
  25.2 10.4 %collective-permute-start.6 = (f32[96,128]{1,0:T(8,128)S(1)}, f32[96,128]{1,0:T(8,128)S(1)}, u32[]{:S(2)}, u32[]{:S(2)}) collective-permute-start(f32[96,128]{1,0:T(8,128)S(1)} %get-tuple-element.42), channel_id=1, source_target_pairs={{0,4},{1,5},{2,6},{3,7},{4,0},{5,1},{6,2},{7,3},{8,12},{9,13},{10,... | collective-permute-start | bytes 147464 | tf_op jit(solution)/shard_map/ppermute | solution.py:444
  26.8 8.9 %collective-permute-start.7 = (f32[96,128]{1,0:T(8,128)S(1)}, f32[96,128]{1,0:T(8,128)S(1)}, u32[]{:S(2)}, u32[]{:S(2)}) collective-permute-start(f32[96,128]{1,0:T(8,128)S(1)} %get-tuple-element.43), channel_id=1, source_target_pairs={{0,5},{1,4},{2,7},{3,6},{4,1},{5,0},{6,3},{7,2},{8,13},{9,12},{10,... | collective-permute-start | bytes 147464 | tf_op jit(solution)/shard_map/ppermute | solution.py:444
  29.6 6.1 %collective-permute-start.8 = (f32[96,128]{1,0:T(8,128)S(1)}, f32[96,128]{1,0:T(8,128)S(1)}, u32[]{:S(2)}, u32[]{:S(2)}) collective-permute-start(f32[96,128]{1,0:T(8,128)S(1)} %get-tuple-element.44), channel_id=1, source_target_pairs={{0,6},{1,7},{2,4},{3,5},{4,2},{5,3},{6,0},{7,1},{8,14},{9,15},{10,... | collective-permute-start | bytes 147464 | tf_op jit(solution)/shard_map/ppermute | solution.py:444
  32.2 6.8 %collective-permute-start.9 = (f32[96,128]{1,0:T(8,128)S(1)}, f32[96,128]{1,0:T(8,128)S(1)}, u32[]{:S(2)}, u32[]{:S(2)}) collective-permute-start(f32[96,128]{1,0:T(8,128)S(1)} %get-tuple-element.45), channel_id=1, source_target_pairs={{0,7},{1,6},{2,5},{3,4},{4,3},{5,2},{6,1},{7,0},{8,15},{9,14},{10,... | collective-permute-start | bytes 147464 | tf_op jit(solution)/shard_map/ppermute | solution.py:444
  42.7 6.0 %collective-permute-start.12 = (f32[96,128]{1,0:T(8,128)S(1)}, f32[96,128]{1,0:T(8,128)S(1)}, u32[]{:S(2)}, u32[]{:S(2)}) collective-permute-start(f32[96,128]{1,0:T(8,128)S(1)} %get-tuple-element.59), channel_id=1, source_target_pairs={{0,1},{1,0},{2,3},{3,2},{4,5},{5,4},{6,7},{7,6},{8,9},{9,8},{10,11... | collective-permute-start | bytes 147464 | tf_op jit(solution)/shard_map/ppermute | solution.py:444
  42.8 7.2 %collective-permute-start.13 = (f32[96,128]{1,0:T(8,128)S(1)}, f32[96,128]{1,0:T(8,128)S(1)}, u32[]{:S(2)}, u32[]{:S(2)}) collective-permute-start(f32[96,128]{1,0:T(8,128)S(1)} %get-tuple-element.60), channel_id=1, source_target_pairs={{0,2},{1,3},{2,0},{3,1},{4,6},{5,7},{6,4},{7,5},{8,10},{9,11},{10,... | collective-permute-start | bytes 147464 | tf_op jit(solution)/shard_map/ppermute | solution.py:444
  42.9 11.1 %collective-permute-start.14 = (f32[96,128]{1,0:T(8,128)S(1)}, f32[96,128]{1,0:T(8,128)S(1)}, u32[]{:S(2)}, u32[]{:S(2)}) collective-permute-start(f32[96,128]{1,0:T(8,128)S(1)} %get-tuple-element.61), channel_id=1, source_target_pairs={{0,3},{1,2},{2,1},{3,0},{4,7},{5,6},{6,5},{7,4},{8,11},{9,10},{10,... | collective-permute-start | bytes 147464 | tf_op jit(solution)/shard_map/ppermute | solution.py:444
  46.3 7.7 %collective-permute-start.15 = (f32[96,128]{1,0:T(8,128)S(1)}, f32[96,128]{1,0:T(8,128)S(1)}, u32[]{:S(2)}, u32[]{:S(2)}) collective-permute-start(f32[96,128]{1,0:T(8,128)S(1)} %get-tuple-element.62), channel_id=1, source_target_pairs={{0,4},{1,5},{2,6},{3,7},{4,0},{5,1},{6,2},{7,3},{8,12},{9,13},{10,... | collective-permute-start | bytes 147464 | tf_op jit(solution)/shard_map/ppermute | solution.py:444
  46.3 7.7 %collective-permute-start.16 = (f32[96,128]{1,0:T(8,128)S(1)}, f32[96,128]{1,0:T(8,128)S(1)}, u32[]{:S(2)}, u32[]{:S(2)}) collective-permute-start(f32[96,128]{1,0:T(8,128)S(1)} %get-tuple-element.63), channel_id=1, source_target_pairs={{0,5},{1,4},{2,7},{3,6},{4,1},{5,0},{6,3},{7,2},{8,13},{9,12},{10,... | collective-permute-start | bytes 147464 | tf_op jit(solution)/shard_map/ppermute | solution.py:444
  48.7 6.0 %collective-permute-start.17 = (f32[96,128]{1,0:T(8,128)S(1)}, f32[96,128]{1,0:T(8,128)S(1)}, u32[]{:S(2)}, u32[]{:S(2)}) collective-permute-start(f32[96,128]{1,0:T(8,128)S(1)} %get-tuple-element.64), channel_id=1, source_target_pairs={{0,6},{1,7},{2,4},{3,5},{4,2},{5,3},{6,0},{7,1},{8,14},{9,15},{10,... | collective-permute-start | bytes 147464 | tf_op jit(solution)/shard_map/ppermute | solution.py:444
  50.0 6.8 %collective-permute-start.18 = (f32[96,128]{1,0:T(8,128)S(1)}, f32[96,128]{1,0:T(8,128)S(1)}, u32[]{:S(2)}, u32[]{:S(2)}) collective-permute-start(f32[96,128]{1,0:T(8,128)S(1)} %get-tuple-element.65), channel_id=1, source_target_pairs={{0,7},{1,6},{2,5},{3,4},{4,3},{5,2},{6,1},{7,0},{8,15},{9,14},{10,... | collective-permute-start | bytes 147464 | tf_op jit(solution)/shard_map/ppermute | solution.py:444
  61.4 1.9 %collective-permute-start.19 = (f32[96,256]{1,0:T(8,128)S(1)}, f32[96,256]{1,0:T(8,128)S(1)}, u32[]{:S(2)}, u32[]{:S(2)}) collective-permute-start(f32[96,256]{1,0:T(8,128)S(1)} %get-tuple-element.67), channel_id=1, source_target_pairs={{0,8},{8,0},{16,24},{24,16},{1,9},{9,1},{17,25},{25,17},{2,10},{10... | collective-permute-start | bytes 294920 | tf_op jit(solution)/shard_map/ppermute | solution.py:444
  61.5 5.7 %collective-permute-start.20 = (f32[96,256]{1,0:T(8,128)S(1)}, f32[96,256]{1,0:T(8,128)S(1)}, u32[]{:S(2)}, u32[]{:S(2)}) collective-permute-start(f32[96,256]{1,0:T(8,128)S(1)} %get-tuple-element.68), channel_id=1, source_target_pairs={{0,16},{8,24},{16,0},{24,8},{1,17},{9,25},{17,1},{25,9},{2,18},{10... | collective-permute-start | bytes 294920 | tf_op jit(solution)/shard_map/ppermute | solution.py:444
  63.0 5.3 %collective-permute-start.21 = (f32[96,256]{1,0:T(8,128)S(1)}, f32[96,256]{1,0:T(8,128)S(1)}, u32[]{:S(2)}, u32[]{:S(2)}) collective-permute-start(f32[96,256]{1,0:T(8,128)S(1)} %get-tuple-element.69), channel_id=1, source_target_pairs={{0,24},{8,16},{16,8},{24,0},{1,25},{9,17},{17,9},{25,1},{2,26},{10... | collective-permute-start | bytes 294920 | tf_op jit(solution)/shard_map/ppermute | solution.py:444

commit v3 on v2

--- a/solution.py
+++ b/solution.py
@@ -38,41 +38,88 @@
     cells = count_x * width
     if count_x * 2 * cells * count_y * 2 * rows * 2 > constant_limit:
         return None
-    place = np.arange(cells)[None, :, None, None]
+    place = np.arange(cells)[None, None, :, None]
     wave = (
         np.arange(count_x)[:, None, None, None] * (count_y * rows)
-        + np.arange(count_y)[None, None, :, None] * rows
+        + np.arange(count_y)[None, :, None, None] * rows
         + np.arange(rows)[None, None, None, :]
     )
     angle = (place * wave % (2 * cells)) * (2.0 * math.pi / (2 * cells))
-    table = np.stack([np.cos(angle), -np.sin(angle)], 3)
-    table = table.reshape(count_x, count_x, width, count_y * 2 * rows)
+    table = np.concatenate([np.cos(angle), -np.sin(angle)], 3)
+    table = table.reshape(count_x, count_y, count_x, width, 2 * rows)
     high, low = split_table(table)
-    return np.stack([high, low], 1)
-
-
-def line_table_here(count_x, count_y, width, rows):
+    return np.stack([high, low], 2)
+
+
+def line_table_here(count_x, width, rows, order):
     cells = count_x * width
+    count_y = len(order)
     place = jnp.arange(cells, dtype=jnp.int32)[:, None, None]
+    block = lax.bitwise_xor(lax.axis_index("gy"), jnp.array(order, jnp.int32))
     wave = (
         lax.axis_index("gx") * (count_y * rows)
-        + jnp.arange(count_y, dtype=jnp.int32)[None, :, None] * rows
+        + block[None, :, None] * rows
         + jnp.arange(rows, dtype=jnp.int32)[None, None, :]
     )
     angle = (place * wave % (2 * cells)).astype(jnp.float32) * (math.pi / cells)
-    table = jnp.stack([jnp.cos(angle), -jnp.sin(angle)], 2).reshape(cells, count_y * 2 * rows)
-    return jnp.stack(split_high(table)).reshape(1, 2, count_x, width, count_y * 2 * rows)
-
-
-def column_tables(height):
-    angle = (np.arange(2 * height)[:, None] * np.arange(height)[None, :] % (2 * height)) * (
-        math.pi / height
-    )
+    table = jnp.concatenate([jnp.cos(angle), -jnp.sin(angle)], 2)
+    table = table.reshape(1, 1, count_x, width, count_y * 2 * rows)
+    return jnp.stack(split_high(table), 2)
+
+
+def column_tables(count_y, local, order):
+    height = count_y * local
+    wave = np.arange(2 * height)
+    block = np.arange(count_y)[:, None] ^ np.array(order)[None, :]
+    place = (block[:, :, None] * local + np.arange(local)).reshape(count_y, height)
+    angle = (wave[None, :, None] * place[:, None, :] % (2 * height)) * (math.pi / height)
+    high, low = split_table(np.concatenate([np.cos(angle), np.sin(angle)], 2))
+    forward = np.concatenate([high, high, low], 2)
+    angle = angle.transpose(0, 2, 1)
     high, low = split_table(np.concatenate([np.cos(angle), np.sin(angle)], 1))
-    forward = np.concatenate([high, high, low], 1)
-    high, low = split_table(np.concatenate([np.cos(angle.T), np.sin(angle.T)], 0))
-    inverse = np.concatenate([high, high, low], 1)
+    inverse = np.concatenate([high, high, low], 2)
     return forward, inverse
+
+
+def column_tables_here(count_y, local, order):
+    height = count_y * local
+    wave = jnp.arange(2 * height, dtype=jnp.int32)
+    block = lax.bitwise_xor(lax.axis_index("gy"), jnp.array(order, jnp.int32))
+    place = (block[:, None] * local + jnp.arange(local, dtype=jnp.int32)).reshape(height)
+    angle = (wave[:, None] * place % (2 * height)).astype(jnp.float32) * (math.pi / height)
+    high, low = split_high(jnp.concatenate([jnp.cos(angle), jnp.sin(angle)], 1))
+    forward = jnp.concatenate([high, high, low], 1)
+    high, low = split_high(jnp.concatenate([jnp.cos(angle.T), jnp.sin(angle.T)], 0))
+    inverse = jnp.concatenate([high, high, low], 1)
+    return forward[None], inverse[None]
+
+
+def load_kernel(order_x, order_y, place, *refs):
+    table_ref, forward_ref, inverse_ref, table, forward, inverse, sem = refs
+    gx, gy = place[0], place[1]
+    mine_x = gx if table_ref.shape[0] > 1 else 0
+    mine_y = gy if forward_ref.shape[0] > 1 else 0
+    lanes = table_ref.shape[5]
+    copies = [
+        pltpu.make_async_copy(forward_ref.at[mine_y], forward, sem.at[0]),
+        pltpu.make_async_copy(inverse_ref.at[mine_y], inverse, sem.at[1]),
+    ]
+    for spot_x, number_x in enumerate(order_x):
+        block_x = lax.bitwise_xor(gx, number_x)
+        for spot_y in range(table_ref.shape[1]):
+            block_y = lax.bitwise_xor(gy, order_y[spot_y]) if table_ref.shape[1] > 1 else 0
+            columns = slice(spot_y * lanes, (spot_y + 1) * lanes)
+            copies.append(
+                pltpu.make_async_copy(
+                    table_ref.at[mine_x, block_y, :, block_x],
+                    table.at[:, spot_x, :, columns],
+                    sem.at[len(copies)],
+                )
+            )
+    for copy in copies:
+        copy.start()
+    for copy in copies:
+        copy.wait()
 
 
 def sine_cosine(angle):
@@ -128,62 +175,36 @@
         last_ref[index] = value[:, height - 1]
 
 
-def table_copies(table_ref, table, sems, gx):
-    mine = gx if table_ref.shape[0] > 1 else 0
-    copies = []
-    for number in range(table_ref.shape[2]):
-        block = lax.bitwise_xor(gx, number)
-        copies.append(
-            pltpu.make_async_copy(table_ref.at[mine, :, block], table.at[number], sems.at[number])
-        )
-    for copy in copies:
-        copy.start()
-    return copies
-
-
 def lines_kernel(count_x, count_y, *refs):
-    raw_refs, (region, place, table_ref) = refs[:count_x], refs[count_x : count_x + 3]
-    out_refs = refs[count_x + 3 : count_x + 3 + count_y]
-    table, ordered, sems = refs[count_x + 3 + count_y :]
-    gx, gy = place[0], place[1]
-    copies = table_copies(table_ref, table, sems, gx)
-    halves = []
-    for raw_ref in raw_refs:
-        unit = directions(raw_ref[0], raw_ref[1])
-        saturation = looked_up(raw_ref[2], region)
+    raw_refs, (region_ref, table) = refs[:count_x], refs[count_x : count_x + 2]
+    out_refs, (region, sem) = refs[count_x + 2 : -2], refs[-2:]
+    fetch = pltpu.make_async_copy(region_ref, region, sem)
+    fetch.start()
+    units = [directions(raw_ref[0], raw_ref[1]) for raw_ref in raw_refs]
+    fetch.wait()
+    total = None
+    for number in range(count_x):
+        saturation = looked_up(raw_refs[number][2], region)
         rows = saturation.shape[0] * saturation.shape[1]
-        block = jnp.concatenate([(part * saturation).reshape(rows, -1) for part in unit], 0)
-        halves.append(split_high(block))
-    lines = 3 * rows
-    total = None
-    for (high, low), copy, number in zip(halves, copies, range(count_x)):
-        copy.wait()
-        both = dot(jnp.concatenate([high, low], 0), table[number, 0])
-        part = both[:lines] + both[lines:] + dot(high, table[number, 1])
+        block = [(part * saturation).reshape(rows, -1) for part in units[number]]
+        high, low = split_high(jnp.concatenate(block, 0))
+        both = dot(jnp.concatenate([high, low], 0), table[0, number])
+        part = both[: 3 * rows] + both[3 * rows :] + dot(high, table[1, number])
         total = part if total is None else total + part
-    lanes = ordered.shape[2]
-    for index in range(count_y):
-        ordered[index] = total[:, index * lanes : (index + 1) * lanes]
+    lanes = out_refs[0].shape[1]
     for number in range(count_y):
-        out_refs[number][...] = ordered[lax.bitwise_xor(gy, number)]
+        out_refs[number][...] = total[:, number * lanes : (number + 1) * lanes]
 
 
 def back_lines_kernel(count_x, count_y, *refs):
-    in_refs, (place, table_ref) = refs[:count_y], refs[count_y : count_y + 2]
-    out_refs = refs[count_y + 2 : count_y + 2 + count_x]
-    table, ordered, sems = refs[count_y + 2 + count_x :]
-    gx, gy = place[0], place[1]
-    copies = table_copies(table_ref, table, sems, gx)
-    for number in range(count_y):
-        ordered[lax.bitwise_xor(gy, number)] = in_refs[number][...]
-    high, low = split_high(jnp.concatenate([ordered[g] for g in range(count_y)], 1))
+    in_refs, table, out_refs = refs[:count_y], refs[count_y], refs[count_y + 1 :]
+    high, low = split_high(jnp.concatenate([ref[...] for ref in in_refs], 1))
     both = jnp.concatenate([high, low], 0)
     lines = high.shape[0]
     for number in range(count_x):
-        copies[number].wait()
-        wide = dot(both, table[number, 0], ((1,), (1,)))
+        wide = dot(both, table[0, number], ((1,), (1,)))
         out_refs[number][...] = (
-            wide[:lines] + wide[lines:] + dot(high, table[number, 1], ((1,), (1,)))
+            wide[:lines] + wide[lines:] + dot(high, table[1, number], ((1,), (1,)))
         )
 
 
@@ -252,13 +273,9 @@
 
 
 def waves_kernel(scale, count_y, *refs):
-    spec_refs, (place, tensor_ref, forward_ref, inverse_ref) = refs[:count_y], refs[count_y : count_y + 4]
-    out_refs = refs[count_y + 4 : 2 * count_y + 4]
-    ordered, wave_ref, back_ref = refs[2 * count_y + 4 :]
-    gy = place[1]
+    spec_refs, (tensor_ref, forward_ref, inverse_ref) = refs[:count_y], refs[count_y : count_y + 3]
+    out_refs, (wave_ref, back_ref) = refs[count_y + 3 : -2], refs[-2:]
     lines, lanes = spec_refs[0].shape
-    for number in range(count_y):
-        ordered[lax.bitwise_xor(gy, number)] = spec_refs[number][...]
     local = 8
     planes = lines // local
     height = count_y * local
@@ -267,7 +284,9 @@
     ).astype(jnp.float32)
     columns = []
     for plane in range(planes):
-        value = ordered[:, plane * local : (plane + 1) * local, :].reshape(height, lanes)
+        value = jnp.concatenate(
+            [ref[plane * local : (plane + 1) * local] for ref in spec_refs], 0
+        )
         value = jnp.concatenate([value, turn(value, sign)], 0)
         high, low = split_high(value)
         columns.append(jnp.concatenate([high, low, high], 0))
@@ -306,18 +325,20 @@
     for plane in range(planes):
         part = slice(plane * lanes, (plane + 1) * lanes)
         value = back[:height, part] - turn(back[height:, part], sign)
-        ordered[:, plane * local : (plane + 1) * local, :] = value.reshape(count_y, local, lanes)
-    for number in range(count_y):
-        out_refs[number][...] = ordered[lax.bitwise_xor(gy, number)]
-
-
-def exchange_kernel(count_x, count_y, *refs):
+        for number in range(count_y):
+            out_refs[number][plane * local : (plane + 1) * local] = value[
+                number * local : (number + 1) * local
+            ]
+
+
+def exchange_kernel(order_x, count_y, *refs):
+    count_x = len(order_x)
     raw_refs, (before_ref, after_ref, place, ms_ref, aex_ref) = refs[:count_x], refs[count_x : count_x + 5]
     exchange_ref, unit_ref, raw_ref = refs[count_x + 5 :]
     depth, height, width = raw_ref.shape[2:]
     gx, gy = place[0], place[1]
-    for number in range(count_x):
-        raw_ref[lax.bitwise_xor(gx, number)] = raw_refs[number][...]
+    for spot, number in enumerate(order_x):
+        raw_ref[lax.bitwise_xor(gx, number)] = raw_refs[spot][...]
     left, right = jnp.maximum(gx - 1, 0), jnp.minimum(gx + 1, count_x - 1)
     shape = (depth, height, width)
     lane = lax.broadcasted_iota(jnp.int32, shape, 2)
@@ -419,12 +440,12 @@
     ]
     size = sum(math.prod(o.shape) * o.dtype.itemsize for o in operands)
     outs = out if isinstance(out, (list, tuple)) else [out]
-    size += sum(math.prod(o.shape) * o.dtype.itemsize for o in outs)
+    size += sum(math.prod(o.shape) * jnp.dtype(o.dtype).itemsize for o in outs)
     return pl.pallas_call(
         body,
         out_shape=out,
         in_specs=ins,
-        out_specs=jax.tree.map(lambda _: vmem, out),
+        out_specs=[vmem] * len(outs) if outs is out else vmem,
         scratch_shapes=list(scratch),
         compiler_params=pltpu.CompilerParams(vmem_limit_bytes=grant),
         cost_estimate=pl.CostEstimate(flops=flops, bytes_accessed=size, transcendentals=0),
@@ -436,13 +457,17 @@
     return jax.ShapeDtypeStruct(shape, jnp.float32)
 
 
-def exchanged(chunks, axis):
-    devices = lax.axis_size(axis)
+def exchanged(chunks, axis, order):
+    devices = len(order)
     out = [chunks[0]] + [None] * (devices - 1)
-    for number in reversed(range(1, devices)):
+    for spot, number in enumerate(order[1:]):
         pairs = [(i, i ^ number) for i in range(devices)]
-        out[number] = lax.ppermute(chunks[number], axis, pairs)
+        out[spot + 1] = lax.ppermute(chunks[spot + 1], axis, pairs)
     return out
+
+
+def partners(devices):
+    return [0] + list(range(devices - 1, 0, -1))
 
 
 def per_device(theta, phi, labels, ms_region, aex_region, kernel):
@@ -456,16 +481,15 @@
 
     place = jnp.stack([gx, gy]).astype(jnp.int32)
     cells = f32(3, depth, height, width)
+    order_x, order_y = partners(count_x), partners(count_y)
     table = line_table(count_x, count_y, width, rows)
     if table is None:
-        table = line_table_here(count_x, count_y, width, rows)
-    table = jnp.asarray(table)
-    forward, inverse = column_tables(whole_y)
+        table = line_table_here(count_x, width, rows, order_y)
+        columns_tables = column_tables_here(count_y, height, order_y)
+    else:
+        columns_tables = column_tables(count_y, height, order_y)
+    sources = [jnp.asarray(t) for t in (table, *columns_tables)]
     twice = np.concatenate([np.eye(rows), np.eye(rows)], 1).astype(ml_dtypes.bfloat16)
-    table_scratch = pltpu.VMEM((count_x, 2, width, count_y * lanes), jnp.bfloat16)
-    ordered = pltpu.VMEM((count_y, lines, lanes), jnp.float32)
-    table_grant = (12 << 20) + 5 * math.prod(table_scratch.shape)
-    table_sems = pltpu.SemaphoreType.DMA((count_x,))
     transform_flops = 6 * lines * count_x * width * count_y * lanes
 
     packed, first, last = call(
@@ -480,11 +504,24 @@
         ),
         name="pack",
     )
-    gathered = exchanged([packed] * count_x, "gx")
+    gathered = exchanged([packed] * count_x, "gx", order_x)
     up = [(i, i + 1) for i in range(count_y - 1)]
     down = [(j, i) for i, j in up]
     before = lax.ppermute(last, "gy", up)
     after = lax.ppermute(first, "gy", down)
+    gathered, before, after = lax.optimization_barrier((gathered, before, after))
+    table, forward, inverse = call(
+        functools.partial(load_kernel, order_x, order_y),
+        [
+            pltpu.VMEM((2, count_x, width, count_y * lanes), jnp.bfloat16),
+            pltpu.VMEM(sources[1].shape[1:], jnp.bfloat16),
+            pltpu.VMEM(sources[2].shape[1:], jnp.bfloat16),
+        ],
+        [smem] + [hbm] * 3,
+        (place, *sources),
+        scratch=(pltpu.SemaphoreType.DMA((2 + count_x * count_y,)),),
+        name="load",
+    )
 
     tensor = call(
         tensor_kernel,
@@ -497,16 +534,15 @@
     spectrum = call(
         functools.partial(lines_kernel, count_x, count_y),
         [f32(lines, lanes)] * count_y,
-        [vmem] * count_x + [smem, smem, hbm],
-        (*gathered, ms_region, place, table),
-        scratch=(table_scratch, ordered, table_sems),
-        grant=table_grant,
+        [vmem] * count_x + [hbm, vmem],
+        (*gathered, ms_region, table),
+        scratch=(pltpu.SMEM(ms_region.shape, jnp.float32), pltpu.SemaphoreType.DMA),
         flops=transform_flops,
         name="lines",
     )
-    columns = exchanged(spectrum, "gy")
+    columns = exchanged(spectrum, "gy", order_y)
     exchange, unit = call(
-        functools.partial(exchange_kernel, count_x, count_y),
+        functools.partial(exchange_kernel, order_x, count_y),
         [cells, cells],
         [vmem] * (count_x + 2) + [smem] * 3,
         (*gathered, before, after, place, ms_region, aex_region),
@@ -519,28 +555,25 @@
     waves = call(
         functools.partial(waves_kernel, scale, count_y),
         [f32(lines, lanes)] * count_y,
-        [vmem] * count_y + [smem] + [vmem] * 3,
-        (*columns, place, tensor, jnp.asarray(forward), jnp.asarray(inverse)),
+        [vmem] * (count_y + 3),
+        (*columns, tensor, forward, inverse),
         scratch=(
-            ordered,
             pltpu.VMEM((2 * whole_y, 3 * depth * lanes), jnp.float32),
             pltpu.VMEM((6 * whole_y, 3 * depth * lanes), jnp.bfloat16),
         ),
         flops=20 * whole_y * whole_y * 3 * depth * lanes,
         name="waves",
     )
-    returned = exchanged(waves, "gy")
+    returned = exchanged(waves, "gy", order_y)
     partial = call(
         functools.partial(back_lines_kernel, count_x, count_y),
         [f32(lines, width)] * count_x,
-        [vmem] * count_y + [smem, hbm],
-        (*returned, place, table),
-        scratch=(table_scratch, ordered, table_sems),
-        grant=table_grant,
+        [vmem] * (count_y + 1),
+        (*returned, table),
         flops=transform_flops,
         name="back_lines",
     )
-    parts = exchanged(partial, "gx")
+    parts = exchanged(partial, "gx", order_x)
     field, predicted = call(
         functools.partial(final_kernel, count_x),
         [cells, cells],

time: 69.2 us -> 58.3 us (0.84)
  waiting for transfers between devices: 15.9 us -> 10.2 us
  starting transfers between devices: 35.8 us -> 33.3 us
  Pallas kernels: 15.8 us -> 13.6 us
    ppermute x20, waiting for transfers between devices: 15.9 us -> 9.27 us  [exchanged(): out[spot + 1] = lax.ppermute(chunks[spot + 1], axis, pairs)]
    ppermute x20, starting transfers between devices: 32.1 us -> 28.3 us  [exchanged(): out[spot + 1] = lax.ppermute(chunks[spot + 1], axis, pairs)]
    pallas_call x7 -> x8, Pallas kernels: 15.8 us -> 13.6 us  [call(): pl.pallas_call(body, out_shape=out, in_specs=ins, out_specs=[vmem] * len(...]
    ppermute x1, starting transfers between devices: 2.4 us -> 3.65 us  [per_device(): before = lax.ppermute(last, 'gy', up)]
    ppermute x1, waiting for transfers between devices: 0.01 us -> 0.96 us  [per_device(): after = lax.ppermute(first, 'gy', down)]
  transfers between devices with their start and end apart: 22 -> 22, of which waited for: 7 -> 10; matrix products, arithmetic and copies ran while one was open for 0% -> 0% of each run, Pallas kernels for 4% -> 10%
where the time goes in v3:
time: 58.3 us; the launch traced here: 58.1 us
  starting transfers between devices  33.3 us (57%)
  Pallas kernels  13.6 us (23%)
  waiting for transfers between devices  10.2 us (17%)
  between operations  0.82 us (1%)
    ppermute x20, starting transfers between devices, exchanged(): out[spot + 1] = lax.ppermute(chunks[spot + 1], axis, pairs)  28.3 us
    pallas_call x8, Pallas kernels, call(): pl.pallas_call(body, out_shape=out, in_specs=ins, out_specs=[vmem] * len(...  13.6 us
    ppermute x20, waiting for transfers between devices, exchanged(): out[spot + 1] = lax.ppermute(chunks[spot + 1], axis, pairs)  9.27 us
    ppermute x1, starting transfers between devices, per_device(): before = lax.ppermute(last, 'gy', up)  3.65 us
    ppermute x1, starting transfers between devices, per_device(): after = lax.ppermute(first, 'gy', down)  1.29 us
  transfers between devices with their start and end apart: 22, of which 10 were waited for; matrix products, arithmetic and copies ran while one was open for 0% of the time, Pallas kernels for 10%

profile of v3, /device:TPU:0, one launch (start us, length us, event | category | flops | bytes accessed | tf_op | source)
XLA Modules:
  0.0 58.1 jit_solution(7455464545481359266)
XLA Ops:
  0.6 0.8 %pack.1 = (f32[3,4,8,256]{3,2,1,0:T(8,128)S(1)}, f32[3,4,256]{2,1,0:T(4,128)S(1)}, f32[3,4,256]{2,1,0:T(4,128)S(1)}) custom-call(f32[4,8,256]{2,1,0:T(8,128)} %theta_ref.1, f32[4,8,256]{2,1,0:T(8,128)} %phi_ref.1, s32[4,8,256]{2,1,0:T(8,128)} %labels_ref.1), custom_call_target="tpu_custom_call" | custom-call | bytes 221184 | tf_op jit(solution)/shard_map/pack/pallas_call | solution.py:444
  2.0 2.6 %collective-permute-start.1 = (f32[3,4,8,256]{3,2,1,0:T(8,128)S(1)}, f32[3,4,8,256]{3,2,1,0:T(8,128)S(1)}, u32[]{:S(2)}, u32[]{:S(2)}) collective-permute-start(f32[3,4,8,256]{3,2,1,0:T(8,128)S(1)} %get-tuple-element.49.refs_0_), channel_id=1, source_target_pairs={{0,16},{8,24},{16,0},{24,8},{1,17},{9,25},{17,1},{25,9},{2,18},{10... | collective-permute-start | bytes 294920 | tf_op jit(solution)/shard_map/ppermute | solution.py:465
  4.6 3.6 %collective-permute-start.3 = (f32[3,4,256]{2,1,0:T(4,128)S(1)}, f32[3,4,256]{2,1,0:T(4,128)S(1)}, u32[]{:S(2)}, u32[]{:S(2)}) collective-permute-start(f32[3,4,256]{2,1,0:T(4,128)S(1)} %get-tuple-element.47), channel_id=1, source_target_pairs={{0,1},{1,2},{2,3},{3,4},{4,5},{5,6},{6,7},{8,9},{9,10},{10,11},{11... | collective-permute-start | bytes 36872 | tf_op jit(solution)/shard_map/ppermute | solution.py:510
  8.3 1.3 %collective-permute-start.4 = (f32[3,4,256]{2,1,0:T(4,128)S(1)}, f32[3,4,256]{2,1,0:T(4,128)S(1)}, u32[]{:S(2)}, u32[]{:S(2)}) collective-permute-start(f32[3,4,256]{2,1,0:T(4,128)S(1)} %get-tuple-element.48), channel_id=1, source_target_pairs={{1,0},{2,1},{3,2},{4,3},{5,4},{6,5},{7,6},{9,8},{10,9},{11,10},{12... | collective-permute-start | bytes 36872 | tf_op jit(solution)/shard_map/ppermute | solution.py:511
  9.7 3.2 %load.1 = (bf16[2,4,256,1024]{3,2,1,0:T(8,128)(2,1)S(1)}, bf16[128,384]{1,0:T(8,128)(2,1)S(1)}, bf16[128,384]{1,0:T(8,128)(2,1)S(1)}) custom-call(s32[2]{0:T(128)S(1)} %pad_add_fusion.place.refs_6_, bf16[4,8,2,4,256,128]{5,4,3,2,1,0:T(8,128)(2,1)} %constant.16.clone.refs_0_, bf16[8,128,384]{2,1,0:T(8,128)(2,1)} %constant.17.clone.refs_1_, ...), custom_call_target="tpu_custom_call" | custom-call | bytes 22741000 | tf_op jit(solution)/shard_map/load/pallas_call | solution.py:444
  12.9 1.0 %collective-permute-done.4.refs_5_ = f32[3,4,256]{2,1,0:T(4,128)S(1)} collective-permute-done((f32[3,4,256]{2,1,0:T(4,128)S(1)}, f32[3,4,256]{2,1,0:T(4,128)S(1)}, u32[]{:S(2)}, u32[]{:S(2)}) %collective-permute-start.4) | collective-permute-done | bytes 12320 | tf_op jit(solution)/shard_map/ppermute | solution.py:511
  13.9 1.6 %lines.1 = (f32[96,128]{1,0:T(8,128)S(1)}, f32[96,128]{1,0:T(8,128)S(1)}, f32[96,128]{1,0:T(8,128)S(1)}, f32[96,128]{1,0:T(8,128)S(1)}, f32[96,128]{1,0:T(8,128)...) custom-call(f32[3,4,8,256]{3,2,1,0:T(8,128)S(1)} %get-tuple-element.49.refs_0_, ...), custom_call_target="tpu_custom_call" | custom-call | flops 603979776 | bytes 4980800 | tf_op jit(solution)/shard_map/lines/pallas_call | solution.py:444
  15.5 5.0 %collective-permute-start.5 = (f32[96,128]{1,0:T(8,128)S(1)}, f32[96,128]{1,0:T(8,128)S(1)}, u32[]{:S(2)}, u32[]{:S(2)}) collective-permute-start(f32[96,128]{1,0:T(8,128)S(1)} %get-tuple-element.55), channel_id=1, source_target_pairs={{0,7},{1,6},{2,5},{3,4},{4,3},{5,2},{6,1},{7,0},{8,15},{9,14},{10,... | collective-permute-start | bytes 147464 | tf_op jit(solution)/shard_map/ppermute | solution.py:465
  20.4 0.8 %collective-permute-start.6 = (f32[96,128]{1,0:T(8,128)S(1)}, f32[96,128]{1,0:T(8,128)S(1)}, u32[]{:S(2)}, u32[]{:S(2)}) collective-permute-start(f32[96,128]{1,0:T(8,128)S(1)} %get-tuple-element.56), channel_id=1, source_target_pairs={{0,6},{1,7},{2,4},{3,5},{4,2},{5,3},{6,0},{7,1},{8,14},{9,15},{10,... | collective-permute-start | bytes 147464 | tf_op jit(solution)/shard_map/ppermute | solution.py:465
  21.2 1.1 %collective-permute-start.7 = (f32[96,128]{1,0:T(8,128)S(1)}, f32[96,128]{1,0:T(8,128)S(1)}, u32[]{:S(2)}, u32[]{:S(2)}) collective-permute-start(f32[96,128]{1,0:T(8,128)S(1)} %get-tuple-element.57), channel_id=1, source_target_pairs={{0,5},{1,4},{2,7},{3,6},{4,1},{5,0},{6,3},{7,2},{8,13},{9,12},{10,... | collective-permute-start | bytes 147464 | tf_op jit(solution)/shard_map/ppermute | solution.py:465
  22.3 1.9 %collective-permute-start.8 = (f32[96,128]{1,0:T(8,128)S(1)}, f32[96,128]{1,0:T(8,128)S(1)}, u32[]{:S(2)}, u32[]{:S(2)}) collective-permute-start(f32[96,128]{1,0:T(8,128)S(1)} %get-tuple-element.58), channel_id=1, source_target_pairs={{0,4},{1,5},{2,6},{3,7},{4,0},{5,1},{6,2},{7,3},{8,12},{9,13},{10,... | collective-permute-start | bytes 147464 | tf_op jit(solution)/shard_map/ppermute | solution.py:465
  24.2 1.5 %collective-permute-start.9 = (f32[96,128]{1,0:T(8,128)S(1)}, f32[96,128]{1,0:T(8,128)S(1)}, u32[]{:S(2)}, u32[]{:S(2)}) collective-permute-start(f32[96,128]{1,0:T(8,128)S(1)} %get-tuple-element.59), channel_id=1, source_target_pairs={{0,3},{1,2},{2,1},{3,0},{4,7},{5,6},{6,5},{7,4},{8,11},{9,10},{10,... | collective-permute-start | bytes 147464 | tf_op jit(solution)/shard_map/ppermute | solution.py:465
  25.7 1.4 %collective-permute-start.10 = (f32[96,128]{1,0:T(8,128)S(1)}, f32[96,128]{1,0:T(8,128)S(1)}, u32[]{:S(2)}, u32[]{:S(2)}) collective-permute-start(f32[96,128]{1,0:T(8,128)S(1)} %get-tuple-element.60), channel_id=1, source_target_pairs={{0,2},{1,3},{2,0},{3,1},{4,6},{5,7},{6,4},{7,5},{8,10},{9,11},{10,... | collective-permute-start | bytes 147464 | tf_op jit(solution)/shard_map/ppermute | solution.py:465
  27.1 0.7 %collective-permute-start.11 = (f32[96,128]{1,0:T(8,128)S(1)}, f32[96,128]{1,0:T(8,128)S(1)}, u32[]{:S(2)}, u32[]{:S(2)}) collective-permute-start(f32[96,128]{1,0:T(8,128)S(1)} %get-tuple-element.61), channel_id=1, source_target_pairs={{0,1},{1,0},{2,3},{3,2},{4,5},{5,4},{6,7},{7,6},{8,9},{9,8},{10,11... | collective-permute-start | bytes 147464 | tf_op jit(solution)/shard_map/ppermute | solution.py:465
  27.8 1.6 %tensor.1.refs_8_ = bf16[48,128,128]{2,1,0:T(8,128)(2,1)S(1)} custom-call(bf16[48,64,128]{2,1,0:T(8,128)(2,1)S(1)} %bitcast.3, bf16[64,128]{1,0:T(8,128)(2,1)S(1)} %copy-done.1), custom_call_target="tpu_custom_call" | custom-call | flops 100663296 | bytes 2375680 | tf_op jit(solution)/shard_map/tensor/pallas_call | solution.py:444
  29.4 1.1 %exchange.1 = (f32[3,4,8,256]{3,2,1,0:T(8,128)S(1)}, f32[3,4,8,256]{3,2,1,0:T(8,128)S(1)}) custom-call(f32[3,4,8,256]{3,2,1,0:T(8,128)S(1)} %get-tuple-element.49.refs_0_, f32[3,4,8,256]{3,2,1,0:T(8,128)S(1)} %collective-permute-done.refs_1_, f32[3,4,8,256]{3,2,1,0:T(8,128)S(1)} %collective-permute-done.1.refs_2_, ...), custom_call_target="tpu_custom_call" | custom-call | flops 2457600 | bytes 614536 | tf_op jit(solution)/shard_map/exchange/pallas_call | solution.py:444
  30.6 0.6 %collective-permute-done.11.refs_7_ = f32[96,128]{1,0:T(8,128)S(1)} collective-permute-done((f32[96,128]{1,0:T(8,128)S(1)}, f32[96,128]{1,0:T(8,128)S(1)}, u32[]{:S(2)}, u32[]{:S(2)}) %collective-permute-start.11) | collective-permute-done | bytes 49184 | tf_op jit(solution)/shard_map/ppermute | solution.py:465
  31.2 3.1 %waves.1 = (f32[96,128]{1,0:T(8,128)S(1)}, f32[96,128]{1,0:T(8,128)S(1)}, f32[96,128]{1,0:T(8,128)S(1)}, f32[96,128]{1,0:T(8,128)S(1)}, f32[96,128]{1,0:T(8,128)...) custom-call(f32[96,128]{1,0:T(8,128)S(1)} %get-tuple-element.66.refs_0_, ...), custom_call_target="tpu_custom_call" | custom-call | flops 125829120 | bytes 2555904 | tf_op jit(solution)/shard_map/waves/pallas_call | solution.py:444
  34.3 3.9 %collective-permute-start.12 = (f32[96,128]{1,0:T(8,128)S(1)}, f32[96,128]{1,0:T(8,128)S(1)}, u32[]{:S(2)}, u32[]{:S(2)}) collective-permute-start(f32[96,128]{1,0:T(8,128)S(1)} %get-tuple-element.77), channel_id=1, source_target_pairs={{0,7},{1,6},{2,5},{3,4},{4,3},{5,2},{6,1},{7,0},{8,15},{9,14},{10,... | collective-permute-start | bytes 147464 | tf_op jit(solution)/shard_map/ppermute | solution.py:465
  38.4 0.7 %collective-permute-start.14 = (f32[96,128]{1,0:T(8,128)S(1)}, f32[96,128]{1,0:T(8,128)S(1)}, u32[]{:S(2)}, u32[]{:S(2)}) collective-permute-start(f32[96,128]{1,0:T(8,128)S(1)} %get-tuple-element.79), channel_id=1, source_target_pairs={{0,5},{1,4},{2,7},{3,6},{4,1},{5,0},{6,3},{7,2},{8,13},{9,12},{10,... | collective-permute-start | bytes 147464 | tf_op jit(solution)/shard_map/ppermute | solution.py:465
  39.1 3.0 %collective-permute-start.15 = (f32[96,128]{1,0:T(8,128)S(1)}, f32[96,128]{1,0:T(8,128)S(1)}, u32[]{:S(2)}, u32[]{:S(2)}) collective-permute-start(f32[96,128]{1,0:T(8,128)S(1)} %get-tuple-element.80), channel_id=1, source_target_pairs={{0,4},{1,5},{2,6},{3,7},{4,0},{5,1},{6,2},{7,3},{8,12},{9,13},{10,... | collective-permute-start | bytes 147464 | tf_op jit(solution)/shard_map/ppermute | solution.py:465
  42.0 1.5 %collective-permute-start.16 = (f32[96,128]{1,0:T(8,128)S(1)}, f32[96,128]{1,0:T(8,128)S(1)}, u32[]{:S(2)}, u32[]{:S(2)}) collective-permute-start(f32[96,128]{1,0:T(8,128)S(1)} %get-tuple-element.81), channel_id=1, source_target_pairs={{0,3},{1,2},{2,1},{3,0},{4,7},{5,6},{6,5},{7,4},{8,11},{9,10},{10,... | collective-permute-start | bytes 147464 | tf_op jit(solution)/shard_map/ppermute | solution.py:465
  43.6 0.7 %collective-permute-start.17 = (f32[96,128]{1,0:T(8,128)S(1)}, f32[96,128]{1,0:T(8,128)S(1)}, u32[]{:S(2)}, u32[]{:S(2)}) collective-permute-start(f32[96,128]{1,0:T(8,128)S(1)} %get-tuple-element.82), channel_id=1, source_target_pairs={{0,2},{1,3},{2,0},{3,1},{4,6},{5,7},{6,4},{7,5},{8,10},{9,11},{10,... | collective-permute-start | bytes 147464 | tf_op jit(solution)/shard_map/ppermute | solution.py:465
  44.5 1.0 %collective-permute-start.18 = (f32[96,128]{1,0:T(8,128)S(1)}, f32[96,128]{1,0:T(8,128)S(1)}, u32[]{:S(2)}, u32[]{:S(2)}) collective-permute-start(f32[96,128]{1,0:T(8,128)S(1)} %get-tuple-element.83), channel_id=1, source_target_pairs={{0,1},{1,0},{2,3},{3,2},{4,5},{5,4},{6,7},{7,6},{8,9},{9,8},{10,11... | collective-permute-start | bytes 147464 | tf_op jit(solution)/shard_map/ppermute | solution.py:465
  45.7 1.3 %collective-permute-done.16.refs_5_ = f32[96,128]{1,0:T(8,128)S(1)} collective-permute-done((f32[96,128]{1,0:T(8,128)S(1)}, f32[96,128]{1,0:T(8,128)S(1)}, u32[]{:S(2)}, u32[]{:S(2)}) %collective-permute-start.16) | collective-permute-done | bytes 49184 | tf_op jit(solution)/shard_map/ppermute | solution.py:465
  47.0 0.6 %collective-permute-done.17.refs_6_ = f32[96,128]{1,0:T(8,128)S(1)} collective-permute-done((f32[96,128]{1,0:T(8,128)S(1)}, f32[96,128]{1,0:T(8,128)S(1)}, u32[]{:S(2)}, u32[]{:S(2)}) %collective-permute-start.17) | collective-permute-done | bytes 49184 | tf_op jit(solution)/shard_map/ppermute | solution.py:465
  47.6 0.9 %collective-permute-done.18.refs_7_ = f32[96,128]{1,0:T(8,128)S(1)} collective-permute-done((f32[96,128]{1,0:T(8,128)S(1)}, f32[96,128]{1,0:T(8,128)S(1)}, u32[]{:S(2)}, u32[]{:S(2)}) %collective-permute-start.18) | collective-permute-done | bytes 49184 | tf_op jit(solution)/shard_map/ppermute | solution.py:465
  48.6 1.4 %back_lines.1 = (f32[96,256]{1,0:T(8,128)S(1)}, f32[96,256]{1,0:T(8,128)S(1)}, f32[96,256]{1,0:T(8,128)S(1)}, f32[96,256]{1,0:T(8,128)S(1)}) custom-call(f32[96,128]{1,0:T(8,128)S(1)} %get-tuple-element.76.refs_0_, f32[96,128]{1,0:T(8,128)S(1)} %collective-permute-done.12.refs_1_, f32[96,128]{1,0:T(8,128)S(1)} %collective-permute-done.13.refs_2_, ...), custom_call_target="tpu_custom_call" | custom-call | flops 603979776 | bytes 4980736 | tf_op jit(solution)/shard_map/back_lines/pallas_call | solution.py:444
  50.1 1.5 %collective-permute-start.20 = (f32[96,256]{1,0:T(8,128)S(1)}, f32[96,256]{1,0:T(8,128)S(1)}, u32[]{:S(2)}, u32[]{:S(2)}) collective-permute-start(f32[96,256]{1,0:T(8,128)S(1)} %get-tuple-element.86), channel_id=1, source_target_pairs={{0,16},{8,24},{16,0},{24,8},{1,17},{9,25},{17,1},{25,9},{2,18},{10... | collective-permute-start | bytes 294920 | tf_op jit(solution)/shard_map/ppermute | solution.py:465
  52.0 3.2 %collective-permute-done.19.refs_1_ = f32[96,256]{1,0:T(8,128)S(1)} collective-permute-done((f32[96,256]{1,0:T(8,128)S(1)}, f32[96,256]{1,0:T(8,128)S(1)}, u32[]{:S(2)}, u32[]{:S(2)}) %collective-permute-start.19) | collective-permute-done | bytes 98336 | tf_op jit(solution)/shard_map/ppermute | solution.py:465
  55.2 2.1 %collective-permute-done.20.refs_2_ = f32[96,256]{1,0:T(8,128)S(1)} collective-permute-done((f32[96,256]{1,0:T(8,128)S(1)}, f32[96,256]{1,0:T(8,128)S(1)}, u32[]{:S(2)}, u32[]{:S(2)}) %collective-permute-start.20) | collective-permute-done | bytes 98336 | tf_op jit(solution)/shard_map/ppermute | solution.py:465
  57.3 0.7 %predict.1 = (f32[3,4,8,256]{3,2,1,0:T(8,128)}, f32[3,4,8,256]{3,2,1,0:T(8,128)}) custom-call(f32[96,256]{1,0:T(8,128)S(1)} %get-tuple-element.84.refs_0_, f32[96,256]{1,0:T(8,128)S(1)} %collective-permute-done.19.refs_1_, f32[96,256]{1,0:T(8,128)S(1)} %collective-permute-done.20.refs_2_, f32[96,256]{1,0:T(8,128)S(1)} %collective-permute-done.21.refs_3_, ...), custom_call_target="tpu_custom_call" | custom-call | flops 491520 | bytes 786432 | tf_op jit(solution)/shard_map/predict/pallas_call | solution.py:444
  (29 shorter events, 1.6 us)
Async XLA Ops:
  1.5 12.4 %collective-permute-start.2 = (f32[3,4,8,256]{3,2,1,0:T(8,128)S(1)}, f32[3,4,8,256]{3,2,1,0:T(8,128)S(1)}, u32[]{:S(2)}, u32[]{:S(2)}) collective-permute-start(f32[3,4,8,256]{3,2,1,0:T(8,128)S(1)} %get-tuple-element.49.refs_0_), channel_id=1, source_target_pairs={{0,8},{8,0},{16,24},{24,16},{1,9},{9,1},{17,25},{25,17},{2,10},{10... | collective-permute-start | bytes 294920 | tf_op jit(solution)/shard_map/ppermute | solution.py:465
  2.0 11.9 %collective-permute-start.1 = (f32[3,4,8,256]{3,2,1,0:T(8,128)S(1)}, f32[3,4,8,256]{3,2,1,0:T(8,128)S(1)}, u32[]{:S(2)}, u32[]{:S(2)}) collective-permute-start(f32[3,4,8,256]{3,2,1,0:T(8,128)S(1)} %get-tuple-element.49.refs_0_), channel_id=1, source_target_pairs={{0,16},{8,24},{16,0},{24,8},{1,17},{9,25},{17,1},{25,9},{2,18},{10... | collective-permute-start | bytes 294920 | tf_op jit(solution)/shard_map/ppermute | solution.py:465
  4.6 9.3 %collective-permute-start = (f32[3,4,8,256]{3,2,1,0:T(8,128)S(1)}, f32[3,4,8,256]{3,2,1,0:T(8,128)S(1)}, u32[]{:S(2)}, u32[]{:S(2)}) collective-permute-start(f32[3,4,8,256]{3,2,1,0:T(8,128)S(1)} %get-tuple-element.49.refs_0_), channel_id=1, source_target_pairs={{0,24},{8,16},{16,8},{24,0},{1,25},{9,17},{17,9},{25,1},{2,26},{10... | collective-permute-start | bytes 294920 | tf_op jit(solution)/shard_map/ppermute | solution.py:465
  4.6 8.3 %collective-permute-start.3 = (f32[3,4,256]{2,1,0:T(4,128)S(1)}, f32[3,4,256]{2,1,0:T(4,128)S(1)}, u32[]{:S(2)}, u32[]{:S(2)}) collective-permute-start(f32[3,4,256]{2,1,0:T(4,128)S(1)} %get-tuple-element.47), channel_id=1, source_target_pairs={{0,1},{1,2},{2,3},{3,4},{4,5},{5,6},{6,7},{8,9},{9,10},{10,11},{11... | collective-permute-start | bytes 36872 | tf_op jit(solution)/shard_map/ppermute | solution.py:510
  8.3 5.6 %collective-permute-start.4 = (f32[3,4,256]{2,1,0:T(4,128)S(1)}, f32[3,4,256]{2,1,0:T(4,128)S(1)}, u32[]{:S(2)}, u32[]{:S(2)}) collective-permute-start(f32[3,4,256]{2,1,0:T(4,128)S(1)} %get-tuple-element.48), channel_id=1, source_target_pairs={{1,0},{2,1},{3,2},{4,3},{5,4},{6,5},{7,6},{9,8},{10,9},{11,10},{12... | collective-permute-start | bytes 36872 | tf_op jit(solution)/shard_map/ppermute | solution.py:511
  12.9 14.9 %copy-start = (bf16[6,8,64,128]{3,2,1,0:T(8,128)(2,1)S(1)}, bf16[6,8,64,128]{3,2,1,0:T(8,128)(2,1)}, u32[]{:S(2)}) copy-start(bf16[6,8,64,128]{3,2,1,0:T(8,128)(2,1)} %param.15) | copy-start | bytes 2359300
  12.9 14.9 %copy-start.1 = (bf16[64,128]{1,0:T(8,128)(2,1)S(1)}, bf16[64,128]{1,0:T(8,128)(2,1)}, u32[]{:S(2)}) copy-start(bf16[64,128]{1,0:T(8,128)(2,1)} %constant.19.clone.twice_ref) | copy-start | bytes 49156
  12.9 16.5 %copy-start.2 = (f32[16]{0:T(128)S(1)}, f32[16]{0:T(128)}, u32[]{:S(2)}) copy-start(f32[16]{0:T(128)} %refs_7_.1) | copy-start | bytes 196
  12.9 16.5 %copy-start.3 = (f32[16]{0:T(128)S(1)}, f32[16]{0:T(128)}, u32[]{:S(2)}) copy-start(f32[16]{0:T(128)} %refs_8_.1) | copy-start | bytes 196
  15.5 10.2 %collective-permute-start.5 = (f32[96,128]{1,0:T(8,128)S(1)}, f32[96,128]{1,0:T(8,128)S(1)}, u32[]{:S(2)}, u32[]{:S(2)}) collective-permute-start(f32[96,128]{1,0:T(8,128)S(1)} %get-tuple-element.55), channel_id=1, source_target_pairs={{0,7},{1,6},{2,5},{3,4},{4,3},{5,2},{6,1},{7,0},{8,15},{9,14},{10,... | collective-permute-start | bytes 147464 | tf_op jit(solution)/shard_map/ppermute | solution.py:465
  20.4 6.7 %collective-permute-start.6 = (f32[96,128]{1,0:T(8,128)S(1)}, f32[96,128]{1,0:T(8,128)S(1)}, u32[]{:S(2)}, u32[]{:S(2)}) collective-permute-start(f32[96,128]{1,0:T(8,128)S(1)} %get-tuple-element.56), channel_id=1, source_target_pairs={{0,6},{1,7},{2,4},{3,5},{4,2},{5,3},{6,0},{7,1},{8,14},{9,15},{10,... | collective-permute-start | bytes 147464 | tf_op jit(solution)/shard_map/ppermute | solution.py:465
  21.2 9.3 %collective-permute-start.7 = (f32[96,128]{1,0:T(8,128)S(1)}, f32[96,128]{1,0:T(8,128)S(1)}, u32[]{:S(2)}, u32[]{:S(2)}) collective-permute-start(f32[96,128]{1,0:T(8,128)S(1)} %get-tuple-element.57), channel_id=1, source_target_pairs={{0,5},{1,4},{2,7},{3,6},{4,1},{5,0},{6,3},{7,2},{8,13},{9,12},{10,... | collective-permute-start | bytes 147464 | tf_op jit(solution)/shard_map/ppermute | solution.py:465
  22.3 8.3 %collective-permute-start.8 = (f32[96,128]{1,0:T(8,128)S(1)}, f32[96,128]{1,0:T(8,128)S(1)}, u32[]{:S(2)}, u32[]{:S(2)}) collective-permute-start(f32[96,128]{1,0:T(8,128)S(1)} %get-tuple-element.58), channel_id=1, source_target_pairs={{0,4},{1,5},{2,6},{3,7},{4,0},{5,1},{6,2},{7,3},{8,12},{9,13},{10,... | collective-permute-start | bytes 147464 | tf_op jit(solution)/shard_map/ppermute | solution.py:465
  24.2 6.4 %collective-permute-start.9 = (f32[96,128]{1,0:T(8,128)S(1)}, f32[96,128]{1,0:T(8,128)S(1)}, u32[]{:S(2)}, u32[]{:S(2)}) collective-permute-start(f32[96,128]{1,0:T(8,128)S(1)} %get-tuple-element.59), channel_id=1, source_target_pairs={{0,3},{1,2},{2,1},{3,0},{4,7},{5,6},{6,5},{7,4},{8,11},{9,10},{10,... | collective-permute-start | bytes 147464 | tf_op jit(solution)/shard_map/ppermute | solution.py:465
  25.7 4.8 %collective-permute-start.10 = (f32[96,128]{1,0:T(8,128)S(1)}, f32[96,128]{1,0:T(8,128)S(1)}, u32[]{:S(2)}, u32[]{:S(2)}) collective-permute-start(f32[96,128]{1,0:T(8,128)S(1)} %get-tuple-element.60), channel_id=1, source_target_pairs={{0,2},{1,3},{2,0},{3,1},{4,6},{5,7},{6,4},{7,5},{8,10},{9,11},{10,... | collective-permute-start | bytes 147464 | tf_op jit(solution)/shard_map/ppermute | solution.py:465
  27.1 4.1 %collective-permute-start.11 = (f32[96,128]{1,0:T(8,128)S(1)}, f32[96,128]{1,0:T(8,128)S(1)}, u32[]{:S(2)}, u32[]{:S(2)}) collective-permute-start(f32[96,128]{1,0:T(8,128)S(1)} %get-tuple-element.61), channel_id=1, source_target_pairs={{0,1},{1,0},{2,3},{3,2},{4,5},{5,4},{6,7},{7,6},{8,9},{9,8},{10,11... | collective-permute-start | bytes 147464 | tf_op jit(solution)/shard_map/ppermute | solution.py:465
  34.3 9.2 %collective-permute-start.12 = (f32[96,128]{1,0:T(8,128)S(1)}, f32[96,128]{1,0:T(8,128)S(1)}, u32[]{:S(2)}, u32[]{:S(2)}) collective-permute-start(f32[96,128]{1,0:T(8,128)S(1)} %get-tuple-element.77), channel_id=1, source_target_pairs={{0,7},{1,6},{2,5},{3,4},{4,3},{5,2},{6,1},{7,0},{8,15},{9,14},{10,... | collective-permute-start | bytes 147464 | tf_op jit(solution)/shard_map/ppermute | solution.py:465
  38.3 6.2 %collective-permute-start.13 = (f32[96,128]{1,0:T(8,128)S(1)}, f32[96,128]{1,0:T(8,128)S(1)}, u32[]{:S(2)}, u32[]{:S(2)}) collective-permute-start(f32[96,128]{1,0:T(8,128)S(1)} %get-tuple-element.78), channel_id=1, source_target_pairs={{0,6},{1,7},{2,4},{3,5},{4,2},{5,3},{6,0},{7,1},{8,14},{9,15},{10,... | collective-permute-start | bytes 147464 | tf_op jit(solution)/shard_map/ppermute | solution.py:465
  38.4 7.2 %collective-permute-start.14 = (f32[96,128]{1,0:T(8,128)S(1)}, f32[96,128]{1,0:T(8,128)S(1)}, u32[]{:S(2)}, u32[]{:S(2)}) collective-permute-start(f32[96,128]{1,0:T(8,128)S(1)} %get-tuple-element.79), channel_id=1, source_target_pairs={{0,5},{1,4},{2,7},{3,6},{4,1},{5,0},{6,3},{7,2},{8,13},{9,12},{10,... | collective-permute-start | bytes 147464 | tf_op jit(solution)/shard_map/ppermute | solution.py:465
  39.1 6.6 %collective-permute-start.15 = (f32[96,128]{1,0:T(8,128)S(1)}, f32[96,128]{1,0:T(8,128)S(1)}, u32[]{:S(2)}, u32[]{:S(2)}) collective-permute-start(f32[96,128]{1,0:T(8,128)S(1)} %get-tuple-element.80), channel_id=1, source_target_pairs={{0,4},{1,5},{2,6},{3,7},{4,0},{5,1},{6,2},{7,3},{8,12},{9,13},{10,... | collective-permute-start | bytes 147464 | tf_op jit(solution)/shard_map/ppermute | solution.py:465
  42.0 5.0 %collective-permute-start.16 = (f32[96,128]{1,0:T(8,128)S(1)}, f32[96,128]{1,0:T(8,128)S(1)}, u32[]{:S(2)}, u32[]{:S(2)}) collective-permute-start(f32[96,128]{1,0:T(8,128)S(1)} %get-tuple-element.81), channel_id=1, source_target_pairs={{0,3},{1,2},{2,1},{3,0},{4,7},{5,6},{6,5},{7,4},{8,11},{9,10},{10,... | collective-permute-start | bytes 147464 | tf_op jit(solution)/shard_map/ppermute | solution.py:465
  43.6 4.1 %collective-permute-start.17 = (f32[96,128]{1,0:T(8,128)S(1)}, f32[96,128]{1,0:T(8,128)S(1)}, u32[]{:S(2)}, u32[]{:S(2)}) collective-permute-start(f32[96,128]{1,0:T(8,128)S(1)} %get-tuple-element.82), channel_id=1, source_target_pairs={{0,2},{1,3},{2,0},{3,1},{4,6},{5,7},{6,4},{7,5},{8,10},{9,11},{10,... | collective-permute-start | bytes 147464 | tf_op jit(solution)/shard_map/ppermute | solution.py:465
  44.5 4.1 %collective-permute-start.18 = (f32[96,128]{1,0:T(8,128)S(1)}, f32[96,128]{1,0:T(8,128)S(1)}, u32[]{:S(2)}, u32[]{:S(2)}) collective-permute-start(f32[96,128]{1,0:T(8,128)S(1)} %get-tuple-element.83), channel_id=1, source_target_pairs={{0,1},{1,0},{2,3},{3,2},{4,5},{5,4},{6,7},{7,6},{8,9},{9,8},{10,11... | collective-permute-start | bytes 147464 | tf_op jit(solution)/shard_map/ppermute | solution.py:465
  50.0 5.1 %collective-permute-start.19 = (f32[96,256]{1,0:T(8,128)S(1)}, f32[96,256]{1,0:T(8,128)S(1)}, u32[]{:S(2)}, u32[]{:S(2)}) collective-permute-start(f32[96,256]{1,0:T(8,128)S(1)} %get-tuple-element.85), channel_id=1, source_target_pairs={{0,24},{8,16},{16,8},{24,0},{1,25},{9,17},{17,9},{25,1},{2,26},{10... | collective-permute-start | bytes 294920 | tf_op jit(solution)/shard_map/ppermute | solution.py:465
  50.1 7.2 %collective-permute-start.20 = (f32[96,256]{1,0:T(8,128)S(1)}, f32[96,256]{1,0:T(8,128)S(1)}, u32[]{:S(2)}, u32[]{:S(2)}) collective-permute-start(f32[96,256]{1,0:T(8,128)S(1)} %get-tuple-element.86), channel_id=1, source_target_pairs={{0,16},{8,24},{16,0},{24,8},{1,17},{9,25},{17,1},{25,9},{2,18},{10... | collective-permute-start | bytes 294920 | tf_op jit(solution)/shard_map/ppermute | solution.py:465
  51.7 5.6 %collective-permute-start.21 = (f32[96,256]{1,0:T(8,128)S(1)}, f32[96,256]{1,0:T(8,128)S(1)}, u32[]{:S(2)}, u32[]{:S(2)}) collective-permute-start(f32[96,256]{1,0:T(8,128)S(1)} %get-tuple-element.87), channel_id=1, source_target_pairs={{0,8},{8,0},{16,24},{24,16},{1,9},{9,1},{17,25},{25,17},{2,10},{10... | collective-permute-start | bytes 294920 | tf_op jit(solution)/shard_map/ppermute | solution.py:465

commit v4 on v3

--- a/solution.py
+++ b/solution.py
@@ -158,8 +158,7 @@
     return result
 
 
-def pack_kernel(theta_ref, phi_ref, labels_ref, raw_ref, first_ref, last_ref, angle, label, sems):
-    height = theta_ref.shape[1]
+def pack_kernel(theta_ref, phi_ref, labels_ref, raw_ref, angle, label, sems):
     copies = [
         pltpu.make_async_copy(theta_ref, angle.at[0], sems.at[0]),
         pltpu.make_async_copy(phi_ref, angle.at[1], sems.at[1]),
@@ -171,13 +170,12 @@
         copy.wait()
     for index, value in enumerate((angle[0], angle[1], label[...].astype(jnp.float32))):
         raw_ref[index] = value
-        first_ref[index] = value[:, 0]
-        last_ref[index] = value[:, height - 1]
-
-
-def lines_kernel(count_x, count_y, *refs):
-    raw_refs, (region_ref, table) = refs[:count_x], refs[count_x : count_x + 2]
-    out_refs, (region, sem) = refs[count_x + 2 : -2], refs[-2:]
+
+
+def lines_kernel(count_x, order_y, *refs):
+    raw_refs, (region_ref, place, table) = refs[:count_x], refs[count_x : count_x + 3]
+    out_refs, (region, sem) = refs[count_x + 3 : -2], refs[-2:]
+    gy = place[1]
     fetch = pltpu.make_async_copy(region_ref, region, sem)
     fetch.start()
     units = [directions(raw_ref[0], raw_ref[1]) for raw_ref in raw_refs]
@@ -192,8 +190,35 @@
         part = both[: 3 * rows] + both[3 * rows :] + dot(high, table[1, number])
         total = part if total is None else total + part
     lanes = out_refs[0].shape[1]
-    for number in range(count_y):
-        out_refs[number][...] = total[:, number * lanes : (number + 1) * lanes]
+    last_row = raw_refs[0].shape[2] - 1
+    for spot, number in enumerate(order_y):
+        out_refs[spot][: 3 * rows] = total[:, spot * lanes : (spot + 1) * lanes]
+        if number in meeting(len(order_y)):
+            up = lax.bitwise_xor(gy, number) > gy
+            for field in range(3):
+                value = raw_refs[0][field]
+                edge = jnp.where(up, value[:, last_row], value[:, 0])
+                put_edge(out_refs[spot], 3 * rows, field, edge)
+
+
+def meeting(devices):
+    return [number for number in range(1, devices) if (number & (number + 1)) == 0]
+
+
+def edge_spots(depth, width, lanes, start, field):
+    pieces = width // lanes
+    return [start + (field * pieces + piece) * depth for piece in range(pieces)]
+
+
+def put_edge(ref, start, field, edge):
+    lanes = ref.shape[1]
+    for piece, row in enumerate(edge_spots(*edge.shape, lanes, start, field)):
+        ref[row : row + edge.shape[0]] = edge[:, piece * lanes : (piece + 1) * lanes]
+
+
+def get_edge(ref, depth, width, start, field):
+    spots = edge_spots(depth, width, ref.shape[1], start, field)
+    return jnp.concatenate([ref[row : row + depth] for row in spots], 1)
 
 
 def back_lines_kernel(count_x, count_y, *refs):
@@ -285,7 +310,7 @@
     columns = []
     for plane in range(planes):
         value = jnp.concatenate(
-            [ref[plane * local : (plane + 1) * local] for ref in spec_refs], 0
+            [spec_ref[plane * local : (plane + 1) * local] for spec_ref in spec_refs], 0
         )
         value = jnp.concatenate([value, turn(value, sign)], 0)
         high, low = split_high(value)
@@ -332,11 +357,20 @@
 
 
 def exchange_kernel(order_x, count_y, *refs):
-    count_x = len(order_x)
-    raw_refs, (before_ref, after_ref, place, ms_ref, aex_ref) = refs[:count_x], refs[count_x : count_x + 5]
-    exchange_ref, unit_ref, raw_ref = refs[count_x + 5 :]
+    count_x, numbers = len(order_x), meeting(count_y)
+    raw_refs, edge_refs, (place, ms_ref, aex_ref) = refs[:count_x], refs[count_x:-6], refs[-6:-3]
+    exchange_ref, unit_ref, raw_ref = refs[-3:]
     depth, height, width = raw_ref.shape[2:]
     gx, gy = place[0], place[1]
+
+    def row_meeting(field, other):
+        value = None
+        for number, edge_ref in zip(numbers, edge_refs):
+            edge = get_edge(edge_ref, depth, width, 3 * depth * height, field)
+            match = lax.bitwise_xor(gy, number) == other
+            value = edge if value is None else jnp.where(match, edge, value)
+        return jnp.broadcast_to(value[:, None, :], (depth, height, width))
+
     for spot, number in enumerate(order_x):
         raw_ref[lax.bitwise_xor(gx, number)] = raw_refs[spot][...]
     left, right = jnp.maximum(gx - 1, 0), jnp.minimum(gx + 1, count_x - 1)
@@ -351,14 +385,7 @@
     here = quantities(raw)
     side = quantities([jnp.where(lane == 0, raw_ref[right, f], raw_ref[left, f]) for f in range(3)])
     above = quantities(
-        [
-            jnp.where(
-                row == 0,
-                jnp.broadcast_to(after_ref[f][:, None, :], shape),
-                jnp.broadcast_to(before_ref[f][:, None, :], shape),
-            )
-            for f in range(3)
-        ]
+        [jnp.where(row == 0, row_meeting(f, gy + 1), row_meeting(f, gy - 1)) for f in range(3)]
     )
     saturation = looked_up(raw[2], ms_ref)
     total = [jnp.zeros(shape, jnp.float32) for _ in range(3)]
@@ -492,9 +519,9 @@
     twice = np.concatenate([np.eye(rows), np.eye(rows)], 1).astype(ml_dtypes.bfloat16)
     transform_flops = 6 * lines * count_x * width * count_y * lanes
 
-    packed, first, last = call(
+    packed = call(
         pack_kernel,
-        [cells, f32(3, depth, width), f32(3, depth, width)],
+        cells,
         [hbm] * 3,
         (theta, phi, labels),
         scratch=(
@@ -505,11 +532,6 @@
         name="pack",
     )
     gathered = exchanged([packed] * count_x, "gx", order_x)
-    up = [(i, i + 1) for i in range(count_y - 1)]
-    down = [(j, i) for i, j in up]
-    before = lax.ppermute(last, "gy", up)
-    after = lax.ppermute(first, "gy", down)
-    gathered, before, after = lax.optimization_barrier((gathered, before, after))
     table, forward, inverse = call(
         functools.partial(load_kernel, order_x, order_y),
         [
@@ -531,26 +553,18 @@
         flops=48 * 2 * rows * lanes * 2 * whole_y,
         name="tensor",
     )
+    gathered, tensor = lax.optimization_barrier((gathered, tensor))
+    edge_rows = 3 * depth * width // lanes
     spectrum = call(
-        functools.partial(lines_kernel, count_x, count_y),
-        [f32(lines, lanes)] * count_y,
-        [vmem] * count_x + [hbm, vmem],
-        (*gathered, ms_region, table),
+        functools.partial(lines_kernel, count_x, order_y),
+        [f32(lines + (edge_rows if n in meeting(count_y) else 0), lanes) for n in order_y],
+        [vmem] * count_x + [hbm, smem, vmem],
+        (*gathered, ms_region, place, table),
         scratch=(pltpu.SMEM(ms_region.shape, jnp.float32), pltpu.SemaphoreType.DMA),
         flops=transform_flops,
         name="lines",
     )
     columns = exchanged(spectrum, "gy", order_y)
-    exchange, unit = call(
-        functools.partial(exchange_kernel, order_x, count_y),
-        [cells, cells],
-        [vmem] * (count_x + 2) + [smem] * 3,
-        (*gathered, before, after, place, ms_region, aex_region),
-        scratch=(pltpu.VMEM((count_x, 3, depth, height, width), jnp.float32),),
-        flops=300 * depth * height * width,
-        name="exchange",
-    )
-    columns, exchange, unit = lax.optimization_barrier((columns, exchange, unit))
     scale = -1.0 / (2 * depth * 2 * whole_y * 2 * count_x * width)
     waves = call(
         functools.partial(waves_kernel, scale, count_y),
@@ -573,6 +587,17 @@
         flops=transform_flops,
         name="back_lines",
     )
+    edges = [columns[order_y.index(number)] for number in meeting(count_y)]
+    edges, partial = lax.optimization_barrier((edges, partial))
+    exchange, unit = call(
+        functools.partial(exchange_kernel, order_x, count_y),
+        [cells, cells],
+        [vmem] * (count_x + len(edges)) + [smem] * 3,
+        (*gathered, *edges, place, ms_region, aex_region),
+        scratch=(pltpu.VMEM((count_x, 3, depth, height, width), jnp.float32),),
+        flops=300 * depth * height * width,
+        name="exchange",
+    )
     parts = exchanged(partial, "gx", order_x)
     field, predicted = call(
         functools.partial(final_kernel, count_x),

time: 58.3 us -> 55.1 us (0.945)
  starting transfers between devices: 33.3 us -> 27.5 us
  waiting for transfers between devices: 10.2 us -> 12.3 us
  Pallas kernels: 13.6 us -> 14.2 us
    ppermute x2 -> x0, starting transfers between devices: 4.94 us -> none  [the longest x1 3.65 us: per_device(): before = lax.ppermute(last, 'gy', up)]
    ppermute x20, waiting for transfers between devices: 9.27 us -> 12.3 us  [exchanged(): out[spot + 1] = lax.ppermute(chunks[spot + 1], axis, pairs)]
    ppermute x2 -> x0, waiting for transfers between devices: 0.96 us -> none  [the longest x1 0.96 us: per_device(): after = lax.ppermute(first, 'gy', down)]
    ppermute x20, starting transfers between devices: 28.3 us -> 27.5 us  [exchanged(): out[spot + 1] = lax.ppermute(chunks[spot + 1], axis, pairs)]
    pallas_call x8, Pallas kernels: 13.6 us -> 14.2 us  [call(): pl.pallas_call(body, out_shape=out, in_specs=ins, out_specs=[vmem] * len(...]
  transfers between devices with their start and end apart: 22 -> 20, of which waited for: 10 -> 8; matrix products, arithmetic and copies ran while one was open for 0% -> 0% of each run, Pallas kernels for 10% -> 11%
where the time goes in v4:
time: 55.1 us; the launch traced here: 54.9 us
  starting transfers between devices  27.5 us (50%)
  Pallas kernels  14.2 us (26%)
  waiting for transfers between devices  12.3 us (22%)
  between operations  0.76 us (1%)
    ppermute x20, starting transfers between devices, exchanged(): out[spot + 1] = lax.ppermute(chunks[spot + 1], axis, pairs)  27.5 us
    pallas_call x8, Pallas kernels, call(): pl.pallas_call(body, out_shape=out, in_specs=ins, out_specs=[vmem] * len(...  14.2 us
    ppermute x20, waiting for transfers between devices, exchanged(): out[spot + 1] = lax.ppermute(chunks[spot + 1], axis, pairs)  12.3 us
  transfers between devices with their start and end apart: 20, of which 8 were waited for; matrix products, arithmetic and copies ran while one was open for 0% of the time, Pallas kernels for 11%

profile of v4, /device:TPU:0, one launch (start us, length us, event | category | flops | bytes accessed | tf_op | source)
XLA Modules:
  0.0 54.9 jit_solution(2501913486391128059)
XLA Ops:
  0.6 0.8 %pack.1.refs_0_ = f32[3,4,8,256]{3,2,1,0:T(8,128)S(1)} custom-call(f32[4,8,256]{2,1,0:T(8,128)} %theta_ref.1, f32[4,8,256]{2,1,0:T(8,128)} %phi_ref.1, s32[4,8,256]{2,1,0:T(8,128)} %labels_ref.1), custom_call_target="tpu_custom_call" | custom-call | bytes 196608 | tf_op jit(solution)/shard_map/pack/pallas_call | solution.py:471
  1.5 0.5 collective-permute-start.2
  2.0 2.6 %collective-permute-start.1 = (f32[3,4,8,256]{3,2,1,0:T(8,128)S(1)}, f32[3,4,8,256]{3,2,1,0:T(8,128)S(1)}, u32[]{:S(2)}, u32[]{:S(2)}) collective-permute-start(f32[3,4,8,256]{3,2,1,0:T(8,128)S(1)} %pack.1.refs_0_), channel_id=1, source_target_pairs={{0,16},{8,24},{16,0},{24,8},{1,17},{9,25},{17,1},{25,9},{2,18},{10... | collective-permute-start | bytes 294920 | tf_op jit(solution)/shard_map/ppermute | solution.py:492
  4.7 3.2 %load.1 = (bf16[2,4,256,1024]{3,2,1,0:T(8,128)(2,1)S(1)}, bf16[128,384]{1,0:T(8,128)(2,1)S(1)}, bf16[128,384]{1,0:T(8,128)(2,1)S(1)}) custom-call(s32[2]{0:T(128)S(1)} %pad_add_fusion.place.refs_5_.refs_7_, bf16[4,8,2,4,256,128]{5,4,3,2,1,0:T(8,128)(2,1)} %constant.16.clone.refs_0_, bf16[8,128,384]{2,1,0:T(8,128)(2,1)} %constant.17.clone.refs_1_, ...), custom_call_target="tpu_custom_call" | custom-call | bytes 22741000 | tf_op jit(solution)/shard_map/load/pallas_call | solution.py:471
  7.9 1.6 %tensor.1.refs_8_ = bf16[48,128,128]{2,1,0:T(8,128)(2,1)S(1)} custom-call(bf16[48,64,128]{2,1,0:T(8,128)(2,1)S(1)} %bitcast.3, bf16[64,128]{1,0:T(8,128)(2,1)S(1)} %copy-done.1), custom_call_target="tpu_custom_call" | custom-call | flops 100663296 | bytes 2375680 | tf_op jit(solution)/shard_map/tensor/pallas_call | solution.py:471
  9.5 0.3 collective-permute-done.refs_1_
  9.8 2.2 %lines.1 = (f32[96,128]{1,0:T(8,128)S(1)}, f32[120,128]{1,0:T(8,128)S(1)}, f32[96,128]{1,0:T(8,128)S(1)}, f32[96,128]{1,0:T(8,128)S(1)}, f32[96,128]{1,0:T(8,128...) custom-call(f32[3,4,8,256]{3,2,1,0:T(8,128)S(1)} %pack.1.refs_0_, ...), custom_call_target="tpu_custom_call" | custom-call | flops 603979776 | bytes 5017672 | tf_op jit(solution)/shard_map/lines/pallas_call | solution.py:471
  12.0 3.7 %collective-permute-start.6 = (f32[96,128]{1,0:T(8,128)S(1)}, f32[96,128]{1,0:T(8,128)S(1)}, u32[]{:S(2)}, u32[]{:S(2)}) collective-permute-start(f32[96,128]{1,0:T(8,128)S(1)} %get-tuple-element.48), channel_id=1, source_target_pairs={{0,6},{1,7},{2,4},{3,5},{4,2},{5,3},{6,0},{7,1},{8,14},{9,15},{10,... | collective-permute-start | bytes 147464 | tf_op jit(solution)/shard_map/ppermute | solution.py:492
  15.7 0.4 collective-permute-start.7
  16.1 1.1 %collective-permute-start.3 = (f32[120,128]{1,0:T(8,128)S(1)}, f32[120,128]{1,0:T(8,128)S(1)}, u32[]{:S(2)}, u32[]{:S(2)}) collective-permute-start(f32[120,128]{1,0:T(8,128)S(1)} %get-tuple-element.44), channel_id=1, source_target_pairs={{0,1},{1,0},{2,3},{3,2},{4,5},{5,4},{6,7},{7,6},{8,9},{9,8},{10,11... | collective-permute-start | bytes 184328 | tf_op jit(solution)/shard_map/ppermute | solution.py:492
  17.3 1.7 %collective-permute-start.4 = (f32[120,128]{1,0:T(8,128)S(1)}, f32[120,128]{1,0:T(8,128)S(1)}, u32[]{:S(2)}, u32[]{:S(2)}) collective-permute-start(f32[120,128]{1,0:T(8,128)S(1)} %get-tuple-element.45), channel_id=1, source_target_pairs={{0,3},{1,2},{2,1},{3,0},{4,7},{5,6},{6,5},{7,4},{8,11},{9,10},{10,... | collective-permute-start | bytes 184328 | tf_op jit(solution)/shard_map/ppermute | solution.py:492
  18.9 3.5 %collective-permute-start.5 = (f32[120,128]{1,0:T(8,128)S(1)}, f32[120,128]{1,0:T(8,128)S(1)}, u32[]{:S(2)}, u32[]{:S(2)}) collective-permute-start(f32[120,128]{1,0:T(8,128)S(1)} %get-tuple-element.46), channel_id=1, source_target_pairs={{0,7},{1,6},{2,5},{3,4},{4,3},{5,2},{6,1},{7,0},{8,15},{9,14},{10,... | collective-permute-start | bytes 184328 | tf_op jit(solution)/shard_map/ppermute | solution.py:492
  22.5 0.7 %collective-permute-start.9 = (f32[96,128]{1,0:T(8,128)S(1)}, f32[96,128]{1,0:T(8,128)S(1)}, u32[]{:S(2)}, u32[]{:S(2)}) collective-permute-start(f32[96,128]{1,0:T(8,128)S(1)} %get-tuple-element.51), channel_id=1, source_target_pairs={{0,2},{1,3},{2,0},{3,1},{4,6},{5,7},{6,4},{7,5},{8,10},{9,11},{10,... | collective-permute-start | bytes 147464 | tf_op jit(solution)/shard_map/ppermute | solution.py:492
  23.2 4.3 %collective-permute-done.8.refs_4_ = f32[96,128]{1,0:T(8,128)S(1)} collective-permute-done((f32[96,128]{1,0:T(8,128)S(1)}, f32[96,128]{1,0:T(8,128)S(1)}, u32[]{:S(2)}, u32[]{:S(2)}) %collective-permute-start.8) | collective-permute-done | bytes 49184 | tf_op jit(solution)/shard_map/ppermute | solution.py:492
  27.5 0.1 collective-permute-done.9.refs_6_
  27.6 3.2 %waves.1 = (f32[96,128]{1,0:T(8,128)S(1)}, f32[96,128]{1,0:T(8,128)S(1)}, f32[96,128]{1,0:T(8,128)S(1)}, f32[96,128]{1,0:T(8,128)S(1)}, f32[96,128]{1,0:T(8,128)...) custom-call(f32[96,128]{1,0:T(8,128)S(1)} %get-tuple-element.47.refs_0_, ...), custom_call_target="tpu_custom_call" | custom-call | flops 125829120 | bytes 2592768 | tf_op jit(solution)/shard_map/waves/pallas_call | solution.py:471
  30.8 2.5 %collective-permute-start.10 = (f32[96,128]{1,0:T(8,128)S(1)}, f32[96,128]{1,0:T(8,128)S(1)}, u32[]{:S(2)}, u32[]{:S(2)}) collective-permute-start(f32[96,128]{1,0:T(8,128)S(1)} %get-tuple-element.56), channel_id=1, source_target_pairs={{0,7},{1,6},{2,5},{3,4},{4,3},{5,2},{6,1},{7,0},{8,15},{9,14},{10,... | collective-permute-start | bytes 147464 | tf_op jit(solution)/shard_map/ppermute | solution.py:492
  33.3 2.2 %collective-permute-start.11 = (f32[96,128]{1,0:T(8,128)S(1)}, f32[96,128]{1,0:T(8,128)S(1)}, u32[]{:S(2)}, u32[]{:S(2)}) collective-permute-start(f32[96,128]{1,0:T(8,128)S(1)} %get-tuple-element.57), channel_id=1, source_target_pairs={{0,6},{1,7},{2,4},{3,5},{4,2},{5,3},{6,0},{7,1},{8,14},{9,15},{10,... | collective-permute-start | bytes 147464 | tf_op jit(solution)/shard_map/ppermute | solution.py:492
  35.5 0.2 collective-permute-start.12
  35.7 2.8 %collective-permute-start.13 = (f32[96,128]{1,0:T(8,128)S(1)}, f32[96,128]{1,0:T(8,128)S(1)}, u32[]{:S(2)}, u32[]{:S(2)}) collective-permute-start(f32[96,128]{1,0:T(8,128)S(1)} %get-tuple-element.59), channel_id=1, source_target_pairs={{0,4},{1,5},{2,6},{3,7},{4,0},{5,1},{6,2},{7,3},{8,12},{9,13},{10,... | collective-permute-start | bytes 147464 | tf_op jit(solution)/shard_map/ppermute | solution.py:492
  38.6 2.7 %collective-permute-start.15 = (f32[96,128]{1,0:T(8,128)S(1)}, f32[96,128]{1,0:T(8,128)S(1)}, u32[]{:S(2)}, u32[]{:S(2)}) collective-permute-start(f32[96,128]{1,0:T(8,128)S(1)} %get-tuple-element.61), channel_id=1, source_target_pairs={{0,2},{1,3},{2,0},{3,1},{4,6},{5,7},{6,4},{7,5},{8,10},{9,11},{10,... | collective-permute-start | bytes 147464 | tf_op jit(solution)/shard_map/ppermute | solution.py:492
  41.4 0.7 %collective-permute-start.16 = (f32[96,128]{1,0:T(8,128)S(1)}, f32[96,128]{1,0:T(8,128)S(1)}, u32[]{:S(2)}, u32[]{:S(2)}) collective-permute-start(f32[96,128]{1,0:T(8,128)S(1)} %get-tuple-element.62), channel_id=1, source_target_pairs={{0,1},{1,0},{2,3},{3,2},{4,5},{5,4},{6,7},{7,6},{8,9},{9,8},{10,11... | collective-permute-start | bytes 147464 | tf_op jit(solution)/shard_map/ppermute | solution.py:492
  42.0 1.5 %collective-permute-done.14.refs_5_ = f32[96,128]{1,0:T(8,128)S(1)} collective-permute-done((f32[96,128]{1,0:T(8,128)S(1)}, f32[96,128]{1,0:T(8,128)S(1)}, u32[]{:S(2)}, u32[]{:S(2)}) %collective-permute-start.14) | collective-permute-done | bytes 49184 | tf_op jit(solution)/shard_map/ppermute | solution.py:492
  43.5 0.4 collective-permute-done.15.refs_6_
  43.9 1.5 %collective-permute-done.16.refs_7_ = f32[96,128]{1,0:T(8,128)S(1)} collective-permute-done((f32[96,128]{1,0:T(8,128)S(1)}, f32[96,128]{1,0:T(8,128)S(1)}, u32[]{:S(2)}, u32[]{:S(2)}) %collective-permute-start.16) | collective-permute-done | bytes 49184 | tf_op jit(solution)/shard_map/ppermute | solution.py:492
  45.4 1.5 %back_lines.1 = (f32[96,256]{1,0:T(8,128)S(1)}, f32[96,256]{1,0:T(8,128)S(1)}, f32[96,256]{1,0:T(8,128)S(1)}, f32[96,256]{1,0:T(8,128)S(1)}) custom-call(f32[96,128]{1,0:T(8,128)S(1)} %get-tuple-element.55.refs_0_, f32[96,128]{1,0:T(8,128)S(1)} %collective-permute-done.10.refs_1_, f32[96,128]{1,0:T(8,128)S(1)} %collective-permute-done.11.refs_2_, ...), custom_call_target="tpu_custom_call" | custom-call | flops 603979776 | bytes 4980736 | tf_op jit(solution)/shard_map/back_lines/pallas_call | solution.py:471
  47.0 1.6 %collective-permute-start.18 = (f32[96,256]{1,0:T(8,128)S(1)}, f32[96,256]{1,0:T(8,128)S(1)}, u32[]{:S(2)}, u32[]{:S(2)}) collective-permute-start(f32[96,256]{1,0:T(8,128)S(1)} %get-tuple-element.69), channel_id=1, source_target_pairs={{0,16},{8,24},{16,0},{24,8},{1,17},{9,25},{17,1},{25,9},{2,18},{10... | collective-permute-start | bytes 294920 | tf_op jit(solution)/shard_map/ppermute | solution.py:492
  48.5 0.3 collective-permute-start.19
  48.8 1.1 %exchange.1 = (f32[3,4,8,256]{3,2,1,0:T(8,128)S(1)}, f32[3,4,8,256]{3,2,1,0:T(8,128)S(1)}) custom-call(f32[3,4,8,256]{3,2,1,0:T(8,128)S(1)} %pack.1.refs_0_, f32[3,4,8,256]{3,2,1,0:T(8,128)S(1)} %collective-permute-done.refs_1_, f32[3,4,8,256]{3,2,1,0:T(8,128)S(1)} %collective-permute-done.1.refs_2_, f32[3,4,8,256]{3,2,1,0:T(8,128)S(1)} %collective-permute-done.2.refs_3_, ...), custom_call_target="tpu_custom_call" | custom-call | flops 2457600 | bytes 774280 | tf_op jit(solution)/shard_map/exchange/pallas_call | solution.py:471
  50.0 2.0 %collective-permute-done.17.refs_1_ = f32[96,256]{1,0:T(8,128)S(1)} collective-permute-done((f32[96,256]{1,0:T(8,128)S(1)}, f32[96,256]{1,0:T(8,128)S(1)}, u32[]{:S(2)}, u32[]{:S(2)}) %collective-permute-start.17) | collective-permute-done | bytes 98336 | tf_op jit(solution)/shard_map/ppermute | solution.py:492
  52.0 2.2 %collective-permute-done.18.refs_2_ = f32[96,256]{1,0:T(8,128)S(1)} collective-permute-done((f32[96,256]{1,0:T(8,128)S(1)}, f32[96,256]{1,0:T(8,128)S(1)}, u32[]{:S(2)}, u32[]{:S(2)}) %collective-permute-start.18) | collective-permute-done | bytes 98336 | tf_op jit(solution)/shard_map/ppermute | solution.py:492
  54.2 0.7 %predict.1 = (f32[3,4,8,256]{3,2,1,0:T(8,128)}, f32[3,4,8,256]{3,2,1,0:T(8,128)}) custom-call(f32[96,256]{1,0:T(8,128)S(1)} %get-tuple-element.67.refs_0_, f32[96,256]{1,0:T(8,128)S(1)} %collective-permute-done.17.refs_1_, f32[96,256]{1,0:T(8,128)S(1)} %collective-permute-done.18.refs_2_, f32[96,256]{1,0:T(8,128)S(1)} %collective-permute-done.19.refs_3_, ...), custom_call_target="tpu_custom_call" | custom-call | flops 491520 | bytes 786432 | tf_op jit(solution)/shard_map/predict/pallas_call | solution.py:471
  (25 shorter events, 0.4 us)
Async XLA Ops:
  1.5 8.0 %collective-permute-start.2 = (f32[3,4,8,256]{3,2,1,0:T(8,128)S(1)}, f32[3,4,8,256]{3,2,1,0:T(8,128)S(1)}, u32[]{:S(2)}, u32[]{:S(2)}) collective-permute-start(f32[3,4,8,256]{3,2,1,0:T(8,128)S(1)} %pack.1.refs_0_), channel_id=1, source_target_pairs={{0,8},{8,0},{16,24},{24,16},{1,9},{9,1},{17,25},{25,17},{2,10},{10... | collective-permute-start | bytes 294920 | tf_op jit(solution)/shard_map/ppermute | solution.py:492
  2.0 7.5 %collective-permute-start.1 = (f32[3,4,8,256]{3,2,1,0:T(8,128)S(1)}, f32[3,4,8,256]{3,2,1,0:T(8,128)S(1)}, u32[]{:S(2)}, u32[]{:S(2)}) collective-permute-start(f32[3,4,8,256]{3,2,1,0:T(8,128)S(1)} %pack.1.refs_0_), channel_id=1, source_target_pairs={{0,16},{8,24},{16,0},{24,8},{1,17},{9,25},{17,1},{25,9},{2,18},{10... | collective-permute-start | bytes 294920 | tf_op jit(solution)/shard_map/ppermute | solution.py:492
  4.5 5.2 %collective-permute-start = (f32[3,4,8,256]{3,2,1,0:T(8,128)S(1)}, f32[3,4,8,256]{3,2,1,0:T(8,128)S(1)}, u32[]{:S(2)}, u32[]{:S(2)}) collective-permute-start(f32[3,4,8,256]{3,2,1,0:T(8,128)S(1)} %pack.1.refs_0_), channel_id=1, source_target_pairs={{0,24},{8,16},{16,8},{24,0},{1,25},{9,17},{17,9},{25,1},{2,26},{10... | collective-permute-start | bytes 294920 | tf_op jit(solution)/shard_map/ppermute | solution.py:492
  4.7 3.2 %copy-start = (bf16[6,8,64,128]{3,2,1,0:T(8,128)(2,1)S(1)}, bf16[6,8,64,128]{3,2,1,0:T(8,128)(2,1)}, u32[]{:S(2)}) copy-start(bf16[6,8,64,128]{3,2,1,0:T(8,128)(2,1)} %param.15) | copy-start | bytes 2359300
  4.7 3.2 %copy-start.1 = (bf16[64,128]{1,0:T(8,128)(2,1)S(1)}, bf16[64,128]{1,0:T(8,128)(2,1)}, u32[]{:S(2)}) copy-start(bf16[64,128]{1,0:T(8,128)(2,1)} %constant.19.clone.twice_ref) | copy-start | bytes 49156
  12.0 36.9 %copy-start.2 = (f32[16]{0:T(128)S(1)}, f32[16]{0:T(128)}, u32[]{:S(2)}) copy-start(f32[16]{0:T(128)} %refs_8_.1) | copy-start | bytes 196
  12.0 36.9 %copy-start.3 = (f32[16]{0:T(128)S(1)}, f32[16]{0:T(128)}, u32[]{:S(2)}) copy-start(f32[16]{0:T(128)} %refs_9_.1) | copy-start | bytes 196
  12.0 10.5 %collective-permute-start.6 = (f32[96,128]{1,0:T(8,128)S(1)}, f32[96,128]{1,0:T(8,128)S(1)}, u32[]{:S(2)}, u32[]{:S(2)}) collective-permute-start(f32[96,128]{1,0:T(8,128)S(1)} %get-tuple-element.48), channel_id=1, source_target_pairs={{0,6},{1,7},{2,4},{3,5},{4,2},{5,3},{6,0},{7,1},{8,14},{9,15},{10,... | collective-permute-start | bytes 147464 | tf_op jit(solution)/shard_map/ppermute | solution.py:492
  15.7 6.8 %collective-permute-start.7 = (f32[96,128]{1,0:T(8,128)S(1)}, f32[96,128]{1,0:T(8,128)S(1)}, u32[]{:S(2)}, u32[]{:S(2)}) collective-permute-start(f32[96,128]{1,0:T(8,128)S(1)} %get-tuple-element.49), channel_id=1, source_target_pairs={{0,5},{1,4},{2,7},{3,6},{4,1},{5,0},{6,3},{7,2},{8,13},{9,12},{10,... | collective-permute-start | bytes 147464 | tf_op jit(solution)/shard_map/ppermute | solution.py:492
  16.1 11.5 %collective-permute-start.3 = (f32[120,128]{1,0:T(8,128)S(1)}, f32[120,128]{1,0:T(8,128)S(1)}, u32[]{:S(2)}, u32[]{:S(2)}) collective-permute-start(f32[120,128]{1,0:T(8,128)S(1)} %get-tuple-element.44), channel_id=1, source_target_pairs={{0,1},{1,0},{2,3},{3,2},{4,5},{5,4},{6,7},{7,6},{8,9},{9,8},{10,11... | collective-permute-start | bytes 184328 | tf_op jit(solution)/shard_map/ppermute | solution.py:492
  17.3 10.4 %collective-permute-start.4 = (f32[120,128]{1,0:T(8,128)S(1)}, f32[120,128]{1,0:T(8,128)S(1)}, u32[]{:S(2)}, u32[]{:S(2)}) collective-permute-start(f32[120,128]{1,0:T(8,128)S(1)} %get-tuple-element.45), channel_id=1, source_target_pairs={{0,3},{1,2},{2,1},{3,0},{4,7},{5,6},{6,5},{7,4},{8,11},{9,10},{10,... | collective-permute-start | bytes 184328 | tf_op jit(solution)/shard_map/ppermute | solution.py:492
  18.9 8.7 %collective-permute-start.5 = (f32[120,128]{1,0:T(8,128)S(1)}, f32[120,128]{1,0:T(8,128)S(1)}, u32[]{:S(2)}, u32[]{:S(2)}) collective-permute-start(f32[120,128]{1,0:T(8,128)S(1)} %get-tuple-element.46), channel_id=1, source_target_pairs={{0,7},{1,6},{2,5},{3,4},{4,3},{5,2},{6,1},{7,0},{8,15},{9,14},{10,... | collective-permute-start | bytes 184328 | tf_op jit(solution)/shard_map/ppermute | solution.py:492
  22.5 5.0 %collective-permute-start.8 = (f32[96,128]{1,0:T(8,128)S(1)}, f32[96,128]{1,0:T(8,128)S(1)}, u32[]{:S(2)}, u32[]{:S(2)}) collective-permute-start(f32[96,128]{1,0:T(8,128)S(1)} %get-tuple-element.50), channel_id=1, source_target_pairs={{0,4},{1,5},{2,6},{3,7},{4,0},{5,1},{6,2},{7,3},{8,12},{9,13},{10,... | collective-permute-start | bytes 147464 | tf_op jit(solution)/shard_map/ppermute | solution.py:492
  22.5 5.1 %collective-permute-start.9 = (f32[96,128]{1,0:T(8,128)S(1)}, f32[96,128]{1,0:T(8,128)S(1)}, u32[]{:S(2)}, u32[]{:S(2)}) collective-permute-start(f32[96,128]{1,0:T(8,128)S(1)} %get-tuple-element.51), channel_id=1, source_target_pairs={{0,2},{1,3},{2,0},{3,1},{4,6},{5,7},{6,4},{7,5},{8,10},{9,11},{10,... | collective-permute-start | bytes 147464 | tf_op jit(solution)/shard_map/ppermute | solution.py:492
  30.8 7.8 %collective-permute-start.10 = (f32[96,128]{1,0:T(8,128)S(1)}, f32[96,128]{1,0:T(8,128)S(1)}, u32[]{:S(2)}, u32[]{:S(2)}) collective-permute-start(f32[96,128]{1,0:T(8,128)S(1)} %get-tuple-element.56), channel_id=1, source_target_pairs={{0,7},{1,6},{2,5},{3,4},{4,3},{5,2},{6,1},{7,0},{8,15},{9,14},{10,... | collective-permute-start | bytes 147464 | tf_op jit(solution)/shard_map/ppermute | solution.py:492
  33.3 8.0 %collective-permute-start.11 = (f32[96,128]{1,0:T(8,128)S(1)}, f32[96,128]{1,0:T(8,128)S(1)}, u32[]{:S(2)}, u32[]{:S(2)}) collective-permute-start(f32[96,128]{1,0:T(8,128)S(1)} %get-tuple-element.57), channel_id=1, source_target_pairs={{0,6},{1,7},{2,4},{3,5},{4,2},{5,3},{6,0},{7,1},{8,14},{9,15},{10,... | collective-permute-start | bytes 147464 | tf_op jit(solution)/shard_map/ppermute | solution.py:492
  35.5 6.5 %collective-permute-start.12 = (f32[96,128]{1,0:T(8,128)S(1)}, f32[96,128]{1,0:T(8,128)S(1)}, u32[]{:S(2)}, u32[]{:S(2)}) collective-permute-start(f32[96,128]{1,0:T(8,128)S(1)} %get-tuple-element.58), channel_id=1, source_target_pairs={{0,5},{1,4},{2,7},{3,6},{4,1},{5,0},{6,3},{7,2},{8,13},{9,12},{10,... | collective-permute-start | bytes 147464 | tf_op jit(solution)/shard_map/ppermute | solution.py:492
  35.7 6.4 %collective-permute-start.13 = (f32[96,128]{1,0:T(8,128)S(1)}, f32[96,128]{1,0:T(8,128)S(1)}, u32[]{:S(2)}, u32[]{:S(2)}) collective-permute-start(f32[96,128]{1,0:T(8,128)S(1)} %get-tuple-element.59), channel_id=1, source_target_pairs={{0,4},{1,5},{2,6},{3,7},{4,0},{5,1},{6,2},{7,3},{8,12},{9,13},{10,... | collective-permute-start | bytes 147464 | tf_op jit(solution)/shard_map/ppermute | solution.py:492
  38.5 5.0 %collective-permute-start.14 = (f32[96,128]{1,0:T(8,128)S(1)}, f32[96,128]{1,0:T(8,128)S(1)}, u32[]{:S(2)}, u32[]{:S(2)}) collective-permute-start(f32[96,128]{1,0:T(8,128)S(1)} %get-tuple-element.60), channel_id=1, source_target_pairs={{0,3},{1,2},{2,1},{3,0},{4,7},{5,6},{6,5},{7,4},{8,11},{9,10},{10,... | collective-permute-start | bytes 147464 | tf_op jit(solution)/shard_map/ppermute | solution.py:492
  38.6 5.3 %collective-permute-start.15 = (f32[96,128]{1,0:T(8,128)S(1)}, f32[96,128]{1,0:T(8,128)S(1)}, u32[]{:S(2)}, u32[]{:S(2)}) collective-permute-start(f32[96,128]{1,0:T(8,128)S(1)} %get-tuple-element.61), channel_id=1, source_target_pairs={{0,2},{1,3},{2,0},{3,1},{4,6},{5,7},{6,4},{7,5},{8,10},{9,11},{10,... | collective-permute-start | bytes 147464 | tf_op jit(solution)/shard_map/ppermute | solution.py:492
  41.4 4.1 %collective-permute-start.16 = (f32[96,128]{1,0:T(8,128)S(1)}, f32[96,128]{1,0:T(8,128)S(1)}, u32[]{:S(2)}, u32[]{:S(2)}) collective-permute-start(f32[96,128]{1,0:T(8,128)S(1)} %get-tuple-element.62), channel_id=1, source_target_pairs={{0,1},{1,0},{2,3},{3,2},{4,5},{5,4},{6,7},{7,6},{8,9},{9,8},{10,11... | collective-permute-start | bytes 147464 | tf_op jit(solution)/shard_map/ppermute | solution.py:492
  46.9 5.1 %collective-permute-start.17 = (f32[96,256]{1,0:T(8,128)S(1)}, f32[96,256]{1,0:T(8,128)S(1)}, u32[]{:S(2)}, u32[]{:S(2)}) collective-permute-start(f32[96,256]{1,0:T(8,128)S(1)} %get-tuple-element.68), channel_id=1, source_target_pairs={{0,24},{8,16},{16,8},{24,0},{1,25},{9,17},{17,9},{25,1},{2,26},{10... | collective-permute-start | bytes 294920 | tf_op jit(solution)/shard_map/ppermute | solution.py:492
  47.0 7.2 %collective-permute-start.18 = (f32[96,256]{1,0:T(8,128)S(1)}, f32[96,256]{1,0:T(8,128)S(1)}, u32[]{:S(2)}, u32[]{:S(2)}) collective-permute-start(f32[96,256]{1,0:T(8,128)S(1)} %get-tuple-element.69), channel_id=1, source_target_pairs={{0,16},{8,24},{16,0},{24,8},{1,17},{9,25},{17,1},{25,9},{2,18},{10... | collective-permute-start | bytes 294920 | tf_op jit(solution)/shard_map/ppermute | solution.py:492
  48.5 5.6 %collective-permute-start.19 = (f32[96,256]{1,0:T(8,128)S(1)}, f32[96,256]{1,0:T(8,128)S(1)}, u32[]{:S(2)}, u32[]{:S(2)}) collective-permute-start(f32[96,256]{1,0:T(8,128)S(1)} %get-tuple-element.70), channel_id=1, source_target_pairs={{0,8},{8,0},{16,24},{24,16},{1,9},{9,1},{17,25},{25,17},{2,10},{10... | collective-permute-start | bytes 294920 | tf_op jit(solution)/shard_map/ppermute | solution.py:492

commit v5 on v4

--- a/solution.py
+++ b/solution.py
@@ -298,20 +298,32 @@
 
 
 def waves_kernel(scale, count_y, *refs):
-    spec_refs, (tensor_ref, forward_ref, inverse_ref) = refs[:count_y], refs[count_y : count_y + 3]
-    out_refs, (wave_ref, back_ref) = refs[count_y + 3 : -2], refs[-2:]
+    spec_refs, tables = refs[:count_y], refs[count_y : count_y + 3]
+    out_refs, scratch = refs[count_y + 3 : -2], refs[-2:]
     lines, lanes = spec_refs[0].shape
     local = 8
-    planes = lines // local
-    height = count_y * local
+
+    def read(plane):
+        rows = slice(plane * local, (plane + 1) * local)
+        return jnp.concatenate([spec_ref[rows] for spec_ref in spec_refs], 0)
+
+    def write(plane, value):
+        for number in range(count_y):
+            out_refs[number][plane * local : (plane + 1) * local] = value[
+                number * local : (number + 1) * local
+            ]
+
+    waves(scale, count_y * local, lines // local, lanes, read, write, tables, scratch)
+
+
+def waves(scale, height, planes, lanes, read, write, tables, scratch):
+    (tensor_ref, forward_ref, inverse_ref), (wave_ref, back_ref) = tables, scratch
     sign = jnp.where(
         lax.broadcasted_iota(jnp.int32, (1, lanes), 1) < lanes // 2, 1.0, -1.0
     ).astype(jnp.float32)
     columns = []
     for plane in range(planes):
-        value = jnp.concatenate(
-            [spec_ref[plane * local : (plane + 1) * local] for spec_ref in spec_refs], 0
-        )
+        value = read(plane)
         value = jnp.concatenate([value, turn(value, sign)], 0)
         high, low = split_high(value)
         columns.append(jnp.concatenate([high, low, high], 0))
@@ -350,17 +362,14 @@
     for plane in range(planes):
         part = slice(plane * lanes, (plane + 1) * lanes)
         value = back[:height, part] - turn(back[height:, part], sign)
-        for number in range(count_y):
-            out_refs[number][plane * local : (plane + 1) * local] = value[
-                number * local : (number + 1) * local
-            ]
+        write(plane, value)
 
 
 def exchange_kernel(order_x, count_y, *refs):
     count_x, numbers = len(order_x), meeting(count_y)
     raw_refs, edge_refs, (place, ms_ref, aex_ref) = refs[:count_x], refs[count_x:-6], refs[-6:-3]
     exchange_ref, unit_ref, raw_ref = refs[-3:]
-    depth, height, width = raw_ref.shape[2:]
+    depth, height, width = shape = raw_ref.shape[2:]
     gx, gy = place[0], place[1]
 
     def row_meeting(field, other):
@@ -369,24 +378,31 @@
             edge = get_edge(edge_ref, depth, width, 3 * depth * height, field)
             match = lax.bitwise_xor(gy, number) == other
             value = edge if value is None else jnp.where(match, edge, value)
-        return jnp.broadcast_to(value[:, None, :], (depth, height, width))
+        return jnp.broadcast_to(value[:, None, :], shape)
 
     for spot, number in enumerate(order_x):
         raw_ref[lax.bitwise_xor(gx, number)] = raw_refs[spot][...]
     left, right = jnp.maximum(gx - 1, 0), jnp.minimum(gx + 1, count_x - 1)
-    shape = (depth, height, width)
     lane = lax.broadcasted_iota(jnp.int32, shape, 2)
     row = lax.broadcasted_iota(jnp.int32, shape, 1)
+    raw = [raw_refs[0][f] for f in range(3)]
+    side = [jnp.where(lane == 0, raw_ref[right, f], raw_ref[left, f]) for f in range(3)]
+    above = [
+        jnp.where(row == 0, row_meeting(f, gy + 1), row_meeting(f, gy - 1)) for f in range(3)
+    ]
+    exchange(raw, side, above, (gx, count_x, gy, count_y), ms_ref, aex_ref, exchange_ref, unit_ref)
+
+
+def exchange(raw, side, above, spots, ms_ref, aex_ref, exchange_ref, unit_ref):
+    depth, height, width = shape = raw[0].shape
+    gx, count_x, gy, count_y = spots
+    lane = lax.broadcasted_iota(jnp.int32, shape, 2)
+    row = lax.broadcasted_iota(jnp.int32, shape, 1)
 
     def quantities(values):
         return directions(values[0], values[1]) + [looked_up(values[2], aex_ref)]
 
-    raw = [raw_refs[0][f] for f in range(3)]
-    here = quantities(raw)
-    side = quantities([jnp.where(lane == 0, raw_ref[right, f], raw_ref[left, f]) for f in range(3)])
-    above = quantities(
-        [jnp.where(row == 0, row_meeting(f, gy + 1), row_meeting(f, gy - 1)) for f in range(3)]
-    )
+    here, side, above = quantities(raw), quantities(side), quantities(above)
     saturation = looked_up(raw[2], ms_ref)
     total = [jnp.zeros(shape, jnp.float32) for _ in range(3)]
 
@@ -433,15 +449,22 @@
 
 def final_kernel(count_x, *refs):
     part_refs, (exchange_ref, unit_ref, field_ref, predicted_ref) = refs[:count_x], refs[count_x:]
-    depth, height, width = unit_ref.shape[1:]
-    rows = depth * height
-    unit, field = [], []
+    rows = unit_ref.shape[1] * unit_ref.shape[2]
+    demag = []
     for c in range(3):
         place = slice(c * rows, (c + 1) * rows)
         total = part_refs[0][place]
         for part_ref in part_refs[1:]:
             total = total + part_ref[place]
-        field.append(exchange_ref[c] + total.reshape(depth, height, width))
+        demag.append(total)
+    predict(demag, exchange_ref, unit_ref, field_ref, predicted_ref)
+
+
+def predict(demag, exchange_ref, unit_ref, field_ref, predicted_ref):
+    depth, height, width = unit_ref.shape[1:]
+    unit, field = [], []
+    for c in range(3):
+        field.append(exchange_ref[c] + demag[c].reshape(depth, height, width))
         unit.append(unit_ref[c])
         field_ref[c] = field[c]
     twist = cross(unit, field)
@@ -453,6 +476,225 @@
     length = jnp.sqrt(moved[0] * moved[0] + moved[1] * moved[1] + moved[2] * moved[2])
     for c in range(3):
         predicted_ref[c] = moved[c] / length
+
+
+def sorted_table(count_x, count_y, width, rows):
+    place = sorted_cells(width).reshape(2, 1, width // 2)
+    place = (place + np.arange(count_x)[None, :, None] * width)[..., None, None, None]
+    wave = np.arange(count_y)[:, None, None] * rows + np.arange(rows)[None, None, :]
+    length = 2 * count_x * width
+    angle = (place * wave % length) * (2.0 * math.pi / length)
+    table = np.concatenate([np.cos(angle), -np.sin(angle)], -2)
+    return np.stack(split_table(table.reshape(2, count_x, width // 2, count_y * 2 * rows)))
+
+
+def sorted_cells(width):
+    return (np.array([0, 2, 1, 3])[:, None] + 4 * np.arange(width // 4)[None, :]).reshape(width)
+
+
+def sorting_kernel(order_x, *refs):
+    theta_ref, phi_ref, labels_ref, region_ref, place, sort_ref = refs[:6]
+    out_refs, (first_ref, last_ref) = refs[6:-8], refs[-8:-6]
+    angle, label, region, sort, layers, sems = refs[-6:]
+    copies = [
+        pltpu.make_async_copy(theta_ref, angle.at[0], sems.at[0]),
+        pltpu.make_async_copy(phi_ref, angle.at[1], sems.at[1]),
+        pltpu.make_async_copy(labels_ref, label, sems.at[2]),
+        pltpu.make_async_copy(region_ref, region, sems.at[3]),
+        pltpu.make_async_copy(sort_ref, sort, sems.at[4]),
+    ]
+    for copy in copies:
+        copy.start()
+    for copy in copies:
+        copy.wait()
+    gx = place[0]
+    depth, height, width = label.shape
+    raw = [angle[0], angle[1], label[...].astype(jnp.float32)]
+    saturation = looked_up(raw[2], region)
+    rows = depth * height
+    moment = [(part * saturation).reshape(rows, width) for part in directions(raw[0], raw[1])]
+    high, low = split_high(jnp.concatenate(moment, 0))
+    both = dot(jnp.concatenate([high, low], 0), sort[...])
+    moment = both[: 3 * rows] + both[3 * rows :]
+    for c in range(3):
+        layers[:, c * height : (c + 1) * height] = moment[c * rows : (c + 1) * rows].reshape(
+            depth, height, width
+        )
+    lane = lax.broadcasted_iota(jnp.int32, (height, width), 1)
+    sides = []
+    for column in (0, width - 1):
+        side = jnp.zeros((height, width), jnp.float32)
+        for field in range(3):
+            for z in range(depth):
+                value = raw[field][z][:, column : column + 1]
+                side = jnp.where(lane == field * depth + z, value, side)
+        sides.append(side)
+    for spot, number in enumerate(order_x):
+        other = lax.bitwise_xor(gx, number)
+        out_refs[spot][: 3 * height] = layers[other]
+        out_refs[spot][3 * height :] = jnp.where(other > gx, sides[1], sides[0])
+    for field in range(3):
+        first_ref[field] = raw[field][:, 0]
+        last_ref[field] = raw[field][:, height - 1]
+
+
+def fetch_kernel(table_ref, table, sems):
+    copies = [
+        pltpu.make_async_copy(table_ref.at[half, parity], table.at[half, parity], sems.at[half, parity])
+        for half in range(2)
+        for parity in range(2)
+    ]
+    for copy in copies:
+        copy.start()
+    for copy in copies:
+        copy.wait()
+
+
+def pair_sign(lanes):
+    spot = lax.broadcasted_iota(jnp.int32, (1, lanes), 1)
+    return jnp.where((spot & 64) == 0, 1.0, -1.0).astype(jnp.float32)
+
+
+def turn_all(value, sign):
+    lanes = value.shape[1]
+    return jnp.concatenate([turn(value[:, i : i + 128], sign) for i in range(0, lanes, 128)], 1)
+
+
+def layer_lines_kernel(order_x, *refs):
+    count_x = len(order_x)
+    chunk_refs, (place, table, out_ref, blocks) = refs[:count_x], refs[count_x:]
+    gx = place[0]
+    rows = blocks.shape[1]
+    for spot, number in enumerate(order_x):
+        blocks[lax.bitwise_xor(gx, number)] = chunk_refs[spot][:rows]
+    sums = []
+    for parity in range(2):
+        value = jnp.concatenate(
+            [blocks[g, :, parity * 128 : (parity + 1) * 128] for g in range(count_x)], 1
+        )
+        flipped = value * pair_sign(value.shape[1])
+        high, low = split_high(jnp.concatenate([value, flipped], 0))
+        wide = table[0, parity].reshape(value.shape[1], -1)
+        fine = table[1, parity].reshape(value.shape[1], -1)
+        both = dot(jnp.concatenate([high, low], 0), wide)
+        sums.append(both[: 2 * rows] + both[2 * rows :] + dot(high, fine))
+    sign = pair_sign(128)
+    even, even_flipped = sums[0][:rows], sums[0][rows:]
+    odd, odd_turned = sums[1][:rows], turn_all(sums[1][rows:], sign)
+    waves = [even + odd, even_flipped + odd_turned, even - odd, even_flipped - odd_turned]
+    count_y = out_ref.shape[0] // count_x
+    for g in range(count_x):
+        for y in range(count_y):
+            out_ref[g * count_y + y] = waves[g][:, y * 128 : (y + 1) * 128]
+
+
+def layer_back_kernel(order_x, *refs):
+    count_x = len(order_x)
+    (spec_ref, place, table), out_refs, blocks = refs[:3], refs[3:-1], refs[-1]
+    gx = place[0]
+    rows = spec_ref.shape[1]
+    count_y = spec_ref.shape[0] // count_x
+    w0, w1, w2, w3 = [
+        jnp.concatenate([spec_ref[g * count_y + y] for y in range(count_y)], 1)
+        for g in range(count_x)
+    ]
+    sign = pair_sign(128)
+    even, odd = w0 + w2, w1 + w3
+    cross_even, cross_odd = w0 - w2, turn_all(w1 - w3, sign)
+    pairs = [(even + odd, even - odd), (cross_even - cross_odd, cross_even + cross_odd)]
+    for parity in range(2):
+        high, low = split_high(jnp.concatenate(pairs[parity], 0))
+        wide = table[0, parity].reshape(count_x * 128, -1)
+        fine = table[1, parity].reshape(count_x * 128, -1)
+        both = dot(jnp.concatenate([high, low], 0), wide, ((1,), (1,)))
+        both = both[: 2 * rows] + both[2 * rows :] + dot(high, fine, ((1,), (1,)))
+        value = jnp.where(pair_sign(both.shape[1]) > 0.0, both[:rows], both[rows:])
+        for g in range(count_x):
+            blocks[g, :, parity * 128 : (parity + 1) * 128] = value[:, g * 128 : (g + 1) * 128]
+    for spot, number in enumerate(order_x):
+        out_refs[spot][...] = blocks[lax.bitwise_xor(gx, number)]
+
+
+def layer_waves_kernel(scale, count_y, spec_ref, *refs):
+    tables, out_ref, scratch = refs[:3], refs[3], refs[4:]
+    count, lines, lanes = spec_ref.shape
+    depth, local = count // count_y, lines // 3
+
+    def place(plane):
+        c, z = divmod(plane, depth)
+        return slice(z * count_y, (z + 1) * count_y), slice(c * local, (c + 1) * local)
+
+    def read(plane):
+        blocks, rows = place(plane)
+        return spec_ref[blocks, rows].reshape(count_y * local, lanes)
+
+    def write(plane, value):
+        blocks, rows = place(plane)
+        out_ref[blocks, rows] = value.reshape(count_y, local, lanes)
+
+    waves(scale, count_y * local, 3 * depth, lanes, read, write, tables, scratch)
+
+
+def layer_exchange_kernel(order_x, count_y, *refs):
+    count_x = len(order_x)
+    theta_ref, phi_ref, labels_ref, before_ref, after_ref = refs[:5]
+    chunk_refs, (place, ms_ref, aex_ref, exchange_ref, unit_ref) = refs[5:-5], refs[-5:]
+    depth, height, width = shape = theta_ref.shape
+    gx, gy = place[0], place[1]
+    lane = lax.broadcasted_iota(jnp.int32, shape, 2)
+    row = lax.broadcasted_iota(jnp.int32, shape, 1)
+
+    def side_tile(other):
+        value = None
+        for spot, number in enumerate(order_x[1:]):
+            tile = chunk_refs[spot][3 * height :]
+            match = lax.bitwise_xor(gx, number) == other
+            value = tile if value is None else jnp.where(match, tile, value)
+        return value
+
+    def spread(tile, field):
+        columns = [tile[:, field * depth + z : field * depth + z + 1] for z in range(depth)]
+        return jnp.stack([jnp.broadcast_to(c, (height, width)) for c in columns])
+
+    left, right = side_tile(gx - 1), side_tile(gx + 1)
+    raw = [theta_ref[...], phi_ref[...], labels_ref[...].astype(jnp.float32)]
+    side = [jnp.where(lane == 0, spread(right, f), spread(left, f)) for f in range(3)]
+    above = [
+        jnp.where(
+            row == 0,
+            jnp.broadcast_to(after_ref[f][:, None, :], shape),
+            jnp.broadcast_to(before_ref[f][:, None, :], shape),
+        )
+        for f in range(3)
+    ]
+    exchange(raw, side, above, (gx, count_x, gy, count_y), ms_ref, aex_ref, exchange_ref, unit_ref)
+
+
+def layer_final_kernel(order_x, *refs):
+    count_x = len(order_x)
+    part_refs, (place, unsort, exchange_ref, unit_ref) = refs[:count_x], refs[count_x : count_x + 4]
+    field_ref, predicted_ref, layers = refs[count_x + 4 :]
+    gx = place[0]
+    depth, height, width = unit_ref.shape[1:]
+    for spot, number in enumerate(order_x):
+        layers[lax.bitwise_xor(gx, number)] = part_refs[spot][...]
+    value = jnp.concatenate(
+        [layers[:, c * height : (c + 1) * height].reshape(depth * height, width) for c in range(3)], 0
+    )
+    high = value.astype(jnp.bfloat16)
+    rest = value - high.astype(jnp.float32)
+    middle, low = split_high(rest)
+    rows = value.shape[0]
+    sorted_back = dot(jnp.concatenate([high, middle, low], 0), unsort[...])
+    value = sorted_back[:rows] + (sorted_back[rows : 2 * rows] + sorted_back[2 * rows :])
+    size = depth * height
+    predict(
+        [value[c * size : (c + 1) * size] for c in range(3)],
+        exchange_ref,
+        unit_ref,
+        field_ref,
+        predicted_ref,
+    )
 
 
 vmem = pl.BlockSpec(memory_space=pltpu.VMEM)
@@ -497,12 +739,126 @@
     return [0] + list(range(devices - 1, 0, -1))
 
 
+def tensor_here(kernel):
+    rows, columns = kernel.shape[2:]
+    twice = np.concatenate([np.eye(rows), np.eye(rows)], 1).astype(ml_dtypes.bfloat16)
+    return call(
+        tensor_kernel,
+        jax.ShapeDtypeStruct((48, columns, 2 * rows), jnp.bfloat16),
+        [vmem, vmem],
+        (kernel.reshape(48, rows, columns), jnp.asarray(twice)),
+        flops=48 * 4 * rows * rows * columns,
+        name="tensor",
+    )
+
+
+def per_layer(theta, phi, labels, ms_region, aex_region, kernel):
+    count_x, count_y = lax.axis_size("gx"), lax.axis_size("gy")
+    depth, height, width = theta.shape
+    rows = kernel.shape[2]
+    lanes = 2 * rows
+    whole_y = count_y * height
+    lines = 3 * height
+    cells, edge = f32(3, depth, height, width), f32(3, depth, width)
+    order_x = partners(count_x)
+    place = jnp.stack([lax.axis_index("gx"), lax.axis_index("gy")]).astype(jnp.int32)
+    sort = np.eye(width)[:, sorted_cells(width)]
+    table = jnp.asarray(sorted_table(count_x, count_y, width, rows))
+    forward, inverse = [jnp.asarray(t[0]) for t in column_tables(count_y, height, range(count_y))]
+    transform_flops = 6 * lines * count_x * width * count_y * lanes
+
+    *chunks, first, last = call(
+        functools.partial(sorting_kernel, order_x),
+        [f32(lines + height, width)] * count_x + [edge, edge],
+        [hbm] * 4 + [smem, hbm],
+        (theta, phi, labels, ms_region, place, jnp.asarray(sort.astype(ml_dtypes.bfloat16))),
+        scratch=(
+            pltpu.VMEM((2, depth, height, width), jnp.float32),
+            pltpu.VMEM((depth, height, width), jnp.int32),
+            pltpu.SMEM(ms_region.shape, jnp.float32),
+            pltpu.VMEM((width, width), jnp.bfloat16),
+            pltpu.VMEM((depth, lines, width), jnp.float32),
+            pltpu.SemaphoreType.DMA((5,)),
+        ),
+        name="sort",
+    )
+    chunks = exchanged(chunks, "gx", order_x)
+    table = call(
+        fetch_kernel,
+        [pltpu.VMEM(table.shape, jnp.bfloat16)],
+        [hbm],
+        (table,),
+        scratch=(pltpu.SemaphoreType.DMA((2, 2)),),
+        name="fetch",
+    )[0]
+    tensor = tensor_here(kernel)
+    spectrum = call(
+        functools.partial(layer_lines_kernel, order_x),
+        f32(count_x * count_y, lines, lanes),
+        [vmem] * count_x + [smem, vmem],
+        (*chunks, place, table),
+        scratch=(pltpu.VMEM((count_x, lines, width), jnp.float32),),
+        flops=transform_flops,
+        name="lines",
+    )
+    spectrum, first, last = lax.optimization_barrier((spectrum, first, last))
+    axes = ("gx", "gy")
+    columns = lax.all_to_all(spectrum, axes, split_axis=0, concat_axis=0, tiled=True)
+    scale = -1.0 / (2 * depth * 2 * whole_y * 2 * count_x * width)
+    images = call(
+        functools.partial(layer_waves_kernel, scale, count_y),
+        f32(count_x * count_y, lines, lanes),
+        [vmem] * 4,
+        (columns, tensor, forward, inverse),
+        scratch=(
+            pltpu.VMEM((2 * whole_y, 3 * depth * lanes), jnp.float32),
+            pltpu.VMEM((6 * whole_y, 3 * depth * lanes), jnp.bfloat16),
+        ),
+        flops=20 * whole_y * whole_y * 3 * depth * lanes,
+        name="waves",
+    )
+    returned = lax.all_to_all(images, axes, split_axis=0, concat_axis=0, tiled=True)
+    up = [(i, i + 1) for i in range(count_y - 1)]
+    before = lax.ppermute(last, "gy", up)
+    after = lax.ppermute(first, "gy", [(j, i) for i, j in up])
+    exchange_field, unit = call(
+        functools.partial(layer_exchange_kernel, order_x, count_y),
+        [cells, cells],
+        [vmem] * (4 + count_x) + [smem] * 3,
+        (theta, phi, labels, before, after, *chunks[1:], place, ms_region, aex_region),
+        flops=300 * depth * height * width,
+        name="exchange",
+    )
+    returned, exchange_field, unit = lax.optimization_barrier((returned, exchange_field, unit))
+    partial = call(
+        functools.partial(layer_back_kernel, order_x),
+        [f32(lines, width)] * count_x,
+        [vmem, smem, vmem],
+        (returned, place, table),
+        scratch=(pltpu.VMEM((count_x, lines, width), jnp.float32),),
+        flops=transform_flops,
+        name="back_lines",
+    )
+    parts = exchanged(partial, "gx", order_x)
+    return call(
+        functools.partial(layer_final_kernel, order_x),
+        [cells, cells],
+        [vmem] * count_x + [smem] + [vmem] * 3,
+        (*parts, place, jnp.asarray(sort.T.astype(ml_dtypes.bfloat16)), exchange_field, unit),
+        scratch=(pltpu.VMEM((depth, lines, width), jnp.float32),),
+        flops=60 * depth * height * width,
+        name="predict",
+    )
+
+
 def per_device(theta, phi, labels, ms_region, aex_region, kernel):
     count_x, count_y = lax.axis_size("gx"), lax.axis_size("gy")
     gx, gy = lax.axis_index("gx"), lax.axis_index("gy")
     depth, height, width = theta.shape
     rows = kernel.shape[2]
     lanes = 2 * rows
+    if count_x == depth == 4 and lanes == 128 and width == 256 and height == 8:
+        return tuple(per_layer(theta, phi, labels, ms_region, aex_region, kernel))
     lines = 3 * depth * height
     whole_y = count_y * height
 
@@ -516,7 +872,6 @@
     else:
         columns_tables = column_tables(count_y, height, order_y)
     sources = [jnp.asarray(t) for t in (table, *columns_tables)]
-    twice = np.concatenate([np.eye(rows), np.eye(rows)], 1).astype(ml_dtypes.bfloat16)
     transform_flops = 6 * lines * count_x * width * count_y * lanes
 
     packed = call(
@@ -545,14 +900,7 @@
         name="load",
     )
 
-    tensor = call(
-        tensor_kernel,
-        jax.ShapeDtypeStruct((48, 2 * whole_y, lanes), jnp.bfloat16),
-        [vmem, vmem],
-        (kernel.reshape(48, rows, 2 * whole_y), jnp.asarray(twice)),
-        flops=48 * 2 * rows * lanes * 2 * whole_y,
-        name="tensor",
-    )
+    tensor = tensor_here(kernel)
     gathered, tensor = lax.optimization_barrier((gathered, tensor))
     edge_rows = 3 * depth * width // lanes
     spectrum = call(
@@ -589,7 +937,7 @@
     )
     edges = [columns[order_y.index(number)] for number in meeting(count_y)]
     edges, partial = lax.optimization_barrier((edges, partial))
-    exchange, unit = call(
+    exchange_field, unit = call(
         functools.partial(exchange_kernel, order_x, count_y),
         [cells, cells],
         [vmem] * (count_x + len(edges)) + [smem] * 3,
@@ -603,7 +951,7 @@
         functools.partial(final_kernel, count_x),
         [cells, cells],
         [vmem] * (count_x + 2),
-        (*parts, exchange, unit),
+        (*parts, exchange_field, unit),
         flops=60 * depth * height * width,
         name="predict",
     )

time: 55.1 us -> 62.4 us (1.13)
  waiting for transfers between devices: 12.3 us -> 22.9 us
  starting transfers between devices: 27.5 us -> 17.8 us
  local copies, waits for them, and re-layouts: 0.02 us -> 4.18 us
  Pallas kernels: 14.2 us -> 16.2 us
    ppermute x20 -> x6, starting transfers between devices: 27.5 us -> 5.05 us  [exchanged(): out[spot + 1] = lax.ppermute(chunks[spot + 1], axis, pairs)]
    all_to_all x0 -> x2, waiting for transfers between devices: none -> 15.1 us  [the longest x1 11.9 us: per_layer(): lax.all_to_all(spectrum, axes, split_axis=0, concat_axis=0, tiled=True)]
    ppermute x20 -> x6, waiting for transfers between devices: 12.3 us -> 3.46 us  [exchanged(): out[spot + 1] = lax.ppermute(chunks[spot + 1], axis, pairs)]
    all_to_all x0 -> x2, starting transfers between devices: none -> 7.95 us  [the longest x1 5.36 us: per_layer(): lax.all_to_all(spectrum, axes, split_axis=0, concat_axis=0, tiled=True)]
    ppermute x0 -> x2, starting transfers between devices: none -> 4.85 us  [the longest x1 3.56 us: per_layer(): before = lax.ppermute(last, 'gy', up)]
    ppermute x0 -> x2, waiting for transfers between devices: none -> 4.35 us  [the longest x1 4.26 us: per_layer(): after = lax.ppermute(first, 'gy', [(j, i) for i, j in up])]
    unnamed x8 -> x24, local copies, waits for them, and re-layouts: 0.02 us -> 4.18 us
    pallas_call x8, Pallas kernels: 14.2 us -> 16.2 us  [call(): pl.pallas_call(body, out_shape=out, in_specs=ins, out_specs=[vmem] * len(...]
  transfers between devices with their start and end apart: 20 -> 10, of which waited for: 8 -> 7; matrix products, arithmetic and copies ran while one was open for 0% -> 0% of each run, Pallas kernels for 11% -> 8%
where the time goes in v5:
time: 62.4 us; the launch traced here: 62 us
  waiting for transfers between devices  22.9 us (37%)
  starting transfers between devices  17.8 us (29%)
  Pallas kernels  16.2 us (26%)
  local copies, waits for them, and re-layouts  4.18 us (7%)
  between operations  0.81 us (1%)
    pallas_call x8, Pallas kernels, call(): pl.pallas_call(body, out_shape=out, in_specs=ins, out_specs=[vmem] * len(...  16.2 us
    all_to_all x1, waiting for transfers between devices, per_layer(): lax.all_to_all(spectrum, axes, split_axis=0, concat_axis=0, tiled=True)  11.9 us
    all_to_all x1, starting transfers between devices, per_layer(): lax.all_to_all(spectrum, axes, split_axis=0, concat_axis=0, tiled=True)  5.36 us
    ppermute x6, starting transfers between devices, exchanged(): out[spot + 1] = lax.ppermute(chunks[spot + 1], axis, pairs)  5.05 us
    ppermute x1, waiting for transfers between devices, per_layer(): after = lax.ppermute(first, 'gy', [(j, i) for i, j in up])  4.26 us
    unnamed x24, local copies, waits for them, and re-layouts  4.18 us
    ppermute x1, starting transfers between devices, per_layer(): before = lax.ppermute(last, 'gy', up)  3.56 us
    ppermute x6, waiting for transfers between devices, exchanged(): out[spot + 1] = lax.ppermute(chunks[spot + 1], axis, pairs)  3.46 us
  transfers between devices with their start and end apart: 10, of which 7 were waited for; matrix products, arithmetic and copies ran while one was open for 0% of the time, Pallas kernels for 8%

profile of v5, /device:TPU:0, one launch (start us, length us, event | category | flops | bytes accessed | tf_op | source)
XLA Modules:
  0.0 62.0 jit_solution(8575403828289292713)
XLA Ops:
  0.6 0.1 pad_add_fusion.refs_4_.refs_8_.refs_1_
  0.7 1.8 %sort.1 = (f32[32,256]{1,0:T(8,128)S(1)}, f32[32,256]{1,0:T(8,128)S(1)}, f32[32,256]{1,0:T(8,128)S(1)}, f32[32,256]{1,0:T(8,128)S(1)}, f32[3,4,256]{2,1,0:T(4,128)S(1)}, /*index=5*/f32[3,4,256]{2,1,0:T(4,128)S(1)}) custom-call(f32[4,8,256]{2,1,0:T(8,128)} %refs_0_.3, f32[4,8,256]{2,1,0:T(8,128)} %refs_1_.4, s32[4,8,256]{2,1,0:T(8,128)} %refs_2_.4, ...), custom_call_target="tpu_custom_call" | custom-call | bytes 385096 | tf_op jit(solution)/shard_map/sort/pallas_call | solution.py:713
  2.6 2.4 %collective-permute-start = (f32[32,256]{1,0:T(8,128)S(1)}, f32[32,256]{1,0:T(8,128)S(1)}, u32[]{:S(2)}, u32[]{:S(2)}) collective-permute-start(f32[32,256]{1,0:T(8,128)S(1)} %get-tuple-element.21), channel_id=1, source_target_pairs={{0,24},{8,16},{16,8},{24,0},{1,25},{9,17},{17,9},{25,1},{2,26},{10... | collective-permute-start | bytes 98312 | tf_op jit(solution)/shard_map/ppermute | solution.py:734
  5.0 0.6 %collective-permute-start.1 = (f32[32,256]{1,0:T(8,128)S(1)}, f32[32,256]{1,0:T(8,128)S(1)}, u32[]{:S(2)}, u32[]{:S(2)}) collective-permute-start(f32[32,256]{1,0:T(8,128)S(1)} %get-tuple-element.22), channel_id=1, source_target_pairs={{0,16},{8,24},{16,0},{24,8},{1,17},{9,25},{17,1},{25,9},{2,18},{10... | collective-permute-start | bytes 98312 | tf_op jit(solution)/shard_map/ppermute | solution.py:734
  5.6 0.0 collective-permute-start.2
  5.7 2.2 %fetch.1.refs_5_.refs_2_ = bf16[2,2,4,128,1024]{4,3,2,1,0:T(8,128)(2,1)S(1)} custom-call(bf16[2,2,4,128,1024]{4,3,2,1,0:T(8,128)(2,1)} %constant.20.clone.table_ref), custom_call_target="tpu_custom_call" | custom-call | bytes 8388608 | tf_op jit(solution)/shard_map/fetch/pallas_call | solution.py:713
  7.9 0.0 copy-start.9
  7.9 0.0 copy-start.7
  7.9 0.0 copy-start.8
  8.0 1.0 %collective-permute-done.1.refs_2_.refs_6_ = f32[32,256]{1,0:T(8,128)S(1)} collective-permute-done((f32[32,256]{1,0:T(8,128)S(1)}, f32[32,256]{1,0:T(8,128)S(1)}, u32[]{:S(2)}, u32[]{:S(2)}) %collective-permute-start.1) | collective-permute-done | bytes 32800 | tf_op jit(solution)/shard_map/ppermute | solution.py:734
  9.0 2.2 %lines.1 = f32[32,24,128]{2,1,0:T(8,128)} custom-call(f32[32,256]{1,0:T(8,128)S(1)} %get-tuple-element.20.refs_0_, f32[32,256]{1,0:T(8,128)S(1)} %collective-permute-done.refs_1_.refs_5_, f32[32,256]{1,0:T(8,128)S(1)} %collective-permute-done.1.refs_2_.refs_6_, f32[32,256]{1,0:T(8,128)S(1)} %collective-permute-done.2.refs_3_.refs_7_, ...), custom_call_target="tpu_custom_call" | custom-call | flops 150994944 | bytes 4718600 | tf_op jit(solution)/shard_map/lines/pallas_call | solution.py:713
  11.2 1.9 %copy-done = bf16[2,2,4,128,1024]{4,3,2,1,0:T(8,128)(2,1)} copy-done((bf16[2,2,4,128,1024]{4,3,2,1,0:T(8,128)(2,1)}, bf16[2,2,4,128,1024]{4,3,2,1,0:T(8,128)(2,1)S(1)}, u32[]{:S(2)}) %copy-start) | copy-done | bytes 4194328
  13.1 5.4 %all-to-all-start = ((f32[32,24,128]{2,1,0:T(8,128)}), f32[32,24,128]{2,1,0:T(8,128)S(1)}, u32[]{:S(2)}, u32[]{:S(2)}) async-start(f32[32,24,128]{2,1,0:T(8,128)} %lines.1), calls=%async_computation | async-start | bytes 786432 | tf_op jit(solution)/shard_map/all_to_all | solution.py:806
  18.5 1.6 %tensor.1.refs_0_ = bf16[48,128,128]{2,1,0:T(8,128)(2,1)S(1)} custom-call(bf16[48,64,128]{2,1,0:T(8,128)(2,1)S(1)} %bitcast.3, bf16[64,128]{1,0:T(8,128)(2,1)S(1)} %copy-done.9), custom_call_target="tpu_custom_call" | custom-call | flops 100663296 | bytes 2375680 | tf_op jit(solution)/shard_map/tensor/pallas_call | solution.py:713
  20.1 0.0 copy-start.6
  20.1 11.9 %all-to-all-done.spec_ref = f32[32,24,128]{2,1,0:T(8,128)S(1)} async-done(((f32[32,24,128]{2,1,0:T(8,128)}), f32[32,24,128]{2,1,0:T(8,128)S(1)}, u32[]{:S(2)}, u32[]{:S(2)}) %all-to-all-start) | async-done | bytes 393248 | tf_op jit(solution)/shard_map/all_to_all | solution.py:806
  32.0 3.9 %waves.1 = f32[32,24,128]{2,1,0:T(8,128)} custom-call(f32[32,24,128]{2,1,0:T(8,128)S(1)} %all-to-all-done.spec_ref, bf16[48,128,128]{2,1,0:T(8,128)(2,1)S(1)} %tensor.1.refs_0_, bf16[128,384]{1,0:T(8,128)(2,1)S(1)} %copy-done.7, bf16[128,384]{1,0:T(8,128)(2,1)S(1)} %copy-done.8), custom_call_target="tpu_custom_call" | custom-call | flops 125829120 | bytes 2555904 | tf_op jit(solution)/shard_map/waves/pallas_call | solution.py:713
  35.9 2.6 %all-to-all-start.1 = ((f32[32,24,128]{2,1,0:T(8,128)}), f32[32,24,128]{2,1,0:T(8,128)S(1)}, u32[]{:S(2)}, u32[]{:S(2)}) async-start(f32[32,24,128]{2,1,0:T(8,128)} %waves.1), calls=%async_computation.1 | async-start | bytes 786432 | tf_op jit(solution)/shard_map/all_to_all | solution.py:820
  38.5 3.6 %collective-permute-start.3 = (f32[3,4,256]{2,1,0:T(4,128)S(1)}, f32[3,4,256]{2,1,0:T(4,128)S(1)}, u32[]{:S(2)}, u32[]{:S(2)}) collective-permute-start(f32[3,4,256]{2,1,0:T(4,128)S(1)} %get-tuple-element.27), channel_id=1, source_target_pairs={{0,1},{1,2},{2,3},{3,4},{4,5},{5,6},{6,7},{8,9},{9,10},{10,11},{11... | collective-permute-start | bytes 36872 | tf_op jit(solution)/shard_map/ppermute | solution.py:822
  42.1 1.3 %collective-permute-start.4 = (f32[3,4,256]{2,1,0:T(4,128)S(1)}, f32[3,4,256]{2,1,0:T(4,128)S(1)}, u32[]{:S(2)}, u32[]{:S(2)}) collective-permute-start(f32[3,4,256]{2,1,0:T(4,128)S(1)} %get-tuple-element.28), channel_id=1, source_target_pairs={{1,0},{2,1},{3,2},{4,3},{5,4},{6,5},{7,6},{9,8},{10,9},{11,10},{12... | collective-permute-start | bytes 36872 | tf_op jit(solution)/shard_map/ppermute | solution.py:823
  43.4 0.1 collective-permute-done.3.refs_3_
  43.5 4.3 %collective-permute-done.4.refs_4_ = f32[3,4,256]{2,1,0:T(4,128)S(1)} collective-permute-done((f32[3,4,256]{2,1,0:T(4,128)S(1)}, f32[3,4,256]{2,1,0:T(4,128)S(1)}, u32[]{:S(2)}, u32[]{:S(2)}) %collective-permute-start.4) | collective-permute-done | bytes 12320 | tf_op jit(solution)/shard_map/ppermute | solution.py:823
  47.8 1.1 %exchange.1 = (f32[3,4,8,256]{3,2,1,0:T(8,128)S(1)}, f32[3,4,8,256]{3,2,1,0:T(8,128)S(1)}) custom-call(f32[4,8,256]{2,1,0:T(8,128)S(1)} %copy-done.3, f32[4,8,256]{2,1,0:T(8,128)S(1)} %copy-done.4, s32[4,8,256]{2,1,0:T(8,128)S(1)} %copy-done.5, f32[3,4,256]{2,1,0:T(4,128)S(1)} %collective-permute-done.3.refs_3_, ...), custom_call_target="tpu_custom_call" | custom-call | flops 2457600 | bytes 417928 | tf_op jit(solution)/shard_map/exchange/pallas_call | solution.py:713
  48.9 3.2 %all-to-all-done.1.refs_0_ = f32[32,24,128]{2,1,0:T(8,128)S(1)} async-done(((f32[32,24,128]{2,1,0:T(8,128)}), f32[32,24,128]{2,1,0:T(8,128)S(1)}, u32[]{:S(2)}, u32[]{:S(2)}) %all-to-all-start.1) | async-done | bytes 393248 | tf_op jit(solution)/shard_map/all_to_all | solution.py:820
  52.1 2.2 %copy-done.1 = bf16[2,2,4,128,1024]{4,3,2,1,0:T(8,128)(2,1)S(1)} copy-done((bf16[2,2,4,128,1024]{4,3,2,1,0:T(8,128)(2,1)S(1)}, bf16[2,2,4,128,1024]{4,3,2,1,0:T(8,128)(2,1)}, u32[]{:S(2)}) %copy-start.1) | copy-done | bytes 4194328
  54.3 1.9 %back_lines.1 = (f32[24,256]{1,0:T(8,128)S(1)}, f32[24,256]{1,0:T(8,128)S(1)}, f32[24,256]{1,0:T(8,128)S(1)}, f32[24,256]{1,0:T(8,128)S(1)}) custom-call(f32[32,24,128]{2,1,0:T(8,128)S(1)} %all-to-all-done.1.refs_0_, s32[2]{0:T(128)S(1)} %pad_add_fusion.refs_4_.refs_8_.refs_1_, bf16[2,2,4,128,1024]{4,3,2,1,0:T(8,128)(2,1)S(1)} %copy-done.1), custom_call_target="tpu_custom_call" | custom-call | flops 150994944 | bytes 4685832 | tf_op jit(solution)/shard_map/back_lines/pallas_call | solution.py:713
  56.2 0.5 collective-permute-start.5
  56.7 0.8 %collective-permute-start.6 = (f32[24,256]{1,0:T(8,128)S(1)}, f32[24,256]{1,0:T(8,128)S(1)}, u32[]{:S(2)}, u32[]{:S(2)}) collective-permute-start(f32[24,256]{1,0:T(8,128)S(1)} %get-tuple-element.34), channel_id=1, source_target_pairs={{0,16},{8,24},{16,0},{24,8},{1,17},{9,25},{17,1},{25,9},{2,18},{10... | collective-permute-start | bytes 73736 | tf_op jit(solution)/shard_map/ppermute | solution.py:734
  57.6 0.6 collective-permute-start.7
  58.1 1.5 %collective-permute-done.5.refs_1_ = f32[24,256]{1,0:T(8,128)S(1)} collective-permute-done((f32[24,256]{1,0:T(8,128)S(1)}, f32[24,256]{1,0:T(8,128)S(1)}, u32[]{:S(2)}, u32[]{:S(2)}) %collective-permute-start.5) | collective-permute-done | bytes 24608 | tf_op jit(solution)/shard_map/ppermute | solution.py:734
  59.7 0.9 %collective-permute-done.6.refs_2_ = f32[24,256]{1,0:T(8,128)S(1)} collective-permute-done((f32[24,256]{1,0:T(8,128)S(1)}, f32[24,256]{1,0:T(8,128)S(1)}, u32[]{:S(2)}, u32[]{:S(2)}) %collective-permute-start.6) | collective-permute-done | bytes 24608 | tf_op jit(solution)/shard_map/ppermute | solution.py:734
  60.6 1.4 %predict.1 = (f32[3,4,8,256]{3,2,1,0:T(8,128)}, f32[3,4,8,256]{3,2,1,0:T(8,128)}) custom-call(f32[24,256]{1,0:T(8,128)S(1)} %get-tuple-element.32.refs_0_, f32[24,256]{1,0:T(8,128)S(1)} %collective-permute-done.5.refs_1_, f32[24,256]{1,0:T(8,128)S(1)} %collective-permute-done.6.refs_2_, f32[24,256]{1,0:T(8,128)S(1)} %collective-permute-done.7.refs_3_, ...), custom_call_target="tpu_custom_call" | custom-call | flops 491520 | bytes 622600 | tf_op jit(solution)/shard_map/predict/pallas_call | solution.py:713
  (21 shorter events, 0.0 us)
Async XLA Ops:
  2.6 5.4 %collective-permute-start = (f32[32,256]{1,0:T(8,128)S(1)}, f32[32,256]{1,0:T(8,128)S(1)}, u32[]{:S(2)}, u32[]{:S(2)}) collective-permute-start(f32[32,256]{1,0:T(8,128)S(1)} %get-tuple-element.21), channel_id=1, source_target_pairs={{0,24},{8,16},{16,8},{24,0},{1,25},{9,17},{17,9},{25,1},{2,26},{10... | collective-permute-start | bytes 98312 | tf_op jit(solution)/shard_map/ppermute | solution.py:734
  5.0 4.0 %collective-permute-start.1 = (f32[32,256]{1,0:T(8,128)S(1)}, f32[32,256]{1,0:T(8,128)S(1)}, u32[]{:S(2)}, u32[]{:S(2)}) collective-permute-start(f32[32,256]{1,0:T(8,128)S(1)} %get-tuple-element.22), channel_id=1, source_target_pairs={{0,16},{8,24},{16,0},{24,8},{1,17},{9,25},{17,1},{25,9},{2,18},{10... | collective-permute-start | bytes 98312 | tf_op jit(solution)/shard_map/ppermute | solution.py:734
  5.6 3.3 %collective-permute-start.2 = (f32[32,256]{1,0:T(8,128)S(1)}, f32[32,256]{1,0:T(8,128)S(1)}, u32[]{:S(2)}, u32[]{:S(2)}) collective-permute-start(f32[32,256]{1,0:T(8,128)S(1)} %get-tuple-element.23), channel_id=1, source_target_pairs={{0,8},{8,0},{16,24},{24,16},{1,9},{9,1},{17,25},{25,17},{2,10},{10... | collective-permute-start | bytes 98312 | tf_op jit(solution)/shard_map/ppermute | solution.py:734
  7.9 10.6 %copy-start.2 = (bf16[6,8,64,128]{3,2,1,0:T(8,128)(2,1)S(1)}, bf16[6,8,64,128]{3,2,1,0:T(8,128)(2,1)}, u32[]{:S(2)}) copy-start(bf16[6,8,64,128]{3,2,1,0:T(8,128)(2,1)} %param.17) | copy-start | bytes 2359300
  7.9 10.6 %copy-start.9 = (bf16[64,128]{1,0:T(8,128)(2,1)S(1)}, bf16[64,128]{1,0:T(8,128)(2,1)}, u32[]{:S(2)}) copy-start(bf16[64,128]{1,0:T(8,128)(2,1)} %constant.24.clone.twice_ref) | copy-start | bytes 49156
  7.9 24.1 %copy-start.7 = (bf16[128,384]{1,0:T(8,128)(2,1)S(1)}, bf16[128,384]{1,0:T(8,128)(2,1)}, u32[]{:S(2)}) copy-start(bf16[128,384]{1,0:T(8,128)(2,1)} %constant.21.clone.refs_1_) | copy-start | bytes 294916
  7.9 24.1 %copy-start.8 = (bf16[128,384]{1,0:T(8,128)(2,1)S(1)}, bf16[128,384]{1,0:T(8,128)(2,1)}, u32[]{:S(2)}) copy-start(bf16[128,384]{1,0:T(8,128)(2,1)} %constant.22.clone.refs_2_) | copy-start | bytes 294916
  11.2 1.9 %copy-start = (bf16[2,2,4,128,1024]{4,3,2,1,0:T(8,128)(2,1)}, bf16[2,2,4,128,1024]{4,3,2,1,0:T(8,128)(2,1)S(1)}, u32[]{:S(2)}) copy-start(bf16[2,2,4,128,1024]{4,3,2,1,0:T(8,128)(2,1)S(1)} %fetch.1.refs_5_.refs_2_) | copy-start | bytes 12582916
  13.1 34.7 %copy-start.3 = (f32[4,8,256]{2,1,0:T(8,128)S(1)}, f32[4,8,256]{2,1,0:T(8,128)}, u32[]{:S(2)}) copy-start(f32[4,8,256]{2,1,0:T(8,128)} %refs_0_.3) | copy-start | bytes 98308
  13.1 34.7 %copy-start.4 = (f32[4,8,256]{2,1,0:T(8,128)S(1)}, f32[4,8,256]{2,1,0:T(8,128)}, u32[]{:S(2)}) copy-start(f32[4,8,256]{2,1,0:T(8,128)} %refs_1_.4) | copy-start | bytes 98308
  13.1 34.7 %copy-start.5 = (s32[4,8,256]{2,1,0:T(8,128)S(1)}, s32[4,8,256]{2,1,0:T(8,128)}, u32[]{:S(2)}) copy-start(s32[4,8,256]{2,1,0:T(8,128)} %refs_2_.4) | copy-start | bytes 98308
  13.1 34.7 %copy-start.10 = (f32[16]{0:T(128)S(1)}, f32[16]{0:T(128)}, u32[]{:S(2)}) copy-start(f32[16]{0:T(128)} %refs_9_.1) | copy-start | bytes 196
  13.1 34.7 %copy-start.11 = (f32[16]{0:T(128)S(1)}, f32[16]{0:T(128)}, u32[]{:S(2)}) copy-start(f32[16]{0:T(128)} %refs_10_.1) | copy-start | bytes 196
  13.1 18.9 %all-to-all-start = ((f32[32,24,128]{2,1,0:T(8,128)}), f32[32,24,128]{2,1,0:T(8,128)S(1)}, u32[]{:S(2)}, u32[]{:S(2)}) async-start(f32[32,24,128]{2,1,0:T(8,128)} %lines.1), calls=%async_computation | async-start | bytes 786432 | tf_op jit(solution)/shard_map/all_to_all | solution.py:806
  20.1 40.5 %copy-start.6 = (bf16[256,256]{1,0:T(8,128)(2,1)S(1)}, bf16[256,256]{1,0:T(8,128)(2,1)}, u32[]{:S(2)}) copy-start(bf16[256,256]{1,0:T(8,128)(2,1)} %constant.25.clone.refs_5_) | copy-start | bytes 393220
  35.9 16.1 %all-to-all-start.1 = ((f32[32,24,128]{2,1,0:T(8,128)}), f32[32,24,128]{2,1,0:T(8,128)S(1)}, u32[]{:S(2)}, u32[]{:S(2)}) async-start(f32[32,24,128]{2,1,0:T(8,128)} %waves.1), calls=%async_computation.1 | async-start | bytes 786432 | tf_op jit(solution)/shard_map/all_to_all | solution.py:820
  38.5 5.0 %collective-permute-start.3 = (f32[3,4,256]{2,1,0:T(4,128)S(1)}, f32[3,4,256]{2,1,0:T(4,128)S(1)}, u32[]{:S(2)}, u32[]{:S(2)}) collective-permute-start(f32[3,4,256]{2,1,0:T(4,128)S(1)} %get-tuple-element.27), channel_id=1, source_target_pairs={{0,1},{1,2},{2,3},{3,4},{4,5},{5,6},{6,7},{8,9},{9,10},{10,11},{11... | collective-permute-start | bytes 36872 | tf_op jit(solution)/shard_map/ppermute | solution.py:822
  42.1 5.6 %collective-permute-start.4 = (f32[3,4,256]{2,1,0:T(4,128)S(1)}, f32[3,4,256]{2,1,0:T(4,128)S(1)}, u32[]{:S(2)}, u32[]{:S(2)}) collective-permute-start(f32[3,4,256]{2,1,0:T(4,128)S(1)} %get-tuple-element.28), channel_id=1, source_target_pairs={{1,0},{2,1},{3,2},{4,3},{5,4},{6,5},{7,6},{9,8},{10,9},{11,10},{12... | collective-permute-start | bytes 36872 | tf_op jit(solution)/shard_map/ppermute | solution.py:823
  52.1 2.2 %copy-start.1 = (bf16[2,2,4,128,1024]{4,3,2,1,0:T(8,128)(2,1)S(1)}, bf16[2,2,4,128,1024]{4,3,2,1,0:T(8,128)(2,1)}, u32[]{:S(2)}) copy-start(bf16[2,2,4,128,1024]{4,3,2,1,0:T(8,128)(2,1)} %copy-done) | copy-start | bytes 12582916
  56.2 3.4 %collective-permute-start.5 = (f32[24,256]{1,0:T(8,128)S(1)}, f32[24,256]{1,0:T(8,128)S(1)}, u32[]{:S(2)}, u32[]{:S(2)}) collective-permute-start(f32[24,256]{1,0:T(8,128)S(1)} %get-tuple-element.33), channel_id=1, source_target_pairs={{0,24},{8,16},{16,8},{24,0},{1,25},{9,17},{17,9},{25,1},{2,26},{10... | collective-permute-start | bytes 73736 | tf_op jit(solution)/shard_map/ppermute | solution.py:734
  56.7 3.8 %collective-permute-start.6 = (f32[24,256]{1,0:T(8,128)S(1)}, f32[24,256]{1,0:T(8,128)S(1)}, u32[]{:S(2)}, u32[]{:S(2)}) collective-permute-start(f32[24,256]{1,0:T(8,128)S(1)} %get-tuple-element.34), channel_id=1, source_target_pairs={{0,16},{8,24},{16,0},{24,8},{1,17},{9,25},{17,1},{25,9},{2,18},{10... | collective-permute-start | bytes 73736 | tf_op jit(solution)/shard_map/ppermute | solution.py:734
  57.6 3.0 %collective-permute-start.7 = (f32[24,256]{1,0:T(8,128)S(1)}, f32[24,256]{1,0:T(8,128)S(1)}, u32[]{:S(2)}, u32[]{:S(2)}) collective-permute-start(f32[24,256]{1,0:T(8,128)S(1)} %get-tuple-element.35), channel_id=1, source_target_pairs={{0,8},{8,0},{16,24},{24,16},{1,9},{9,1},{17,25},{25,17},{2,10},{10... | collective-permute-start | bytes 73736 | tf_op jit(solution)/shard_map/ppermute | solution.py:734

commit v6 on v4

--- a/solution.py
+++ b/solution.py
@@ -172,33 +172,44 @@
         raw_ref[index] = value
 
 
-def lines_kernel(count_x, order_y, *refs):
+def lines_kernel(count_x, order_y, far, *refs):
     raw_refs, (region_ref, place, table) = refs[:count_x], refs[count_x : count_x + 3]
-    out_refs, (region, sem) = refs[count_x + 3 : -2], refs[-2:]
-    gy = place[1]
+    out_refs, (both_ref, region, sem) = refs[count_x + 3 : -3], refs[-3:]
     fetch = pltpu.make_async_copy(region_ref, region, sem)
     fetch.start()
     units = [directions(raw_ref[0], raw_ref[1]) for raw_ref in raw_refs]
     fetch.wait()
-    total = None
     for number in range(count_x):
         saturation = looked_up(raw_refs[number][2], region)
         rows = saturation.shape[0] * saturation.shape[1]
         block = [(part * saturation).reshape(rows, -1) for part in units[number]]
         high, low = split_high(jnp.concatenate(block, 0))
-        both = dot(jnp.concatenate([high, low], 0), table[0, number])
-        part = both[: 3 * rows] + both[3 * rows :] + dot(high, table[1, number])
+        both_ref[number] = jnp.concatenate([high, low], 0)
+    put_chunks(both_ref, table, raw_refs[0], place[1], order_y, 0, out_refs)
+
+
+def near_lines_kernel(order_y, far, both_ref, raw_ref, place, table, *out_refs):
+    put_chunks(both_ref, table, raw_ref, place[1], order_y, far, out_refs)
+
+
+def put_chunks(both_ref, table, raw_ref, gy, order_y, start, out_refs):
+    lines, lanes = both_ref.shape[1] // 2, out_refs[-1].shape[1]
+    columns = slice(start * lanes, (start + len(out_refs)) * lanes)
+    total = None
+    for number in range(both_ref.shape[0]):
+        both = dot(both_ref[number], table[0, number, :, columns])
+        part = both[:lines] + both[lines:] + dot(both_ref[number, :lines], table[1, number, :, columns])
         total = part if total is None else total + part
-    lanes = out_refs[0].shape[1]
-    last_row = raw_refs[0].shape[2] - 1
-    for spot, number in enumerate(order_y):
-        out_refs[spot][: 3 * rows] = total[:, spot * lanes : (spot + 1) * lanes]
+    last_row = raw_ref.shape[2] - 1
+    for spot, out_ref in enumerate(out_refs):
+        out_ref[:lines] = total[:, spot * lanes : (spot + 1) * lanes]
+        number = order_y[start + spot]
         if number in meeting(len(order_y)):
             up = lax.bitwise_xor(gy, number) > gy
             for field in range(3):
-                value = raw_refs[0][field]
+                value = raw_ref[field]
                 edge = jnp.where(up, value[:, last_row], value[:, 0])
-                put_edge(out_refs[spot], 3 * rows, field, edge)
+                put_edge(out_ref, lines, field, edge)
 
 
 def meeting(devices):
@@ -221,16 +232,14 @@
     return jnp.concatenate([ref[row : row + depth] for row in spots], 1)
 
 
-def back_lines_kernel(count_x, count_y, *refs):
+def back_lines_kernel(numbers, count_y, *refs):
     in_refs, table, out_refs = refs[:count_y], refs[count_y], refs[count_y + 1 :]
     high, low = split_high(jnp.concatenate([ref[...] for ref in in_refs], 1))
     both = jnp.concatenate([high, low], 0)
     lines = high.shape[0]
-    for number in range(count_x):
+    for number, out_ref in zip(numbers, out_refs):
         wide = dot(both, table[0, number], ((1,), (1,)))
-        out_refs[number][...] = (
-            wide[:lines] + wide[lines:] + dot(high, table[1, number], ((1,), (1,)))
-        )
+        out_ref[...] = wide[:lines] + wide[lines:] + dot(high, table[1, number], ((1,), (1,)))
 
 
 def tensor_kernel(kernel_ref, twice_ref, out_ref):
@@ -300,7 +309,7 @@
 def waves_kernel(scale, count_y, *refs):
     spec_refs, (tensor_ref, forward_ref, inverse_ref) = refs[:count_y], refs[count_y : count_y + 3]
     out_refs, (wave_ref, back_ref) = refs[count_y + 3 : -2], refs[-2:]
-    lines, lanes = spec_refs[0].shape
+    lines, lanes = out_refs[0].shape
     local = 8
     planes = lines // local
     height = count_y * local
@@ -484,17 +493,42 @@
     return jax.ShapeDtypeStruct(shape, jnp.float32)
 
 
+def swapped(chunk, axis, number):
+    devices = lax.axis_size(axis)
+    return lax.ppermute(chunk, axis, [(i, i ^ number) for i in range(devices)])
+
+
 def exchanged(chunks, axis, order):
-    devices = len(order)
-    out = [chunks[0]] + [None] * (devices - 1)
-    for spot, number in enumerate(order[1:]):
-        pairs = [(i, i ^ number) for i in range(devices)]
-        out[spot + 1] = lax.ppermute(chunks[spot + 1], axis, pairs)
-    return out
-
-
-def partners(devices):
-    return [0] + list(range(devices - 1, 0, -1))
+    return [swapped(c, axis, n) if n else c for c, n in zip(chunks, order)]
+
+
+def after(value, other):
+    return lax.optimization_barrier((value, other))[0]
+
+
+def spread(block, axis, first):
+    blocks = {0: block}
+    bit = lax.axis_size(axis) // 2
+    while bit:
+        for number in list(blocks):
+            blocks[number ^ bit] = swapped(blocks[number], axis, bit)
+        if first is not None:
+            blocks[bit], first = lax.optimization_barrier((blocks[bit], first))
+            ready, first = first, None
+        bit //= 2
+    return [blocks[number] for number in range(lax.axis_size(axis))], ready
+
+
+def gathered_sums(blocks, axis):
+    blocks = {number: [block] for number, block in enumerate(blocks)}
+    bit = 1
+    while bit < lax.axis_size(axis):
+        for number in sorted(blocks, reverse=True):
+            if number & bit:
+                block = functools.reduce(jnp.add, blocks.pop(number))
+                blocks[number ^ bit].append(swapped(block, axis, bit))
+        bit *= 2
+    return blocks[0]
 
 
 def per_device(theta, phi, labels, ms_region, aex_region, kernel):
@@ -508,7 +542,7 @@
 
     place = jnp.stack([gx, gy]).astype(jnp.int32)
     cells = f32(3, depth, height, width)
-    order_x, order_y = partners(count_x), partners(count_y)
+    order_x, order_y = list(range(count_x)), list(range(count_y - 1, -1, -1))
     table = line_table(count_x, count_y, width, rows)
     if table is None:
         table = line_table_here(count_x, width, rows, order_y)
@@ -531,7 +565,6 @@
         ),
         name="pack",
     )
-    gathered = exchanged([packed] * count_x, "gx", order_x)
     table, forward, inverse = call(
         functools.partial(load_kernel, order_x, order_y),
         [
@@ -545,6 +578,7 @@
         name="load",
     )
 
+    gathered, table = spread(packed, "gx", table)
     tensor = call(
         tensor_kernel,
         jax.ShapeDtypeStruct((48, 2 * whole_y, lanes), jnp.bfloat16),
@@ -553,18 +587,30 @@
         flops=48 * 2 * rows * lanes * 2 * whole_y,
         name="tensor",
     )
-    gathered, tensor = lax.optimization_barrier((gathered, tensor))
     edge_rows = 3 * depth * width // lanes
-    spectrum = call(
-        functools.partial(lines_kernel, count_x, order_y),
-        [f32(lines + (edge_rows if n in meeting(count_y) else 0), lanes) for n in order_y],
+    far = count_y // 2
+    chunk_shapes = [f32(lines + (edge_rows if n in meeting(count_y) else 0), lanes) for n in order_y]
+    *far_chunks, both = call(
+        functools.partial(lines_kernel, count_x, order_y, far),
+        chunk_shapes[:far] + [jax.ShapeDtypeStruct((count_x, 2 * lines, width), jnp.bfloat16)],
         [vmem] * count_x + [hbm, smem, vmem],
         (*gathered, ms_region, place, table),
         scratch=(pltpu.SMEM(ms_region.shape, jnp.float32), pltpu.SemaphoreType.DMA),
-        flops=transform_flops,
-        name="lines",
-    )
-    columns = exchanged(spectrum, "gy", order_y)
+        flops=transform_flops // 2,
+        name="far_lines",
+    )
+    far_columns = exchanged(far_chunks, "gy", order_y[:far])
+    both = after(both, far_columns[0])
+    near_chunks = call(
+        functools.partial(near_lines_kernel, order_y, far),
+        chunk_shapes[far:],
+        [vmem, vmem, smem, vmem],
+        (both, gathered[0], place, table),
+        flops=transform_flops // 2,
+        name="near_lines",
+    )
+    columns = [*far_columns, *exchanged(near_chunks, "gy", order_y[far:])]
+    columns = lax.optimization_barrier(columns)
     scale = -1.0 / (2 * depth * 2 * whole_y * 2 * count_x * width)
     waves = call(
         functools.partial(waves_kernel, scale, count_y),
@@ -579,16 +625,22 @@
         name="waves",
     )
     returned = exchanged(waves, "gy", order_y)
-    partial = call(
-        functools.partial(back_lines_kernel, count_x, count_y),
-        [f32(lines, width)] * count_x,
-        [vmem] * (count_y + 1),
-        (*returned, table),
-        flops=transform_flops,
-        name="back_lines",
-    )
+    across = [number for number in range(count_x) if number % 2]
+    within = [number for number in range(count_x) if not number % 2]
+    partial = [None] * count_x
+    for numbers, name in ((across, "back_across"), (within, "back_within")):
+        blocks = call(
+            functools.partial(back_lines_kernel, numbers, count_y),
+            [f32(lines, width)] * len(numbers),
+            [vmem] * (count_y + 1),
+            (*returned, table),
+            flops=transform_flops // 2,
+            name=name,
+        )
+        for number, block in zip(numbers, blocks):
+            partial[number] = block
     edges = [columns[order_y.index(number)] for number in meeting(count_y)]
-    edges, partial = lax.optimization_barrier((edges, partial))
+    edges, partial[0] = lax.optimization_barrier((edges, partial[0]))
     exchange, unit = call(
         functools.partial(exchange_kernel, order_x, count_y),
         [cells, cells],
@@ -598,11 +650,11 @@
         flops=300 * depth * height * width,
         name="exchange",
     )
-    parts = exchanged(partial, "gx", order_x)
+    parts = gathered_sums(partial, "gx")
     field, predicted = call(
-        functools.partial(final_kernel, count_x),
+        functools.partial(final_kernel, len(parts)),
         [cells, cells],
-        [vmem] * (count_x + 2),
+        [vmem] * (len(parts) + 2),
         (*parts, exchange, unit),
         flops=60 * depth * height * width,
         name="predict",

time: 55.1 us -> 56.5 us (1.025)
  starting transfers between devices: 27.5 us -> 28.5 us
  Pallas kernels: 14.2 us -> 15 us
    ppermute x20, starting transfers between devices: 27.5 us -> 28.5 us  [swapped(): return lax.ppermute(chunk, axis, [(i, i ^ number) for i in range(devices)])]
    pallas_call x8 -> x10, Pallas kernels: 14.2 us -> 15 us  [call(): pl.pallas_call(body, out_shape=out, in_specs=ins, out_specs=[vmem] * len(...]
  transfers between devices with their start and end apart: 20 -> 20, of which waited for: 8 -> 7; matrix products, arithmetic and copies ran while one was open for 0% -> 0% of each run, Pallas kernels for 11% -> 14%
where the time goes in v6:
time: 56.5 us; the launch traced here: 56.3 us
  starting transfers between devices  28.5 us (50%)
  Pallas kernels  15 us (27%)
  waiting for transfers between devices  11.9 us (21%)
  between operations  0.77 us (1%)
    ppermute x20, starting transfers between devices, swapped(): return lax.ppermute(chunk, axis, [(i, i ^ number) for i in range(devices)])  28.5 us
    pallas_call x10, Pallas kernels, call(): pl.pallas_call(body, out_shape=out, in_specs=ins, out_specs=[vmem] * len(...  15 us
    ppermute x20, waiting for transfers between devices, swapped(): return lax.ppermute(chunk, axis, [(i, i ^ number) for i in range(devices)])  11.9 us
  transfers between devices with their start and end apart: 20, of which 7 were waited for; matrix products, arithmetic and copies ran while one was open for 0% of the time, Pallas kernels for 14%

profile of v6, /device:TPU:0, one launch (start us, length us, event | category | flops | bytes accessed | tf_op | source)
XLA Modules:
  0.0 56.3 jit_solution(11035271132520162506)
XLA Ops:
  0.6 0.8 %pack.1.refs_0_.raw_ref = f32[3,4,8,256]{3,2,1,0:T(8,128)S(1)} custom-call(f32[4,8,256]{2,1,0:T(8,128)} %theta_ref.1, f32[4,8,256]{2,1,0:T(8,128)} %phi_ref.1, s32[4,8,256]{2,1,0:T(8,128)} %labels_ref.1), custom_call_target="tpu_custom_call" | custom-call | bytes 196608 | tf_op jit(solution)/shard_map/pack/pallas_call | solution.py:480
  1.5 3.0 %collective-permute-start.1 = (f32[3,4,8,256]{3,2,1,0:T(8,128)S(1)}, f32[3,4,8,256]{3,2,1,0:T(8,128)S(1)}, u32[]{:S(2)}, u32[]{:S(2)}) collective-permute-start(f32[3,4,8,256]{3,2,1,0:T(8,128)S(1)} %pack.1.refs_0_.raw_ref), channel_id=1, source_target_pairs={{0,16},{8,24},{16,0},{24,8},{1,17},{9,25},{17,1},{25,9},{2,18},{10... | collective-permute-start | bytes 294920 | tf_op jit(solution)/shard_map/ppermute | solution.py:498
  4.5 3.2 %load.1 = (bf16[2,4,256,1024]{3,2,1,0:T(8,128)(2,1)S(1)}, bf16[128,384]{1,0:T(8,128)(2,1)S(1)}, bf16[128,384]{1,0:T(8,128)(2,1)S(1)}) custom-call(s32[2]{0:T(128)S(1)} %pad_add_fusion.place.refs_5_.refs_7_, bf16[4,8,2,4,256,128]{5,4,3,2,1,0:T(8,128)(2,1)} %constant.16.clone.refs_0_, bf16[8,128,384]{2,1,0:T(8,128)(2,1)} %constant.17.clone.refs_1_, ...), custom_call_target="tpu_custom_call" | custom-call | bytes 22741000 | tf_op jit(solution)/shard_map/load/pallas_call | solution.py:480
  7.8 0.6 %collective-permute-start.2 = (f32[3,4,8,256]{3,2,1,0:T(8,128)S(1)}, f32[3,4,8,256]{3,2,1,0:T(8,128)S(1)}, u32[]{:S(2)}, u32[]{:S(2)}) collective-permute-start(f32[3,4,8,256]{3,2,1,0:T(8,128)S(1)} %collective-permute-done.1.refs_2_), channel_id=1, source_target_pairs={{0,8},{8,0},{16,24},{24,16},{1,9},{9,1},{17,25},{25,17},{2,10},{10... | collective-permute-start | bytes 294920 | tf_op jit(solution)/shard_map/ppermute | solution.py:498
  8.3 0.9 %collective-permute-done.2.refs_3_ = f32[3,4,8,256]{3,2,1,0:T(8,128)S(1)} collective-permute-done((f32[3,4,8,256]{3,2,1,0:T(8,128)S(1)}, f32[3,4,8,256]{3,2,1,0:T(8,128)S(1)}, u32[]{:S(2)}, u32[]{:S(2)}) %collective-permute-start.2) | collective-permute-done | bytes 98336 | tf_op jit(solution)/shard_map/ppermute | solution.py:498
  9.3 1.8 %far_lines.1 = (f32[120,128]{1,0:T(8,128)S(1)}, f32[96,128]{1,0:T(8,128)S(1)}, f32[96,128]{1,0:T(8,128)S(1)}, f32[96,128]{1,0:T(8,128)S(1)}, bf16[4,192,256]{2,1,0:T(8,128)(2,1)S(1)}) custom-call(f32[3,4,8,256]{3,2,1,0:T(8,128)S(1)} %pack.1.refs_0_.raw_ref, f32[3,4,8,256]{3,2,1,0:T(8,128)S(1)} %collective-permute-done.refs_1_, ...), custom_call_target="tpu_custom_call" | custom-call | flops 301989888 | bytes 5189704 | tf_op jit(solution)/shard_map/far_lines/pallas_call | solution.py:480
  11.1 4.6 %collective-permute-start.3 = (f32[120,128]{1,0:T(8,128)S(1)}, f32[120,128]{1,0:T(8,128)S(1)}, u32[]{:S(2)}, u32[]{:S(2)}) collective-permute-start(f32[120,128]{1,0:T(8,128)S(1)} %get-tuple-element.46), channel_id=1, source_target_pairs={{0,7},{1,6},{2,5},{3,4},{4,3},{5,2},{6,1},{7,0},{8,15},{9,14},{10,... | collective-permute-start | bytes 184328 | tf_op jit(solution)/shard_map/ppermute | solution.py:498
  15.9 2.4 %collective-permute-done.3.refs_0_.refs_6_ = f32[120,128]{1,0:T(8,128)S(1)} collective-permute-done((f32[120,128]{1,0:T(8,128)S(1)}, f32[120,128]{1,0:T(8,128)S(1)}, u32[]{:S(2)}, u32[]{:S(2)}) %collective-permute-start.3) | collective-permute-done | bytes 61472 | tf_op jit(solution)/shard_map/ppermute | solution.py:498
  18.3 1.1 %near_lines.1 = (f32[120,128]{1,0:T(8,128)S(1)}, f32[96,128]{1,0:T(8,128)S(1)}, f32[120,128]{1,0:T(8,128)S(1)}, f32[96,128]{1,0:T(8,128)S(1)}) custom-call(bf16[4,192,256]{2,1,0:T(8,128)(2,1)S(1)} %get-tuple-element.51.both_ref, f32[3,4,8,256]{3,2,1,0:T(8,128)S(1)} %pack.1.refs_0_.raw_ref, s32[2]{0:T(128)S(1)} %pad_add_fusion.place.refs_5_.refs_7_, ...), custom_call_target="tpu_custom_call" | custom-call | flops 301989888 | bytes 4907016 | tf_op jit(solution)/shard_map/near_lines/pallas_call | solution.py:480
  19.4 2.3 %collective-permute-start.7 = (f32[120,128]{1,0:T(8,128)S(1)}, f32[120,128]{1,0:T(8,128)S(1)}, u32[]{:S(2)}, u32[]{:S(2)}) collective-permute-start(f32[120,128]{1,0:T(8,128)S(1)} %get-tuple-element.52), channel_id=1, source_target_pairs={{0,3},{1,2},{2,1},{3,0},{4,7},{5,6},{6,5},{7,4},{8,11},{9,10},{10,... | collective-permute-start | bytes 184328 | tf_op jit(solution)/shard_map/ppermute | solution.py:498
  21.7 0.4 collective-permute-start.9
  22.1 4.3 %collective-permute-start.5 = (f32[96,128]{1,0:T(8,128)S(1)}, f32[96,128]{1,0:T(8,128)S(1)}, u32[]{:S(2)}, u32[]{:S(2)}) collective-permute-start(f32[96,128]{1,0:T(8,128)S(1)} %get-tuple-element.48), channel_id=1, source_target_pairs={{0,5},{1,4},{2,7},{3,6},{4,1},{5,0},{6,3},{7,2},{8,13},{9,12},{10,... | collective-permute-start | bytes 147464 | tf_op jit(solution)/shard_map/ppermute | solution.py:498
  26.5 0.3 collective-permute-start.8
  26.7 1.6 %tensor.1.refs_8_ = bf16[48,128,128]{2,1,0:T(8,128)(2,1)S(1)} custom-call(bf16[48,64,128]{2,1,0:T(8,128)(2,1)S(1)} %bitcast.3, bf16[64,128]{1,0:T(8,128)(2,1)S(1)} %copy-done.1), custom_call_target="tpu_custom_call" | custom-call | flops 100663296 | bytes 2375680 | tf_op jit(solution)/shard_map/tensor/pallas_call | solution.py:480
  28.3 1.5 %collective-permute-done.5.refs_2_ = f32[96,128]{1,0:T(8,128)S(1)} collective-permute-done((f32[96,128]{1,0:T(8,128)S(1)}, f32[96,128]{1,0:T(8,128)S(1)}, u32[]{:S(2)}, u32[]{:S(2)}) %collective-permute-start.5) | collective-permute-done | bytes 49184 | tf_op jit(solution)/shard_map/ppermute | solution.py:498
  29.8 1.6 %collective-permute-done.6.refs_3_ = f32[96,128]{1,0:T(8,128)S(1)} collective-permute-done((f32[96,128]{1,0:T(8,128)S(1)}, f32[96,128]{1,0:T(8,128)S(1)}, u32[]{:S(2)}, u32[]{:S(2)}) %collective-permute-start.6) | collective-permute-done | bytes 49184 | tf_op jit(solution)/shard_map/ppermute | solution.py:498
  31.4 3.1 %waves.1 = (f32[96,128]{1,0:T(8,128)S(1)}, f32[96,128]{1,0:T(8,128)S(1)}, f32[96,128]{1,0:T(8,128)S(1)}, f32[96,128]{1,0:T(8,128)S(1)}, f32[96,128]{1,0:T(8,128)...) custom-call(f32[120,128]{1,0:T(8,128)S(1)} %collective-permute-done.3.refs_0_.refs_6_, ...), custom_call_target="tpu_custom_call" | custom-call | flops 125829120 | bytes 2592768 | tf_op jit(solution)/shard_map/waves/pallas_call | solution.py:480
  34.6 1.6 %collective-permute-start.10 = (f32[96,128]{1,0:T(8,128)S(1)}, f32[96,128]{1,0:T(8,128)S(1)}, u32[]{:S(2)}, u32[]{:S(2)}) collective-permute-start(f32[96,128]{1,0:T(8,128)S(1)} %get-tuple-element.66), channel_id=1, source_target_pairs={{0,7},{1,6},{2,5},{3,4},{4,3},{5,2},{6,1},{7,0},{8,15},{9,14},{10,... | collective-permute-start | bytes 147464 | tf_op jit(solution)/shard_map/ppermute | solution.py:498
  36.2 2.3 %collective-permute-start.11 = (f32[96,128]{1,0:T(8,128)S(1)}, f32[96,128]{1,0:T(8,128)S(1)}, u32[]{:S(2)}, u32[]{:S(2)}) collective-permute-start(f32[96,128]{1,0:T(8,128)S(1)} %get-tuple-element.67), channel_id=1, source_target_pairs={{0,6},{1,7},{2,4},{3,5},{4,2},{5,3},{6,0},{7,1},{8,14},{9,15},{10,... | collective-permute-start | bytes 147464 | tf_op jit(solution)/shard_map/ppermute | solution.py:498
  38.5 1.1 %collective-permute-start.12 = (f32[96,128]{1,0:T(8,128)S(1)}, f32[96,128]{1,0:T(8,128)S(1)}, u32[]{:S(2)}, u32[]{:S(2)}) collective-permute-start(f32[96,128]{1,0:T(8,128)S(1)} %get-tuple-element.68), channel_id=1, source_target_pairs={{0,5},{1,4},{2,7},{3,6},{4,1},{5,0},{6,3},{7,2},{8,13},{9,12},{10,... | collective-permute-start | bytes 147464 | tf_op jit(solution)/shard_map/ppermute | solution.py:498
  39.6 2.7 %collective-permute-start.13 = (f32[96,128]{1,0:T(8,128)S(1)}, f32[96,128]{1,0:T(8,128)S(1)}, u32[]{:S(2)}, u32[]{:S(2)}) collective-permute-start(f32[96,128]{1,0:T(8,128)S(1)} %get-tuple-element.69), channel_id=1, source_target_pairs={{0,4},{1,5},{2,6},{3,7},{4,0},{5,1},{6,2},{7,3},{8,12},{9,13},{10,... | collective-permute-start | bytes 147464 | tf_op jit(solution)/shard_map/ppermute | solution.py:498
  42.3 2.1 %collective-permute-start.15 = (f32[96,128]{1,0:T(8,128)S(1)}, f32[96,128]{1,0:T(8,128)S(1)}, u32[]{:S(2)}, u32[]{:S(2)}) collective-permute-start(f32[96,128]{1,0:T(8,128)S(1)} %get-tuple-element.71), channel_id=1, source_target_pairs={{0,2},{1,3},{2,0},{3,1},{4,6},{5,7},{6,4},{7,5},{8,10},{9,11},{10,... | collective-permute-start | bytes 147464 | tf_op jit(solution)/shard_map/ppermute | solution.py:498
  44.4 1.4 %collective-permute-start.16 = (f32[96,128]{1,0:T(8,128)S(1)}, f32[96,128]{1,0:T(8,128)S(1)}, u32[]{:S(2)}, u32[]{:S(2)}) collective-permute-start(f32[96,128]{1,0:T(8,128)S(1)} %get-tuple-element.72), channel_id=1, source_target_pairs={{0,1},{1,0},{2,3},{3,2},{4,5},{5,4},{6,7},{7,6},{8,9},{9,8},{10,11... | collective-permute-start | bytes 147464 | tf_op jit(solution)/shard_map/ppermute | solution.py:498
  45.8 1.5 %collective-permute-done.14.refs_4_ = f32[96,128]{1,0:T(8,128)S(1)} collective-permute-done((f32[96,128]{1,0:T(8,128)S(1)}, f32[96,128]{1,0:T(8,128)S(1)}, u32[]{:S(2)}, u32[]{:S(2)}) %collective-permute-start.14) | collective-permute-done | bytes 49184 | tf_op jit(solution)/shard_map/ppermute | solution.py:498
  47.3 1.2 %collective-permute-done.16.refs_6_ = f32[96,128]{1,0:T(8,128)S(1)} collective-permute-done((f32[96,128]{1,0:T(8,128)S(1)}, f32[96,128]{1,0:T(8,128)S(1)}, u32[]{:S(2)}, u32[]{:S(2)}) %collective-permute-start.16) | collective-permute-done | bytes 49184 | tf_op jit(solution)/shard_map/ppermute | solution.py:498
  48.5 0.8 %back_across.1 = (f32[96,256]{1,0:T(8,128)S(1)}, f32[96,256]{1,0:T(8,128)S(1)}) custom-call(f32[96,128]{1,0:T(8,128)S(1)} %collective-permute-done.10.refs_0_, f32[96,128]{1,0:T(8,128)S(1)} %collective-permute-done.11.refs_1_, f32[96,128]{1,0:T(8,128)S(1)} %collective-permute-done.12.refs_2_, f32[96,128]{1,0:T(8,128)S(1)} %collective-permute-done.13.refs_3_, ...), custom_call_target="tpu_custom_call" | custom-call | flops 301989888 | bytes 4784128 | tf_op jit(solution)/shard_map/back_across/pallas_call | solution.py:480
  49.4 0.5 collective-permute-start.17
  49.9 0.8 %back_within.1 = (f32[96,256]{1,0:T(8,128)S(1)}, f32[96,256]{1,0:T(8,128)S(1)}) custom-call(f32[96,128]{1,0:T(8,128)S(1)} %collective-permute-done.10.refs_0_, f32[96,128]{1,0:T(8,128)S(1)} %collective-permute-done.11.refs_1_, f32[96,128]{1,0:T(8,128)S(1)} %collective-permute-done.12.refs_2_, f32[96,128]{1,0:T(8,128)S(1)} %collective-permute-done.13.refs_3_, ...), custom_call_target="tpu_custom_call" | custom-call | flops 301989888 | bytes 4784128 | tf_op jit(solution)/shard_map/back_within/pallas_call | solution.py:480
  50.7 1.0 %collective-permute-start.19 = (f32[96,256]{1,0:T(8,128)S(1)}, f32[96,256]{1,0:T(8,128)S(1)}, u32[]{:S(2)}, u32[]{:S(2)}) collective-permute-start(f32[96,256]{1,0:T(8,128)S(1)} %add.3), channel_id=1, source_target_pairs={{0,16},{8,24},{16,0},{24,8},{1,17},{9,25},{17,1},{25,9},{2,18},{10... | collective-permute-start | bytes 294920 | tf_op jit(solution)/shard_map/ppermute | solution.py:498
  51.7 1.1 %exchange.1 = (f32[3,4,8,256]{3,2,1,0:T(8,128)S(1)}, f32[3,4,8,256]{3,2,1,0:T(8,128)S(1)}) custom-call(f32[3,4,8,256]{3,2,1,0:T(8,128)S(1)} %pack.1.refs_0_.raw_ref, f32[3,4,8,256]{3,2,1,0:T(8,128)S(1)} %collective-permute-done.refs_1_, f32[3,4,8,256]{3,2,1,0:T(8,128)S(1)} %collective-permute-done.1.refs_2_, ...), custom_call_target="tpu_custom_call" | custom-call | flops 2457600 | bytes 774280 | tf_op jit(solution)/shard_map/exchange/pallas_call | solution.py:480
  52.8 2.8 %collective-permute-done.19.refs_2_ = f32[96,256]{1,0:T(8,128)S(1)} collective-permute-done((f32[96,256]{1,0:T(8,128)S(1)}, f32[96,256]{1,0:T(8,128)S(1)}, u32[]{:S(2)}, u32[]{:S(2)}) %collective-permute-start.19) | collective-permute-done | bytes 98336 | tf_op jit(solution)/shard_map/ppermute | solution.py:498
  55.6 0.7 %predict.1 = (f32[3,4,8,256]{3,2,1,0:T(8,128)}, f32[3,4,8,256]{3,2,1,0:T(8,128)}) custom-call(f32[96,256]{1,0:T(8,128)S(1)} %get-tuple-element.75.refs_0_, f32[96,256]{1,0:T(8,128)S(1)} %collective-permute-done.17.refs_1_, f32[96,256]{1,0:T(8,128)S(1)} %collective-permute-done.19.refs_2_, f32[3,4,8,256]{3,2,1,0:T(8,128)S(1)} %get-tuple-element.82.refs_3_, ...), custom_call_target="tpu_custom_call" | custom-call | flops 491520 | bytes 688128 | tf_op jit(solution)/shard_map/predict/pallas_call | solution.py:480
  (28 shorter events, 0.5 us)
Async XLA Ops:
  1.5 6.3 %collective-permute-start.1 = (f32[3,4,8,256]{3,2,1,0:T(8,128)S(1)}, f32[3,4,8,256]{3,2,1,0:T(8,128)S(1)}, u32[]{:S(2)}, u32[]{:S(2)}) collective-permute-start(f32[3,4,8,256]{3,2,1,0:T(8,128)S(1)} %pack.1.refs_0_.raw_ref), channel_id=1, source_target_pairs={{0,16},{8,24},{16,0},{24,8},{1,17},{9,25},{17,1},{25,9},{2,18},{10... | collective-permute-start | bytes 294920 | tf_op jit(solution)/shard_map/ppermute | solution.py:498
  4.5 3.9 %collective-permute-start = (f32[3,4,8,256]{3,2,1,0:T(8,128)S(1)}, f32[3,4,8,256]{3,2,1,0:T(8,128)S(1)}, u32[]{:S(2)}, u32[]{:S(2)}) collective-permute-start(f32[3,4,8,256]{3,2,1,0:T(8,128)S(1)} %pack.1.refs_0_.raw_ref), channel_id=1, source_target_pairs={{0,8},{8,0},{16,24},{24,16},{1,9},{9,1},{17,25},{25,17},{2,10},{10... | collective-permute-start | bytes 294920 | tf_op jit(solution)/shard_map/ppermute | solution.py:498
  7.7 19.0 %copy-start = (bf16[6,8,64,128]{3,2,1,0:T(8,128)(2,1)S(1)}, bf16[6,8,64,128]{3,2,1,0:T(8,128)(2,1)}, u32[]{:S(2)}) copy-start(bf16[6,8,64,128]{3,2,1,0:T(8,128)(2,1)} %param.15) | copy-start | bytes 2359300
  7.8 19.0 %copy-start.1 = (bf16[64,128]{1,0:T(8,128)(2,1)S(1)}, bf16[64,128]{1,0:T(8,128)(2,1)}, u32[]{:S(2)}) copy-start(bf16[64,128]{1,0:T(8,128)(2,1)} %constant.19.clone.twice_ref) | copy-start | bytes 49156
  7.8 1.5 %collective-permute-start.2 = (f32[3,4,8,256]{3,2,1,0:T(8,128)S(1)}, f32[3,4,8,256]{3,2,1,0:T(8,128)S(1)}, u32[]{:S(2)}, u32[]{:S(2)}) collective-permute-start(f32[3,4,8,256]{3,2,1,0:T(8,128)S(1)} %collective-permute-done.1.refs_2_), channel_id=1, source_target_pairs={{0,8},{8,0},{16,24},{24,16},{1,9},{9,1},{17,25},{25,17},{2,10},{10... | collective-permute-start | bytes 294920 | tf_op jit(solution)/shard_map/ppermute | solution.py:498
  11.1 7.2 %collective-permute-start.3 = (f32[120,128]{1,0:T(8,128)S(1)}, f32[120,128]{1,0:T(8,128)S(1)}, u32[]{:S(2)}, u32[]{:S(2)}) collective-permute-start(f32[120,128]{1,0:T(8,128)S(1)} %get-tuple-element.46), channel_id=1, source_target_pairs={{0,7},{1,6},{2,5},{3,4},{4,3},{5,2},{6,1},{7,0},{8,15},{9,14},{10,... | collective-permute-start | bytes 184328 | tf_op jit(solution)/shard_map/ppermute | solution.py:498
  15.7 10.8 %collective-permute-start.4 = (f32[96,128]{1,0:T(8,128)S(1)}, f32[96,128]{1,0:T(8,128)S(1)}, u32[]{:S(2)}, u32[]{:S(2)}) collective-permute-start(f32[96,128]{1,0:T(8,128)S(1)} %get-tuple-element.47), channel_id=1, source_target_pairs={{0,6},{1,7},{2,4},{3,5},{4,2},{5,3},{6,0},{7,1},{8,14},{9,15},{10,... | collective-permute-start | bytes 147464 | tf_op jit(solution)/shard_map/ppermute | solution.py:498
  19.4 12.0 %collective-permute-start.7 = (f32[120,128]{1,0:T(8,128)S(1)}, f32[120,128]{1,0:T(8,128)S(1)}, u32[]{:S(2)}, u32[]{:S(2)}) collective-permute-start(f32[120,128]{1,0:T(8,128)S(1)} %get-tuple-element.52), channel_id=1, source_target_pairs={{0,3},{1,2},{2,1},{3,0},{4,7},{5,6},{6,5},{7,4},{8,11},{9,10},{10,... | collective-permute-start | bytes 184328 | tf_op jit(solution)/shard_map/ppermute | solution.py:498
  21.7 9.7 %collective-permute-start.9 = (f32[120,128]{1,0:T(8,128)S(1)}, f32[120,128]{1,0:T(8,128)S(1)}, u32[]{:S(2)}, u32[]{:S(2)}) collective-permute-start(f32[120,128]{1,0:T(8,128)S(1)} %get-tuple-element.54), channel_id=1, source_target_pairs={{0,1},{1,0},{2,3},{3,2},{4,5},{5,4},{6,7},{7,6},{8,9},{9,8},{10,11... | collective-permute-start | bytes 184328 | tf_op jit(solution)/shard_map/ppermute | solution.py:498
  22.1 7.7 %collective-permute-start.5 = (f32[96,128]{1,0:T(8,128)S(1)}, f32[96,128]{1,0:T(8,128)S(1)}, u32[]{:S(2)}, u32[]{:S(2)}) collective-permute-start(f32[96,128]{1,0:T(8,128)S(1)} %get-tuple-element.48), channel_id=1, source_target_pairs={{0,5},{1,4},{2,7},{3,6},{4,1},{5,0},{6,3},{7,2},{8,13},{9,12},{10,... | collective-permute-start | bytes 147464 | tf_op jit(solution)/shard_map/ppermute | solution.py:498
  26.4 5.0 %collective-permute-start.6 = (f32[96,128]{1,0:T(8,128)S(1)}, f32[96,128]{1,0:T(8,128)S(1)}, u32[]{:S(2)}, u32[]{:S(2)}) collective-permute-start(f32[96,128]{1,0:T(8,128)S(1)} %get-tuple-element.49), channel_id=1, source_target_pairs={{0,4},{1,5},{2,6},{3,7},{4,0},{5,1},{6,2},{7,3},{8,12},{9,13},{10,... | collective-permute-start | bytes 147464 | tf_op jit(solution)/shard_map/ppermute | solution.py:498
  26.5 5.0 %collective-permute-start.8 = (f32[96,128]{1,0:T(8,128)S(1)}, f32[96,128]{1,0:T(8,128)S(1)}, u32[]{:S(2)}, u32[]{:S(2)}) collective-permute-start(f32[96,128]{1,0:T(8,128)S(1)} %get-tuple-element.53), channel_id=1, source_target_pairs={{0,2},{1,3},{2,0},{3,1},{4,6},{5,7},{6,4},{7,5},{8,10},{9,11},{10,... | collective-permute-start | bytes 147464 | tf_op jit(solution)/shard_map/ppermute | solution.py:498
  34.6 7.7 %collective-permute-start.10 = (f32[96,128]{1,0:T(8,128)S(1)}, f32[96,128]{1,0:T(8,128)S(1)}, u32[]{:S(2)}, u32[]{:S(2)}) collective-permute-start(f32[96,128]{1,0:T(8,128)S(1)} %get-tuple-element.66), channel_id=1, source_target_pairs={{0,7},{1,6},{2,5},{3,4},{4,3},{5,2},{6,1},{7,0},{8,15},{9,14},{10,... | collective-permute-start | bytes 147464 | tf_op jit(solution)/shard_map/ppermute | solution.py:498
  36.2 8.2 %collective-permute-start.11 = (f32[96,128]{1,0:T(8,128)S(1)}, f32[96,128]{1,0:T(8,128)S(1)}, u32[]{:S(2)}, u32[]{:S(2)}) collective-permute-start(f32[96,128]{1,0:T(8,128)S(1)} %get-tuple-element.67), channel_id=1, source_target_pairs={{0,6},{1,7},{2,4},{3,5},{4,2},{5,3},{6,0},{7,1},{8,14},{9,15},{10,... | collective-permute-start | bytes 147464 | tf_op jit(solution)/shard_map/ppermute | solution.py:498
  38.5 7.3 %collective-permute-start.12 = (f32[96,128]{1,0:T(8,128)S(1)}, f32[96,128]{1,0:T(8,128)S(1)}, u32[]{:S(2)}, u32[]{:S(2)}) collective-permute-start(f32[96,128]{1,0:T(8,128)S(1)} %get-tuple-element.68), channel_id=1, source_target_pairs={{0,5},{1,4},{2,7},{3,6},{4,1},{5,0},{6,3},{7,2},{8,13},{9,12},{10,... | collective-permute-start | bytes 147464 | tf_op jit(solution)/shard_map/ppermute | solution.py:498
  39.6 6.2 %collective-permute-start.13 = (f32[96,128]{1,0:T(8,128)S(1)}, f32[96,128]{1,0:T(8,128)S(1)}, u32[]{:S(2)}, u32[]{:S(2)}) collective-permute-start(f32[96,128]{1,0:T(8,128)S(1)} %get-tuple-element.69), channel_id=1, source_target_pairs={{0,4},{1,5},{2,6},{3,7},{4,0},{5,1},{6,2},{7,3},{8,12},{9,13},{10,... | collective-permute-start | bytes 147464 | tf_op jit(solution)/shard_map/ppermute | solution.py:498
  42.3 5.0 %collective-permute-start.14 = (f32[96,128]{1,0:T(8,128)S(1)}, f32[96,128]{1,0:T(8,128)S(1)}, u32[]{:S(2)}, u32[]{:S(2)}) collective-permute-start(f32[96,128]{1,0:T(8,128)S(1)} %get-tuple-element.70), channel_id=1, source_target_pairs={{0,3},{1,2},{2,1},{3,0},{4,7},{5,6},{6,5},{7,4},{8,11},{9,10},{10,... | collective-permute-start | bytes 147464 | tf_op jit(solution)/shard_map/ppermute | solution.py:498
  42.3 5.0 %collective-permute-start.15 = (f32[96,128]{1,0:T(8,128)S(1)}, f32[96,128]{1,0:T(8,128)S(1)}, u32[]{:S(2)}, u32[]{:S(2)}) collective-permute-start(f32[96,128]{1,0:T(8,128)S(1)} %get-tuple-element.71), channel_id=1, source_target_pairs={{0,2},{1,3},{2,0},{3,1},{4,6},{5,7},{6,4},{7,5},{8,10},{9,11},{10,... | collective-permute-start | bytes 147464 | tf_op jit(solution)/shard_map/ppermute | solution.py:498
  44.4 4.1 %collective-permute-start.16 = (f32[96,128]{1,0:T(8,128)S(1)}, f32[96,128]{1,0:T(8,128)S(1)}, u32[]{:S(2)}, u32[]{:S(2)}) collective-permute-start(f32[96,128]{1,0:T(8,128)S(1)} %get-tuple-element.72), channel_id=1, source_target_pairs={{0,1},{1,0},{2,3},{3,2},{4,5},{5,4},{6,7},{7,6},{8,9},{9,8},{10,11... | collective-permute-start | bytes 147464 | tf_op jit(solution)/shard_map/ppermute | solution.py:498
  48.5 3.2 %copy-start.2 = (f32[16]{0:T(128)S(1)}, f32[16]{0:T(128)}, u32[]{:S(2)}) copy-start(f32[16]{0:T(128)} %refs_8_.1) | copy-start | bytes 196
  48.5 3.2 %copy-start.3 = (f32[16]{0:T(128)S(1)}, f32[16]{0:T(128)}, u32[]{:S(2)}) copy-start(f32[16]{0:T(128)} %refs_9_.1) | copy-start | bytes 196
  49.3 1.4 %collective-permute-start.18 = (f32[96,256]{1,0:T(8,128)S(1)}, f32[96,256]{1,0:T(8,128)S(1)}, u32[]{:S(2)}, u32[]{:S(2)}) collective-permute-start(f32[96,256]{1,0:T(8,128)S(1)} %get-tuple-element.78), channel_id=1, source_target_pairs={{0,8},{8,0},{16,24},{24,16},{1,9},{9,1},{17,25},{25,17},{2,10},{10... | collective-permute-start | bytes 294920 | tf_op jit(solution)/shard_map/ppermute | solution.py:498
  49.4 3.4 %collective-permute-start.17 = (f32[96,256]{1,0:T(8,128)S(1)}, f32[96,256]{1,0:T(8,128)S(1)}, u32[]{:S(2)}, u32[]{:S(2)}) collective-permute-start(f32[96,256]{1,0:T(8,128)S(1)} %get-tuple-element.76), channel_id=1, source_target_pairs={{0,8},{8,0},{16,24},{24,16},{1,9},{9,1},{17,25},{25,17},{2,10},{10... | collective-permute-start | bytes 294920 | tf_op jit(solution)/shard_map/ppermute | solution.py:498
  50.7 4.9 %collective-permute-start.19 = (f32[96,256]{1,0:T(8,128)S(1)}, f32[96,256]{1,0:T(8,128)S(1)}, u32[]{:S(2)}, u32[]{:S(2)}) collective-permute-start(f32[96,256]{1,0:T(8,128)S(1)} %add.3), channel_id=1, source_target_pairs={{0,16},{8,24},{16,0},{24,8},{1,17},{9,25},{17,1},{25,9},{2,18},{10... | collective-permute-start | bytes 294920 | tf_op jit(solution)/shard_map/ppermute | solution.py:498

commit v7 on v6

--- a/solution.py
+++ b/solution.py
@@ -158,7 +158,8 @@
     return result
 
 
-def pack_kernel(theta_ref, phi_ref, labels_ref, raw_ref, angle, label, sems):
+def pack_kernel(theta_ref, phi_ref, labels_ref, raw_ref, first_ref, last_ref, angle, label, sems):
+    height = theta_ref.shape[1]
     copies = [
         pltpu.make_async_copy(theta_ref, angle.at[0], sems.at[0]),
         pltpu.make_async_copy(phi_ref, angle.at[1], sems.at[1]),
@@ -170,66 +171,29 @@
         copy.wait()
     for index, value in enumerate((angle[0], angle[1], label[...].astype(jnp.float32))):
         raw_ref[index] = value
-
-
-def lines_kernel(count_x, order_y, far, *refs):
-    raw_refs, (region_ref, place, table) = refs[:count_x], refs[count_x : count_x + 3]
-    out_refs, (both_ref, region, sem) = refs[count_x + 3 : -3], refs[-3:]
+        first_ref[index] = value[:, 0]
+        last_ref[index] = value[:, height - 1]
+
+
+def lines_kernel(count_x, *refs):
+    raw_refs, (region_ref, table) = refs[:count_x], refs[count_x : count_x + 2]
+    out_refs, (region, sem) = refs[count_x + 2 : -2], refs[-2:]
     fetch = pltpu.make_async_copy(region_ref, region, sem)
     fetch.start()
     units = [directions(raw_ref[0], raw_ref[1]) for raw_ref in raw_refs]
     fetch.wait()
+    total = None
     for number in range(count_x):
         saturation = looked_up(raw_refs[number][2], region)
         rows = saturation.shape[0] * saturation.shape[1]
         block = [(part * saturation).reshape(rows, -1) for part in units[number]]
         high, low = split_high(jnp.concatenate(block, 0))
-        both_ref[number] = jnp.concatenate([high, low], 0)
-    put_chunks(both_ref, table, raw_refs[0], place[1], order_y, 0, out_refs)
-
-
-def near_lines_kernel(order_y, far, both_ref, raw_ref, place, table, *out_refs):
-    put_chunks(both_ref, table, raw_ref, place[1], order_y, far, out_refs)
-
-
-def put_chunks(both_ref, table, raw_ref, gy, order_y, start, out_refs):
-    lines, lanes = both_ref.shape[1] // 2, out_refs[-1].shape[1]
-    columns = slice(start * lanes, (start + len(out_refs)) * lanes)
-    total = None
-    for number in range(both_ref.shape[0]):
-        both = dot(both_ref[number], table[0, number, :, columns])
-        part = both[:lines] + both[lines:] + dot(both_ref[number, :lines], table[1, number, :, columns])
+        both = dot(jnp.concatenate([high, low], 0), table[0, number])
+        part = both[: 3 * rows] + both[3 * rows :] + dot(high, table[1, number])
         total = part if total is None else total + part
-    last_row = raw_ref.shape[2] - 1
+    lanes = out_refs[0].shape[1]
     for spot, out_ref in enumerate(out_refs):
-        out_ref[:lines] = total[:, spot * lanes : (spot + 1) * lanes]
-        number = order_y[start + spot]
-        if number in meeting(len(order_y)):
-            up = lax.bitwise_xor(gy, number) > gy
-            for field in range(3):
-                value = raw_ref[field]
-                edge = jnp.where(up, value[:, last_row], value[:, 0])
-                put_edge(out_ref, lines, field, edge)
-
-
-def meeting(devices):
-    return [number for number in range(1, devices) if (number & (number + 1)) == 0]
-
-
-def edge_spots(depth, width, lanes, start, field):
-    pieces = width // lanes
-    return [start + (field * pieces + piece) * depth for piece in range(pieces)]
-
-
-def put_edge(ref, start, field, edge):
-    lanes = ref.shape[1]
-    for piece, row in enumerate(edge_spots(*edge.shape, lanes, start, field)):
-        ref[row : row + edge.shape[0]] = edge[:, piece * lanes : (piece + 1) * lanes]
-
-
-def get_edge(ref, depth, width, start, field):
-    spots = edge_spots(depth, width, ref.shape[1], start, field)
-    return jnp.concatenate([ref[row : row + depth] for row in spots], 1)
+        out_ref[...] = total[:, spot * lanes : (spot + 1) * lanes]
 
 
 def back_lines_kernel(numbers, count_y, *refs):
@@ -366,19 +330,11 @@
 
 
 def exchange_kernel(order_x, count_y, *refs):
-    count_x, numbers = len(order_x), meeting(count_y)
-    raw_refs, edge_refs, (place, ms_ref, aex_ref) = refs[:count_x], refs[count_x:-6], refs[-6:-3]
+    count_x = len(order_x)
+    raw_refs, (before_ref, after_ref, place, ms_ref, aex_ref) = refs[:count_x], refs[count_x:-3]
     exchange_ref, unit_ref, raw_ref = refs[-3:]
     depth, height, width = raw_ref.shape[2:]
     gx, gy = place[0], place[1]
-
-    def row_meeting(field, other):
-        value = None
-        for number, edge_ref in zip(numbers, edge_refs):
-            edge = get_edge(edge_ref, depth, width, 3 * depth * height, field)
-            match = lax.bitwise_xor(gy, number) == other
-            value = edge if value is None else jnp.where(match, edge, value)
-        return jnp.broadcast_to(value[:, None, :], (depth, height, width))
 
     for spot, number in enumerate(order_x):
         raw_ref[lax.bitwise_xor(gx, number)] = raw_refs[spot][...]
@@ -394,7 +350,7 @@
     here = quantities(raw)
     side = quantities([jnp.where(lane == 0, raw_ref[right, f], raw_ref[left, f]) for f in range(3)])
     above = quantities(
-        [jnp.where(row == 0, row_meeting(f, gy + 1), row_meeting(f, gy - 1)) for f in range(3)]
+        [jnp.where(row == 0, after_ref[f][:, None, :], before_ref[f][:, None, :]) for f in range(3)]
     )
     saturation = looked_up(raw[2], ms_ref)
     total = [jnp.zeros(shape, jnp.float32) for _ in range(3)]
@@ -528,7 +484,7 @@
                 block = functools.reduce(jnp.add, blocks.pop(number))
                 blocks[number ^ bit].append(swapped(block, axis, bit))
         bit *= 2
-    return blocks[0]
+    return blocks[0], block
 
 
 def per_device(theta, phi, labels, ms_region, aex_region, kernel):
@@ -553,9 +509,10 @@
     twice = np.concatenate([np.eye(rows), np.eye(rows)], 1).astype(ml_dtypes.bfloat16)
     transform_flops = 6 * lines * count_x * width * count_y * lanes
 
-    packed = call(
+    edge = f32(3, depth, width)
+    packed, first, last = call(
         pack_kernel,
-        cells,
+        [cells, edge, edge],
         [hbm] * 3,
         (theta, phi, labels),
         scratch=(
@@ -587,30 +544,17 @@
         flops=48 * 2 * rows * lanes * 2 * whole_y,
         name="tensor",
     )
-    edge_rows = 3 * depth * width // lanes
-    far = count_y // 2
-    chunk_shapes = [f32(lines + (edge_rows if n in meeting(count_y) else 0), lanes) for n in order_y]
-    *far_chunks, both = call(
-        functools.partial(lines_kernel, count_x, order_y, far),
-        chunk_shapes[:far] + [jax.ShapeDtypeStruct((count_x, 2 * lines, width), jnp.bfloat16)],
-        [vmem] * count_x + [hbm, smem, vmem],
-        (*gathered, ms_region, place, table),
+    gathered, tensor = lax.optimization_barrier((gathered, tensor))
+    spectrum = call(
+        functools.partial(lines_kernel, count_x),
+        [f32(lines, lanes)] * count_y,
+        [vmem] * count_x + [hbm, vmem],
+        (*gathered, ms_region, table),
         scratch=(pltpu.SMEM(ms_region.shape, jnp.float32), pltpu.SemaphoreType.DMA),
-        flops=transform_flops // 2,
-        name="far_lines",
-    )
-    far_columns = exchanged(far_chunks, "gy", order_y[:far])
-    both = after(both, far_columns[0])
-    near_chunks = call(
-        functools.partial(near_lines_kernel, order_y, far),
-        chunk_shapes[far:],
-        [vmem, vmem, smem, vmem],
-        (both, gathered[0], place, table),
-        flops=transform_flops // 2,
-        name="near_lines",
-    )
-    columns = [*far_columns, *exchanged(near_chunks, "gy", order_y[far:])]
-    columns = lax.optimization_barrier(columns)
+        flops=transform_flops,
+        name="lines",
+    )
+    columns = exchanged(spectrum, "gy", order_y)
     scale = -1.0 / (2 * depth * 2 * whole_y * 2 * count_x * width)
     waves = call(
         functools.partial(waves_kernel, scale, count_y),
@@ -639,18 +583,20 @@
         )
         for number, block in zip(numbers, blocks):
             partial[number] = block
-    edges = [columns[order_y.index(number)] for number in meeting(count_y)]
-    edges, partial[0] = lax.optimization_barrier((edges, partial[0]))
+    parts, far_sum = gathered_sums(partial, "gx")
+    first, last = after((first, last), far_sum)
+    up = [(i, i + 1) for i in range(count_y - 1)]
+    row_before = lax.ppermute(last, "gy", up)
+    row_after = lax.ppermute(first, "gy", [(j, i) for i, j in up])
     exchange, unit = call(
         functools.partial(exchange_kernel, order_x, count_y),
         [cells, cells],
-        [vmem] * (count_x + len(edges)) + [smem] * 3,
-        (*gathered, *edges, place, ms_region, aex_region),
+        [vmem] * (count_x + 2) + [smem] * 3,
+        (*gathered, row_before, row_after, place, ms_region, aex_region),
         scratch=(pltpu.VMEM((count_x, 3, depth, height, width), jnp.float32),),
         flops=300 * depth * height * width,
         name="exchange",
     )
-    parts = gathered_sums(partial, "gx")
     field, predicted = call(
         functools.partial(final_kernel, len(parts)),
         [cells, cells],

time: 56.5 us -> 57.8 us (1.023)
  starting transfers between devices: 28.5 us -> 32.4 us
  waiting for transfers between devices: 11.9 us -> 10.4 us
  Pallas kernels: 15 us -> 13.8 us
    ppermute x20, waiting for transfers between devices: 11.9 us -> 6.14 us  [swapped(): return lax.ppermute(chunk, axis, [(i, i ^ number) for i in range(devices)])]
    ppermute x0 -> x2, starting transfers between devices: none -> 4.48 us  [the longest x1 3.18 us: per_device(): row_before = lax.ppermute(last, 'gy', up)]
    ppermute x0 -> x2, waiting for transfers between devices: none -> 4.29 us  [the longest x1 4.2 us: per_device(): row_after = lax.ppermute(first, 'gy', [(j, i) for i, j in up])]
    pallas_call x10 -> x9, Pallas kernels: 15 us -> 13.8 us  [call(): pl.pallas_call(body, out_shape=out, in_specs=ins, out_specs=[vmem] * len(...]
  transfers between devices with their start and end apart: 20 -> 22, of which waited for: 7 -> 10; matrix products, arithmetic and copies ran while one was open for 0% -> 0% of each run, Pallas kernels for 14% -> 12%
where the time goes in v7:
time: 57.8 us; the launch traced here: 57.5 us
  starting transfers between devices  32.4 us (56%)
  Pallas kernels  13.8 us (24%)
  waiting for transfers between devices  10.4 us (18%)
  between operations  0.79 us (1%)
    ppermute x20, starting transfers between devices, swapped(): return lax.ppermute(chunk, axis, [(i, i ^ number) for i in range(devices)])  27.9 us
    pallas_call x9, Pallas kernels, call(): pl.pallas_call(body, out_shape=out, in_specs=ins, out_specs=[vmem] * len(...  13.8 us
    ppermute x20, waiting for transfers between devices, swapped(): return lax.ppermute(chunk, axis, [(i, i ^ number) for i in range(devices)])  6.14 us
    ppermute x1, waiting for transfers between devices, per_device(): row_after = lax.ppermute(first, 'gy', [(j, i) for i, j in up])  4.2 us
    ppermute x1, starting transfers between devices, per_device(): row_before = lax.ppermute(last, 'gy', up)  3.18 us
    ppermute x1, starting transfers between devices, per_device(): row_after = lax.ppermute(first, 'gy', [(j, i) for i, j in up])  1.29 us
  transfers between devices with their start and end apart: 22, of which 10 were waited for; matrix products, arithmetic and copies ran while one was open for 0% of the time, Pallas kernels for 12%

profile of v7, /device:TPU:0, one launch (start us, length us, event | category | flops | bytes accessed | tf_op | source)
XLA Modules:
  0.0 57.5 jit_solution(4906190809213264422)
XLA Ops:
  0.6 0.8 %pack.1 = (f32[3,4,8,256]{3,2,1,0:T(8,128)S(1)}, f32[3,4,256]{2,1,0:T(4,128)S(1)}, f32[3,4,256]{2,1,0:T(4,128)S(1)}) custom-call(f32[4,8,256]{2,1,0:T(8,128)} %theta_ref.1, f32[4,8,256]{2,1,0:T(8,128)} %phi_ref.1, s32[4,8,256]{2,1,0:T(8,128)} %labels_ref.1), custom_call_target="tpu_custom_call" | custom-call | bytes 221184 | tf_op jit(solution)/shard_map/pack/pallas_call | solution.py:436
  1.5 3.0 %collective-permute-start.1 = (f32[3,4,8,256]{3,2,1,0:T(8,128)S(1)}, f32[3,4,8,256]{3,2,1,0:T(8,128)S(1)}, u32[]{:S(2)}, u32[]{:S(2)}) collective-permute-start(f32[3,4,8,256]{3,2,1,0:T(8,128)S(1)} %get-tuple-element.42.refs_0_), channel_id=1, source_target_pairs={{0,16},{8,24},{16,0},{24,8},{1,17},{9,25},{17,1},{25,9},{2,18},{10... | collective-permute-start | bytes 294920 | tf_op jit(solution)/shard_map/ppermute | solution.py:454
  4.6 3.2 %load.1 = (bf16[2,4,256,1024]{3,2,1,0:T(8,128)(2,1)S(1)}, bf16[128,384]{1,0:T(8,128)(2,1)S(1)}, bf16[128,384]{1,0:T(8,128)(2,1)S(1)}) custom-call(s32[2]{0:T(128)S(1)} %pad_add_fusion.place.refs_6_, bf16[4,8,2,4,256,128]{5,4,3,2,1,0:T(8,128)(2,1)} %constant.16.clone.refs_0_, bf16[8,128,384]{2,1,0:T(8,128)(2,1)} %constant.17.clone.refs_1_, ...), custom_call_target="tpu_custom_call" | custom-call | bytes 22741000 | tf_op jit(solution)/shard_map/load/pallas_call | solution.py:436
  7.8 0.6 collective-permute-start.2
  8.3 1.6 %tensor.1.refs_8_ = bf16[48,128,128]{2,1,0:T(8,128)(2,1)S(1)} custom-call(bf16[48,64,128]{2,1,0:T(8,128)(2,1)S(1)} %bitcast.3, bf16[64,128]{1,0:T(8,128)(2,1)S(1)} %copy-done.1), custom_call_target="tpu_custom_call" | custom-call | flops 100663296 | bytes 2375680 | tf_op jit(solution)/shard_map/tensor/pallas_call | solution.py:436
  9.9 1.6 %lines.1 = (f32[96,128]{1,0:T(8,128)S(1)}, f32[96,128]{1,0:T(8,128)S(1)}, f32[96,128]{1,0:T(8,128)S(1)}, f32[96,128]{1,0:T(8,128)S(1)}, f32[96,128]{1,0:T(8,128)...) custom-call(f32[3,4,8,256]{3,2,1,0:T(8,128)S(1)} %get-tuple-element.42.refs_0_, ...), custom_call_target="tpu_custom_call" | custom-call | flops 603979776 | bytes 4980800 | tf_op jit(solution)/shard_map/lines/pallas_call | solution.py:436
  11.5 4.6 %collective-permute-start.3 = (f32[96,128]{1,0:T(8,128)S(1)}, f32[96,128]{1,0:T(8,128)S(1)}, u32[]{:S(2)}, u32[]{:S(2)}) collective-permute-start(f32[96,128]{1,0:T(8,128)S(1)} %get-tuple-element.47), channel_id=1, source_target_pairs={{0,7},{1,6},{2,5},{3,4},{4,3},{5,2},{6,1},{7,0},{8,15},{9,14},{10,... | collective-permute-start | bytes 147464 | tf_op jit(solution)/shard_map/ppermute | solution.py:454
  16.4 0.7 %collective-permute-start.5 = (f32[96,128]{1,0:T(8,128)S(1)}, f32[96,128]{1,0:T(8,128)S(1)}, u32[]{:S(2)}, u32[]{:S(2)}) collective-permute-start(f32[96,128]{1,0:T(8,128)S(1)} %get-tuple-element.49), channel_id=1, source_target_pairs={{0,5},{1,4},{2,7},{3,6},{4,1},{5,0},{6,3},{7,2},{8,13},{9,12},{10,... | collective-permute-start | bytes 147464 | tf_op jit(solution)/shard_map/ppermute | solution.py:454
  17.1 2.1 %collective-permute-start.6 = (f32[96,128]{1,0:T(8,128)S(1)}, f32[96,128]{1,0:T(8,128)S(1)}, u32[]{:S(2)}, u32[]{:S(2)}) collective-permute-start(f32[96,128]{1,0:T(8,128)S(1)} %get-tuple-element.50), channel_id=1, source_target_pairs={{0,4},{1,5},{2,6},{3,7},{4,0},{5,1},{6,2},{7,3},{8,12},{9,13},{10,... | collective-permute-start | bytes 147464 | tf_op jit(solution)/shard_map/ppermute | solution.py:454
  19.3 2.2 %collective-permute-start.7 = (f32[96,128]{1,0:T(8,128)S(1)}, f32[96,128]{1,0:T(8,128)S(1)}, u32[]{:S(2)}, u32[]{:S(2)}) collective-permute-start(f32[96,128]{1,0:T(8,128)S(1)} %get-tuple-element.51), channel_id=1, source_target_pairs={{0,3},{1,2},{2,1},{3,0},{4,7},{5,6},{6,5},{7,4},{8,11},{9,10},{10,... | collective-permute-start | bytes 147464 | tf_op jit(solution)/shard_map/ppermute | solution.py:454
  21.4 0.8 %collective-permute-start.8 = (f32[96,128]{1,0:T(8,128)S(1)}, f32[96,128]{1,0:T(8,128)S(1)}, u32[]{:S(2)}, u32[]{:S(2)}) collective-permute-start(f32[96,128]{1,0:T(8,128)S(1)} %get-tuple-element.52), channel_id=1, source_target_pairs={{0,2},{1,3},{2,0},{3,1},{4,6},{5,7},{6,4},{7,5},{8,10},{9,11},{10,... | collective-permute-start | bytes 147464 | tf_op jit(solution)/shard_map/ppermute | solution.py:454
  22.8 0.9 %collective-permute-done.5.refs_2_ = f32[96,128]{1,0:T(8,128)S(1)} collective-permute-done((f32[96,128]{1,0:T(8,128)S(1)}, f32[96,128]{1,0:T(8,128)S(1)}, u32[]{:S(2)}, u32[]{:S(2)}) %collective-permute-start.5) | collective-permute-done | bytes 49184 | tf_op jit(solution)/shard_map/ppermute | solution.py:454
  23.6 0.8 %collective-permute-done.6.refs_3_ = f32[96,128]{1,0:T(8,128)S(1)} collective-permute-done((f32[96,128]{1,0:T(8,128)S(1)}, f32[96,128]{1,0:T(8,128)S(1)}, u32[]{:S(2)}, u32[]{:S(2)}) %collective-permute-start.6) | collective-permute-done | bytes 49184 | tf_op jit(solution)/shard_map/ppermute | solution.py:454
  24.5 1.1 %collective-permute-done.7.refs_4_ = f32[96,128]{1,0:T(8,128)S(1)} collective-permute-done((f32[96,128]{1,0:T(8,128)S(1)}, f32[96,128]{1,0:T(8,128)S(1)}, u32[]{:S(2)}, u32[]{:S(2)}) %collective-permute-start.7) | collective-permute-done | bytes 49184 | tf_op jit(solution)/shard_map/ppermute | solution.py:454
  25.8 0.6 %collective-permute-done.9.refs_6_ = f32[96,128]{1,0:T(8,128)S(1)} collective-permute-done((f32[96,128]{1,0:T(8,128)S(1)}, f32[96,128]{1,0:T(8,128)S(1)}, u32[]{:S(2)}, u32[]{:S(2)}) %collective-permute-start.9) | collective-permute-done | bytes 49184 | tf_op jit(solution)/shard_map/ppermute | solution.py:454
  26.3 3.1 %waves.1 = (f32[96,128]{1,0:T(8,128)S(1)}, f32[96,128]{1,0:T(8,128)S(1)}, f32[96,128]{1,0:T(8,128)S(1)}, f32[96,128]{1,0:T(8,128)S(1)}, f32[96,128]{1,0:T(8,128)...) custom-call(f32[96,128]{1,0:T(8,128)S(1)} %collective-permute-done.3.refs_0_, ...), custom_call_target="tpu_custom_call" | custom-call | flops 125829120 | bytes 2555904 | tf_op jit(solution)/shard_map/waves/pallas_call | solution.py:436
  29.5 3.6 %collective-permute-start.10 = (f32[96,128]{1,0:T(8,128)S(1)}, f32[96,128]{1,0:T(8,128)S(1)}, u32[]{:S(2)}, u32[]{:S(2)}) collective-permute-start(f32[96,128]{1,0:T(8,128)S(1)} %get-tuple-element.58), channel_id=1, source_target_pairs={{0,7},{1,6},{2,5},{3,4},{4,3},{5,2},{6,1},{7,0},{8,15},{9,14},{10,... | collective-permute-start | bytes 147464 | tf_op jit(solution)/shard_map/ppermute | solution.py:454
  33.7 1.0 %collective-permute-start.12 = (f32[96,128]{1,0:T(8,128)S(1)}, f32[96,128]{1,0:T(8,128)S(1)}, u32[]{:S(2)}, u32[]{:S(2)}) collective-permute-start(f32[96,128]{1,0:T(8,128)S(1)} %get-tuple-element.60), channel_id=1, source_target_pairs={{0,5},{1,4},{2,7},{3,6},{4,1},{5,0},{6,3},{7,2},{8,13},{9,12},{10,... | collective-permute-start | bytes 147464 | tf_op jit(solution)/shard_map/ppermute | solution.py:454
  34.7 2.5 %collective-permute-start.13 = (f32[96,128]{1,0:T(8,128)S(1)}, f32[96,128]{1,0:T(8,128)S(1)}, u32[]{:S(2)}, u32[]{:S(2)}) collective-permute-start(f32[96,128]{1,0:T(8,128)S(1)} %get-tuple-element.61), channel_id=1, source_target_pairs={{0,4},{1,5},{2,6},{3,7},{4,0},{5,1},{6,2},{7,3},{8,12},{9,13},{10,... | collective-permute-start | bytes 147464 | tf_op jit(solution)/shard_map/ppermute | solution.py:454
  37.2 1.2 %collective-permute-start.14 = (f32[96,128]{1,0:T(8,128)S(1)}, f32[96,128]{1,0:T(8,128)S(1)}, u32[]{:S(2)}, u32[]{:S(2)}) collective-permute-start(f32[96,128]{1,0:T(8,128)S(1)} %get-tuple-element.62), channel_id=1, source_target_pairs={{0,3},{1,2},{2,1},{3,0},{4,7},{5,6},{6,5},{7,4},{8,11},{9,10},{10,... | collective-permute-start | bytes 147464 | tf_op jit(solution)/shard_map/ppermute | solution.py:454
  38.4 1.1 %collective-permute-start.15 = (f32[96,128]{1,0:T(8,128)S(1)}, f32[96,128]{1,0:T(8,128)S(1)}, u32[]{:S(2)}, u32[]{:S(2)}) collective-permute-start(f32[96,128]{1,0:T(8,128)S(1)} %get-tuple-element.63), channel_id=1, source_target_pairs={{0,2},{1,3},{2,0},{3,1},{4,6},{5,7},{6,4},{7,5},{8,10},{9,11},{10,... | collective-permute-start | bytes 147464 | tf_op jit(solution)/shard_map/ppermute | solution.py:454
  39.5 1.6 %collective-permute-start.16 = (f32[96,128]{1,0:T(8,128)S(1)}, f32[96,128]{1,0:T(8,128)S(1)}, u32[]{:S(2)}, u32[]{:S(2)}) collective-permute-start(f32[96,128]{1,0:T(8,128)S(1)} %get-tuple-element.64), channel_id=1, source_target_pairs={{0,1},{1,0},{2,3},{3,2},{4,5},{5,4},{6,7},{7,6},{8,9},{9,8},{10,11... | collective-permute-start | bytes 147464 | tf_op jit(solution)/shard_map/ppermute | solution.py:454
  41.1 1.1 %collective-permute-done.14.refs_4_ = f32[96,128]{1,0:T(8,128)S(1)} collective-permute-done((f32[96,128]{1,0:T(8,128)S(1)}, f32[96,128]{1,0:T(8,128)S(1)}, u32[]{:S(2)}, u32[]{:S(2)}) %collective-permute-start.14) | collective-permute-done | bytes 49184 | tf_op jit(solution)/shard_map/ppermute | solution.py:454
  42.5 1.1 %collective-permute-done.16.refs_6_ = f32[96,128]{1,0:T(8,128)S(1)} collective-permute-done((f32[96,128]{1,0:T(8,128)S(1)}, f32[96,128]{1,0:T(8,128)S(1)}, u32[]{:S(2)}, u32[]{:S(2)}) %collective-permute-start.16) | collective-permute-done | bytes 49184 | tf_op jit(solution)/shard_map/ppermute | solution.py:454
  43.6 0.8 %back_across.1 = (f32[96,256]{1,0:T(8,128)S(1)}, f32[96,256]{1,0:T(8,128)S(1)}) custom-call(f32[96,128]{1,0:T(8,128)S(1)} %collective-permute-done.10.refs_0_, f32[96,128]{1,0:T(8,128)S(1)} %collective-permute-done.11.refs_1_, f32[96,128]{1,0:T(8,128)S(1)} %collective-permute-done.12.refs_2_, f32[96,128]{1,0:T(8,128)S(1)} %collective-permute-done.13.refs_3_, ...), custom_call_target="tpu_custom_call" | custom-call | flops 301989888 | bytes 4784128 | tf_op jit(solution)/shard_map/back_across/pallas_call | solution.py:436
  45.0 0.8 %back_within.1 = (f32[96,256]{1,0:T(8,128)S(1)}, f32[96,256]{1,0:T(8,128)S(1)}) custom-call(f32[96,128]{1,0:T(8,128)S(1)} %collective-permute-done.10.refs_0_, f32[96,128]{1,0:T(8,128)S(1)} %collective-permute-done.11.refs_1_, f32[96,128]{1,0:T(8,128)S(1)} %collective-permute-done.12.refs_2_, f32[96,128]{1,0:T(8,128)S(1)} %collective-permute-done.13.refs_3_, ...), custom_call_target="tpu_custom_call" | custom-call | flops 301989888 | bytes 4784128 | tf_op jit(solution)/shard_map/back_within/pallas_call | solution.py:436
  45.8 1.0 %collective-permute-start.19 = (f32[96,256]{1,0:T(8,128)S(1)}, f32[96,256]{1,0:T(8,128)S(1)}, u32[]{:S(2)}, u32[]{:S(2)}) collective-permute-start(f32[96,256]{1,0:T(8,128)S(1)} %add.3), channel_id=1, source_target_pairs={{0,16},{8,24},{16,0},{24,8},{1,17},{9,25},{17,1},{25,9},{2,18},{10... | collective-permute-start | bytes 294920 | tf_op jit(solution)/shard_map/ppermute | solution.py:454
  46.8 3.2 %collective-permute-start.20 = (f32[3,4,256]{2,1,0:T(4,128)S(1)}, f32[3,4,256]{2,1,0:T(4,128)S(1)}, u32[]{:S(2)}, u32[]{:S(2)}) collective-permute-start(f32[3,4,256]{2,1,0:T(4,128)S(1)} %get-tuple-element.72), channel_id=1, source_target_pairs={{0,1},{1,2},{2,3},{3,4},{4,5},{5,6},{6,7},{8,9},{9,10},{10,11},{11... | collective-permute-start | bytes 36872 | tf_op jit(solution)/shard_map/ppermute | solution.py:589
  50.0 1.3 %collective-permute-start.21 = (f32[3,4,256]{2,1,0:T(4,128)S(1)}, f32[3,4,256]{2,1,0:T(4,128)S(1)}, u32[]{:S(2)}, u32[]{:S(2)}) collective-permute-start(f32[3,4,256]{2,1,0:T(4,128)S(1)} %get-tuple-element.73), channel_id=1, source_target_pairs={{1,0},{2,1},{3,2},{4,3},{5,4},{6,5},{7,6},{9,8},{10,9},{11,10},{12... | collective-permute-start | bytes 36872 | tf_op jit(solution)/shard_map/ppermute | solution.py:590
  51.4 4.2 %collective-permute-done.21.refs_5_ = f32[3,4,256]{2,1,0:T(4,128)S(1)} collective-permute-done((f32[3,4,256]{2,1,0:T(4,128)S(1)}, f32[3,4,256]{2,1,0:T(4,128)S(1)}, u32[]{:S(2)}, u32[]{:S(2)}) %collective-permute-start.21) | collective-permute-done | bytes 12320 | tf_op jit(solution)/shard_map/ppermute | solution.py:590
  55.6 1.1 %exchange.1 = (f32[3,4,8,256]{3,2,1,0:T(8,128)S(1)}, f32[3,4,8,256]{3,2,1,0:T(8,128)S(1)}) custom-call(f32[3,4,8,256]{3,2,1,0:T(8,128)S(1)} %get-tuple-element.42.refs_0_, f32[3,4,8,256]{3,2,1,0:T(8,128)S(1)} %collective-permute-done.refs_1_, f32[3,4,8,256]{3,2,1,0:T(8,128)S(1)} %collective-permute-done.1.refs_2_, ...), custom_call_target="tpu_custom_call" | custom-call | flops 2457600 | bytes 614536 | tf_op jit(solution)/shard_map/exchange/pallas_call | solution.py:436
  56.8 0.7 %predict.1 = (f32[3,4,8,256]{3,2,1,0:T(8,128)}, f32[3,4,8,256]{3,2,1,0:T(8,128)}) custom-call(f32[96,256]{1,0:T(8,128)S(1)} %get-tuple-element.66.refs_0_, f32[96,256]{1,0:T(8,128)S(1)} %collective-permute-done.17.refs_1_, f32[96,256]{1,0:T(8,128)S(1)} %collective-permute-done.19.refs_2_, f32[3,4,8,256]{3,2,1,0:T(8,128)S(1)} %get-tuple-element.74.refs_3_, ...), custom_call_target="tpu_custom_call" | custom-call | flops 491520 | bytes 688128 | tf_op jit(solution)/shard_map/predict/pallas_call | solution.py:436
  (31 shorter events, 2.7 us)
Async XLA Ops:
  1.5 6.3 %collective-permute-start.1 = (f32[3,4,8,256]{3,2,1,0:T(8,128)S(1)}, f32[3,4,8,256]{3,2,1,0:T(8,128)S(1)}, u32[]{:S(2)}, u32[]{:S(2)}) collective-permute-start(f32[3,4,8,256]{3,2,1,0:T(8,128)S(1)} %get-tuple-element.42.refs_0_), channel_id=1, source_target_pairs={{0,16},{8,24},{16,0},{24,8},{1,17},{9,25},{17,1},{25,9},{2,18},{10... | collective-permute-start | bytes 294920 | tf_op jit(solution)/shard_map/ppermute | solution.py:454
  4.5 5.5 %collective-permute-start = (f32[3,4,8,256]{3,2,1,0:T(8,128)S(1)}, f32[3,4,8,256]{3,2,1,0:T(8,128)S(1)}, u32[]{:S(2)}, u32[]{:S(2)}) collective-permute-start(f32[3,4,8,256]{3,2,1,0:T(8,128)S(1)} %get-tuple-element.42.refs_0_), channel_id=1, source_target_pairs={{0,8},{8,0},{16,24},{24,16},{1,9},{9,1},{17,25},{25,17},{2,10},{10... | collective-permute-start | bytes 294920 | tf_op jit(solution)/shard_map/ppermute | solution.py:454
  4.6 3.8 %copy-start = (bf16[6,8,64,128]{3,2,1,0:T(8,128)(2,1)S(1)}, bf16[6,8,64,128]{3,2,1,0:T(8,128)(2,1)}, u32[]{:S(2)}) copy-start(bf16[6,8,64,128]{3,2,1,0:T(8,128)(2,1)} %param.15) | copy-start | bytes 2359300
  4.6 3.8 %copy-start.1 = (bf16[64,128]{1,0:T(8,128)(2,1)S(1)}, bf16[64,128]{1,0:T(8,128)(2,1)}, u32[]{:S(2)}) copy-start(bf16[64,128]{1,0:T(8,128)(2,1)} %constant.19.clone.twice_ref) | copy-start | bytes 49156
  7.8 2.2 %collective-permute-start.2 = (f32[3,4,8,256]{3,2,1,0:T(8,128)S(1)}, f32[3,4,8,256]{3,2,1,0:T(8,128)S(1)}, u32[]{:S(2)}, u32[]{:S(2)}) collective-permute-start(f32[3,4,8,256]{3,2,1,0:T(8,128)S(1)} %collective-permute-done.1.refs_2_), channel_id=1, source_target_pairs={{0,8},{8,0},{16,24},{24,16},{1,9},{9,1},{17,25},{25,17},{2,10},{10... | collective-permute-start | bytes 294920 | tf_op jit(solution)/shard_map/ppermute | solution.py:454
  11.5 9.9 %collective-permute-start.3 = (f32[96,128]{1,0:T(8,128)S(1)}, f32[96,128]{1,0:T(8,128)S(1)}, u32[]{:S(2)}, u32[]{:S(2)}) collective-permute-start(f32[96,128]{1,0:T(8,128)S(1)} %get-tuple-element.47), channel_id=1, source_target_pairs={{0,7},{1,6},{2,5},{3,4},{4,3},{5,2},{6,1},{7,0},{8,15},{9,14},{10,... | collective-permute-start | bytes 147464 | tf_op jit(solution)/shard_map/ppermute | solution.py:454
  16.2 6.1 %collective-permute-start.4 = (f32[96,128]{1,0:T(8,128)S(1)}, f32[96,128]{1,0:T(8,128)S(1)}, u32[]{:S(2)}, u32[]{:S(2)}) collective-permute-start(f32[96,128]{1,0:T(8,128)S(1)} %get-tuple-element.48), channel_id=1, source_target_pairs={{0,6},{1,7},{2,4},{3,5},{4,2},{5,3},{6,0},{7,1},{8,14},{9,15},{10,... | collective-permute-start | bytes 147464 | tf_op jit(solution)/shard_map/ppermute | solution.py:454
  16.4 7.3 %collective-permute-start.5 = (f32[96,128]{1,0:T(8,128)S(1)}, f32[96,128]{1,0:T(8,128)S(1)}, u32[]{:S(2)}, u32[]{:S(2)}) collective-permute-start(f32[96,128]{1,0:T(8,128)S(1)} %get-tuple-element.49), channel_id=1, source_target_pairs={{0,5},{1,4},{2,7},{3,6},{4,1},{5,0},{6,3},{7,2},{8,13},{9,12},{10,... | collective-permute-start | bytes 147464 | tf_op jit(solution)/shard_map/ppermute | solution.py:454
  17.1 7.3 %collective-permute-start.6 = (f32[96,128]{1,0:T(8,128)S(1)}, f32[96,128]{1,0:T(8,128)S(1)}, u32[]{:S(2)}, u32[]{:S(2)}) collective-permute-start(f32[96,128]{1,0:T(8,128)S(1)} %get-tuple-element.50), channel_id=1, source_target_pairs={{0,4},{1,5},{2,6},{3,7},{4,0},{5,1},{6,2},{7,3},{8,12},{9,13},{10,... | collective-permute-start | bytes 147464 | tf_op jit(solution)/shard_map/ppermute | solution.py:454
  19.3 6.3 %collective-permute-start.7 = (f32[96,128]{1,0:T(8,128)S(1)}, f32[96,128]{1,0:T(8,128)S(1)}, u32[]{:S(2)}, u32[]{:S(2)}) collective-permute-start(f32[96,128]{1,0:T(8,128)S(1)} %get-tuple-element.51), channel_id=1, source_target_pairs={{0,3},{1,2},{2,1},{3,0},{4,7},{5,6},{6,5},{7,4},{8,11},{9,10},{10,... | collective-permute-start | bytes 147464 | tf_op jit(solution)/shard_map/ppermute | solution.py:454
  21.4 4.3 %collective-permute-start.8 = (f32[96,128]{1,0:T(8,128)S(1)}, f32[96,128]{1,0:T(8,128)S(1)}, u32[]{:S(2)}, u32[]{:S(2)}) collective-permute-start(f32[96,128]{1,0:T(8,128)S(1)} %get-tuple-element.52), channel_id=1, source_target_pairs={{0,2},{1,3},{2,0},{3,1},{4,6},{5,7},{6,4},{7,5},{8,10},{9,11},{10,... | collective-permute-start | bytes 147464 | tf_op jit(solution)/shard_map/ppermute | solution.py:454
  22.2 4.1 %collective-permute-start.9 = (f32[96,128]{1,0:T(8,128)S(1)}, f32[96,128]{1,0:T(8,128)S(1)}, u32[]{:S(2)}, u32[]{:S(2)}) collective-permute-start(f32[96,128]{1,0:T(8,128)S(1)} %get-tuple-element.53), channel_id=1, source_target_pairs={{0,1},{1,0},{2,3},{3,2},{4,5},{5,4},{6,7},{7,6},{8,9},{9,8},{10,11... | collective-permute-start | bytes 147464 | tf_op jit(solution)/shard_map/ppermute | solution.py:454
  29.5 8.9 %collective-permute-start.10 = (f32[96,128]{1,0:T(8,128)S(1)}, f32[96,128]{1,0:T(8,128)S(1)}, u32[]{:S(2)}, u32[]{:S(2)}) collective-permute-start(f32[96,128]{1,0:T(8,128)S(1)} %get-tuple-element.58), channel_id=1, source_target_pairs={{0,7},{1,6},{2,5},{3,4},{4,3},{5,2},{6,1},{7,0},{8,15},{9,14},{10,... | collective-permute-start | bytes 147464 | tf_op jit(solution)/shard_map/ppermute | solution.py:454
  33.1 6.4 %collective-permute-start.11 = (f32[96,128]{1,0:T(8,128)S(1)}, f32[96,128]{1,0:T(8,128)S(1)}, u32[]{:S(2)}, u32[]{:S(2)}) collective-permute-start(f32[96,128]{1,0:T(8,128)S(1)} %get-tuple-element.59), channel_id=1, source_target_pairs={{0,6},{1,7},{2,4},{3,5},{4,2},{5,3},{6,0},{7,1},{8,14},{9,15},{10,... | collective-permute-start | bytes 147464 | tf_op jit(solution)/shard_map/ppermute | solution.py:454
  33.7 7.4 %collective-permute-start.12 = (f32[96,128]{1,0:T(8,128)S(1)}, f32[96,128]{1,0:T(8,128)S(1)}, u32[]{:S(2)}, u32[]{:S(2)}) collective-permute-start(f32[96,128]{1,0:T(8,128)S(1)} %get-tuple-element.60), channel_id=1, source_target_pairs={{0,5},{1,4},{2,7},{3,6},{4,1},{5,0},{6,3},{7,2},{8,13},{9,12},{10,... | collective-permute-start | bytes 147464 | tf_op jit(solution)/shard_map/ppermute | solution.py:454
  34.7 6.4 %collective-permute-start.13 = (f32[96,128]{1,0:T(8,128)S(1)}, f32[96,128]{1,0:T(8,128)S(1)}, u32[]{:S(2)}, u32[]{:S(2)}) collective-permute-start(f32[96,128]{1,0:T(8,128)S(1)} %get-tuple-element.61), channel_id=1, source_target_pairs={{0,4},{1,5},{2,6},{3,7},{4,0},{5,1},{6,2},{7,3},{8,12},{9,13},{10,... | collective-permute-start | bytes 147464 | tf_op jit(solution)/shard_map/ppermute | solution.py:454
  37.2 5.0 %collective-permute-start.14 = (f32[96,128]{1,0:T(8,128)S(1)}, f32[96,128]{1,0:T(8,128)S(1)}, u32[]{:S(2)}, u32[]{:S(2)}) collective-permute-start(f32[96,128]{1,0:T(8,128)S(1)} %get-tuple-element.62), channel_id=1, source_target_pairs={{0,3},{1,2},{2,1},{3,0},{4,7},{5,6},{6,5},{7,4},{8,11},{9,10},{10,... | collective-permute-start | bytes 147464 | tf_op jit(solution)/shard_map/ppermute | solution.py:454
  38.4 4.1 %collective-permute-start.15 = (f32[96,128]{1,0:T(8,128)S(1)}, f32[96,128]{1,0:T(8,128)S(1)}, u32[]{:S(2)}, u32[]{:S(2)}) collective-permute-start(f32[96,128]{1,0:T(8,128)S(1)} %get-tuple-element.63), channel_id=1, source_target_pairs={{0,2},{1,3},{2,0},{3,1},{4,6},{5,7},{6,4},{7,5},{8,10},{9,11},{10,... | collective-permute-start | bytes 147464 | tf_op jit(solution)/shard_map/ppermute | solution.py:454
  39.5 4.1 %collective-permute-start.16 = (f32[96,128]{1,0:T(8,128)S(1)}, f32[96,128]{1,0:T(8,128)S(1)}, u32[]{:S(2)}, u32[]{:S(2)}) collective-permute-start(f32[96,128]{1,0:T(8,128)S(1)} %get-tuple-element.64), channel_id=1, source_target_pairs={{0,1},{1,0},{2,3},{3,2},{4,5},{5,4},{6,7},{7,6},{8,9},{9,8},{10,11... | collective-permute-start | bytes 147464 | tf_op jit(solution)/shard_map/ppermute | solution.py:454
  43.6 12.0 %copy-start.2 = (f32[16]{0:T(128)S(1)}, f32[16]{0:T(128)}, u32[]{:S(2)}) copy-start(f32[16]{0:T(128)} %refs_7_.1) | copy-start | bytes 196
  43.6 12.0 %copy-start.3 = (f32[16]{0:T(128)S(1)}, f32[16]{0:T(128)}, u32[]{:S(2)}) copy-start(f32[16]{0:T(128)} %refs_8_.1) | copy-start | bytes 196
  44.4 1.4 %collective-permute-start.18 = (f32[96,256]{1,0:T(8,128)S(1)}, f32[96,256]{1,0:T(8,128)S(1)}, u32[]{:S(2)}, u32[]{:S(2)}) collective-permute-start(f32[96,256]{1,0:T(8,128)S(1)} %get-tuple-element.69), channel_id=1, source_target_pairs={{0,8},{8,0},{16,24},{24,16},{1,9},{9,1},{17,25},{25,17},{2,10},{10... | collective-permute-start | bytes 294920 | tf_op jit(solution)/shard_map/ppermute | solution.py:454
  44.5 12.3 %collective-permute-start.17 = (f32[96,256]{1,0:T(8,128)S(1)}, f32[96,256]{1,0:T(8,128)S(1)}, u32[]{:S(2)}, u32[]{:S(2)}) collective-permute-start(f32[96,256]{1,0:T(8,128)S(1)} %get-tuple-element.67), channel_id=1, source_target_pairs={{0,8},{8,0},{16,24},{24,16},{1,9},{9,1},{17,25},{25,17},{2,10},{10... | collective-permute-start | bytes 294920 | tf_op jit(solution)/shard_map/ppermute | solution.py:454
  45.8 11.0 %collective-permute-start.19 = (f32[96,256]{1,0:T(8,128)S(1)}, f32[96,256]{1,0:T(8,128)S(1)}, u32[]{:S(2)}, u32[]{:S(2)}) collective-permute-start(f32[96,256]{1,0:T(8,128)S(1)} %add.3), channel_id=1, source_target_pairs={{0,16},{8,24},{16,0},{24,8},{1,17},{9,25},{17,1},{25,9},{2,18},{10... | collective-permute-start | bytes 294920 | tf_op jit(solution)/shard_map/ppermute | solution.py:454
  46.8 4.6 %collective-permute-start.20 = (f32[3,4,256]{2,1,0:T(4,128)S(1)}, f32[3,4,256]{2,1,0:T(4,128)S(1)}, u32[]{:S(2)}, u32[]{:S(2)}) collective-permute-start(f32[3,4,256]{2,1,0:T(4,128)S(1)} %get-tuple-element.72), channel_id=1, source_target_pairs={{0,1},{1,2},{2,3},{3,4},{4,5},{5,6},{6,7},{8,9},{9,10},{10,11},{11... | collective-permute-start | bytes 36872 | tf_op jit(solution)/shard_map/ppermute | solution.py:589
  50.0 5.6 %collective-permute-start.21 = (f32[3,4,256]{2,1,0:T(4,128)S(1)}, f32[3,4,256]{2,1,0:T(4,128)S(1)}, u32[]{:S(2)}, u32[]{:S(2)}) collective-permute-start(f32[3,4,256]{2,1,0:T(4,128)S(1)} %get-tuple-element.73), channel_id=1, source_target_pairs={{1,0},{2,1},{3,2},{4,3},{5,4},{6,5},{7,6},{9,8},{10,9},{11,10},{12... | collective-permute-start | bytes 36872 | tf_op jit(solution)/shard_map/ppermute | solution.py:590

commit v8 on v7

--- a/solution.py
+++ b/solution.py
@@ -329,12 +329,24 @@
             ]
 
 
+def meeting(devices):
+    return [number for number in range(devices - 1, 0, -1) if (number & (number + 1)) == 0]
+
+
 def exchange_kernel(order_x, count_y, *refs):
-    count_x = len(order_x)
-    raw_refs, (before_ref, after_ref, place, ms_ref, aex_ref) = refs[:count_x], refs[count_x:-3]
+    count_x, numbers = len(order_x), meeting(count_y)
+    raw_refs, edge_refs, (place, ms_ref, aex_ref) = refs[:count_x], refs[count_x:-6], refs[-6:-3]
     exchange_ref, unit_ref, raw_ref = refs[-3:]
     depth, height, width = raw_ref.shape[2:]
     gx, gy = place[0], place[1]
+
+    def row_beside(field, other):
+        value = None
+        for number, edge_ref in zip(numbers, edge_refs):
+            edge = edge_ref[field]
+            match = lax.bitwise_xor(gy, number) == other
+            value = edge if value is None else jnp.where(match, edge, value)
+        return value[:, None, :]
 
     for spot, number in enumerate(order_x):
         raw_ref[lax.bitwise_xor(gx, number)] = raw_refs[spot][...]
@@ -350,7 +362,7 @@
     here = quantities(raw)
     side = quantities([jnp.where(lane == 0, raw_ref[right, f], raw_ref[left, f]) for f in range(3)])
     above = quantities(
-        [jnp.where(row == 0, after_ref[f][:, None, :], before_ref[f][:, None, :]) for f in range(3)]
+        [jnp.where(row == 0, row_beside(f, gy + 1), row_beside(f, gy - 1)) for f in range(3)]
     )
     saturation = looked_up(raw[2], ms_ref)
     total = [jnp.zeros(shape, jnp.float32) for _ in range(3)]
@@ -555,6 +567,12 @@
         name="lines",
     )
     columns = exchanged(spectrum, "gy", order_y)
+    first, last = after((first, last), columns[1])
+    edges = [
+        swapped(jnp.where(lax.bitwise_xor(gy, number) > gy, last, first), "gy", number)
+        for number in meeting(count_y)
+    ]
+    columns, edges = lax.optimization_barrier((columns, edges))
     scale = -1.0 / (2 * depth * 2 * whole_y * 2 * count_x * width)
     waves = call(
         functools.partial(waves_kernel, scale, count_y),
@@ -584,15 +602,12 @@
         for number, block in zip(numbers, blocks):
             partial[number] = block
     parts, far_sum = gathered_sums(partial, "gx")
-    first, last = after((first, last), far_sum)
-    up = [(i, i + 1) for i in range(count_y - 1)]
-    row_before = lax.ppermute(last, "gy", up)
-    row_after = lax.ppermute(first, "gy", [(j, i) for i, j in up])
+    edges, far_sum = lax.optimization_barrier((edges, far_sum))
     exchange, unit = call(
         functools.partial(exchange_kernel, order_x, count_y),
         [cells, cells],
-        [vmem] * (count_x + 2) + [smem] * 3,
-        (*gathered, row_before, row_after, place, ms_region, aex_region),
+        [vmem] * (count_x + len(edges)) + [smem] * 3,
+        (*gathered, *edges, place, ms_region, aex_region),
         scratch=(pltpu.VMEM((count_x, 3, depth, height, width), jnp.float32),),
         flops=300 * depth * height * width,
         name="exchange",

time: 57.8 us -> 62 us (1.073)
  local copies, waits for them, and re-layouts: 0.01 us -> 4.16 us
  starting transfers between devices: 32.4 us -> 33.5 us
  waiting for transfers between devices: 10.4 us -> 9.52 us
    ppermute x20 -> x23, starting transfers between devices: 27.9 us -> 33.5 us  [swapped(): return lax.ppermute(chunk, axis, [(i, i ^ number) for i in range(devices)])]
    ppermute x2 -> x0, starting transfers between devices: 4.48 us -> none  [the longest x1 3.18 us: per_device(): row_before = lax.ppermute(last, 'gy', up)]
    ppermute x2 -> x0, waiting for transfers between devices: 4.29 us -> none  [the longest x1 4.2 us: per_device(): row_after = lax.ppermute(first, 'gy', [(j, i) for i, j in up])]
    unnamed x8 -> x12, local copies, waits for them, and re-layouts: 0.01 us -> 4.16 us
    ppermute x20 -> x23, waiting for transfers between devices: 6.14 us -> 9.52 us  [swapped(): return lax.ppermute(chunk, axis, [(i, i ^ number) for i in range(devices)])]
  transfers between devices with their start and end apart: 22 -> 23, of which waited for: 10 -> 6; matrix products, arithmetic and copies ran while one was open for 0% -> 0% of each run, Pallas kernels for 12% -> 11%
where the time goes in v8:
time: 62 us; the launch traced here: 61.8 us
  starting transfers between devices  33.5 us (54%)
  Pallas kernels  13.8 us (22%)
  waiting for transfers between devices  9.52 us (15%)
  local copies, waits for them, and re-layouts  4.16 us (7%)
  between operations  0.78 us (1%)
    ppermute x23, starting transfers between devices, swapped(): return lax.ppermute(chunk, axis, [(i, i ^ number) for i in range(devices)])  33.5 us
    pallas_call x9, Pallas kernels, call(): pl.pallas_call(body, out_shape=out, in_specs=ins, out_specs=[vmem] * len(...  13.8 us
    ppermute x23, waiting for transfers between devices, swapped(): return lax.ppermute(chunk, axis, [(i, i ^ number) for i in range(devices)])  9.52 us
    unnamed x12, local copies, waits for them, and re-layouts  4.16 us
  transfers between devices with their start and end apart: 23, of which 6 were waited for; matrix products, arithmetic and copies ran while one was open for 0% of the time, Pallas kernels for 11%

profile of v8, /device:TPU:0, one launch (start us, length us, event | category | flops | bytes accessed | tf_op | source)
XLA Modules:
  0.0 61.8 jit_solution(11860583570632273161)
XLA Ops:
  0.6 0.8 %pack.1 = (f32[3,4,8,256]{3,2,1,0:T(8,128)S(1)}, f32[3,4,256]{2,1,0:T(4,128)S(1)}, f32[3,4,256]{2,1,0:T(4,128)S(1)}) custom-call(f32[4,8,256]{2,1,0:T(8,128)} %theta_ref.1, f32[4,8,256]{2,1,0:T(8,128)} %phi_ref.1, s32[4,8,256]{2,1,0:T(8,128)} %labels_ref.1), custom_call_target="tpu_custom_call" | custom-call | bytes 221184 | tf_op jit(solution)/shard_map/pack/pallas_call | solution.py:448
  1.5 3.0 %collective-permute-start.1 = (f32[3,4,8,256]{3,2,1,0:T(8,128)S(1)}, f32[3,4,8,256]{3,2,1,0:T(8,128)S(1)}, u32[]{:S(2)}, u32[]{:S(2)}) collective-permute-start(f32[3,4,8,256]{3,2,1,0:T(8,128)S(1)} %get-tuple-element.56.refs_0_), channel_id=1, source_target_pairs={{0,16},{8,24},{16,0},{24,8},{1,17},{9,25},{17,1},{25,9},{2,18},{10... | collective-permute-start | bytes 294920 | tf_op jit(solution)/shard_map/ppermute | solution.py:466
  4.6 3.2 %load.1 = (bf16[2,4,256,1024]{3,2,1,0:T(8,128)(2,1)S(1)}, bf16[128,384]{1,0:T(8,128)(2,1)S(1)}, bf16[128,384]{1,0:T(8,128)(2,1)S(1)}) custom-call(s32[2]{0:T(128)S(1)} %pad_add_fusion.place.refs_7_, bf16[4,8,2,4,256,128]{5,4,3,2,1,0:T(8,128)(2,1)} %constant.22.clone.refs_0_, bf16[8,128,384]{2,1,0:T(8,128)(2,1)} %constant.23.clone.refs_1_, ...), custom_call_target="tpu_custom_call" | custom-call | bytes 22741000 | tf_op jit(solution)/shard_map/load/pallas_call | solution.py:448
  8.3 1.6 %tensor.1.refs_8_ = bf16[48,128,128]{2,1,0:T(8,128)(2,1)S(1)} custom-call(bf16[48,64,128]{2,1,0:T(8,128)(2,1)S(1)} %bitcast.3, bf16[64,128]{1,0:T(8,128)(2,1)S(1)} %copy-done.3), custom_call_target="tpu_custom_call" | custom-call | flops 100663296 | bytes 2375680 | tf_op jit(solution)/shard_map/tensor/pallas_call | solution.py:448
  9.9 1.6 %lines.1 = (f32[96,128]{1,0:T(8,128)S(1)}, f32[96,128]{1,0:T(8,128)S(1)}, f32[96,128]{1,0:T(8,128)S(1)}, f32[96,128]{1,0:T(8,128)S(1)}, f32[96,128]{1,0:T(8,128)...) custom-call(f32[3,4,8,256]{3,2,1,0:T(8,128)S(1)} %get-tuple-element.56.refs_0_, ...), custom_call_target="tpu_custom_call" | custom-call | flops 603979776 | bytes 4980800 | tf_op jit(solution)/shard_map/lines/pallas_call | solution.py:448
  11.6 2.0 %copy-done = bf16[2,4,256,1024]{3,2,1,0:T(8,128)(2,1)} copy-done((bf16[2,4,256,1024]{3,2,1,0:T(8,128)(2,1)}, bf16[2,4,256,1024]{3,2,1,0:T(8,128)(2,1)S(1)}, u32[]{:S(2)}) %copy-start) | copy-done | bytes 4194328
  13.5 3.6 %collective-permute-start.4 = (f32[96,128]{1,0:T(8,128)S(1)}, f32[96,128]{1,0:T(8,128)S(1)}, u32[]{:S(2)}, u32[]{:S(2)}) collective-permute-start(f32[96,128]{1,0:T(8,128)S(1)} %get-tuple-element.62), channel_id=1, source_target_pairs={{0,6},{1,7},{2,4},{3,5},{4,2},{5,3},{6,0},{7,1},{8,14},{9,15},{10,... | collective-permute-start | bytes 147464 | tf_op jit(solution)/shard_map/ppermute | solution.py:466
  17.1 1.2 %collective-permute-start.3 = (f32[96,128]{1,0:T(8,128)S(1)}, f32[96,128]{1,0:T(8,128)S(1)}, u32[]{:S(2)}, u32[]{:S(2)}) collective-permute-start(f32[96,128]{1,0:T(8,128)S(1)} %get-tuple-element.61), channel_id=1, source_target_pairs={{0,7},{1,6},{2,5},{3,4},{4,3},{5,2},{6,1},{7,0},{8,15},{9,14},{10,... | collective-permute-start | bytes 147464 | tf_op jit(solution)/shard_map/ppermute | solution.py:466
  19.0 2.1 %collective-permute-start.6 = (f32[96,128]{1,0:T(8,128)S(1)}, f32[96,128]{1,0:T(8,128)S(1)}, u32[]{:S(2)}, u32[]{:S(2)}) collective-permute-start(f32[96,128]{1,0:T(8,128)S(1)} %get-tuple-element.64), channel_id=1, source_target_pairs={{0,4},{1,5},{2,6},{3,7},{4,0},{5,1},{6,2},{7,3},{8,12},{9,13},{10,... | collective-permute-start | bytes 147464 | tf_op jit(solution)/shard_map/ppermute | solution.py:466
  21.2 2.2 %collective-permute-start.7 = (f32[96,128]{1,0:T(8,128)S(1)}, f32[96,128]{1,0:T(8,128)S(1)}, u32[]{:S(2)}, u32[]{:S(2)}) collective-permute-start(f32[96,128]{1,0:T(8,128)S(1)} %get-tuple-element.65), channel_id=1, source_target_pairs={{0,3},{1,2},{2,1},{3,0},{4,7},{5,6},{6,5},{7,4},{8,11},{9,10},{10,... | collective-permute-start | bytes 147464 | tf_op jit(solution)/shard_map/ppermute | solution.py:466
  23.3 0.8 %collective-permute-start.8 = (f32[96,128]{1,0:T(8,128)S(1)}, f32[96,128]{1,0:T(8,128)S(1)}, u32[]{:S(2)}, u32[]{:S(2)}) collective-permute-start(f32[96,128]{1,0:T(8,128)S(1)} %get-tuple-element.66), channel_id=1, source_target_pairs={{0,2},{1,3},{2,0},{3,1},{4,6},{5,7},{6,4},{7,5},{8,10},{9,11},{10,... | collective-permute-start | bytes 147464 | tf_op jit(solution)/shard_map/ppermute | solution.py:466
  24.1 1.3 %collective-permute-start.9 = (f32[96,128]{1,0:T(8,128)S(1)}, f32[96,128]{1,0:T(8,128)S(1)}, u32[]{:S(2)}, u32[]{:S(2)}) collective-permute-start(f32[96,128]{1,0:T(8,128)S(1)} %get-tuple-element.67), channel_id=1, source_target_pairs={{0,1},{1,0},{2,3},{3,2},{4,5},{5,4},{6,7},{7,6},{8,9},{9,8},{10,11... | collective-permute-start | bytes 147464 | tf_op jit(solution)/shard_map/ppermute | solution.py:466
  25.5 1.6 %collective-permute-start.12 = (f32[3,4,256]{2,1,0:T(4,128)S(1)}, f32[3,4,256]{2,1,0:T(4,128)S(1)}, u32[]{:S(2)}, u32[]{:S(2)}) collective-permute-start(f32[3,4,256]{2,1,0:T(4,128)S(1)} %get-tuple-element.104), channel_id=1, source_target_pairs={{0,1},{1,0},{2,3},{3,2},{4,5},{5,4},{6,7},{7,6},{8,9},{9,8},{10,11... | collective-permute-start | bytes 36872 | tf_op jit(solution)/shard_map/ppermute | solution.py:466
  27.1 1.4 %collective-permute-start.11 = (f32[3,4,256]{2,1,0:T(4,128)S(1)}, f32[3,4,256]{2,1,0:T(4,128)S(1)}, u32[]{:S(2)}, u32[]{:S(2)}) collective-permute-start(f32[3,4,256]{2,1,0:T(4,128)S(1)} %get-tuple-element.105), channel_id=1, source_target_pairs={{0,3},{1,2},{2,1},{3,0},{4,7},{5,6},{6,5},{7,4},{8,11},{9,10},{10,... | collective-permute-start | bytes 36872 | tf_op jit(solution)/shard_map/ppermute | solution.py:466
  28.5 2.4 %collective-permute-start.10 = (f32[3,4,256]{2,1,0:T(4,128)S(1)}, f32[3,4,256]{2,1,0:T(4,128)S(1)}, u32[]{:S(2)}, u32[]{:S(2)}) collective-permute-start(f32[3,4,256]{2,1,0:T(4,128)S(1)} %get-tuple-element.106), channel_id=1, source_target_pairs={{0,7},{1,6},{2,5},{3,4},{4,3},{5,2},{6,1},{7,0},{8,15},{9,14},{10,... | collective-permute-start | bytes 36872 | tf_op jit(solution)/shard_map/ppermute | solution.py:466
  30.9 0.8 %collective-permute-done.11.refs_5_ = f32[3,4,256]{2,1,0:T(4,128)S(1)} collective-permute-done((f32[3,4,256]{2,1,0:T(4,128)S(1)}, f32[3,4,256]{2,1,0:T(4,128)S(1)}, u32[]{:S(2)}, u32[]{:S(2)}) %collective-permute-start.11) | collective-permute-done | bytes 12320 | tf_op jit(solution)/shard_map/ppermute | solution.py:466
  31.8 3.1 %collective-permute-done.10.refs_4_ = f32[3,4,256]{2,1,0:T(4,128)S(1)} collective-permute-done((f32[3,4,256]{2,1,0:T(4,128)S(1)}, f32[3,4,256]{2,1,0:T(4,128)S(1)}, u32[]{:S(2)}, u32[]{:S(2)}) %collective-permute-start.10) | collective-permute-done | bytes 12320 | tf_op jit(solution)/shard_map/ppermute | solution.py:466
  34.9 3.1 %waves.1 = (f32[96,128]{1,0:T(8,128)S(1)}, f32[96,128]{1,0:T(8,128)S(1)}, f32[96,128]{1,0:T(8,128)S(1)}, f32[96,128]{1,0:T(8,128)S(1)}, f32[96,128]{1,0:T(8,128)...) custom-call(f32[96,128]{1,0:T(8,128)S(1)} %collective-permute-done.3.refs_0_, ...), custom_call_target="tpu_custom_call" | custom-call | flops 125829120 | bytes 2555904 | tf_op jit(solution)/shard_map/waves/pallas_call | solution.py:448
  38.0 2.5 %collective-permute-start.13 = (f32[96,128]{1,0:T(8,128)S(1)}, f32[96,128]{1,0:T(8,128)S(1)}, u32[]{:S(2)}, u32[]{:S(2)}) collective-permute-start(f32[96,128]{1,0:T(8,128)S(1)} %get-tuple-element.84), channel_id=1, source_target_pairs={{0,7},{1,6},{2,5},{3,4},{4,3},{5,2},{6,1},{7,0},{8,15},{9,14},{10,... | collective-permute-start | bytes 147464 | tf_op jit(solution)/shard_map/ppermute | solution.py:466
  40.5 1.3 %collective-permute-start.14 = (f32[96,128]{1,0:T(8,128)S(1)}, f32[96,128]{1,0:T(8,128)S(1)}, u32[]{:S(2)}, u32[]{:S(2)}) collective-permute-start(f32[96,128]{1,0:T(8,128)S(1)} %get-tuple-element.85), channel_id=1, source_target_pairs={{0,6},{1,7},{2,4},{3,5},{4,2},{5,3},{6,0},{7,1},{8,14},{9,15},{10,... | collective-permute-start | bytes 147464 | tf_op jit(solution)/shard_map/ppermute | solution.py:466
  41.8 3.9 %collective-permute-start.16 = (f32[96,128]{1,0:T(8,128)S(1)}, f32[96,128]{1,0:T(8,128)S(1)}, u32[]{:S(2)}, u32[]{:S(2)}) collective-permute-start(f32[96,128]{1,0:T(8,128)S(1)} %get-tuple-element.87), channel_id=1, source_target_pairs={{0,4},{1,5},{2,6},{3,7},{4,0},{5,1},{6,2},{7,3},{8,12},{9,13},{10,... | collective-permute-start | bytes 147464 | tf_op jit(solution)/shard_map/ppermute | solution.py:466
  45.8 1.9 %collective-permute-start.18 = (f32[96,128]{1,0:T(8,128)S(1)}, f32[96,128]{1,0:T(8,128)S(1)}, u32[]{:S(2)}, u32[]{:S(2)}) collective-permute-start(f32[96,128]{1,0:T(8,128)S(1)} %get-tuple-element.89), channel_id=1, source_target_pairs={{0,2},{1,3},{2,0},{3,1},{4,6},{5,7},{6,4},{7,5},{8,10},{9,11},{10,... | collective-permute-start | bytes 147464 | tf_op jit(solution)/shard_map/ppermute | solution.py:466
  47.7 1.6 %collective-permute-start.19 = (f32[96,128]{1,0:T(8,128)S(1)}, f32[96,128]{1,0:T(8,128)S(1)}, u32[]{:S(2)}, u32[]{:S(2)}) collective-permute-start(f32[96,128]{1,0:T(8,128)S(1)} %get-tuple-element.90), channel_id=1, source_target_pairs={{0,1},{1,0},{2,3},{3,2},{4,5},{5,4},{6,7},{7,6},{8,9},{9,8},{10,11... | collective-permute-start | bytes 147464 | tf_op jit(solution)/shard_map/ppermute | solution.py:466
  49.3 1.5 %collective-permute-done.17.refs_4_ = f32[96,128]{1,0:T(8,128)S(1)} collective-permute-done((f32[96,128]{1,0:T(8,128)S(1)}, f32[96,128]{1,0:T(8,128)S(1)}, u32[]{:S(2)}, u32[]{:S(2)}) %collective-permute-start.17) | collective-permute-done | bytes 49184 | tf_op jit(solution)/shard_map/ppermute | solution.py:466
  50.8 1.0 %collective-permute-done.19.refs_6_ = f32[96,128]{1,0:T(8,128)S(1)} collective-permute-done((f32[96,128]{1,0:T(8,128)S(1)}, f32[96,128]{1,0:T(8,128)S(1)}, u32[]{:S(2)}, u32[]{:S(2)}) %collective-permute-start.19) | collective-permute-done | bytes 49184 | tf_op jit(solution)/shard_map/ppermute | solution.py:466
  51.8 2.2 %copy-done.1 = bf16[2,4,256,1024]{3,2,1,0:T(8,128)(2,1)S(1)} copy-done((bf16[2,4,256,1024]{3,2,1,0:T(8,128)(2,1)S(1)}, bf16[2,4,256,1024]{3,2,1,0:T(8,128)(2,1)}, u32[]{:S(2)}) %copy-start.1) | copy-done | bytes 4194328
  54.0 0.8 %back_across.1 = (f32[96,256]{1,0:T(8,128)S(1)}, f32[96,256]{1,0:T(8,128)S(1)}) custom-call(f32[96,128]{1,0:T(8,128)S(1)} %collective-permute-done.13.refs_0_, f32[96,128]{1,0:T(8,128)S(1)} %collective-permute-done.14.refs_1_, f32[96,128]{1,0:T(8,128)S(1)} %collective-permute-done.15.refs_2_, f32[96,128]{1,0:T(8,128)S(1)} %collective-permute-done.16.refs_3_, ...), custom_call_target="tpu_custom_call" | custom-call | flops 301989888 | bytes 4784128 | tf_op jit(solution)/shard_map/back_across/pallas_call | solution.py:448
  55.3 0.8 %back_within.1 = (f32[96,256]{1,0:T(8,128)S(1)}, f32[96,256]{1,0:T(8,128)S(1)}) custom-call(f32[96,128]{1,0:T(8,128)S(1)} %collective-permute-done.13.refs_0_, f32[96,128]{1,0:T(8,128)S(1)} %collective-permute-done.14.refs_1_, f32[96,128]{1,0:T(8,128)S(1)} %collective-permute-done.15.refs_2_, f32[96,128]{1,0:T(8,128)S(1)} %collective-permute-done.16.refs_3_, ...), custom_call_target="tpu_custom_call" | custom-call | flops 301989888 | bytes 4784128 | tf_op jit(solution)/shard_map/back_within/pallas_call | solution.py:448
  56.2 0.8 %collective-permute-start.22 = (f32[96,256]{1,0:T(8,128)S(1)}, f32[96,256]{1,0:T(8,128)S(1)}, u32[]{:S(2)}, u32[]{:S(2)}) collective-permute-start(f32[96,256]{1,0:T(8,128)S(1)} %add.3), channel_id=1, source_target_pairs={{0,16},{8,24},{16,0},{24,8},{1,17},{9,25},{17,1},{25,9},{2,18},{10... | collective-permute-start | bytes 294920 | tf_op jit(solution)/shard_map/ppermute | solution.py:466
  57.0 1.1 %exchange.1 = (f32[3,4,8,256]{3,2,1,0:T(8,128)S(1)}, f32[3,4,8,256]{3,2,1,0:T(8,128)S(1)}) custom-call(f32[3,4,8,256]{3,2,1,0:T(8,128)S(1)} %get-tuple-element.56.refs_0_, f32[3,4,8,256]{3,2,1,0:T(8,128)S(1)} %collective-permute-done.refs_1_, f32[3,4,8,256]{3,2,1,0:T(8,128)S(1)} %collective-permute-done.1.refs_2_, ...), custom_call_target="tpu_custom_call" | custom-call | flops 2457600 | bytes 626824 | tf_op jit(solution)/shard_map/exchange/pallas_call | solution.py:448
  58.2 2.9 %collective-permute-done.22.refs_2_ = f32[96,256]{1,0:T(8,128)S(1)} collective-permute-done((f32[96,256]{1,0:T(8,128)S(1)}, f32[96,256]{1,0:T(8,128)S(1)}, u32[]{:S(2)}, u32[]{:S(2)}) %collective-permute-start.22) | collective-permute-done | bytes 98336 | tf_op jit(solution)/shard_map/ppermute | solution.py:466
  61.1 0.7 %predict.1 = (f32[3,4,8,256]{3,2,1,0:T(8,128)}, f32[3,4,8,256]{3,2,1,0:T(8,128)}) custom-call(f32[96,256]{1,0:T(8,128)S(1)} %get-tuple-element.92.refs_0_, f32[96,256]{1,0:T(8,128)S(1)} %collective-permute-done.20.refs_1_, f32[96,256]{1,0:T(8,128)S(1)} %collective-permute-done.22.refs_2_, f32[3,4,8,256]{3,2,1,0:T(8,128)S(1)} %get-tuple-element.102.refs_3_, ...), custom_call_target="tpu_custom_call" | custom-call | flops 491520 | bytes 688128 | tf_op jit(solution)/shard_map/predict/pallas_call | solution.py:448
  (38 shorter events, 2.2 us)
Async XLA Ops:
  1.5 6.3 %collective-permute-start.1 = (f32[3,4,8,256]{3,2,1,0:T(8,128)S(1)}, f32[3,4,8,256]{3,2,1,0:T(8,128)S(1)}, u32[]{:S(2)}, u32[]{:S(2)}) collective-permute-start(f32[3,4,8,256]{3,2,1,0:T(8,128)S(1)} %get-tuple-element.56.refs_0_), channel_id=1, source_target_pairs={{0,16},{8,24},{16,0},{24,8},{1,17},{9,25},{17,1},{25,9},{2,18},{10... | collective-permute-start | bytes 294920 | tf_op jit(solution)/shard_map/ppermute | solution.py:466
  4.5 5.5 %collective-permute-start = (f32[3,4,8,256]{3,2,1,0:T(8,128)S(1)}, f32[3,4,8,256]{3,2,1,0:T(8,128)S(1)}, u32[]{:S(2)}, u32[]{:S(2)}) collective-permute-start(f32[3,4,8,256]{3,2,1,0:T(8,128)S(1)} %get-tuple-element.56.refs_0_), channel_id=1, source_target_pairs={{0,8},{8,0},{16,24},{24,16},{1,9},{9,1},{17,25},{25,17},{2,10},{10... | collective-permute-start | bytes 294920 | tf_op jit(solution)/shard_map/ppermute | solution.py:466
  4.6 3.8 %copy-start.2 = (bf16[6,8,64,128]{3,2,1,0:T(8,128)(2,1)S(1)}, bf16[6,8,64,128]{3,2,1,0:T(8,128)(2,1)}, u32[]{:S(2)}) copy-start(bf16[6,8,64,128]{3,2,1,0:T(8,128)(2,1)} %param.15) | copy-start | bytes 2359300
  4.6 3.8 %copy-start.3 = (bf16[64,128]{1,0:T(8,128)(2,1)S(1)}, bf16[64,128]{1,0:T(8,128)(2,1)}, u32[]{:S(2)}) copy-start(bf16[64,128]{1,0:T(8,128)(2,1)} %constant.25.clone.twice_ref) | copy-start | bytes 49156
  7.8 2.2 %collective-permute-start.2 = (f32[3,4,8,256]{3,2,1,0:T(8,128)S(1)}, f32[3,4,8,256]{3,2,1,0:T(8,128)S(1)}, u32[]{:S(2)}, u32[]{:S(2)}) collective-permute-start(f32[3,4,8,256]{3,2,1,0:T(8,128)S(1)} %collective-permute-done.1.refs_2_), channel_id=1, source_target_pairs={{0,8},{8,0},{16,24},{24,16},{1,9},{9,1},{17,25},{25,17},{2,10},{10... | collective-permute-start | bytes 294920 | tf_op jit(solution)/shard_map/ppermute | solution.py:466
  11.5 2.0 %copy-start = (bf16[2,4,256,1024]{3,2,1,0:T(8,128)(2,1)}, bf16[2,4,256,1024]{3,2,1,0:T(8,128)(2,1)S(1)}, u32[]{:S(2)}) copy-start(bf16[2,4,256,1024]{3,2,1,0:T(8,128)(2,1)S(1)} %get-tuple-element.60.refs_5_.refs_8_) | copy-start | bytes 12582916
  13.5 9.8 %collective-permute-start.4 = (f32[96,128]{1,0:T(8,128)S(1)}, f32[96,128]{1,0:T(8,128)S(1)}, u32[]{:S(2)}, u32[]{:S(2)}) collective-permute-start(f32[96,128]{1,0:T(8,128)S(1)} %get-tuple-element.62), channel_id=1, source_target_pairs={{0,6},{1,7},{2,4},{3,5},{4,2},{5,3},{6,0},{7,1},{8,14},{9,15},{10,... | collective-permute-start | bytes 147464 | tf_op jit(solution)/shard_map/ppermute | solution.py:466
  17.1 7.0 %collective-permute-start.3 = (f32[96,128]{1,0:T(8,128)S(1)}, f32[96,128]{1,0:T(8,128)S(1)}, u32[]{:S(2)}, u32[]{:S(2)}) collective-permute-start(f32[96,128]{1,0:T(8,128)S(1)} %get-tuple-element.61), channel_id=1, source_target_pairs={{0,7},{1,6},{2,5},{3,4},{4,3},{5,2},{6,1},{7,0},{8,15},{9,14},{10,... | collective-permute-start | bytes 147464 | tf_op jit(solution)/shard_map/ppermute | solution.py:466
  18.3 7.3 %collective-permute-start.5 = (f32[96,128]{1,0:T(8,128)S(1)}, f32[96,128]{1,0:T(8,128)S(1)}, u32[]{:S(2)}, u32[]{:S(2)}) collective-permute-start(f32[96,128]{1,0:T(8,128)S(1)} %get-tuple-element.63), channel_id=1, source_target_pairs={{0,5},{1,4},{2,7},{3,6},{4,1},{5,0},{6,3},{7,2},{8,13},{9,12},{10,... | collective-permute-start | bytes 147464 | tf_op jit(solution)/shard_map/ppermute | solution.py:466
  19.0 8.1 %collective-permute-start.6 = (f32[96,128]{1,0:T(8,128)S(1)}, f32[96,128]{1,0:T(8,128)S(1)}, u32[]{:S(2)}, u32[]{:S(2)}) collective-permute-start(f32[96,128]{1,0:T(8,128)S(1)} %get-tuple-element.64), channel_id=1, source_target_pairs={{0,4},{1,5},{2,6},{3,7},{4,0},{5,1},{6,2},{7,3},{8,12},{9,13},{10,... | collective-permute-start | bytes 147464 | tf_op jit(solution)/shard_map/ppermute | solution.py:466
  21.2 7.4 %collective-permute-start.7 = (f32[96,128]{1,0:T(8,128)S(1)}, f32[96,128]{1,0:T(8,128)S(1)}, u32[]{:S(2)}, u32[]{:S(2)}) collective-permute-start(f32[96,128]{1,0:T(8,128)S(1)} %get-tuple-element.65), channel_id=1, source_target_pairs={{0,3},{1,2},{2,1},{3,0},{4,7},{5,6},{6,5},{7,4},{8,11},{9,10},{10,... | collective-permute-start | bytes 147464 | tf_op jit(solution)/shard_map/ppermute | solution.py:466
  23.3 7.6 %collective-permute-start.8 = (f32[96,128]{1,0:T(8,128)S(1)}, f32[96,128]{1,0:T(8,128)S(1)}, u32[]{:S(2)}, u32[]{:S(2)}) collective-permute-start(f32[96,128]{1,0:T(8,128)S(1)} %get-tuple-element.66), channel_id=1, source_target_pairs={{0,2},{1,3},{2,0},{3,1},{4,6},{5,7},{6,4},{7,5},{8,10},{9,11},{10,... | collective-permute-start | bytes 147464 | tf_op jit(solution)/shard_map/ppermute | solution.py:466
  24.1 6.8 %collective-permute-start.9 = (f32[96,128]{1,0:T(8,128)S(1)}, f32[96,128]{1,0:T(8,128)S(1)}, u32[]{:S(2)}, u32[]{:S(2)}) collective-permute-start(f32[96,128]{1,0:T(8,128)S(1)} %get-tuple-element.67), channel_id=1, source_target_pairs={{0,1},{1,0},{2,3},{3,2},{4,5},{5,4},{6,7},{7,6},{8,9},{9,8},{10,11... | collective-permute-start | bytes 147464 | tf_op jit(solution)/shard_map/ppermute | solution.py:466
  25.5 5.4 %collective-permute-start.12 = (f32[3,4,256]{2,1,0:T(4,128)S(1)}, f32[3,4,256]{2,1,0:T(4,128)S(1)}, u32[]{:S(2)}, u32[]{:S(2)}) collective-permute-start(f32[3,4,256]{2,1,0:T(4,128)S(1)} %get-tuple-element.104), channel_id=1, source_target_pairs={{0,1},{1,0},{2,3},{3,2},{4,5},{5,4},{6,7},{7,6},{8,9},{9,8},{10,11... | collective-permute-start | bytes 36872 | tf_op jit(solution)/shard_map/ppermute | solution.py:466
  27.1 4.6 %collective-permute-start.11 = (f32[3,4,256]{2,1,0:T(4,128)S(1)}, f32[3,4,256]{2,1,0:T(4,128)S(1)}, u32[]{:S(2)}, u32[]{:S(2)}) collective-permute-start(f32[3,4,256]{2,1,0:T(4,128)S(1)} %get-tuple-element.105), channel_id=1, source_target_pairs={{0,3},{1,2},{2,1},{3,0},{4,7},{5,6},{6,5},{7,4},{8,11},{9,10},{10,... | collective-permute-start | bytes 36872 | tf_op jit(solution)/shard_map/ppermute | solution.py:466
  28.5 6.4 %collective-permute-start.10 = (f32[3,4,256]{2,1,0:T(4,128)S(1)}, f32[3,4,256]{2,1,0:T(4,128)S(1)}, u32[]{:S(2)}, u32[]{:S(2)}) collective-permute-start(f32[3,4,256]{2,1,0:T(4,128)S(1)} %get-tuple-element.106), channel_id=1, source_target_pairs={{0,7},{1,6},{2,5},{3,4},{4,3},{5,2},{6,1},{7,0},{8,15},{9,14},{10,... | collective-permute-start | bytes 36872 | tf_op jit(solution)/shard_map/ppermute | solution.py:466
  38.0 7.8 %collective-permute-start.13 = (f32[96,128]{1,0:T(8,128)S(1)}, f32[96,128]{1,0:T(8,128)S(1)}, u32[]{:S(2)}, u32[]{:S(2)}) collective-permute-start(f32[96,128]{1,0:T(8,128)S(1)} %get-tuple-element.84), channel_id=1, source_target_pairs={{0,7},{1,6},{2,5},{3,4},{4,3},{5,2},{6,1},{7,0},{8,15},{9,14},{10,... | collective-permute-start | bytes 147464 | tf_op jit(solution)/shard_map/ppermute | solution.py:466
  40.5 7.2 %collective-permute-start.14 = (f32[96,128]{1,0:T(8,128)S(1)}, f32[96,128]{1,0:T(8,128)S(1)}, u32[]{:S(2)}, u32[]{:S(2)}) collective-permute-start(f32[96,128]{1,0:T(8,128)S(1)} %get-tuple-element.85), channel_id=1, source_target_pairs={{0,6},{1,7},{2,4},{3,5},{4,2},{5,3},{6,0},{7,1},{8,14},{9,15},{10,... | collective-permute-start | bytes 147464 | tf_op jit(solution)/shard_map/ppermute | solution.py:466
  41.8 7.4 %collective-permute-start.15 = (f32[96,128]{1,0:T(8,128)S(1)}, f32[96,128]{1,0:T(8,128)S(1)}, u32[]{:S(2)}, u32[]{:S(2)}) collective-permute-start(f32[96,128]{1,0:T(8,128)S(1)} %get-tuple-element.86), channel_id=1, source_target_pairs={{0,5},{1,4},{2,7},{3,6},{4,1},{5,0},{6,3},{7,2},{8,13},{9,12},{10,... | collective-permute-start | bytes 147464 | tf_op jit(solution)/shard_map/ppermute | solution.py:466
  41.8 7.4 %collective-permute-start.16 = (f32[96,128]{1,0:T(8,128)S(1)}, f32[96,128]{1,0:T(8,128)S(1)}, u32[]{:S(2)}, u32[]{:S(2)}) collective-permute-start(f32[96,128]{1,0:T(8,128)S(1)} %get-tuple-element.87), channel_id=1, source_target_pairs={{0,4},{1,5},{2,6},{3,7},{4,0},{5,1},{6,2},{7,3},{8,12},{9,13},{10,... | collective-permute-start | bytes 147464 | tf_op jit(solution)/shard_map/ppermute | solution.py:466
  45.8 5.0 %collective-permute-start.17 = (f32[96,128]{1,0:T(8,128)S(1)}, f32[96,128]{1,0:T(8,128)S(1)}, u32[]{:S(2)}, u32[]{:S(2)}) collective-permute-start(f32[96,128]{1,0:T(8,128)S(1)} %get-tuple-element.88), channel_id=1, source_target_pairs={{0,3},{1,2},{2,1},{3,0},{4,7},{5,6},{6,5},{7,4},{8,11},{9,10},{10,... | collective-permute-start | bytes 147464 | tf_op jit(solution)/shard_map/ppermute | solution.py:466
  45.8 4.9 %collective-permute-start.18 = (f32[96,128]{1,0:T(8,128)S(1)}, f32[96,128]{1,0:T(8,128)S(1)}, u32[]{:S(2)}, u32[]{:S(2)}) collective-permute-start(f32[96,128]{1,0:T(8,128)S(1)} %get-tuple-element.89), channel_id=1, source_target_pairs={{0,2},{1,3},{2,0},{3,1},{4,6},{5,7},{6,4},{7,5},{8,10},{9,11},{10,... | collective-permute-start | bytes 147464 | tf_op jit(solution)/shard_map/ppermute | solution.py:466
  47.7 4.1 %collective-permute-start.19 = (f32[96,128]{1,0:T(8,128)S(1)}, f32[96,128]{1,0:T(8,128)S(1)}, u32[]{:S(2)}, u32[]{:S(2)}) collective-permute-start(f32[96,128]{1,0:T(8,128)S(1)} %get-tuple-element.90), channel_id=1, source_target_pairs={{0,1},{1,0},{2,3},{3,2},{4,5},{5,4},{6,7},{7,6},{8,9},{9,8},{10,11... | collective-permute-start | bytes 147464 | tf_op jit(solution)/shard_map/ppermute | solution.py:466
  51.8 2.2 %copy-start.1 = (bf16[2,4,256,1024]{3,2,1,0:T(8,128)(2,1)S(1)}, bf16[2,4,256,1024]{3,2,1,0:T(8,128)(2,1)}, u32[]{:S(2)}) copy-start(bf16[2,4,256,1024]{3,2,1,0:T(8,128)(2,1)} %copy-done) | copy-start | bytes 12582916
  54.0 3.1 %copy-start.4 = (f32[16]{0:T(128)S(1)}, f32[16]{0:T(128)}, u32[]{:S(2)}) copy-start(f32[16]{0:T(128)} %refs_8_.1) | copy-start | bytes 196
  54.0 3.1 %copy-start.5 = (f32[16]{0:T(128)S(1)}, f32[16]{0:T(128)}, u32[]{:S(2)}) copy-start(f32[16]{0:T(128)} %refs_9_.1) | copy-start | bytes 196
  54.8 1.4 %collective-permute-start.21 = (f32[96,256]{1,0:T(8,128)S(1)}, f32[96,256]{1,0:T(8,128)S(1)}, u32[]{:S(2)}, u32[]{:S(2)}) collective-permute-start(f32[96,256]{1,0:T(8,128)S(1)} %get-tuple-element.95), channel_id=1, source_target_pairs={{0,8},{8,0},{16,24},{24,16},{1,9},{9,1},{17,25},{25,17},{2,10},{10... | collective-permute-start | bytes 294920 | tf_op jit(solution)/shard_map/ppermute | solution.py:466
  54.8 3.3 %collective-permute-start.20 = (f32[96,256]{1,0:T(8,128)S(1)}, f32[96,256]{1,0:T(8,128)S(1)}, u32[]{:S(2)}, u32[]{:S(2)}) collective-permute-start(f32[96,256]{1,0:T(8,128)S(1)} %get-tuple-element.93), channel_id=1, source_target_pairs={{0,8},{8,0},{16,24},{24,16},{1,9},{9,1},{17,25},{25,17},{2,10},{10... | collective-permute-start | bytes 294920 | tf_op jit(solution)/shard_map/ppermute | solution.py:466
  56.2 4.9 %collective-permute-start.22 = (f32[96,256]{1,0:T(8,128)S(1)}, f32[96,256]{1,0:T(8,128)S(1)}, u32[]{:S(2)}, u32[]{:S(2)}) collective-permute-start(f32[96,256]{1,0:T(8,128)S(1)} %add.3), channel_id=1, source_target_pairs={{0,16},{8,24},{16,0},{24,8},{1,17},{9,25},{17,1},{25,9},{2,18},{10... | collective-permute-start | bytes 294920 | tf_op jit(solution)/shard_map/ppermute | solution.py:466

commit v9 on v8

--- a/solution.py
+++ b/solution.py
@@ -171,13 +171,34 @@
         copy.wait()
     for index, value in enumerate((angle[0], angle[1], label[...].astype(jnp.float32))):
         raw_ref[index] = value
-        first_ref[index] = value[:, 0]
-        last_ref[index] = value[:, height - 1]
-
-
-def lines_kernel(count_x, *refs):
-    raw_refs, (region_ref, table) = refs[:count_x], refs[count_x : count_x + 2]
-    out_refs, (region, sem) = refs[count_x + 2 : -2], refs[-2:]
+        put_edge(first_ref, index, value[:, 0])
+        put_edge(last_ref, index, value[:, height - 1])
+
+
+def meeting(devices):
+    return [number for number in range(1, devices) if (number & (number + 1)) == 0]
+
+
+def edge_spots(depth, width, lanes, start, field):
+    pieces = width // lanes
+    return [start + (field * pieces + piece) * depth for piece in range(pieces)]
+
+
+def put_edge(ref, field, edge):
+    lanes = ref.shape[1]
+    for piece, row in enumerate(edge_spots(*edge.shape, lanes, 0, field)):
+        ref[row : row + edge.shape[0]] = edge[:, piece * lanes : (piece + 1) * lanes]
+
+
+def get_edge(ref, depth, width, start, field):
+    spots = edge_spots(depth, width, ref.shape[1], start, field)
+    return jnp.concatenate([ref[row : row + depth] for row in spots], 1)
+
+
+def lines_kernel(count_x, order_y, *refs):
+    raw_refs, operands = refs[:count_x], refs[count_x : count_x + 5]
+    first_ref, last_ref, region_ref, place, table = operands
+    out_refs, (region, sem) = refs[count_x + 5 : -2], refs[-2:]
     fetch = pltpu.make_async_copy(region_ref, region, sem)
     fetch.start()
     units = [directions(raw_ref[0], raw_ref[1]) for raw_ref in raw_refs]
@@ -192,8 +213,11 @@
         part = both[: 3 * rows] + both[3 * rows :] + dot(high, table[1, number])
         total = part if total is None else total + part
     lanes = out_refs[0].shape[1]
-    for spot, out_ref in enumerate(out_refs):
-        out_ref[...] = total[:, spot * lanes : (spot + 1) * lanes]
+    for spot, (number, out_ref) in enumerate(zip(order_y, out_refs)):
+        out_ref[: 3 * rows] = total[:, spot * lanes : (spot + 1) * lanes]
+        if number in meeting(len(order_y)):
+            up = lax.bitwise_xor(place[1], number) > place[1]
+            out_ref[3 * rows :] = jnp.where(up, last_ref[...], first_ref[...])
 
 
 def back_lines_kernel(numbers, count_y, *refs):
@@ -329,10 +353,6 @@
             ]
 
 
-def meeting(devices):
-    return [number for number in range(devices - 1, 0, -1) if (number & (number + 1)) == 0]
-
-
 def exchange_kernel(order_x, count_y, *refs):
     count_x, numbers = len(order_x), meeting(count_y)
     raw_refs, edge_refs, (place, ms_ref, aex_ref) = refs[:count_x], refs[count_x:-6], refs[-6:-3]
@@ -343,7 +363,7 @@
     def row_beside(field, other):
         value = None
         for number, edge_ref in zip(numbers, edge_refs):
-            edge = edge_ref[field]
+            edge = get_edge(edge_ref, depth, width, 3 * depth * height, field)
             match = lax.bitwise_xor(gy, number) == other
             value = edge if value is None else jnp.where(match, edge, value)
         return value[:, None, :]
@@ -470,6 +490,10 @@
     return [swapped(c, axis, n) if n else c for c, n in zip(chunks, order)]
 
 
+def held(value):
+    return pltpu.with_memory_space_constraint(value, pltpu.VMEM)
+
+
 def after(value, other):
     return lax.optimization_barrier((value, other))[0]
 
@@ -521,7 +545,8 @@
     twice = np.concatenate([np.eye(rows), np.eye(rows)], 1).astype(ml_dtypes.bfloat16)
     transform_flops = 6 * lines * count_x * width * count_y * lanes
 
-    edge = f32(3, depth, width)
+    edge_rows = 3 * depth * width // lanes
+    edge = f32(edge_rows, lanes)
     packed, first, last = call(
         pack_kernel,
         [cells, edge, edge],
@@ -556,23 +581,16 @@
         flops=48 * 2 * rows * lanes * 2 * whole_y,
         name="tensor",
     )
-    gathered, tensor = lax.optimization_barrier((gathered, tensor))
     spectrum = call(
-        functools.partial(lines_kernel, count_x),
-        [f32(lines, lanes)] * count_y,
-        [vmem] * count_x + [hbm, vmem],
-        (*gathered, ms_region, table),
+        functools.partial(lines_kernel, count_x, order_y),
+        [f32(lines + (edge_rows if n in meeting(count_y) else 0), lanes) for n in order_y],
+        [vmem] * (count_x + 2) + [hbm, smem, vmem],
+        (*gathered, first, last, ms_region, place, held(table)),
         scratch=(pltpu.SMEM(ms_region.shape, jnp.float32), pltpu.SemaphoreType.DMA),
         flops=transform_flops,
         name="lines",
     )
-    columns = exchanged(spectrum, "gy", order_y)
-    first, last = after((first, last), columns[1])
-    edges = [
-        swapped(jnp.where(lax.bitwise_xor(gy, number) > gy, last, first), "gy", number)
-        for number in meeting(count_y)
-    ]
-    columns, edges = lax.optimization_barrier((columns, edges))
+    columns = lax.optimization_barrier(exchanged(spectrum, "gy", order_y))
     scale = -1.0 / (2 * depth * 2 * whole_y * 2 * count_x * width)
     waves = call(
         functools.partial(waves_kernel, scale, count_y),
@@ -595,13 +613,14 @@
             functools.partial(back_lines_kernel, numbers, count_y),
             [f32(lines, width)] * len(numbers),
             [vmem] * (count_y + 1),
-            (*returned, table),
+            (*returned, held(table)),
             flops=transform_flops // 2,
             name=name,
         )
         for number, block in zip(numbers, blocks):
             partial[number] = block
     parts, far_sum = gathered_sums(partial, "gx")
+    edges = [columns[order_y.index(number)] for number in meeting(count_y)]
     edges, far_sum = lax.optimization_barrier((edges, far_sum))
     exchange, unit = call(
         functools.partial(exchange_kernel, order_x, count_y),

time: 62 us -> 53 us (0.85)
  starting transfers between devices: 33.5 us -> 26.9 us
  local copies, waits for them, and re-layouts: 4.16 us -> 0.02 us
  waiting for transfers between devices: 9.52 us -> 10.7 us
    ppermute x23 -> x20, starting transfers between devices: 33.5 us -> 26.9 us  [swapped(): return lax.ppermute(chunk, axis, [(i, i ^ number) for i in range(devices)])]
    unnamed x12 -> x8, local copies, waits for them, and re-layouts: 4.16 us -> 0.02 us
    ppermute x23 -> x20, waiting for transfers between devices: 9.52 us -> 10.7 us  [swapped(): return lax.ppermute(chunk, axis, [(i, i ^ number) for i in range(devices)])]
  transfers between devices with their start and end apart: 23 -> 20, of which waited for: 6 -> 9; matrix products, arithmetic and copies ran while one was open for 0% -> 0% of each run, Pallas kernels for 11% -> 13%
where the time goes in v9:
time: 53 us; the launch traced here: 52.8 us
  starting transfers between devices  26.9 us (51%)
  Pallas kernels  14.3 us (27%)
  waiting for transfers between devices  10.7 us (20%)
  between operations  0.76 us (1%)
    ppermute x20, starting transfers between devices, swapped(): return lax.ppermute(chunk, axis, [(i, i ^ number) for i in range(devices)])  26.9 us
    pallas_call x9, Pallas kernels, call(): pl.pallas_call(body, out_shape=out, in_specs=ins, out_specs=[vmem] * len(...  14.3 us
    ppermute x20, waiting for transfers between devices, swapped(): return lax.ppermute(chunk, axis, [(i, i ^ number) for i in range(devices)])  10.7 us
  transfers between devices with their start and end apart: 20, of which 9 were waited for; matrix products, arithmetic and copies ran while one was open for 0% of the time, Pallas kernels for 13%

profile of v9, /device:TPU:0, one launch (start us, length us, event | category | flops | bytes accessed | tf_op | source)
XLA Modules:
  0.0 52.8 jit_solution(14348761988074415761)
XLA Ops:
  0.6 0.8 %pack.1 = (f32[3,4,8,256]{3,2,1,0:T(8,128)S(1)}, f32[24,128]{1,0:T(8,128)S(1)}, f32[24,128]{1,0:T(8,128)S(1)}) custom-call(f32[4,8,256]{2,1,0:T(8,128)} %theta_ref.1, f32[4,8,256]{2,1,0:T(8,128)} %phi_ref.1, s32[4,8,256]{2,1,0:T(8,128)} %labels_ref.1), custom_call_target="tpu_custom_call" | custom-call | bytes 221184 | tf_op jit(solution)/shard_map/pack/pallas_call | solution.py:468
  1.5 3.0 %collective-permute-start.1 = (f32[3,4,8,256]{3,2,1,0:T(8,128)S(1)}, f32[3,4,8,256]{3,2,1,0:T(8,128)S(1)}, u32[]{:S(2)}, u32[]{:S(2)}) collective-permute-start(f32[3,4,8,256]{3,2,1,0:T(8,128)S(1)} %get-tuple-element.43.refs_0_), channel_id=1, source_target_pairs={{0,16},{8,24},{16,0},{24,8},{1,17},{9,25},{17,1},{25,9},{2,18},{10... | collective-permute-start | bytes 294920 | tf_op jit(solution)/shard_map/ppermute | solution.py:486
  4.5 3.2 %load.1 = (bf16[2,4,256,1024]{3,2,1,0:T(8,128)(2,1)S(1)}, bf16[128,384]{1,0:T(8,128)(2,1)S(1)}, bf16[128,384]{1,0:T(8,128)(2,1)S(1)}) custom-call(s32[2]{0:T(128)S(1)} %pad_add_fusion.place.refs_7_, bf16[4,8,2,4,256,128]{5,4,3,2,1,0:T(8,128)(2,1)} %constant.16.clone.refs_0_, bf16[8,128,384]{2,1,0:T(8,128)(2,1)} %constant.17.clone.refs_1_, ...), custom_call_target="tpu_custom_call" | custom-call | bytes 22741000 | tf_op jit(solution)/shard_map/load/pallas_call | solution.py:468
  7.8 0.6 %collective-permute-start.2 = (f32[3,4,8,256]{3,2,1,0:T(8,128)S(1)}, f32[3,4,8,256]{3,2,1,0:T(8,128)S(1)}, u32[]{:S(2)}, u32[]{:S(2)}) collective-permute-start(f32[3,4,8,256]{3,2,1,0:T(8,128)S(1)} %collective-permute-done.1.refs_2_), channel_id=1, source_target_pairs={{0,8},{8,0},{16,24},{24,16},{1,9},{9,1},{17,25},{25,17},{2,10},{10... | collective-permute-start | bytes 294920 | tf_op jit(solution)/shard_map/ppermute | solution.py:486
  8.4 0.9 %collective-permute-done.2.refs_3_ = f32[3,4,8,256]{3,2,1,0:T(8,128)S(1)} collective-permute-done((f32[3,4,8,256]{3,2,1,0:T(8,128)S(1)}, f32[3,4,8,256]{3,2,1,0:T(8,128)S(1)}, u32[]{:S(2)}, u32[]{:S(2)}) %collective-permute-start.2) | collective-permute-done | bytes 98336 | tf_op jit(solution)/shard_map/ppermute | solution.py:486
  9.3 2.1 %lines.1 = (f32[120,128]{1,0:T(8,128)S(1)}, f32[96,128]{1,0:T(8,128)S(1)}, f32[96,128]{1,0:T(8,128)S(1)}, f32[96,128]{1,0:T(8,128)S(1)}, f32[120,128]{1,0:T(8,12...) custom-call(f32[3,4,8,256]{3,2,1,0:T(8,128)S(1)} %get-tuple-element.43.refs_0_, ...), custom_call_target="tpu_custom_call" | custom-call | flops 603979776 | bytes 5042248 | tf_op jit(solution)/shard_map/lines/pallas_call | solution.py:468
  11.4 3.7 %collective-permute-start.4 = (f32[96,128]{1,0:T(8,128)S(1)}, f32[96,128]{1,0:T(8,128)S(1)}, u32[]{:S(2)}, u32[]{:S(2)}) collective-permute-start(f32[96,128]{1,0:T(8,128)S(1)} %get-tuple-element.50), channel_id=1, source_target_pairs={{0,6},{1,7},{2,4},{3,5},{4,2},{5,3},{6,0},{7,1},{8,14},{9,15},{10,... | collective-permute-start | bytes 147464 | tf_op jit(solution)/shard_map/ppermute | solution.py:486
  15.5 2.4 %collective-permute-start.3 = (f32[120,128]{1,0:T(8,128)S(1)}, f32[120,128]{1,0:T(8,128)S(1)}, u32[]{:S(2)}, u32[]{:S(2)}) collective-permute-start(f32[120,128]{1,0:T(8,128)S(1)} %get-tuple-element.49), channel_id=1, source_target_pairs={{0,7},{1,6},{2,5},{3,4},{4,3},{5,2},{6,1},{7,0},{8,15},{9,14},{10,... | collective-permute-start | bytes 184328 | tf_op jit(solution)/shard_map/ppermute | solution.py:486
  17.9 2.5 %collective-permute-start.7 = (f32[120,128]{1,0:T(8,128)S(1)}, f32[120,128]{1,0:T(8,128)S(1)}, u32[]{:S(2)}, u32[]{:S(2)}) collective-permute-start(f32[120,128]{1,0:T(8,128)S(1)} %get-tuple-element.53), channel_id=1, source_target_pairs={{0,3},{1,2},{2,1},{3,0},{4,7},{5,6},{6,5},{7,4},{8,11},{9,10},{10,... | collective-permute-start | bytes 184328 | tf_op jit(solution)/shard_map/ppermute | solution.py:486
  20.5 0.5 collective-permute-start.9
  21.0 1.0 %collective-permute-start.6 = (f32[96,128]{1,0:T(8,128)S(1)}, f32[96,128]{1,0:T(8,128)S(1)}, u32[]{:S(2)}, u32[]{:S(2)}) collective-permute-start(f32[96,128]{1,0:T(8,128)S(1)} %get-tuple-element.52), channel_id=1, source_target_pairs={{0,4},{1,5},{2,6},{3,7},{4,0},{5,1},{6,2},{7,3},{8,12},{9,13},{10,... | collective-permute-start | bytes 147464 | tf_op jit(solution)/shard_map/ppermute | solution.py:486
  21.9 0.7 %collective-permute-done.5.refs_2_ = f32[96,128]{1,0:T(8,128)S(1)} collective-permute-done((f32[96,128]{1,0:T(8,128)S(1)}, f32[96,128]{1,0:T(8,128)S(1)}, u32[]{:S(2)}, u32[]{:S(2)}) %collective-permute-start.5) | collective-permute-done | bytes 49184 | tf_op jit(solution)/shard_map/ppermute | solution.py:486
  22.6 1.6 %tensor.1.refs_8_ = bf16[48,128,128]{2,1,0:T(8,128)(2,1)S(1)} custom-call(bf16[48,64,128]{2,1,0:T(8,128)(2,1)S(1)} %bitcast.3, bf16[64,128]{1,0:T(8,128)(2,1)S(1)} %copy-done.1), custom_call_target="tpu_custom_call" | custom-call | flops 100663296 | bytes 2375680 | tf_op jit(solution)/shard_map/tensor/pallas_call | solution.py:468
  24.2 2.2 %collective-permute-done.6.refs_3_ = f32[96,128]{1,0:T(8,128)S(1)} collective-permute-done((f32[96,128]{1,0:T(8,128)S(1)}, f32[96,128]{1,0:T(8,128)S(1)}, u32[]{:S(2)}, u32[]{:S(2)}) %collective-permute-start.6) | collective-permute-done | bytes 49184 | tf_op jit(solution)/shard_map/ppermute | solution.py:486
  26.4 0.5 collective-permute-done.8.refs_5_
  26.9 3.1 %waves.1 = (f32[96,128]{1,0:T(8,128)S(1)}, f32[96,128]{1,0:T(8,128)S(1)}, f32[96,128]{1,0:T(8,128)S(1)}, f32[96,128]{1,0:T(8,128)S(1)}, f32[96,128]{1,0:T(8,128)...) custom-call(f32[120,128]{1,0:T(8,128)S(1)} %collective-permute-done.3.refs_0_.refs_6_, ...), custom_call_target="tpu_custom_call" | custom-call | flops 125829120 | bytes 2592768 | tf_op jit(solution)/shard_map/waves/pallas_call | solution.py:468
  30.1 2.7 %collective-permute-start.10 = (f32[96,128]{1,0:T(8,128)S(1)}, f32[96,128]{1,0:T(8,128)S(1)}, u32[]{:S(2)}, u32[]{:S(2)}) collective-permute-start(f32[96,128]{1,0:T(8,128)S(1)} %get-tuple-element.67), channel_id=1, source_target_pairs={{0,7},{1,6},{2,5},{3,4},{4,3},{5,2},{6,1},{7,0},{8,15},{9,14},{10,... | collective-permute-start | bytes 147464 | tf_op jit(solution)/shard_map/ppermute | solution.py:486
  32.7 2.3 %collective-permute-start.11 = (f32[96,128]{1,0:T(8,128)S(1)}, f32[96,128]{1,0:T(8,128)S(1)}, u32[]{:S(2)}, u32[]{:S(2)}) collective-permute-start(f32[96,128]{1,0:T(8,128)S(1)} %get-tuple-element.68), channel_id=1, source_target_pairs={{0,6},{1,7},{2,4},{3,5},{4,2},{5,3},{6,0},{7,1},{8,14},{9,15},{10,... | collective-permute-start | bytes 147464 | tf_op jit(solution)/shard_map/ppermute | solution.py:486
  35.0 2.8 %collective-permute-start.13 = (f32[96,128]{1,0:T(8,128)S(1)}, f32[96,128]{1,0:T(8,128)S(1)}, u32[]{:S(2)}, u32[]{:S(2)}) collective-permute-start(f32[96,128]{1,0:T(8,128)S(1)} %get-tuple-element.70), channel_id=1, source_target_pairs={{0,4},{1,5},{2,6},{3,7},{4,0},{5,1},{6,2},{7,3},{8,12},{9,13},{10,... | collective-permute-start | bytes 147464 | tf_op jit(solution)/shard_map/ppermute | solution.py:486
  38.0 2.8 %collective-permute-start.15 = (f32[96,128]{1,0:T(8,128)S(1)}, f32[96,128]{1,0:T(8,128)S(1)}, u32[]{:S(2)}, u32[]{:S(2)}) collective-permute-start(f32[96,128]{1,0:T(8,128)S(1)} %get-tuple-element.72), channel_id=1, source_target_pairs={{0,2},{1,3},{2,0},{3,1},{4,6},{5,7},{6,4},{7,5},{8,10},{9,11},{10,... | collective-permute-start | bytes 147464 | tf_op jit(solution)/shard_map/ppermute | solution.py:486
  40.9 0.4 collective-permute-start.16
  41.3 0.6 %collective-permute-done.13.refs_3_ = f32[96,128]{1,0:T(8,128)S(1)} collective-permute-done((f32[96,128]{1,0:T(8,128)S(1)}, f32[96,128]{1,0:T(8,128)S(1)}, u32[]{:S(2)}, u32[]{:S(2)}) %collective-permute-start.13) | collective-permute-done | bytes 49184 | tf_op jit(solution)/shard_map/ppermute | solution.py:486
  41.9 0.9 %collective-permute-done.14.refs_4_ = f32[96,128]{1,0:T(8,128)S(1)} collective-permute-done((f32[96,128]{1,0:T(8,128)S(1)}, f32[96,128]{1,0:T(8,128)S(1)}, u32[]{:S(2)}, u32[]{:S(2)}) %collective-permute-start.14) | collective-permute-done | bytes 49184 | tf_op jit(solution)/shard_map/ppermute | solution.py:486
  42.8 0.7 %collective-permute-done.15.refs_5_ = f32[96,128]{1,0:T(8,128)S(1)} collective-permute-done((f32[96,128]{1,0:T(8,128)S(1)}, f32[96,128]{1,0:T(8,128)S(1)}, u32[]{:S(2)}, u32[]{:S(2)}) %collective-permute-start.15) | collective-permute-done | bytes 49184 | tf_op jit(solution)/shard_map/ppermute | solution.py:486
  43.5 1.5 %collective-permute-done.16.refs_6_ = f32[96,128]{1,0:T(8,128)S(1)} collective-permute-done((f32[96,128]{1,0:T(8,128)S(1)}, f32[96,128]{1,0:T(8,128)S(1)}, u32[]{:S(2)}, u32[]{:S(2)}) %collective-permute-start.16) | collective-permute-done | bytes 49184 | tf_op jit(solution)/shard_map/ppermute | solution.py:486
  45.0 0.8 %back_across.1 = (f32[96,256]{1,0:T(8,128)S(1)}, f32[96,256]{1,0:T(8,128)S(1)}) custom-call(f32[96,128]{1,0:T(8,128)S(1)} %collective-permute-done.10.refs_0_, f32[96,128]{1,0:T(8,128)S(1)} %collective-permute-done.11.refs_1_, f32[96,128]{1,0:T(8,128)S(1)} %collective-permute-done.12.refs_2_, f32[96,128]{1,0:T(8,128)S(1)} %collective-permute-done.13.refs_3_, ...), custom_call_target="tpu_custom_call" | custom-call | flops 301989888 | bytes 4784128 | tf_op jit(solution)/shard_map/back_across/pallas_call | solution.py:468
  45.9 0.5 collective-permute-start.17
  46.3 0.8 %back_within.1 = (f32[96,256]{1,0:T(8,128)S(1)}, f32[96,256]{1,0:T(8,128)S(1)}) custom-call(f32[96,128]{1,0:T(8,128)S(1)} %collective-permute-done.10.refs_0_, f32[96,128]{1,0:T(8,128)S(1)} %collective-permute-done.11.refs_1_, f32[96,128]{1,0:T(8,128)S(1)} %collective-permute-done.12.refs_2_, f32[96,128]{1,0:T(8,128)S(1)} %collective-permute-done.13.refs_3_, ...), custom_call_target="tpu_custom_call" | custom-call | flops 301989888 | bytes 4784128 | tf_op jit(solution)/shard_map/back_within/pallas_call | solution.py:468
  47.2 1.0 %collective-permute-start.19 = (f32[96,256]{1,0:T(8,128)S(1)}, f32[96,256]{1,0:T(8,128)S(1)}, u32[]{:S(2)}, u32[]{:S(2)}) collective-permute-start(f32[96,256]{1,0:T(8,128)S(1)} %add.3), channel_id=1, source_target_pairs={{0,16},{8,24},{16,0},{24,8},{1,17},{9,25},{17,1},{25,9},{2,18},{10... | collective-permute-start | bytes 294920 | tf_op jit(solution)/shard_map/ppermute | solution.py:486
  48.2 1.1 %exchange.1 = (f32[3,4,8,256]{3,2,1,0:T(8,128)S(1)}, f32[3,4,8,256]{3,2,1,0:T(8,128)S(1)}) custom-call(f32[3,4,8,256]{3,2,1,0:T(8,128)S(1)} %get-tuple-element.43.refs_0_, f32[3,4,8,256]{3,2,1,0:T(8,128)S(1)} %collective-permute-done.refs_1_, f32[3,4,8,256]{3,2,1,0:T(8,128)S(1)} %collective-permute-done.1.refs_2_, ...), custom_call_target="tpu_custom_call" | custom-call | flops 2457600 | bytes 774280 | tf_op jit(solution)/shard_map/exchange/pallas_call | solution.py:468
  49.4 2.7 %collective-permute-done.19.refs_2_ = f32[96,256]{1,0:T(8,128)S(1)} collective-permute-done((f32[96,256]{1,0:T(8,128)S(1)}, f32[96,256]{1,0:T(8,128)S(1)}, u32[]{:S(2)}, u32[]{:S(2)}) %collective-permute-start.19) | collective-permute-done | bytes 98336 | tf_op jit(solution)/shard_map/ppermute | solution.py:486
  52.1 0.7 %predict.1 = (f32[3,4,8,256]{3,2,1,0:T(8,128)}, f32[3,4,8,256]{3,2,1,0:T(8,128)}) custom-call(f32[96,256]{1,0:T(8,128)S(1)} %get-tuple-element.75.refs_0_, f32[96,256]{1,0:T(8,128)S(1)} %collective-permute-done.17.refs_1_, f32[96,256]{1,0:T(8,128)S(1)} %collective-permute-done.19.refs_2_, f32[3,4,8,256]{3,2,1,0:T(8,128)S(1)} %get-tuple-element.82.refs_3_, ...), custom_call_target="tpu_custom_call" | custom-call | flops 491520 | bytes 688128 | tf_op jit(solution)/shard_map/predict/pallas_call | solution.py:468
  (27 shorter events, 0.9 us)
Async XLA Ops:
  1.5 6.3 %collective-permute-start.1 = (f32[3,4,8,256]{3,2,1,0:T(8,128)S(1)}, f32[3,4,8,256]{3,2,1,0:T(8,128)S(1)}, u32[]{:S(2)}, u32[]{:S(2)}) collective-permute-start(f32[3,4,8,256]{3,2,1,0:T(8,128)S(1)} %get-tuple-element.43.refs_0_), channel_id=1, source_target_pairs={{0,16},{8,24},{16,0},{24,8},{1,17},{9,25},{17,1},{25,9},{2,18},{10... | collective-permute-start | bytes 294920 | tf_op jit(solution)/shard_map/ppermute | solution.py:486
  4.5 3.9 %collective-permute-start = (f32[3,4,8,256]{3,2,1,0:T(8,128)S(1)}, f32[3,4,8,256]{3,2,1,0:T(8,128)S(1)}, u32[]{:S(2)}, u32[]{:S(2)}) collective-permute-start(f32[3,4,8,256]{3,2,1,0:T(8,128)S(1)} %get-tuple-element.43.refs_0_), channel_id=1, source_target_pairs={{0,8},{8,0},{16,24},{24,16},{1,9},{9,1},{17,25},{25,17},{2,10},{10... | collective-permute-start | bytes 294920 | tf_op jit(solution)/shard_map/ppermute | solution.py:486
  7.7 14.9 %copy-start = (bf16[6,8,64,128]{3,2,1,0:T(8,128)(2,1)S(1)}, bf16[6,8,64,128]{3,2,1,0:T(8,128)(2,1)}, u32[]{:S(2)}) copy-start(bf16[6,8,64,128]{3,2,1,0:T(8,128)(2,1)} %param.15) | copy-start | bytes 2359300
  7.8 14.8 %copy-start.1 = (bf16[64,128]{1,0:T(8,128)(2,1)S(1)}, bf16[64,128]{1,0:T(8,128)(2,1)}, u32[]{:S(2)}) copy-start(bf16[64,128]{1,0:T(8,128)(2,1)} %constant.19.clone.twice_ref) | copy-start | bytes 49156
  7.8 1.5 %collective-permute-start.2 = (f32[3,4,8,256]{3,2,1,0:T(8,128)S(1)}, f32[3,4,8,256]{3,2,1,0:T(8,128)S(1)}, u32[]{:S(2)}, u32[]{:S(2)}) collective-permute-start(f32[3,4,8,256]{3,2,1,0:T(8,128)S(1)} %collective-permute-done.1.refs_2_), channel_id=1, source_target_pairs={{0,8},{8,0},{16,24},{24,16},{1,9},{9,1},{17,25},{25,17},{2,10},{10... | collective-permute-start | bytes 294920 | tf_op jit(solution)/shard_map/ppermute | solution.py:486
  11.4 9.5 %collective-permute-start.4 = (f32[96,128]{1,0:T(8,128)S(1)}, f32[96,128]{1,0:T(8,128)S(1)}, u32[]{:S(2)}, u32[]{:S(2)}) collective-permute-start(f32[96,128]{1,0:T(8,128)S(1)} %get-tuple-element.50), channel_id=1, source_target_pairs={{0,6},{1,7},{2,4},{3,5},{4,2},{5,3},{6,0},{7,1},{8,14},{9,15},{10,... | collective-permute-start | bytes 147464 | tf_op jit(solution)/shard_map/ppermute | solution.py:486
  15.1 7.5 %collective-permute-start.5 = (f32[96,128]{1,0:T(8,128)S(1)}, f32[96,128]{1,0:T(8,128)S(1)}, u32[]{:S(2)}, u32[]{:S(2)}) collective-permute-start(f32[96,128]{1,0:T(8,128)S(1)} %get-tuple-element.51), channel_id=1, source_target_pairs={{0,5},{1,4},{2,7},{3,6},{4,1},{5,0},{6,3},{7,2},{8,13},{9,12},{10,... | collective-permute-start | bytes 147464 | tf_op jit(solution)/shard_map/ppermute | solution.py:486
  15.5 11.4 %collective-permute-start.3 = (f32[120,128]{1,0:T(8,128)S(1)}, f32[120,128]{1,0:T(8,128)S(1)}, u32[]{:S(2)}, u32[]{:S(2)}) collective-permute-start(f32[120,128]{1,0:T(8,128)S(1)} %get-tuple-element.49), channel_id=1, source_target_pairs={{0,7},{1,6},{2,5},{3,4},{4,3},{5,2},{6,1},{7,0},{8,15},{9,14},{10,... | collective-permute-start | bytes 184328 | tf_op jit(solution)/shard_map/ppermute | solution.py:486
  17.9 9.0 %collective-permute-start.7 = (f32[120,128]{1,0:T(8,128)S(1)}, f32[120,128]{1,0:T(8,128)S(1)}, u32[]{:S(2)}, u32[]{:S(2)}) collective-permute-start(f32[120,128]{1,0:T(8,128)S(1)} %get-tuple-element.53), channel_id=1, source_target_pairs={{0,3},{1,2},{2,1},{3,0},{4,7},{5,6},{6,5},{7,4},{8,11},{9,10},{10,... | collective-permute-start | bytes 184328 | tf_op jit(solution)/shard_map/ppermute | solution.py:486
  20.5 6.4 %collective-permute-start.9 = (f32[120,128]{1,0:T(8,128)S(1)}, f32[120,128]{1,0:T(8,128)S(1)}, u32[]{:S(2)}, u32[]{:S(2)}) collective-permute-start(f32[120,128]{1,0:T(8,128)S(1)} %get-tuple-element.55), channel_id=1, source_target_pairs={{0,1},{1,0},{2,3},{3,2},{4,5},{5,4},{6,7},{7,6},{8,9},{9,8},{10,11... | collective-permute-start | bytes 184328 | tf_op jit(solution)/shard_map/ppermute | solution.py:486
  21.0 5.4 %collective-permute-start.6 = (f32[96,128]{1,0:T(8,128)S(1)}, f32[96,128]{1,0:T(8,128)S(1)}, u32[]{:S(2)}, u32[]{:S(2)}) collective-permute-start(f32[96,128]{1,0:T(8,128)S(1)} %get-tuple-element.52), channel_id=1, source_target_pairs={{0,4},{1,5},{2,6},{3,7},{4,0},{5,1},{6,2},{7,3},{8,12},{9,13},{10,... | collective-permute-start | bytes 147464 | tf_op jit(solution)/shard_map/ppermute | solution.py:486
  22.6 4.3 %collective-permute-start.8 = (f32[96,128]{1,0:T(8,128)S(1)}, f32[96,128]{1,0:T(8,128)S(1)}, u32[]{:S(2)}, u32[]{:S(2)}) collective-permute-start(f32[96,128]{1,0:T(8,128)S(1)} %get-tuple-element.54), channel_id=1, source_target_pairs={{0,2},{1,3},{2,0},{3,1},{4,6},{5,7},{6,4},{7,5},{8,10},{9,11},{10,... | collective-permute-start | bytes 147464 | tf_op jit(solution)/shard_map/ppermute | solution.py:486
  30.1 8.0 %collective-permute-start.10 = (f32[96,128]{1,0:T(8,128)S(1)}, f32[96,128]{1,0:T(8,128)S(1)}, u32[]{:S(2)}, u32[]{:S(2)}) collective-permute-start(f32[96,128]{1,0:T(8,128)S(1)} %get-tuple-element.67), channel_id=1, source_target_pairs={{0,7},{1,6},{2,5},{3,4},{4,3},{5,2},{6,1},{7,0},{8,15},{9,14},{10,... | collective-permute-start | bytes 147464 | tf_op jit(solution)/shard_map/ppermute | solution.py:486
  32.7 8.1 %collective-permute-start.11 = (f32[96,128]{1,0:T(8,128)S(1)}, f32[96,128]{1,0:T(8,128)S(1)}, u32[]{:S(2)}, u32[]{:S(2)}) collective-permute-start(f32[96,128]{1,0:T(8,128)S(1)} %get-tuple-element.68), channel_id=1, source_target_pairs={{0,6},{1,7},{2,4},{3,5},{4,2},{5,3},{6,0},{7,1},{8,14},{9,15},{10,... | collective-permute-start | bytes 147464 | tf_op jit(solution)/shard_map/ppermute | solution.py:486
  35.0 6.3 %collective-permute-start.12 = (f32[96,128]{1,0:T(8,128)S(1)}, f32[96,128]{1,0:T(8,128)S(1)}, u32[]{:S(2)}, u32[]{:S(2)}) collective-permute-start(f32[96,128]{1,0:T(8,128)S(1)} %get-tuple-element.69), channel_id=1, source_target_pairs={{0,5},{1,4},{2,7},{3,6},{4,1},{5,0},{6,3},{7,2},{8,13},{9,12},{10,... | collective-permute-start | bytes 147464 | tf_op jit(solution)/shard_map/ppermute | solution.py:486
  35.0 6.9 %collective-permute-start.13 = (f32[96,128]{1,0:T(8,128)S(1)}, f32[96,128]{1,0:T(8,128)S(1)}, u32[]{:S(2)}, u32[]{:S(2)}) collective-permute-start(f32[96,128]{1,0:T(8,128)S(1)} %get-tuple-element.70), channel_id=1, source_target_pairs={{0,4},{1,5},{2,6},{3,7},{4,0},{5,1},{6,2},{7,3},{8,12},{9,13},{10,... | collective-permute-start | bytes 147464 | tf_op jit(solution)/shard_map/ppermute | solution.py:486
  37.8 5.0 %collective-permute-start.14 = (f32[96,128]{1,0:T(8,128)S(1)}, f32[96,128]{1,0:T(8,128)S(1)}, u32[]{:S(2)}, u32[]{:S(2)}) collective-permute-start(f32[96,128]{1,0:T(8,128)S(1)} %get-tuple-element.71), channel_id=1, source_target_pairs={{0,3},{1,2},{2,1},{3,0},{4,7},{5,6},{6,5},{7,4},{8,11},{9,10},{10,... | collective-permute-start | bytes 147464 | tf_op jit(solution)/shard_map/ppermute | solution.py:486
  38.0 5.4 %collective-permute-start.15 = (f32[96,128]{1,0:T(8,128)S(1)}, f32[96,128]{1,0:T(8,128)S(1)}, u32[]{:S(2)}, u32[]{:S(2)}) collective-permute-start(f32[96,128]{1,0:T(8,128)S(1)} %get-tuple-element.72), channel_id=1, source_target_pairs={{0,2},{1,3},{2,0},{3,1},{4,6},{5,7},{6,4},{7,5},{8,10},{9,11},{10,... | collective-permute-start | bytes 147464 | tf_op jit(solution)/shard_map/ppermute | solution.py:486
  40.9 4.1 %collective-permute-start.16 = (f32[96,128]{1,0:T(8,128)S(1)}, f32[96,128]{1,0:T(8,128)S(1)}, u32[]{:S(2)}, u32[]{:S(2)}) collective-permute-start(f32[96,128]{1,0:T(8,128)S(1)} %get-tuple-element.73), channel_id=1, source_target_pairs={{0,1},{1,0},{2,3},{3,2},{4,5},{5,4},{6,7},{7,6},{8,9},{9,8},{10,11... | collective-permute-start | bytes 147464 | tf_op jit(solution)/shard_map/ppermute | solution.py:486
  45.0 3.3 %copy-start.2 = (f32[16]{0:T(128)S(1)}, f32[16]{0:T(128)}, u32[]{:S(2)}) copy-start(f32[16]{0:T(128)} %refs_8_.1) | copy-start | bytes 196
  45.0 3.3 %copy-start.3 = (f32[16]{0:T(128)S(1)}, f32[16]{0:T(128)}, u32[]{:S(2)}) copy-start(f32[16]{0:T(128)} %refs_9_.1) | copy-start | bytes 196
  45.8 1.4 %collective-permute-start.18 = (f32[96,256]{1,0:T(8,128)S(1)}, f32[96,256]{1,0:T(8,128)S(1)}, u32[]{:S(2)}, u32[]{:S(2)}) collective-permute-start(f32[96,256]{1,0:T(8,128)S(1)} %get-tuple-element.78), channel_id=1, source_target_pairs={{0,8},{8,0},{16,24},{24,16},{1,9},{9,1},{17,25},{25,17},{2,10},{10... | collective-permute-start | bytes 294920 | tf_op jit(solution)/shard_map/ppermute | solution.py:486
  45.9 3.5 %collective-permute-start.17 = (f32[96,256]{1,0:T(8,128)S(1)}, f32[96,256]{1,0:T(8,128)S(1)}, u32[]{:S(2)}, u32[]{:S(2)}) collective-permute-start(f32[96,256]{1,0:T(8,128)S(1)} %get-tuple-element.76), channel_id=1, source_target_pairs={{0,8},{8,0},{16,24},{24,16},{1,9},{9,1},{17,25},{25,17},{2,10},{10... | collective-permute-start | bytes 294920 | tf_op jit(solution)/shard_map/ppermute | solution.py:486
  47.2 4.9 %collective-permute-start.19 = (f32[96,256]{1,0:T(8,128)S(1)}, f32[96,256]{1,0:T(8,128)S(1)}, u32[]{:S(2)}, u32[]{:S(2)}) collective-permute-start(f32[96,256]{1,0:T(8,128)S(1)} %add.3), channel_id=1, source_target_pairs={{0,16},{8,24},{16,0},{24,8},{1,17},{9,25},{17,1},{25,9},{2,18},{10... | collective-permute-start | bytes 294920 | tf_op jit(solution)/shard_map/ppermute | solution.py:486

commit v10 on v9

--- a/solution.py
+++ b/solution.py
@@ -94,9 +94,9 @@
     return forward[None], inverse[None]
 
 
-def load_kernel(order_x, order_y, place, *refs):
+def load_kernel(order_x, order_y, *refs):
     table_ref, forward_ref, inverse_ref, table, forward, inverse, sem = refs
-    gx, gy = place[0], place[1]
+    gx, gy = lax.axis_index("gx"), lax.axis_index("gy")
     mine_x = gx if table_ref.shape[0] > 1 else 0
     mine_y = gy if forward_ref.shape[0] > 1 else 0
     lanes = table_ref.shape[5]
@@ -196,9 +196,10 @@
 
 
 def lines_kernel(count_x, order_y, *refs):
-    raw_refs, operands = refs[:count_x], refs[count_x : count_x + 5]
-    first_ref, last_ref, region_ref, place, table = operands
-    out_refs, (region, sem) = refs[count_x + 5 : -2], refs[-2:]
+    raw_refs, operands = refs[:count_x], refs[count_x : count_x + 4]
+    first_ref, last_ref, region_ref, table = operands
+    gy = lax.axis_index("gy")
+    out_refs, (region, sem) = refs[count_x + 4 : -2], refs[-2:]
     fetch = pltpu.make_async_copy(region_ref, region, sem)
     fetch.start()
     units = [directions(raw_ref[0], raw_ref[1]) for raw_ref in raw_refs]
@@ -216,7 +217,7 @@
     for spot, (number, out_ref) in enumerate(zip(order_y, out_refs)):
         out_ref[: 3 * rows] = total[:, spot * lanes : (spot + 1) * lanes]
         if number in meeting(len(order_y)):
-            up = lax.bitwise_xor(place[1], number) > place[1]
+            up = lax.bitwise_xor(gy, number) > gy
             out_ref[3 * rows :] = jnp.where(up, last_ref[...], first_ref[...])
 
 
@@ -342,7 +343,7 @@
                 back_ref[pl.ds(pl.multiple_of(2 * double + index * chunk, chunk), chunk), spot] = high
         return carry
 
-    lax.fori_loop(0, double // chunk, step, 0)
+    lax.fori_loop(0, double // chunk, step, 0, unroll=True)
     back = dot(inverse_ref[...], back_ref[...])
     for plane in range(planes):
         part = slice(plane * lanes, (plane + 1) * lanes)
@@ -355,10 +356,10 @@
 
 def exchange_kernel(order_x, count_y, *refs):
     count_x, numbers = len(order_x), meeting(count_y)
-    raw_refs, edge_refs, (place, ms_ref, aex_ref) = refs[:count_x], refs[count_x:-6], refs[-6:-3]
+    raw_refs, edge_refs, (ms_ref, aex_ref) = refs[:count_x], refs[count_x:-5], refs[-5:-3]
     exchange_ref, unit_ref, raw_ref = refs[-3:]
     depth, height, width = raw_ref.shape[2:]
-    gx, gy = place[0], place[1]
+    gx, gy = lax.axis_index("gx"), lax.axis_index("gy")
 
     def row_beside(field, other):
         value = None
@@ -532,7 +533,6 @@
     lines = 3 * depth * height
     whole_y = count_y * height
 
-    place = jnp.stack([gx, gy]).astype(jnp.int32)
     cells = f32(3, depth, height, width)
     order_x, order_y = list(range(count_x)), list(range(count_y - 1, -1, -1))
     table = line_table(count_x, count_y, width, rows)
@@ -566,8 +566,8 @@
             pltpu.VMEM(sources[1].shape[1:], jnp.bfloat16),
             pltpu.VMEM(sources[2].shape[1:], jnp.bfloat16),
         ],
-        [smem] + [hbm] * 3,
-        (place, *sources),
+        [hbm] * 3,
+        tuple(sources),
         scratch=(pltpu.SemaphoreType.DMA((2 + count_x * count_y,)),),
         name="load",
     )
@@ -584,8 +584,8 @@
     spectrum = call(
         functools.partial(lines_kernel, count_x, order_y),
         [f32(lines + (edge_rows if n in meeting(count_y) else 0), lanes) for n in order_y],
-        [vmem] * (count_x + 2) + [hbm, smem, vmem],
-        (*gathered, first, last, ms_region, place, held(table)),
+        [vmem] * (count_x + 2) + [hbm, vmem],
+        (*gathered, first, last, ms_region, held(table)),
         scratch=(pltpu.SMEM(ms_region.shape, jnp.float32), pltpu.SemaphoreType.DMA),
         flops=transform_flops,
         name="lines",
@@ -625,8 +625,8 @@
     exchange, unit = call(
         functools.partial(exchange_kernel, order_x, count_y),
         [cells, cells],
-        [vmem] * (count_x + len(edges)) + [smem] * 3,
-        (*gathered, *edges, place, ms_region, aex_region),
+        [vmem] * (count_x + len(edges)) + [smem] * 2,
+        (*gathered, *edges, ms_region, aex_region),
         scratch=(pltpu.VMEM((count_x, 3, depth, height, width), jnp.float32),),
         flops=300 * depth * height * width,
         name="exchange",

time: 53 us -> 50.6 us (0.955)
  Pallas kernels: 14.3 us -> 11.9 us
  starting transfers between devices: 26.9 us -> 27.5 us
    pallas_call x9, Pallas kernels: 14.3 us -> 11.9 us  [call(): pl.pallas_call(body, out_shape=out, in_specs=ins, out_specs=[vmem] * len(...]
    ppermute x20, starting transfers between devices: 26.9 us -> 27.5 us  [swapped(): return lax.ppermute(chunk, axis, [(i, i ^ number) for i in range(devices)])]
  transfers between devices with their start and end apart: 20 -> 20, of which waited for: 9 -> 10; matrix products, arithmetic and copies ran while one was open for 0% -> 0% of each run, Pallas kernels for 13% -> 12%
where the time goes in v10:
time: 50.6 us; the launch traced here: 50.4 us
  starting transfers between devices  27.5 us (54%)
  Pallas kernels  11.9 us (24%)
  waiting for transfers between devices  10.2 us (20%)
  between operations  0.76 us (2%)
    ppermute x20, starting transfers between devices, swapped(): return lax.ppermute(chunk, axis, [(i, i ^ number) for i in range(devices)])  27.5 us
    pallas_call x9, Pallas kernels, call(): pl.pallas_call(body, out_shape=out, in_specs=ins, out_specs=[vmem] * len(...  11.9 us
    ppermute x20, waiting for transfers between devices, swapped(): return lax.ppermute(chunk, axis, [(i, i ^ number) for i in range(devices)])  10.2 us
  transfers between devices with their start and end apart: 20, of which 10 were waited for; matrix products, arithmetic and copies ran while one was open for 0% of the time, Pallas kernels for 12%

profile of v10, /device:TPU:0, one launch (start us, length us, event | category | flops | bytes accessed | tf_op | source)
XLA Modules:
  0.0 50.4 jit_solution(12772704999178009990)
XLA Ops:
  0.6 0.8 %pack.1 = (f32[3,4,8,256]{3,2,1,0:T(8,128)S(1)}, f32[24,128]{1,0:T(8,128)S(1)}, f32[24,128]{1,0:T(8,128)S(1)}) custom-call(f32[4,8,256]{2,1,0:T(8,128)} %theta_ref.1, f32[4,8,256]{2,1,0:T(8,128)} %phi_ref.1, s32[4,8,256]{2,1,0:T(8,128)} %labels_ref.1), custom_call_target="tpu_custom_call" | custom-call | bytes 221184 | tf_op jit(solution)/shard_map/pack/pallas_call | solution.py:469
  1.5 3.0 %collective-permute-start.1 = (f32[3,4,8,256]{3,2,1,0:T(8,128)S(1)}, f32[3,4,8,256]{3,2,1,0:T(8,128)S(1)}, u32[]{:S(2)}, u32[]{:S(2)}) collective-permute-start(f32[3,4,8,256]{3,2,1,0:T(8,128)S(1)} %get-tuple-element.43.refs_0_), channel_id=1, source_target_pairs={{0,16},{8,24},{16,0},{24,8},{1,17},{9,25},{17,1},{25,9},{2,18},{10... | collective-permute-start | bytes 294920 | tf_op jit(solution)/shard_map/ppermute | solution.py:487
  4.5 2.6 %load.1 = (bf16[2,4,256,1024]{3,2,1,0:T(8,128)(2,1)S(1)}, bf16[128,384]{1,0:T(8,128)(2,1)S(1)}, bf16[128,384]{1,0:T(8,128)(2,1)S(1)}) custom-call(bf16[4,8,2,4,256,128]{5,4,3,2,1,0:T(8,128)(2,1)} %constant.8.clone.refs_0_, bf16[8,128,384]{2,1,0:T(8,128)(2,1)} %constant.9.clone.refs_1_, bf16[8,128,384]{2,1,0:T(8,128)(2,1)} %constant.10.clone.refs_2_), custom_call_target="tpu_custom_call" | custom-call | bytes 22740992 | tf_op jit(solution)/shard_map/load/pallas_call | solution.py:469
  7.3 0.4 collective-permute-start.2
  7.7 0.9 %collective-permute-done.2.refs_3_ = f32[3,4,8,256]{3,2,1,0:T(8,128)S(1)} collective-permute-done((f32[3,4,8,256]{3,2,1,0:T(8,128)S(1)}, f32[3,4,8,256]{3,2,1,0:T(8,128)S(1)}, u32[]{:S(2)}, u32[]{:S(2)}) %collective-permute-start.2) | collective-permute-done | bytes 98336 | tf_op jit(solution)/shard_map/ppermute | solution.py:487
  8.7 1.6 %lines.1 = (f32[120,128]{1,0:T(8,128)S(1)}, f32[96,128]{1,0:T(8,128)S(1)}, f32[96,128]{1,0:T(8,128)S(1)}, f32[96,128]{1,0:T(8,128)S(1)}, f32[120,128]{1,0:T(8,12...) custom-call(f32[3,4,8,256]{3,2,1,0:T(8,128)S(1)} %get-tuple-element.43.refs_0_, ...), custom_call_target="tpu_custom_call" | custom-call | flops 603979776 | bytes 5042240 | tf_op jit(solution)/shard_map/lines/pallas_call | solution.py:469
  10.3 3.9 %collective-permute-start.4 = (f32[96,128]{1,0:T(8,128)S(1)}, f32[96,128]{1,0:T(8,128)S(1)}, u32[]{:S(2)}, u32[]{:S(2)}) collective-permute-start(f32[96,128]{1,0:T(8,128)S(1)} %get-tuple-element.50), channel_id=1, source_target_pairs={{0,6},{1,7},{2,4},{3,5},{4,2},{5,3},{6,0},{7,1},{8,14},{9,15},{10,... | collective-permute-start | bytes 147464 | tf_op jit(solution)/shard_map/ppermute | solution.py:487
  14.2 0.4 collective-permute-start.5
  14.6 2.4 %collective-permute-start.3 = (f32[120,128]{1,0:T(8,128)S(1)}, f32[120,128]{1,0:T(8,128)S(1)}, u32[]{:S(2)}, u32[]{:S(2)}) collective-permute-start(f32[120,128]{1,0:T(8,128)S(1)} %get-tuple-element.49), channel_id=1, source_target_pairs={{0,7},{1,6},{2,5},{3,4},{4,3},{5,2},{6,1},{7,0},{8,15},{9,14},{10,... | collective-permute-start | bytes 184328 | tf_op jit(solution)/shard_map/ppermute | solution.py:487
  17.0 2.5 %collective-permute-start.7 = (f32[120,128]{1,0:T(8,128)S(1)}, f32[120,128]{1,0:T(8,128)S(1)}, u32[]{:S(2)}, u32[]{:S(2)}) collective-permute-start(f32[120,128]{1,0:T(8,128)S(1)} %get-tuple-element.53), channel_id=1, source_target_pairs={{0,3},{1,2},{2,1},{3,0},{4,7},{5,6},{6,5},{7,4},{8,11},{9,10},{10,... | collective-permute-start | bytes 184328 | tf_op jit(solution)/shard_map/ppermute | solution.py:487
  19.6 0.5 %collective-permute-start.9 = (f32[120,128]{1,0:T(8,128)S(1)}, f32[120,128]{1,0:T(8,128)S(1)}, u32[]{:S(2)}, u32[]{:S(2)}) collective-permute-start(f32[120,128]{1,0:T(8,128)S(1)} %get-tuple-element.55), channel_id=1, source_target_pairs={{0,1},{1,0},{2,3},{3,2},{4,5},{5,4},{6,7},{7,6},{8,9},{9,8},{10,11... | collective-permute-start | bytes 184328 | tf_op jit(solution)/shard_map/ppermute | solution.py:487
  20.1 1.0 %collective-permute-start.6 = (f32[96,128]{1,0:T(8,128)S(1)}, f32[96,128]{1,0:T(8,128)S(1)}, u32[]{:S(2)}, u32[]{:S(2)}) collective-permute-start(f32[96,128]{1,0:T(8,128)S(1)} %get-tuple-element.52), channel_id=1, source_target_pairs={{0,4},{1,5},{2,6},{3,7},{4,0},{5,1},{6,2},{7,3},{8,12},{9,13},{10,... | collective-permute-start | bytes 147464 | tf_op jit(solution)/shard_map/ppermute | solution.py:487
  21.0 0.6 %collective-permute-done.5.refs_2_ = f32[96,128]{1,0:T(8,128)S(1)} collective-permute-done((f32[96,128]{1,0:T(8,128)S(1)}, f32[96,128]{1,0:T(8,128)S(1)}, u32[]{:S(2)}, u32[]{:S(2)}) %collective-permute-start.5) | collective-permute-done | bytes 49184 | tf_op jit(solution)/shard_map/ppermute | solution.py:487
  21.6 1.6 %tensor.1.refs_8_ = bf16[48,128,128]{2,1,0:T(8,128)(2,1)S(1)} custom-call(bf16[48,64,128]{2,1,0:T(8,128)(2,1)S(1)} %bitcast.1, bf16[64,128]{1,0:T(8,128)(2,1)S(1)} %copy-done.1), custom_call_target="tpu_custom_call" | custom-call | flops 100663296 | bytes 2375680 | tf_op jit(solution)/shard_map/tensor/pallas_call | solution.py:469
  23.2 2.3 %collective-permute-done.6.refs_3_ = f32[96,128]{1,0:T(8,128)S(1)} collective-permute-done((f32[96,128]{1,0:T(8,128)S(1)}, f32[96,128]{1,0:T(8,128)S(1)}, u32[]{:S(2)}, u32[]{:S(2)}) %collective-permute-start.6) | collective-permute-done | bytes 49184 | tf_op jit(solution)/shard_map/ppermute | solution.py:487
  25.5 0.5 collective-permute-done.8.refs_5_
  26.0 1.7 %waves.1 = (f32[96,128]{1,0:T(8,128)S(1)}, f32[96,128]{1,0:T(8,128)S(1)}, f32[96,128]{1,0:T(8,128)S(1)}, f32[96,128]{1,0:T(8,128)S(1)}, f32[96,128]{1,0:T(8,128)...) custom-call(f32[120,128]{1,0:T(8,128)S(1)} %collective-permute-done.3.refs_0_.refs_6_, ...), custom_call_target="tpu_custom_call" | custom-call | flops 125829120 | bytes 2592768 | tf_op jit(solution)/shard_map/waves/pallas_call | solution.py:469
  27.8 2.5 %collective-permute-start.10 = (f32[96,128]{1,0:T(8,128)S(1)}, f32[96,128]{1,0:T(8,128)S(1)}, u32[]{:S(2)}, u32[]{:S(2)}) collective-permute-start(f32[96,128]{1,0:T(8,128)S(1)} %get-tuple-element.67), channel_id=1, source_target_pairs={{0,7},{1,6},{2,5},{3,4},{4,3},{5,2},{6,1},{7,0},{8,15},{9,14},{10,... | collective-permute-start | bytes 147464 | tf_op jit(solution)/shard_map/ppermute | solution.py:487
  30.2 2.4 %collective-permute-start.11 = (f32[96,128]{1,0:T(8,128)S(1)}, f32[96,128]{1,0:T(8,128)S(1)}, u32[]{:S(2)}, u32[]{:S(2)}) collective-permute-start(f32[96,128]{1,0:T(8,128)S(1)} %get-tuple-element.68), channel_id=1, source_target_pairs={{0,6},{1,7},{2,4},{3,5},{4,2},{5,3},{6,0},{7,1},{8,14},{9,15},{10,... | collective-permute-start | bytes 147464 | tf_op jit(solution)/shard_map/ppermute | solution.py:487
  32.6 2.9 %collective-permute-start.13 = (f32[96,128]{1,0:T(8,128)S(1)}, f32[96,128]{1,0:T(8,128)S(1)}, u32[]{:S(2)}, u32[]{:S(2)}) collective-permute-start(f32[96,128]{1,0:T(8,128)S(1)} %get-tuple-element.70), channel_id=1, source_target_pairs={{0,4},{1,5},{2,6},{3,7},{4,0},{5,1},{6,2},{7,3},{8,12},{9,13},{10,... | collective-permute-start | bytes 147464 | tf_op jit(solution)/shard_map/ppermute | solution.py:487
  35.5 2.9 %collective-permute-start.15 = (f32[96,128]{1,0:T(8,128)S(1)}, f32[96,128]{1,0:T(8,128)S(1)}, u32[]{:S(2)}, u32[]{:S(2)}) collective-permute-start(f32[96,128]{1,0:T(8,128)S(1)} %get-tuple-element.72), channel_id=1, source_target_pairs={{0,2},{1,3},{2,0},{3,1},{4,6},{5,7},{6,4},{7,5},{8,10},{9,11},{10,... | collective-permute-start | bytes 147464 | tf_op jit(solution)/shard_map/ppermute | solution.py:487
  38.5 0.5 %collective-permute-start.16 = (f32[96,128]{1,0:T(8,128)S(1)}, f32[96,128]{1,0:T(8,128)S(1)}, u32[]{:S(2)}, u32[]{:S(2)}) collective-permute-start(f32[96,128]{1,0:T(8,128)S(1)} %get-tuple-element.73), channel_id=1, source_target_pairs={{0,1},{1,0},{2,3},{3,2},{4,5},{5,4},{6,7},{7,6},{8,9},{9,8},{10,11... | collective-permute-start | bytes 147464 | tf_op jit(solution)/shard_map/ppermute | solution.py:487
  39.1 1.3 %collective-permute-done.14.refs_4_ = f32[96,128]{1,0:T(8,128)S(1)} collective-permute-done((f32[96,128]{1,0:T(8,128)S(1)}, f32[96,128]{1,0:T(8,128)S(1)}, u32[]{:S(2)}, u32[]{:S(2)}) %collective-permute-start.14) | collective-permute-done | bytes 49184 | tf_op jit(solution)/shard_map/ppermute | solution.py:487
  40.5 0.6 %collective-permute-done.15.refs_5_ = f32[96,128]{1,0:T(8,128)S(1)} collective-permute-done((f32[96,128]{1,0:T(8,128)S(1)}, f32[96,128]{1,0:T(8,128)S(1)}, u32[]{:S(2)}, u32[]{:S(2)}) %collective-permute-start.15) | collective-permute-done | bytes 49184 | tf_op jit(solution)/shard_map/ppermute | solution.py:487
  41.0 1.5 %collective-permute-done.16.refs_6_ = f32[96,128]{1,0:T(8,128)S(1)} collective-permute-done((f32[96,128]{1,0:T(8,128)S(1)}, f32[96,128]{1,0:T(8,128)S(1)}, u32[]{:S(2)}, u32[]{:S(2)}) %collective-permute-start.16) | collective-permute-done | bytes 49184 | tf_op jit(solution)/shard_map/ppermute | solution.py:487
  42.6 0.8 %back_across.1 = (f32[96,256]{1,0:T(8,128)S(1)}, f32[96,256]{1,0:T(8,128)S(1)}) custom-call(f32[96,128]{1,0:T(8,128)S(1)} %collective-permute-done.10.refs_0_, f32[96,128]{1,0:T(8,128)S(1)} %collective-permute-done.11.refs_1_, f32[96,128]{1,0:T(8,128)S(1)} %collective-permute-done.12.refs_2_, f32[96,128]{1,0:T(8,128)S(1)} %collective-permute-done.13.refs_3_, ...), custom_call_target="tpu_custom_call" | custom-call | flops 301989888 | bytes 4784128 | tf_op jit(solution)/shard_map/back_across/pallas_call | solution.py:469
  43.4 0.5 collective-permute-start.17
  43.9 0.8 %back_within.1 = (f32[96,256]{1,0:T(8,128)S(1)}, f32[96,256]{1,0:T(8,128)S(1)}) custom-call(f32[96,128]{1,0:T(8,128)S(1)} %collective-permute-done.10.refs_0_, f32[96,128]{1,0:T(8,128)S(1)} %collective-permute-done.11.refs_1_, f32[96,128]{1,0:T(8,128)S(1)} %collective-permute-done.12.refs_2_, f32[96,128]{1,0:T(8,128)S(1)} %collective-permute-done.13.refs_3_, ...), custom_call_target="tpu_custom_call" | custom-call | flops 301989888 | bytes 4784128 | tf_op jit(solution)/shard_map/back_within/pallas_call | solution.py:469
  44.8 1.6 %collective-permute-start.19 = (f32[96,256]{1,0:T(8,128)S(1)}, f32[96,256]{1,0:T(8,128)S(1)}, u32[]{:S(2)}, u32[]{:S(2)}) collective-permute-start(f32[96,256]{1,0:T(8,128)S(1)} %add.3), channel_id=1, source_target_pairs={{0,16},{8,24},{16,0},{24,8},{1,17},{9,25},{17,1},{25,9},{2,18},{10... | collective-permute-start | bytes 294920 | tf_op jit(solution)/shard_map/ppermute | solution.py:487
  46.3 1.1 %exchange.1 = (f32[3,4,8,256]{3,2,1,0:T(8,128)S(1)}, f32[3,4,8,256]{3,2,1,0:T(8,128)S(1)}) custom-call(f32[3,4,8,256]{3,2,1,0:T(8,128)S(1)} %get-tuple-element.43.refs_0_, f32[3,4,8,256]{3,2,1,0:T(8,128)S(1)} %collective-permute-done.refs_1_, f32[3,4,8,256]{3,2,1,0:T(8,128)S(1)} %collective-permute-done.1.refs_2_, ...), custom_call_target="tpu_custom_call" | custom-call | flops 2457600 | bytes 774272 | tf_op jit(solution)/shard_map/exchange/pallas_call | solution.py:469
  47.5 2.2 %collective-permute-done.19.refs_2_ = f32[96,256]{1,0:T(8,128)S(1)} collective-permute-done((f32[96,256]{1,0:T(8,128)S(1)}, f32[96,256]{1,0:T(8,128)S(1)}, u32[]{:S(2)}, u32[]{:S(2)}) %collective-permute-start.19) | collective-permute-done | bytes 98336 | tf_op jit(solution)/shard_map/ppermute | solution.py:487
  49.7 0.7 %predict.1 = (f32[3,4,8,256]{3,2,1,0:T(8,128)}, f32[3,4,8,256]{3,2,1,0:T(8,128)}) custom-call(f32[96,256]{1,0:T(8,128)S(1)} %get-tuple-element.75.refs_0_, f32[96,256]{1,0:T(8,128)S(1)} %collective-permute-done.17.refs_1_, f32[96,256]{1,0:T(8,128)S(1)} %collective-permute-done.19.refs_2_, f32[3,4,8,256]{3,2,1,0:T(8,128)S(1)} %get-tuple-element.82.refs_3_, ...), custom_call_target="tpu_custom_call" | custom-call | flops 491520 | bytes 688128 | tf_op jit(solution)/shard_map/predict/pallas_call | solution.py:469
  (26 shorter events, 0.5 us)
Async XLA Ops:
  1.5 5.8 %collective-permute-start.1 = (f32[3,4,8,256]{3,2,1,0:T(8,128)S(1)}, f32[3,4,8,256]{3,2,1,0:T(8,128)S(1)}, u32[]{:S(2)}, u32[]{:S(2)}) collective-permute-start(f32[3,4,8,256]{3,2,1,0:T(8,128)S(1)} %get-tuple-element.43.refs_0_), channel_id=1, source_target_pairs={{0,16},{8,24},{16,0},{24,8},{1,17},{9,25},{17,1},{25,9},{2,18},{10... | collective-permute-start | bytes 294920 | tf_op jit(solution)/shard_map/ppermute | solution.py:487
  4.5 3.2 %collective-permute-start = (f32[3,4,8,256]{3,2,1,0:T(8,128)S(1)}, f32[3,4,8,256]{3,2,1,0:T(8,128)S(1)}, u32[]{:S(2)}, u32[]{:S(2)}) collective-permute-start(f32[3,4,8,256]{3,2,1,0:T(8,128)S(1)} %get-tuple-element.43.refs_0_), channel_id=1, source_target_pairs={{0,8},{8,0},{16,24},{24,16},{1,9},{9,1},{17,25},{25,17},{2,10},{10... | collective-permute-start | bytes 294920 | tf_op jit(solution)/shard_map/ppermute | solution.py:487
  7.1 14.5 %copy-start = (bf16[6,8,64,128]{3,2,1,0:T(8,128)(2,1)S(1)}, bf16[6,8,64,128]{3,2,1,0:T(8,128)(2,1)}, u32[]{:S(2)}) copy-start(bf16[6,8,64,128]{3,2,1,0:T(8,128)(2,1)} %param.15) | copy-start | bytes 2359300
  7.1 14.5 %copy-start.1 = (bf16[64,128]{1,0:T(8,128)(2,1)S(1)}, bf16[64,128]{1,0:T(8,128)(2,1)}, u32[]{:S(2)}) copy-start(bf16[64,128]{1,0:T(8,128)(2,1)} %constant.11.clone.twice_ref) | copy-start | bytes 49156
  7.3 1.4 %collective-permute-start.2 = (f32[3,4,8,256]{3,2,1,0:T(8,128)S(1)}, f32[3,4,8,256]{3,2,1,0:T(8,128)S(1)}, u32[]{:S(2)}, u32[]{:S(2)}) collective-permute-start(f32[3,4,8,256]{3,2,1,0:T(8,128)S(1)} %collective-permute-done.1.refs_2_), channel_id=1, source_target_pairs={{0,8},{8,0},{16,24},{24,16},{1,9},{9,1},{17,25},{25,17},{2,10},{10... | collective-permute-start | bytes 294920 | tf_op jit(solution)/shard_map/ppermute | solution.py:487
  10.3 9.8 %collective-permute-start.4 = (f32[96,128]{1,0:T(8,128)S(1)}, f32[96,128]{1,0:T(8,128)S(1)}, u32[]{:S(2)}, u32[]{:S(2)}) collective-permute-start(f32[96,128]{1,0:T(8,128)S(1)} %get-tuple-element.50), channel_id=1, source_target_pairs={{0,6},{1,7},{2,4},{3,5},{4,2},{5,3},{6,0},{7,1},{8,14},{9,15},{10,... | collective-permute-start | bytes 147464 | tf_op jit(solution)/shard_map/ppermute | solution.py:487
  14.2 7.4 %collective-permute-start.5 = (f32[96,128]{1,0:T(8,128)S(1)}, f32[96,128]{1,0:T(8,128)S(1)}, u32[]{:S(2)}, u32[]{:S(2)}) collective-permute-start(f32[96,128]{1,0:T(8,128)S(1)} %get-tuple-element.51), channel_id=1, source_target_pairs={{0,5},{1,4},{2,7},{3,6},{4,1},{5,0},{6,3},{7,2},{8,13},{9,12},{10,... | collective-permute-start | bytes 147464 | tf_op jit(solution)/shard_map/ppermute | solution.py:487
  14.6 11.4 %collective-permute-start.3 = (f32[120,128]{1,0:T(8,128)S(1)}, f32[120,128]{1,0:T(8,128)S(1)}, u32[]{:S(2)}, u32[]{:S(2)}) collective-permute-start(f32[120,128]{1,0:T(8,128)S(1)} %get-tuple-element.49), channel_id=1, source_target_pairs={{0,7},{1,6},{2,5},{3,4},{4,3},{5,2},{6,1},{7,0},{8,15},{9,14},{10,... | collective-permute-start | bytes 184328 | tf_op jit(solution)/shard_map/ppermute | solution.py:487
  17.0 9.0 %collective-permute-start.7 = (f32[120,128]{1,0:T(8,128)S(1)}, f32[120,128]{1,0:T(8,128)S(1)}, u32[]{:S(2)}, u32[]{:S(2)}) collective-permute-start(f32[120,128]{1,0:T(8,128)S(1)} %get-tuple-element.53), channel_id=1, source_target_pairs={{0,3},{1,2},{2,1},{3,0},{4,7},{5,6},{6,5},{7,4},{8,11},{9,10},{10,... | collective-permute-start | bytes 184328 | tf_op jit(solution)/shard_map/ppermute | solution.py:487
  19.6 6.4 %collective-permute-start.9 = (f32[120,128]{1,0:T(8,128)S(1)}, f32[120,128]{1,0:T(8,128)S(1)}, u32[]{:S(2)}, u32[]{:S(2)}) collective-permute-start(f32[120,128]{1,0:T(8,128)S(1)} %get-tuple-element.55), channel_id=1, source_target_pairs={{0,1},{1,0},{2,3},{3,2},{4,5},{5,4},{6,7},{7,6},{8,9},{9,8},{10,11... | collective-permute-start | bytes 184328 | tf_op jit(solution)/shard_map/ppermute | solution.py:487
  20.1 5.4 %collective-permute-start.6 = (f32[96,128]{1,0:T(8,128)S(1)}, f32[96,128]{1,0:T(8,128)S(1)}, u32[]{:S(2)}, u32[]{:S(2)}) collective-permute-start(f32[96,128]{1,0:T(8,128)S(1)} %get-tuple-element.52), channel_id=1, source_target_pairs={{0,4},{1,5},{2,6},{3,7},{4,0},{5,1},{6,2},{7,3},{8,12},{9,13},{10,... | collective-permute-start | bytes 147464 | tf_op jit(solution)/shard_map/ppermute | solution.py:487
  21.6 4.4 %collective-permute-start.8 = (f32[96,128]{1,0:T(8,128)S(1)}, f32[96,128]{1,0:T(8,128)S(1)}, u32[]{:S(2)}, u32[]{:S(2)}) collective-permute-start(f32[96,128]{1,0:T(8,128)S(1)} %get-tuple-element.54), channel_id=1, source_target_pairs={{0,2},{1,3},{2,0},{3,1},{4,6},{5,7},{6,4},{7,5},{8,10},{9,11},{10,... | collective-permute-start | bytes 147464 | tf_op jit(solution)/shard_map/ppermute | solution.py:487
  27.8 7.8 %collective-permute-start.10 = (f32[96,128]{1,0:T(8,128)S(1)}, f32[96,128]{1,0:T(8,128)S(1)}, u32[]{:S(2)}, u32[]{:S(2)}) collective-permute-start(f32[96,128]{1,0:T(8,128)S(1)} %get-tuple-element.67), channel_id=1, source_target_pairs={{0,7},{1,6},{2,5},{3,4},{4,3},{5,2},{6,1},{7,0},{8,15},{9,14},{10,... | collective-permute-start | bytes 147464 | tf_op jit(solution)/shard_map/ppermute | solution.py:487
  30.2 8.2 %collective-permute-start.11 = (f32[96,128]{1,0:T(8,128)S(1)}, f32[96,128]{1,0:T(8,128)S(1)}, u32[]{:S(2)}, u32[]{:S(2)}) collective-permute-start(f32[96,128]{1,0:T(8,128)S(1)} %get-tuple-element.68), channel_id=1, source_target_pairs={{0,6},{1,7},{2,4},{3,5},{4,2},{5,3},{6,0},{7,1},{8,14},{9,15},{10,... | collective-permute-start | bytes 147464 | tf_op jit(solution)/shard_map/ppermute | solution.py:487
  32.6 6.4 %collective-permute-start.12 = (f32[96,128]{1,0:T(8,128)S(1)}, f32[96,128]{1,0:T(8,128)S(1)}, u32[]{:S(2)}, u32[]{:S(2)}) collective-permute-start(f32[96,128]{1,0:T(8,128)S(1)} %get-tuple-element.69), channel_id=1, source_target_pairs={{0,5},{1,4},{2,7},{3,6},{4,1},{5,0},{6,3},{7,2},{8,13},{9,12},{10,... | collective-permute-start | bytes 147464 | tf_op jit(solution)/shard_map/ppermute | solution.py:487
  32.6 6.5 %collective-permute-start.13 = (f32[96,128]{1,0:T(8,128)S(1)}, f32[96,128]{1,0:T(8,128)S(1)}, u32[]{:S(2)}, u32[]{:S(2)}) collective-permute-start(f32[96,128]{1,0:T(8,128)S(1)} %get-tuple-element.70), channel_id=1, source_target_pairs={{0,4},{1,5},{2,6},{3,7},{4,0},{5,1},{6,2},{7,3},{8,12},{9,13},{10,... | collective-permute-start | bytes 147464 | tf_op jit(solution)/shard_map/ppermute | solution.py:487
  35.5 5.0 %collective-permute-start.14 = (f32[96,128]{1,0:T(8,128)S(1)}, f32[96,128]{1,0:T(8,128)S(1)}, u32[]{:S(2)}, u32[]{:S(2)}) collective-permute-start(f32[96,128]{1,0:T(8,128)S(1)} %get-tuple-element.71), channel_id=1, source_target_pairs={{0,3},{1,2},{2,1},{3,0},{4,7},{5,6},{6,5},{7,4},{8,11},{9,10},{10,... | collective-permute-start | bytes 147464 | tf_op jit(solution)/shard_map/ppermute | solution.py:487
  35.5 5.5 %collective-permute-start.15 = (f32[96,128]{1,0:T(8,128)S(1)}, f32[96,128]{1,0:T(8,128)S(1)}, u32[]{:S(2)}, u32[]{:S(2)}) collective-permute-start(f32[96,128]{1,0:T(8,128)S(1)} %get-tuple-element.72), channel_id=1, source_target_pairs={{0,2},{1,3},{2,0},{3,1},{4,6},{5,7},{6,4},{7,5},{8,10},{9,11},{10,... | collective-permute-start | bytes 147464 | tf_op jit(solution)/shard_map/ppermute | solution.py:487
  38.5 4.1 %collective-permute-start.16 = (f32[96,128]{1,0:T(8,128)S(1)}, f32[96,128]{1,0:T(8,128)S(1)}, u32[]{:S(2)}, u32[]{:S(2)}) collective-permute-start(f32[96,128]{1,0:T(8,128)S(1)} %get-tuple-element.73), channel_id=1, source_target_pairs={{0,1},{1,0},{2,3},{3,2},{4,5},{5,4},{6,7},{7,6},{8,9},{9,8},{10,11... | collective-permute-start | bytes 147464 | tf_op jit(solution)/shard_map/ppermute | solution.py:487
  42.6 3.8 %copy-start.2 = (f32[16]{0:T(128)S(1)}, f32[16]{0:T(128)}, u32[]{:S(2)}) copy-start(f32[16]{0:T(128)} %refs_7_.1) | copy-start | bytes 196
  42.6 3.8 %copy-start.3 = (f32[16]{0:T(128)S(1)}, f32[16]{0:T(128)}, u32[]{:S(2)}) copy-start(f32[16]{0:T(128)} %refs_8_.1) | copy-start | bytes 196
  43.4 1.4 %collective-permute-start.18 = (f32[96,256]{1,0:T(8,128)S(1)}, f32[96,256]{1,0:T(8,128)S(1)}, u32[]{:S(2)}, u32[]{:S(2)}) collective-permute-start(f32[96,256]{1,0:T(8,128)S(1)} %get-tuple-element.78), channel_id=1, source_target_pairs={{0,8},{8,0},{16,24},{24,16},{1,9},{9,1},{17,25},{25,17},{2,10},{10... | collective-permute-start | bytes 294920 | tf_op jit(solution)/shard_map/ppermute | solution.py:487
  43.4 4.0 %collective-permute-start.17 = (f32[96,256]{1,0:T(8,128)S(1)}, f32[96,256]{1,0:T(8,128)S(1)}, u32[]{:S(2)}, u32[]{:S(2)}) collective-permute-start(f32[96,256]{1,0:T(8,128)S(1)} %get-tuple-element.76), channel_id=1, source_target_pairs={{0,8},{8,0},{16,24},{24,16},{1,9},{9,1},{17,25},{25,17},{2,10},{10... | collective-permute-start | bytes 294920 | tf_op jit(solution)/shard_map/ppermute | solution.py:487
  44.8 4.9 %collective-permute-start.19 = (f32[96,256]{1,0:T(8,128)S(1)}, f32[96,256]{1,0:T(8,128)S(1)}, u32[]{:S(2)}, u32[]{:S(2)}) collective-permute-start(f32[96,256]{1,0:T(8,128)S(1)} %add.3), channel_id=1, source_target_pairs={{0,16},{8,24},{16,0},{24,8},{1,17},{9,25},{17,1},{25,9},{2,18},{10... | collective-permute-start | bytes 294920 | tf_op jit(solution)/shard_map/ppermute | solution.py:487

commit v11 on v10

--- a/solution.py
+++ b/solution.py
@@ -195,30 +195,40 @@
     return jnp.concatenate([ref[row : row + depth] for row in spots], 1)
 
 
-def lines_kernel(count_x, order_y, *refs):
-    raw_refs, operands = refs[:count_x], refs[count_x : count_x + 4]
-    first_ref, last_ref, region_ref, table = operands
-    gy = lax.axis_index("gy")
-    out_refs, (region, sem) = refs[count_x + 4 : -2], refs[-2:]
+def lines_of(raw_refs, numbers, region_ref, region, sem, table):
     fetch = pltpu.make_async_copy(region_ref, region, sem)
     fetch.start()
     units = [directions(raw_ref[0], raw_ref[1]) for raw_ref in raw_refs]
     fetch.wait()
     total = None
-    for number in range(count_x):
-        saturation = looked_up(raw_refs[number][2], region)
+    for raw_ref, unit, number in zip(raw_refs, units, numbers):
+        saturation = looked_up(raw_ref[2], region)
         rows = saturation.shape[0] * saturation.shape[1]
-        block = [(part * saturation).reshape(rows, -1) for part in units[number]]
+        block = [(part * saturation).reshape(rows, -1) for part in unit]
         high, low = split_high(jnp.concatenate(block, 0))
         both = dot(jnp.concatenate([high, low], 0), table[0, number])
         part = both[: 3 * rows] + both[3 * rows :] + dot(high, table[1, number])
         total = part if total is None else total + part
-    lanes = out_refs[0].shape[1]
+    return total
+
+
+def early_lines_kernel(numbers, *refs):
+    raw_refs, (region_ref, table, out_ref, region, sem) = refs[: len(numbers)], refs[len(numbers) :]
+    out_ref[...] = lines_of(raw_refs, numbers, region_ref, region, sem, table)
+
+
+def lines_kernel(numbers, order_y, *refs):
+    raw_refs, operands = refs[: len(numbers)], refs[len(numbers) : len(numbers) + 5]
+    early_ref, first_ref, last_ref, region_ref, table = operands
+    gy = lax.axis_index("gy")
+    out_refs, (region, sem) = refs[len(numbers) + 5 : -2], refs[-2:]
+    total = lines_of(raw_refs, numbers, region_ref, region, sem, table) + early_ref[...]
+    lines, lanes = total.shape[0], first_ref.shape[1]
     for spot, (number, out_ref) in enumerate(zip(order_y, out_refs)):
-        out_ref[: 3 * rows] = total[:, spot * lanes : (spot + 1) * lanes]
+        out_ref[:lines] = total[:, spot * lanes : (spot + 1) * lanes]
         if number in meeting(len(order_y)):
             up = lax.bitwise_xor(gy, number) > gy
-            out_ref[3 * rows :] = jnp.where(up, last_ref[...], first_ref[...])
+            out_ref[lines:] = jnp.where(up, last_ref[...], first_ref[...])
 
 
 def back_lines_kernel(numbers, count_y, *refs):
@@ -512,16 +522,16 @@
     return [blocks[number] for number in range(lax.axis_size(axis))], ready
 
 
-def gathered_sums(blocks, axis):
-    blocks = {number: [block] for number, block in enumerate(blocks)}
-    bit = 1
+def far_sums(blocks, axis):
+    blocks = {number: [block] for number, block in blocks.items()}
+    terms, bit, block = [], 1, None
     while bit < lax.axis_size(axis):
         for number in sorted(blocks, reverse=True):
             if number & bit:
                 block = functools.reduce(jnp.add, blocks.pop(number))
-                blocks[number ^ bit].append(swapped(block, axis, bit))
+                blocks.get(number ^ bit, terms).append(swapped(block, axis, bit))
         bit *= 2
-    return blocks[0], block
+    return terms, block
 
 
 def per_device(theta, phi, labels, ms_region, aex_region, kernel):
@@ -581,13 +591,24 @@
         flops=48 * 2 * rows * lanes * 2 * whole_y,
         name="tensor",
     )
+    region_scratch = (pltpu.SMEM(ms_region.shape, jnp.float32), pltpu.SemaphoreType.DMA)
+    early, late = order_x[:-1], order_x[-1:]
+    early_sums = call(
+        functools.partial(early_lines_kernel, early),
+        f32(lines, count_y * lanes),
+        [vmem] * len(early) + [hbm, vmem],
+        (*gathered[:-1], ms_region, held(table)),
+        scratch=region_scratch,
+        flops=transform_flops * len(early) // count_x,
+        name="early_lines",
+    )
     spectrum = call(
-        functools.partial(lines_kernel, count_x, order_y),
+        functools.partial(lines_kernel, late, order_y),
         [f32(lines + (edge_rows if n in meeting(count_y) else 0), lanes) for n in order_y],
-        [vmem] * (count_x + 2) + [hbm, vmem],
-        (*gathered, first, last, ms_region, held(table)),
-        scratch=(pltpu.SMEM(ms_region.shape, jnp.float32), pltpu.SemaphoreType.DMA),
-        flops=transform_flops,
+        [vmem] * 4 + [hbm, vmem],
+        (gathered[-1], early_sums, first, last, ms_region, held(table)),
+        scratch=region_scratch,
+        flops=transform_flops * len(late) // count_x,
         name="lines",
     )
     columns = lax.optimization_barrier(exchanged(spectrum, "gy", order_y))
@@ -605,21 +626,23 @@
         name="waves",
     )
     returned = exchanged(waves, "gy", order_y)
-    across = [number for number in range(count_x) if number % 2]
-    within = [number for number in range(count_x) if not number % 2]
-    partial = [None] * count_x
-    for numbers, name in ((across, "back_across"), (within, "back_within")):
+    def back(numbers, chunks, name):
         blocks = call(
             functools.partial(back_lines_kernel, numbers, count_y),
             [f32(lines, width)] * len(numbers),
             [vmem] * (count_y + 1),
-            (*returned, held(table)),
-            flops=transform_flops // 2,
+            (*chunks, held(table)),
+            flops=transform_flops * len(numbers) // count_x,
             name=name,
         )
-        for number, block in zip(numbers, blocks):
-            partial[number] = block
-    parts, far_sum = gathered_sums(partial, "gx")
+        return dict(zip(numbers, blocks))
+
+    partial = back([n for n in order_x[2:] if n % 2], returned, "back_across")
+    partial |= back([n for n in order_x[2:] if not n % 2] + [1], returned, "back_within")
+    near = swapped(partial.pop(1), "gx", 1)
+    parts, far_sum = far_sums(partial, "gx")
+    returned, far_sum = lax.optimization_barrier((returned, far_sum))
+    parts = [back([0], returned, "back_own")[0], near, *parts]
     edges = [columns[order_y.index(number)] for number in meeting(count_y)]
     edges, far_sum = lax.optimization_barrier((edges, far_sum))
     exchange, unit = call(

time: 50.6 us -> 50.1 us (level)
  waiting for transfers between devices: 10.2 us -> 8.88 us
  Pallas kernels: 11.9 us -> 12.8 us
    ppermute x20, waiting for transfers between devices: 10.2 us -> 8.88 us  [swapped(): return lax.ppermute(chunk, axis, [(i, i ^ number) for i in range(devices)])]
    pallas_call x9 -> x11, Pallas kernels: 11.9 us -> 12.8 us  [call(): pl.pallas_call(body, out_shape=out, in_specs=ins, out_specs=[vmem] * len(...]
  transfers between devices with their start and end apart: 20 -> 20, of which waited for: 10 -> 9; matrix products, arithmetic and copies ran while one was open for 0% -> 0% of each run, Pallas kernels for 12% -> 16%
where the time goes in v11:
time: 50.1 us; the launch traced here: 49.9 us
  starting transfers between devices  27.4 us (55%)
  Pallas kernels  12.8 us (26%)
  waiting for transfers between devices  8.88 us (18%)
  between operations  0.74 us (1%)
    ppermute x20, starting transfers between devices, swapped(): return lax.ppermute(chunk, axis, [(i, i ^ number) for i in range(devices)])  27.4 us
    pallas_call x11, Pallas kernels, call(): pl.pallas_call(body, out_shape=out, in_specs=ins, out_specs=[vmem] * len(...  12.8 us
    ppermute x20, waiting for transfers between devices, swapped(): return lax.ppermute(chunk, axis, [(i, i ^ number) for i in range(devices)])  8.88 us
  transfers between devices with their start and end apart: 20, of which 9 were waited for; matrix products, arithmetic and copies ran while one was open for 0% of the time, Pallas kernels for 16%

profile of v11, /device:TPU:0, one launch (start us, length us, event | category | flops | bytes accessed | tf_op | source)
XLA Modules:
  0.0 49.9 jit_solution(17406963351072785194)
XLA Ops:
  0.6 0.8 %pack.1 = (f32[3,4,8,256]{3,2,1,0:T(8,128)S(1)}, f32[24,128]{1,0:T(8,128)S(1)}, f32[24,128]{1,0:T(8,128)S(1)}) custom-call(f32[4,8,256]{2,1,0:T(8,128)} %theta_ref.1, f32[4,8,256]{2,1,0:T(8,128)} %phi_ref.1, s32[4,8,256]{2,1,0:T(8,128)} %labels_ref.1), custom_call_target="tpu_custom_call" | custom-call | bytes 221184 | tf_op jit(solution)/shard_map/pack/pallas_call | solution.py:479
  1.5 3.0 %collective-permute-start = (f32[3,4,8,256]{3,2,1,0:T(8,128)S(1)}, f32[3,4,8,256]{3,2,1,0:T(8,128)S(1)}, u32[]{:S(2)}, u32[]{:S(2)}) collective-permute-start(f32[3,4,8,256]{3,2,1,0:T(8,128)S(1)} %get-tuple-element.49.refs_0_), channel_id=1, source_target_pairs={{0,16},{8,24},{16,0},{24,8},{1,17},{9,25},{17,1},{25,9},{2,18},{10... | collective-permute-start | bytes 294920 | tf_op jit(solution)/shard_map/ppermute | solution.py:497
  4.5 2.6 %load.1 = (bf16[2,4,256,1024]{3,2,1,0:T(8,128)(2,1)S(1)}, bf16[128,384]{1,0:T(8,128)(2,1)S(1)}, bf16[128,384]{1,0:T(8,128)(2,1)S(1)}) custom-call(bf16[4,8,2,4,256,128]{5,4,3,2,1,0:T(8,128)(2,1)} %constant.8.clone.refs_0_, bf16[8,128,384]{2,1,0:T(8,128)(2,1)} %constant.9.clone.refs_1_, bf16[8,128,384]{2,1,0:T(8,128)(2,1)} %constant.10.clone.refs_2_), custom_call_target="tpu_custom_call" | custom-call | bytes 22740992 | tf_op jit(solution)/shard_map/load/pallas_call | solution.py:479
  7.7 1.4 %early_lines.1.refs_1_ = f32[96,1024]{1,0:T(8,128)S(1)} custom-call(f32[3,4,8,256]{3,2,1,0:T(8,128)S(1)} %get-tuple-element.49.refs_0_, f32[3,4,8,256]{3,2,1,0:T(8,128)S(1)} %collective-permute-done.2.refs_1_, f32[3,4,8,256]{3,2,1,0:T(8,128)S(1)} %collective-permute-done.refs_2_, f32[16]{0:T(128)} %refs_7_.1, ...), custom_call_target="tpu_custom_call" | custom-call | flops 452984832 | bytes 4882496 | tf_op jit(solution)/shard_map/early_lines/pallas_call | solution.py:479
  9.2 1.0 %lines.1 = (f32[120,128]{1,0:T(8,128)S(1)}, f32[96,128]{1,0:T(8,128)S(1)}, f32[96,128]{1,0:T(8,128)S(1)}, f32[96,128]{1,0:T(8,128)S(1)}, f32[120,128]{1,0:T(8,12...) custom-call(f32[3,4,8,256]{3,2,1,0:T(8,128)S(1)} %collective-permute-done.1.refs_0_.refs_3_, ...), custom_call_target="tpu_custom_call" | custom-call | flops 150994944 | bytes 5140544 | tf_op jit(solution)/shard_map/lines/pallas_call | solution.py:479
  10.2 3.8 %collective-permute-start.4 = (f32[96,128]{1,0:T(8,128)S(1)}, f32[96,128]{1,0:T(8,128)S(1)}, u32[]{:S(2)}, u32[]{:S(2)}) collective-permute-start(f32[96,128]{1,0:T(8,128)S(1)} %get-tuple-element.56), channel_id=1, source_target_pairs={{0,6},{1,7},{2,4},{3,5},{4,2},{5,3},{6,0},{7,1},{8,14},{9,15},{10,... | collective-permute-start | bytes 147464 | tf_op jit(solution)/shard_map/ppermute | solution.py:497
  14.4 2.4 %collective-permute-start.3 = (f32[120,128]{1,0:T(8,128)S(1)}, f32[120,128]{1,0:T(8,128)S(1)}, u32[]{:S(2)}, u32[]{:S(2)}) collective-permute-start(f32[120,128]{1,0:T(8,128)S(1)} %get-tuple-element.55), channel_id=1, source_target_pairs={{0,7},{1,6},{2,5},{3,4},{4,3},{5,2},{6,1},{7,0},{8,15},{9,14},{10,... | collective-permute-start | bytes 184328 | tf_op jit(solution)/shard_map/ppermute | solution.py:497
  16.8 2.5 %collective-permute-start.7 = (f32[120,128]{1,0:T(8,128)S(1)}, f32[120,128]{1,0:T(8,128)S(1)}, u32[]{:S(2)}, u32[]{:S(2)}) collective-permute-start(f32[120,128]{1,0:T(8,128)S(1)} %get-tuple-element.59), channel_id=1, source_target_pairs={{0,3},{1,2},{2,1},{3,0},{4,7},{5,6},{6,5},{7,4},{8,11},{9,10},{10,... | collective-permute-start | bytes 184328 | tf_op jit(solution)/shard_map/ppermute | solution.py:497
  19.3 0.5 %collective-permute-start.9 = (f32[120,128]{1,0:T(8,128)S(1)}, f32[120,128]{1,0:T(8,128)S(1)}, u32[]{:S(2)}, u32[]{:S(2)}) collective-permute-start(f32[120,128]{1,0:T(8,128)S(1)} %get-tuple-element.61), channel_id=1, source_target_pairs={{0,1},{1,0},{2,3},{3,2},{4,5},{5,4},{6,7},{7,6},{8,9},{9,8},{10,11... | collective-permute-start | bytes 184328 | tf_op jit(solution)/shard_map/ppermute | solution.py:497
  19.8 1.0 %collective-permute-start.6 = (f32[96,128]{1,0:T(8,128)S(1)}, f32[96,128]{1,0:T(8,128)S(1)}, u32[]{:S(2)}, u32[]{:S(2)}) collective-permute-start(f32[96,128]{1,0:T(8,128)S(1)} %get-tuple-element.58), channel_id=1, source_target_pairs={{0,4},{1,5},{2,6},{3,7},{4,0},{5,1},{6,2},{7,3},{8,12},{9,13},{10,... | collective-permute-start | bytes 147464 | tf_op jit(solution)/shard_map/ppermute | solution.py:497
  20.8 0.7 %collective-permute-done.5.refs_2_ = f32[96,128]{1,0:T(8,128)S(1)} collective-permute-done((f32[96,128]{1,0:T(8,128)S(1)}, f32[96,128]{1,0:T(8,128)S(1)}, u32[]{:S(2)}, u32[]{:S(2)}) %collective-permute-start.5) | collective-permute-done | bytes 49184 | tf_op jit(solution)/shard_map/ppermute | solution.py:497
  21.5 1.6 %tensor.1.refs_8_ = bf16[48,128,128]{2,1,0:T(8,128)(2,1)S(1)} custom-call(bf16[48,64,128]{2,1,0:T(8,128)(2,1)S(1)} %bitcast.1, bf16[64,128]{1,0:T(8,128)(2,1)S(1)} %copy-done.1), custom_call_target="tpu_custom_call" | custom-call | flops 100663296 | bytes 2375680 | tf_op jit(solution)/shard_map/tensor/pallas_call | solution.py:479
  23.1 2.2 %collective-permute-done.6.refs_3_ = f32[96,128]{1,0:T(8,128)S(1)} collective-permute-done((f32[96,128]{1,0:T(8,128)S(1)}, f32[96,128]{1,0:T(8,128)S(1)}, u32[]{:S(2)}, u32[]{:S(2)}) %collective-permute-start.6) | collective-permute-done | bytes 49184 | tf_op jit(solution)/shard_map/ppermute | solution.py:497
  25.3 0.5 %collective-permute-done.8.refs_5_ = f32[96,128]{1,0:T(8,128)S(1)} collective-permute-done((f32[96,128]{1,0:T(8,128)S(1)}, f32[96,128]{1,0:T(8,128)S(1)}, u32[]{:S(2)}, u32[]{:S(2)}) %collective-permute-start.8) | collective-permute-done | bytes 49184 | tf_op jit(solution)/shard_map/ppermute | solution.py:497
  25.8 1.7 %waves.1 = (f32[96,128]{1,0:T(8,128)S(1)}, f32[96,128]{1,0:T(8,128)S(1)}, f32[96,128]{1,0:T(8,128)S(1)}, f32[96,128]{1,0:T(8,128)S(1)}, f32[96,128]{1,0:T(8,128)...) custom-call(f32[120,128]{1,0:T(8,128)S(1)} %collective-permute-done.3.refs_0_.refs_6_, ...), custom_call_target="tpu_custom_call" | custom-call | flops 125829120 | bytes 2592768 | tf_op jit(solution)/shard_map/waves/pallas_call | solution.py:479
  27.5 2.6 %collective-permute-start.10 = (f32[96,128]{1,0:T(8,128)S(1)}, f32[96,128]{1,0:T(8,128)S(1)}, u32[]{:S(2)}, u32[]{:S(2)}) collective-permute-start(f32[96,128]{1,0:T(8,128)S(1)} %get-tuple-element.73), channel_id=1, source_target_pairs={{0,7},{1,6},{2,5},{3,4},{4,3},{5,2},{6,1},{7,0},{8,15},{9,14},{10,... | collective-permute-start | bytes 147464 | tf_op jit(solution)/shard_map/ppermute | solution.py:497
  30.1 2.3 %collective-permute-start.11 = (f32[96,128]{1,0:T(8,128)S(1)}, f32[96,128]{1,0:T(8,128)S(1)}, u32[]{:S(2)}, u32[]{:S(2)}) collective-permute-start(f32[96,128]{1,0:T(8,128)S(1)} %get-tuple-element.74), channel_id=1, source_target_pairs={{0,6},{1,7},{2,4},{3,5},{4,2},{5,3},{6,0},{7,1},{8,14},{9,15},{10,... | collective-permute-start | bytes 147464 | tf_op jit(solution)/shard_map/ppermute | solution.py:497
  32.4 2.8 %collective-permute-start.13 = (f32[96,128]{1,0:T(8,128)S(1)}, f32[96,128]{1,0:T(8,128)S(1)}, u32[]{:S(2)}, u32[]{:S(2)}) collective-permute-start(f32[96,128]{1,0:T(8,128)S(1)} %get-tuple-element.76), channel_id=1, source_target_pairs={{0,4},{1,5},{2,6},{3,7},{4,0},{5,1},{6,2},{7,3},{8,12},{9,13},{10,... | collective-permute-start | bytes 147464 | tf_op jit(solution)/shard_map/ppermute | solution.py:497
  35.4 2.9 %collective-permute-start.15 = (f32[96,128]{1,0:T(8,128)S(1)}, f32[96,128]{1,0:T(8,128)S(1)}, u32[]{:S(2)}, u32[]{:S(2)}) collective-permute-start(f32[96,128]{1,0:T(8,128)S(1)} %get-tuple-element.78), channel_id=1, source_target_pairs={{0,2},{1,3},{2,0},{3,1},{4,6},{5,7},{6,4},{7,5},{8,10},{9,11},{10,... | collective-permute-start | bytes 147464 | tf_op jit(solution)/shard_map/ppermute | solution.py:497
  38.3 0.4 collective-permute-start.16
  38.8 0.6 %collective-permute-done.13.refs_3_ = f32[96,128]{1,0:T(8,128)S(1)} collective-permute-done((f32[96,128]{1,0:T(8,128)S(1)}, f32[96,128]{1,0:T(8,128)S(1)}, u32[]{:S(2)}, u32[]{:S(2)}) %collective-permute-start.13) | collective-permute-done | bytes 49184 | tf_op jit(solution)/shard_map/ppermute | solution.py:497
  39.3 0.9 %collective-permute-done.14.refs_4_ = f32[96,128]{1,0:T(8,128)S(1)} collective-permute-done((f32[96,128]{1,0:T(8,128)S(1)}, f32[96,128]{1,0:T(8,128)S(1)}, u32[]{:S(2)}, u32[]{:S(2)}) %collective-permute-start.14) | collective-permute-done | bytes 49184 | tf_op jit(solution)/shard_map/ppermute | solution.py:497
  40.2 0.6 %collective-permute-done.15.refs_5_ = f32[96,128]{1,0:T(8,128)S(1)} collective-permute-done((f32[96,128]{1,0:T(8,128)S(1)}, f32[96,128]{1,0:T(8,128)S(1)}, u32[]{:S(2)}, u32[]{:S(2)}) %collective-permute-start.15) | collective-permute-done | bytes 49184 | tf_op jit(solution)/shard_map/ppermute | solution.py:497
  40.9 1.5 %collective-permute-done.16.refs_6_ = f32[96,128]{1,0:T(8,128)S(1)} collective-permute-done((f32[96,128]{1,0:T(8,128)S(1)}, f32[96,128]{1,0:T(8,128)S(1)}, u32[]{:S(2)}, u32[]{:S(2)}) %collective-permute-start.16) | collective-permute-done | bytes 49184 | tf_op jit(solution)/shard_map/ppermute | solution.py:497
  42.4 0.5 back_across.1
  42.9 0.8 %back_within.1 = (f32[96,256]{1,0:T(8,128)S(1)}, f32[96,256]{1,0:T(8,128)S(1)}) custom-call(f32[96,128]{1,0:T(8,128)S(1)} %collective-permute-done.10.refs_0_, f32[96,128]{1,0:T(8,128)S(1)} %collective-permute-done.11.refs_1_, f32[96,128]{1,0:T(8,128)S(1)} %collective-permute-done.12.refs_2_, f32[96,128]{1,0:T(8,128)S(1)} %collective-permute-done.13.refs_3_, ...), custom_call_target="tpu_custom_call" | custom-call | flops 301989888 | bytes 4784128 | tf_op jit(solution)/shard_map/back_within/pallas_call | solution.py:479
  43.7 0.6 %collective-permute-start.18 = (f32[96,256]{1,0:T(8,128)S(1)}, f32[96,256]{1,0:T(8,128)S(1)}, u32[]{:S(2)}, u32[]{:S(2)}) collective-permute-start(f32[96,256]{1,0:T(8,128)S(1)} %get-tuple-element.90), channel_id=1, source_target_pairs={{0,8},{8,0},{16,24},{24,16},{1,9},{9,1},{17,25},{25,17},{2,10},{10... | collective-permute-start | bytes 294920 | tf_op jit(solution)/shard_map/ppermute | solution.py:497
  44.3 1.5 %collective-permute-start.19 = (f32[96,256]{1,0:T(8,128)S(1)}, f32[96,256]{1,0:T(8,128)S(1)}, u32[]{:S(2)}, u32[]{:S(2)}) collective-permute-start(f32[96,256]{1,0:T(8,128)S(1)} %add.3), channel_id=1, source_target_pairs={{0,16},{8,24},{16,0},{24,8},{1,17},{9,25},{17,1},{25,9},{2,18},{10... | collective-permute-start | bytes 294920 | tf_op jit(solution)/shard_map/ppermute | solution.py:497
  45.9 1.1 %exchange.1 = (f32[3,4,8,256]{3,2,1,0:T(8,128)S(1)}, f32[3,4,8,256]{3,2,1,0:T(8,128)S(1)}) custom-call(f32[3,4,8,256]{3,2,1,0:T(8,128)S(1)} %get-tuple-element.49.refs_0_, f32[3,4,8,256]{3,2,1,0:T(8,128)S(1)} %collective-permute-done.2.refs_1_, f32[3,4,8,256]{3,2,1,0:T(8,128)S(1)} %collective-permute-done.refs_2_, ...), custom_call_target="tpu_custom_call" | custom-call | flops 2457600 | bytes 774272 | tf_op jit(solution)/shard_map/exchange/pallas_call | solution.py:479
  47.0 0.5 back_own.1.refs_0_
  47.5 1.7 %collective-permute-done.19.refs_2_ = f32[96,256]{1,0:T(8,128)S(1)} collective-permute-done((f32[96,256]{1,0:T(8,128)S(1)}, f32[96,256]{1,0:T(8,128)S(1)}, u32[]{:S(2)}, u32[]{:S(2)}) %collective-permute-start.19) | collective-permute-done | bytes 98336 | tf_op jit(solution)/shard_map/ppermute | solution.py:497
  49.2 0.7 %predict.1 = (f32[3,4,8,256]{3,2,1,0:T(8,128)}, f32[3,4,8,256]{3,2,1,0:T(8,128)}) custom-call(f32[96,256]{1,0:T(8,128)S(1)} %back_own.1.refs_0_, f32[96,256]{1,0:T(8,128)S(1)} %collective-permute-done.18.refs_1_, f32[96,256]{1,0:T(8,128)S(1)} %collective-permute-done.19.refs_2_, f32[3,4,8,256]{3,2,1,0:T(8,128)S(1)} %get-tuple-element.94.refs_3_, ...), custom_call_target="tpu_custom_call" | custom-call | flops 491520 | bytes 688128 | tf_op jit(solution)/shard_map/predict/pallas_call | solution.py:479
  (28 shorter events, 1.3 us)
Async XLA Ops:
  1.5 5.8 %collective-permute-start = (f32[3,4,8,256]{3,2,1,0:T(8,128)S(1)}, f32[3,4,8,256]{3,2,1,0:T(8,128)S(1)}, u32[]{:S(2)}, u32[]{:S(2)}) collective-permute-start(f32[3,4,8,256]{3,2,1,0:T(8,128)S(1)} %get-tuple-element.49.refs_0_), channel_id=1, source_target_pairs={{0,16},{8,24},{16,0},{24,8},{1,17},{9,25},{17,1},{25,9},{2,18},{10... | collective-permute-start | bytes 294920 | tf_op jit(solution)/shard_map/ppermute | solution.py:497
  4.5 3.2 %collective-permute-start.2 = (f32[3,4,8,256]{3,2,1,0:T(8,128)S(1)}, f32[3,4,8,256]{3,2,1,0:T(8,128)S(1)}, u32[]{:S(2)}, u32[]{:S(2)}) collective-permute-start(f32[3,4,8,256]{3,2,1,0:T(8,128)S(1)} %get-tuple-element.49.refs_0_), channel_id=1, source_target_pairs={{0,8},{8,0},{16,24},{24,16},{1,9},{9,1},{17,25},{25,17},{2,10},{10... | collective-permute-start | bytes 294920 | tf_op jit(solution)/shard_map/ppermute | solution.py:497
  7.3 14.2 %copy-start = (bf16[6,8,64,128]{3,2,1,0:T(8,128)(2,1)S(1)}, bf16[6,8,64,128]{3,2,1,0:T(8,128)(2,1)}, u32[]{:S(2)}) copy-start(bf16[6,8,64,128]{3,2,1,0:T(8,128)(2,1)} %param.15) | copy-start | bytes 2359300
  7.3 14.2 %copy-start.1 = (bf16[64,128]{1,0:T(8,128)(2,1)S(1)}, bf16[64,128]{1,0:T(8,128)(2,1)}, u32[]{:S(2)}) copy-start(bf16[64,128]{1,0:T(8,128)(2,1)} %constant.11.clone.twice_ref) | copy-start | bytes 49156
  7.3 1.9 %collective-permute-start.1 = (f32[3,4,8,256]{3,2,1,0:T(8,128)S(1)}, f32[3,4,8,256]{3,2,1,0:T(8,128)S(1)}, u32[]{:S(2)}, u32[]{:S(2)}) collective-permute-start(f32[3,4,8,256]{3,2,1,0:T(8,128)S(1)} %collective-permute-done.refs_2_), channel_id=1, source_target_pairs={{0,8},{8,0},{16,24},{24,16},{1,9},{9,1},{17,25},{25,17},{2,10},{10... | collective-permute-start | bytes 294920 | tf_op jit(solution)/shard_map/ppermute | solution.py:497
  10.2 9.7 %collective-permute-start.4 = (f32[96,128]{1,0:T(8,128)S(1)}, f32[96,128]{1,0:T(8,128)S(1)}, u32[]{:S(2)}, u32[]{:S(2)}) collective-permute-start(f32[96,128]{1,0:T(8,128)S(1)} %get-tuple-element.56), channel_id=1, source_target_pairs={{0,6},{1,7},{2,4},{3,5},{4,2},{5,3},{6,0},{7,1},{8,14},{9,15},{10,... | collective-permute-start | bytes 147464 | tf_op jit(solution)/shard_map/ppermute | solution.py:497
  14.0 7.5 %collective-permute-start.5 = (f32[96,128]{1,0:T(8,128)S(1)}, f32[96,128]{1,0:T(8,128)S(1)}, u32[]{:S(2)}, u32[]{:S(2)}) collective-permute-start(f32[96,128]{1,0:T(8,128)S(1)} %get-tuple-element.57), channel_id=1, source_target_pairs={{0,5},{1,4},{2,7},{3,6},{4,1},{5,0},{6,3},{7,2},{8,13},{9,12},{10,... | collective-permute-start | bytes 147464 | tf_op jit(solution)/shard_map/ppermute | solution.py:497
  14.4 11.4 %collective-permute-start.3 = (f32[120,128]{1,0:T(8,128)S(1)}, f32[120,128]{1,0:T(8,128)S(1)}, u32[]{:S(2)}, u32[]{:S(2)}) collective-permute-start(f32[120,128]{1,0:T(8,128)S(1)} %get-tuple-element.55), channel_id=1, source_target_pairs={{0,7},{1,6},{2,5},{3,4},{4,3},{5,2},{6,1},{7,0},{8,15},{9,14},{10,... | collective-permute-start | bytes 184328 | tf_op jit(solution)/shard_map/ppermute | solution.py:497
  16.8 9.0 %collective-permute-start.7 = (f32[120,128]{1,0:T(8,128)S(1)}, f32[120,128]{1,0:T(8,128)S(1)}, u32[]{:S(2)}, u32[]{:S(2)}) collective-permute-start(f32[120,128]{1,0:T(8,128)S(1)} %get-tuple-element.59), channel_id=1, source_target_pairs={{0,3},{1,2},{2,1},{3,0},{4,7},{5,6},{6,5},{7,4},{8,11},{9,10},{10,... | collective-permute-start | bytes 184328 | tf_op jit(solution)/shard_map/ppermute | solution.py:497
  19.3 6.4 %collective-permute-start.9 = (f32[120,128]{1,0:T(8,128)S(1)}, f32[120,128]{1,0:T(8,128)S(1)}, u32[]{:S(2)}, u32[]{:S(2)}) collective-permute-start(f32[120,128]{1,0:T(8,128)S(1)} %get-tuple-element.61), channel_id=1, source_target_pairs={{0,1},{1,0},{2,3},{3,2},{4,5},{5,4},{6,7},{7,6},{8,9},{9,8},{10,11... | collective-permute-start | bytes 184328 | tf_op jit(solution)/shard_map/ppermute | solution.py:497
  19.8 5.4 %collective-permute-start.6 = (f32[96,128]{1,0:T(8,128)S(1)}, f32[96,128]{1,0:T(8,128)S(1)}, u32[]{:S(2)}, u32[]{:S(2)}) collective-permute-start(f32[96,128]{1,0:T(8,128)S(1)} %get-tuple-element.58), channel_id=1, source_target_pairs={{0,4},{1,5},{2,6},{3,7},{4,0},{5,1},{6,2},{7,3},{8,12},{9,13},{10,... | collective-permute-start | bytes 147464 | tf_op jit(solution)/shard_map/ppermute | solution.py:497
  21.5 4.3 %collective-permute-start.8 = (f32[96,128]{1,0:T(8,128)S(1)}, f32[96,128]{1,0:T(8,128)S(1)}, u32[]{:S(2)}, u32[]{:S(2)}) collective-permute-start(f32[96,128]{1,0:T(8,128)S(1)} %get-tuple-element.60), channel_id=1, source_target_pairs={{0,2},{1,3},{2,0},{3,1},{4,6},{5,7},{6,4},{7,5},{8,10},{9,11},{10,... | collective-permute-start | bytes 147464 | tf_op jit(solution)/shard_map/ppermute | solution.py:497
  27.5 7.9 %collective-permute-start.10 = (f32[96,128]{1,0:T(8,128)S(1)}, f32[96,128]{1,0:T(8,128)S(1)}, u32[]{:S(2)}, u32[]{:S(2)}) collective-permute-start(f32[96,128]{1,0:T(8,128)S(1)} %get-tuple-element.73), channel_id=1, source_target_pairs={{0,7},{1,6},{2,5},{3,4},{4,3},{5,2},{6,1},{7,0},{8,15},{9,14},{10,... | collective-permute-start | bytes 147464 | tf_op jit(solution)/shard_map/ppermute | solution.py:497
  30.1 8.2 %collective-permute-start.11 = (f32[96,128]{1,0:T(8,128)S(1)}, f32[96,128]{1,0:T(8,128)S(1)}, u32[]{:S(2)}, u32[]{:S(2)}) collective-permute-start(f32[96,128]{1,0:T(8,128)S(1)} %get-tuple-element.74), channel_id=1, source_target_pairs={{0,6},{1,7},{2,4},{3,5},{4,2},{5,3},{6,0},{7,1},{8,14},{9,15},{10,... | collective-permute-start | bytes 147464 | tf_op jit(solution)/shard_map/ppermute | solution.py:497
  32.4 6.3 %collective-permute-start.12 = (f32[96,128]{1,0:T(8,128)S(1)}, f32[96,128]{1,0:T(8,128)S(1)}, u32[]{:S(2)}, u32[]{:S(2)}) collective-permute-start(f32[96,128]{1,0:T(8,128)S(1)} %get-tuple-element.75), channel_id=1, source_target_pairs={{0,5},{1,4},{2,7},{3,6},{4,1},{5,0},{6,3},{7,2},{8,13},{9,12},{10,... | collective-permute-start | bytes 147464 | tf_op jit(solution)/shard_map/ppermute | solution.py:497
  32.4 6.9 %collective-permute-start.13 = (f32[96,128]{1,0:T(8,128)S(1)}, f32[96,128]{1,0:T(8,128)S(1)}, u32[]{:S(2)}, u32[]{:S(2)}) collective-permute-start(f32[96,128]{1,0:T(8,128)S(1)} %get-tuple-element.76), channel_id=1, source_target_pairs={{0,4},{1,5},{2,6},{3,7},{4,0},{5,1},{6,2},{7,3},{8,12},{9,13},{10,... | collective-permute-start | bytes 147464 | tf_op jit(solution)/shard_map/ppermute | solution.py:497
  35.3 5.0 %collective-permute-start.14 = (f32[96,128]{1,0:T(8,128)S(1)}, f32[96,128]{1,0:T(8,128)S(1)}, u32[]{:S(2)}, u32[]{:S(2)}) collective-permute-start(f32[96,128]{1,0:T(8,128)S(1)} %get-tuple-element.77), channel_id=1, source_target_pairs={{0,3},{1,2},{2,1},{3,0},{4,7},{5,6},{6,5},{7,4},{8,11},{9,10},{10,... | collective-permute-start | bytes 147464 | tf_op jit(solution)/shard_map/ppermute | solution.py:497
  35.4 5.4 %collective-permute-start.15 = (f32[96,128]{1,0:T(8,128)S(1)}, f32[96,128]{1,0:T(8,128)S(1)}, u32[]{:S(2)}, u32[]{:S(2)}) collective-permute-start(f32[96,128]{1,0:T(8,128)S(1)} %get-tuple-element.78), channel_id=1, source_target_pairs={{0,2},{1,3},{2,0},{3,1},{4,6},{5,7},{6,4},{7,5},{8,10},{9,11},{10,... | collective-permute-start | bytes 147464 | tf_op jit(solution)/shard_map/ppermute | solution.py:497
  38.3 4.1 %collective-permute-start.16 = (f32[96,128]{1,0:T(8,128)S(1)}, f32[96,128]{1,0:T(8,128)S(1)}, u32[]{:S(2)}, u32[]{:S(2)}) collective-permute-start(f32[96,128]{1,0:T(8,128)S(1)} %get-tuple-element.79), channel_id=1, source_target_pairs={{0,1},{1,0},{2,3},{3,2},{4,5},{5,4},{6,7},{7,6},{8,9},{9,8},{10,11... | collective-permute-start | bytes 147464 | tf_op jit(solution)/shard_map/ppermute | solution.py:497
  42.4 3.5 %copy-start.2 = (f32[16]{0:T(128)S(1)}, f32[16]{0:T(128)}, u32[]{:S(2)}) copy-start(f32[16]{0:T(128)} %refs_7_.1) | copy-start | bytes 196
  42.4 3.5 %copy-start.3 = (f32[16]{0:T(128)S(1)}, f32[16]{0:T(128)}, u32[]{:S(2)}) copy-start(f32[16]{0:T(128)} %refs_8_.1) | copy-start | bytes 196
  42.9 1.4 %collective-permute-start.17 = (f32[96,256]{1,0:T(8,128)S(1)}, f32[96,256]{1,0:T(8,128)S(1)}, u32[]{:S(2)}, u32[]{:S(2)}) collective-permute-start(f32[96,256]{1,0:T(8,128)S(1)} %back_across.1), channel_id=1, source_target_pairs={{0,8},{8,0},{16,24},{24,16},{1,9},{9,1},{17,25},{25,17},{2,10},{10... | collective-permute-start | bytes 294920 | tf_op jit(solution)/shard_map/ppermute | solution.py:497
  43.7 3.7 %collective-permute-start.18 = (f32[96,256]{1,0:T(8,128)S(1)}, f32[96,256]{1,0:T(8,128)S(1)}, u32[]{:S(2)}, u32[]{:S(2)}) collective-permute-start(f32[96,256]{1,0:T(8,128)S(1)} %get-tuple-element.90), channel_id=1, source_target_pairs={{0,8},{8,0},{16,24},{24,16},{1,9},{9,1},{17,25},{25,17},{2,10},{10... | collective-permute-start | bytes 294920 | tf_op jit(solution)/shard_map/ppermute | solution.py:497
  44.3 4.8 %collective-permute-start.19 = (f32[96,256]{1,0:T(8,128)S(1)}, f32[96,256]{1,0:T(8,128)S(1)}, u32[]{:S(2)}, u32[]{:S(2)}) collective-permute-start(f32[96,256]{1,0:T(8,128)S(1)} %add.3), channel_id=1, source_target_pairs={{0,16},{8,24},{16,0},{24,8},{1,17},{9,25},{17,1},{25,9},{2,18},{10... | collective-permute-start | bytes 294920 | tf_op jit(solution)/shard_map/ppermute | solution.py:497

commit v12 on v11

--- a/solution.py
+++ b/solution.py
@@ -152,18 +152,22 @@
 
 
 def looked_up(labels, region):
-    result = jnp.zeros_like(labels) + region[0]
+    rows = len(region.shape) > 1
+    value = [region[i : i + 1, :] if rows else region[i] for i in range(region.shape[0])]
+    result = jnp.zeros_like(labels) + value[0]
     for index in range(1, region.shape[0]):
-        result = jnp.where(labels == float(index), region[index], result)
+        result = jnp.where(labels == float(index), value[index], result)
     return result
 
 
-def pack_kernel(theta_ref, phi_ref, labels_ref, raw_ref, first_ref, last_ref, angle, label, sems):
+def pack_kernel(theta_ref, phi_ref, labels_ref, region_ref, *refs):
+    raw_ref, first_ref, last_ref, rows_ref, angle, label, region, sems = refs
     height = theta_ref.shape[1]
     copies = [
         pltpu.make_async_copy(theta_ref, angle.at[0], sems.at[0]),
         pltpu.make_async_copy(phi_ref, angle.at[1], sems.at[1]),
         pltpu.make_async_copy(labels_ref, label, sems.at[2]),
+        pltpu.make_async_copy(region_ref, region, sems.at[3]),
     ]
     for copy in copies:
         copy.start()
@@ -173,6 +177,8 @@
         raw_ref[index] = value
         put_edge(first_ref, index, value[:, 0])
         put_edge(last_ref, index, value[:, height - 1])
+    for index in range(rows_ref.shape[0]):
+        rows_ref[index : index + 1] = jnp.full((1, rows_ref.shape[1]), region[index], jnp.float32)
 
 
 def meeting(devices):
@@ -195,11 +201,8 @@
     return jnp.concatenate([ref[row : row + depth] for row in spots], 1)
 
 
-def lines_of(raw_refs, numbers, region_ref, region, sem, table):
-    fetch = pltpu.make_async_copy(region_ref, region, sem)
-    fetch.start()
+def lines_of(raw_refs, numbers, region, table):
     units = [directions(raw_ref[0], raw_ref[1]) for raw_ref in raw_refs]
-    fetch.wait()
     total = None
     for raw_ref, unit, number in zip(raw_refs, units, numbers):
         saturation = looked_up(raw_ref[2], region)
@@ -213,16 +216,16 @@
 
 
 def early_lines_kernel(numbers, *refs):
-    raw_refs, (region_ref, table, out_ref, region, sem) = refs[: len(numbers)], refs[len(numbers) :]
-    out_ref[...] = lines_of(raw_refs, numbers, region_ref, region, sem, table)
+    raw_refs, (region, table, out_ref) = refs[: len(numbers)], refs[len(numbers) :]
+    out_ref[...] = lines_of(raw_refs, numbers, region, table)
 
 
 def lines_kernel(numbers, order_y, *refs):
     raw_refs, operands = refs[: len(numbers)], refs[len(numbers) : len(numbers) + 5]
-    early_ref, first_ref, last_ref, region_ref, table = operands
+    early_ref, first_ref, last_ref, region, table = operands
     gy = lax.axis_index("gy")
-    out_refs, (region, sem) = refs[len(numbers) + 5 : -2], refs[-2:]
-    total = lines_of(raw_refs, numbers, region_ref, region, sem, table) + early_ref[...]
+    out_refs = refs[len(numbers) + 5 :]
+    total = lines_of(raw_refs, numbers, region, table) + early_ref[...]
     lines, lanes = total.shape[0], first_ref.shape[1]
     for spot, (number, out_ref) in enumerate(zip(order_y, out_refs)):
         out_ref[:lines] = total[:, spot * lanes : (spot + 1) * lanes]
@@ -557,15 +560,16 @@
 
     edge_rows = 3 * depth * width // lanes
     edge = f32(edge_rows, lanes)
-    packed, first, last = call(
+    packed, first, last, ms_rows = call(
         pack_kernel,
-        [cells, edge, edge],
-        [hbm] * 3,
-        (theta, phi, labels),
+        [cells, edge, edge, f32(*ms_region.shape, width)],
+        [hbm] * 4,
+        (theta, phi, labels, ms_region),
         scratch=(
             pltpu.VMEM((2, depth, height, width), jnp.float32),
             pltpu.VMEM((depth, height, width), jnp.int32),
-            pltpu.SemaphoreType.DMA((3,)),
+            pltpu.SMEM(ms_region.shape, jnp.float32),
+            pltpu.SemaphoreType.DMA((4,)),
         ),
         name="pack",
     )
@@ -591,23 +595,20 @@
         flops=48 * 2 * rows * lanes * 2 * whole_y,
         name="tensor",
     )
-    region_scratch = (pltpu.SMEM(ms_region.shape, jnp.float32), pltpu.SemaphoreType.DMA)
     early, late = order_x[:-1], order_x[-1:]
     early_sums = call(
         functools.partial(early_lines_kernel, early),
         f32(lines, count_y * lanes),
-        [vmem] * len(early) + [hbm, vmem],
-        (*gathered[:-1], ms_region, held(table)),
-        scratch=region_scratch,
+        [vmem] * len(early) + [vmem, vmem],
+        (*gathered[:-1], ms_rows, held(table)),
         flops=transform_flops * len(early) // count_x,
         name="early_lines",
     )
     spectrum = call(
         functools.partial(lines_kernel, late, order_y),
         [f32(lines + (edge_rows if n in meeting(count_y) else 0), lanes) for n in order_y],
-        [vmem] * 4 + [hbm, vmem],
-        (gathered[-1], early_sums, first, last, ms_region, held(table)),
-        scratch=region_scratch,
+        [vmem] * 6,
+        (gathered[-1], early_sums, first, last, ms_rows, held(table)),
         flops=transform_flops * len(late) // count_x,
         name="lines",
     )

time: 50.1 us -> 49.2 us (0.982)
  Pallas kernels: 12.8 us -> 11.9 us
    pallas_call x11, Pallas kernels: 12.8 us -> 11.9 us  [call(): pl.pallas_call(body, out_shape=out, in_specs=ins, out_specs=[vmem] * len(...]
where the time goes in v12:
time: 49.2 us; the launch traced here: 49 us
  starting transfers between devices  27.5 us (56%)
  Pallas kernels  11.9 us (24%)
  waiting for transfers between devices  8.87 us (18%)
  between operations  0.73 us (1%)
    ppermute x20, starting transfers between devices, swapped(): return lax.ppermute(chunk, axis, [(i, i ^ number) for i in range(devices)])  27.5 us
    pallas_call x11, Pallas kernels, call(): pl.pallas_call(body, out_shape=out, in_specs=ins, out_specs=[vmem] * len(...  11.9 us
    ppermute x20, waiting for transfers between devices, swapped(): return lax.ppermute(chunk, axis, [(i, i ^ number) for i in range(devices)])  8.87 us
  transfers between devices with their start and end apart: 20, of which 9 were waited for; matrix products, arithmetic and copies ran while one was open for 0% of the time, Pallas kernels for 16%

profile of v12, /device:TPU:0, one launch (start us, length us, event | category | flops | bytes accessed | tf_op | source)
XLA Modules:
  0.0 49.0 jit_solution(8118984040157933015)
XLA Ops:
  0.6 0.9 %pack.1 = (f32[3,4,8,256]{3,2,1,0:T(8,128)S(1)}, f32[24,128]{1,0:T(8,128)S(1)}, f32[24,128]{1,0:T(8,128)S(1)}, f32[16,256]{1,0:T(8,128)S(1)}) custom-call(f32[4,8,256]{2,1,0:T(8,128)} %theta_ref.1, f32[4,8,256]{2,1,0:T(8,128)} %phi_ref.1, s32[4,8,256]{2,1,0:T(8,128)} %labels_ref.1, f32[16]{0:T(128)} %refs_7_.1), custom_call_target="tpu_custom_call" | custom-call | bytes 237632 | tf_op jit(solution)/shard_map/pack/pallas_call | solution.py:482
  1.5 3.0 %collective-permute-start = (f32[3,4,8,256]{3,2,1,0:T(8,128)S(1)}, f32[3,4,8,256]{3,2,1,0:T(8,128)S(1)}, u32[]{:S(2)}, u32[]{:S(2)}) collective-permute-start(f32[3,4,8,256]{3,2,1,0:T(8,128)S(1)} %get-tuple-element.50.refs_0_), channel_id=1, source_target_pairs={{0,16},{8,24},{16,0},{24,8},{1,17},{9,25},{17,1},{25,9},{2,18},{10... | collective-permute-start | bytes 294920 | tf_op jit(solution)/shard_map/ppermute | solution.py:500
  4.5 2.6 %load.1 = (bf16[2,4,256,1024]{3,2,1,0:T(8,128)(2,1)S(1)}, bf16[128,384]{1,0:T(8,128)(2,1)S(1)}, bf16[128,384]{1,0:T(8,128)(2,1)S(1)}) custom-call(bf16[4,8,2,4,256,128]{5,4,3,2,1,0:T(8,128)(2,1)} %constant.8.clone.refs_0_, bf16[8,128,384]{2,1,0:T(8,128)(2,1)} %constant.9.clone.refs_1_, bf16[8,128,384]{2,1,0:T(8,128)(2,1)} %constant.10.clone.refs_2_), custom_call_target="tpu_custom_call" | custom-call | bytes 22740992 | tf_op jit(solution)/shard_map/load/pallas_call | solution.py:482
  7.7 1.0 %early_lines.1.refs_1_ = f32[96,1024]{1,0:T(8,128)S(1)} custom-call(f32[3,4,8,256]{3,2,1,0:T(8,128)S(1)} %get-tuple-element.50.refs_0_, f32[3,4,8,256]{3,2,1,0:T(8,128)S(1)} %collective-permute-done.2.refs_1_, f32[3,4,8,256]{3,2,1,0:T(8,128)S(1)} %collective-permute-done.refs_2_, f32[16,256]{1,0:T(8,128)S(1)} %get-tuple-element.53.refs_3_.refs_4_, ...), custom_call_target="tpu_custom_call" | custom-call | flops 452984832 | bytes 4898816 | tf_op jit(solution)/shard_map/early_lines/pallas_call | solution.py:482
  8.7 0.4 lines.1
  9.2 3.9 %collective-permute-start.4 = (f32[96,128]{1,0:T(8,128)S(1)}, f32[96,128]{1,0:T(8,128)S(1)}, u32[]{:S(2)}, u32[]{:S(2)}) collective-permute-start(f32[96,128]{1,0:T(8,128)S(1)} %get-tuple-element.58), channel_id=1, source_target_pairs={{0,6},{1,7},{2,4},{3,5},{4,2},{5,3},{6,0},{7,1},{8,14},{9,15},{10,... | collective-permute-start | bytes 147464 | tf_op jit(solution)/shard_map/ppermute | solution.py:500
  13.4 2.4 %collective-permute-start.3 = (f32[120,128]{1,0:T(8,128)S(1)}, f32[120,128]{1,0:T(8,128)S(1)}, u32[]{:S(2)}, u32[]{:S(2)}) collective-permute-start(f32[120,128]{1,0:T(8,128)S(1)} %get-tuple-element.57), channel_id=1, source_target_pairs={{0,7},{1,6},{2,5},{3,4},{4,3},{5,2},{6,1},{7,0},{8,15},{9,14},{10,... | collective-permute-start | bytes 184328 | tf_op jit(solution)/shard_map/ppermute | solution.py:500
  15.9 2.5 %collective-permute-start.7 = (f32[120,128]{1,0:T(8,128)S(1)}, f32[120,128]{1,0:T(8,128)S(1)}, u32[]{:S(2)}, u32[]{:S(2)}) collective-permute-start(f32[120,128]{1,0:T(8,128)S(1)} %get-tuple-element.61), channel_id=1, source_target_pairs={{0,3},{1,2},{2,1},{3,0},{4,7},{5,6},{6,5},{7,4},{8,11},{9,10},{10,... | collective-permute-start | bytes 184328 | tf_op jit(solution)/shard_map/ppermute | solution.py:500
  18.4 0.5 %collective-permute-start.9 = (f32[120,128]{1,0:T(8,128)S(1)}, f32[120,128]{1,0:T(8,128)S(1)}, u32[]{:S(2)}, u32[]{:S(2)}) collective-permute-start(f32[120,128]{1,0:T(8,128)S(1)} %get-tuple-element.63), channel_id=1, source_target_pairs={{0,1},{1,0},{2,3},{3,2},{4,5},{5,4},{6,7},{7,6},{8,9},{9,8},{10,11... | collective-permute-start | bytes 184328 | tf_op jit(solution)/shard_map/ppermute | solution.py:500
  18.9 1.0 %collective-permute-start.6 = (f32[96,128]{1,0:T(8,128)S(1)}, f32[96,128]{1,0:T(8,128)S(1)}, u32[]{:S(2)}, u32[]{:S(2)}) collective-permute-start(f32[96,128]{1,0:T(8,128)S(1)} %get-tuple-element.60), channel_id=1, source_target_pairs={{0,4},{1,5},{2,6},{3,7},{4,0},{5,1},{6,2},{7,3},{8,12},{9,13},{10,... | collective-permute-start | bytes 147464 | tf_op jit(solution)/shard_map/ppermute | solution.py:500
  19.9 0.7 %collective-permute-done.5.refs_2_ = f32[96,128]{1,0:T(8,128)S(1)} collective-permute-done((f32[96,128]{1,0:T(8,128)S(1)}, f32[96,128]{1,0:T(8,128)S(1)}, u32[]{:S(2)}, u32[]{:S(2)}) %collective-permute-start.5) | collective-permute-done | bytes 49184 | tf_op jit(solution)/shard_map/ppermute | solution.py:500
  20.6 1.6 %tensor.1.refs_8_ = bf16[48,128,128]{2,1,0:T(8,128)(2,1)S(1)} custom-call(bf16[48,64,128]{2,1,0:T(8,128)(2,1)S(1)} %bitcast.1, bf16[64,128]{1,0:T(8,128)(2,1)S(1)} %copy-done.1), custom_call_target="tpu_custom_call" | custom-call | flops 100663296 | bytes 2375680 | tf_op jit(solution)/shard_map/tensor/pallas_call | solution.py:482
  22.2 2.2 %collective-permute-done.6.refs_3_ = f32[96,128]{1,0:T(8,128)S(1)} collective-permute-done((f32[96,128]{1,0:T(8,128)S(1)}, f32[96,128]{1,0:T(8,128)S(1)}, u32[]{:S(2)}, u32[]{:S(2)}) %collective-permute-start.6) | collective-permute-done | bytes 49184 | tf_op jit(solution)/shard_map/ppermute | solution.py:500
  24.3 0.5 %collective-permute-done.8.refs_5_ = f32[96,128]{1,0:T(8,128)S(1)} collective-permute-done((f32[96,128]{1,0:T(8,128)S(1)}, f32[96,128]{1,0:T(8,128)S(1)}, u32[]{:S(2)}, u32[]{:S(2)}) %collective-permute-start.8) | collective-permute-done | bytes 49184 | tf_op jit(solution)/shard_map/ppermute | solution.py:500
  24.8 1.7 %waves.1 = (f32[96,128]{1,0:T(8,128)S(1)}, f32[96,128]{1,0:T(8,128)S(1)}, f32[96,128]{1,0:T(8,128)S(1)}, f32[96,128]{1,0:T(8,128)S(1)}, f32[96,128]{1,0:T(8,128)...) custom-call(f32[120,128]{1,0:T(8,128)S(1)} %collective-permute-done.3.refs_0_.refs_6_, ...), custom_call_target="tpu_custom_call" | custom-call | flops 125829120 | bytes 2592768 | tf_op jit(solution)/shard_map/waves/pallas_call | solution.py:482
  26.6 2.6 %collective-permute-start.10 = (f32[96,128]{1,0:T(8,128)S(1)}, f32[96,128]{1,0:T(8,128)S(1)}, u32[]{:S(2)}, u32[]{:S(2)}) collective-permute-start(f32[96,128]{1,0:T(8,128)S(1)} %get-tuple-element.75), channel_id=1, source_target_pairs={{0,7},{1,6},{2,5},{3,4},{4,3},{5,2},{6,1},{7,0},{8,15},{9,14},{10,... | collective-permute-start | bytes 147464 | tf_op jit(solution)/shard_map/ppermute | solution.py:500
  29.2 2.3 %collective-permute-start.11 = (f32[96,128]{1,0:T(8,128)S(1)}, f32[96,128]{1,0:T(8,128)S(1)}, u32[]{:S(2)}, u32[]{:S(2)}) collective-permute-start(f32[96,128]{1,0:T(8,128)S(1)} %get-tuple-element.76), channel_id=1, source_target_pairs={{0,6},{1,7},{2,4},{3,5},{4,2},{5,3},{6,0},{7,1},{8,14},{9,15},{10,... | collective-permute-start | bytes 147464 | tf_op jit(solution)/shard_map/ppermute | solution.py:500
  31.5 2.8 %collective-permute-start.13 = (f32[96,128]{1,0:T(8,128)S(1)}, f32[96,128]{1,0:T(8,128)S(1)}, u32[]{:S(2)}, u32[]{:S(2)}) collective-permute-start(f32[96,128]{1,0:T(8,128)S(1)} %get-tuple-element.78), channel_id=1, source_target_pairs={{0,4},{1,5},{2,6},{3,7},{4,0},{5,1},{6,2},{7,3},{8,12},{9,13},{10,... | collective-permute-start | bytes 147464 | tf_op jit(solution)/shard_map/ppermute | solution.py:500
  34.5 2.9 %collective-permute-start.15 = (f32[96,128]{1,0:T(8,128)S(1)}, f32[96,128]{1,0:T(8,128)S(1)}, u32[]{:S(2)}, u32[]{:S(2)}) collective-permute-start(f32[96,128]{1,0:T(8,128)S(1)} %get-tuple-element.80), channel_id=1, source_target_pairs={{0,2},{1,3},{2,0},{3,1},{4,6},{5,7},{6,4},{7,5},{8,10},{9,11},{10,... | collective-permute-start | bytes 147464 | tf_op jit(solution)/shard_map/ppermute | solution.py:500
  37.4 0.4 collective-permute-start.16
  37.8 0.5 %collective-permute-done.13.refs_3_ = f32[96,128]{1,0:T(8,128)S(1)} collective-permute-done((f32[96,128]{1,0:T(8,128)S(1)}, f32[96,128]{1,0:T(8,128)S(1)}, u32[]{:S(2)}, u32[]{:S(2)}) %collective-permute-start.13) | collective-permute-done | bytes 49184 | tf_op jit(solution)/shard_map/ppermute | solution.py:500
  38.3 1.0 %collective-permute-done.14.refs_4_ = f32[96,128]{1,0:T(8,128)S(1)} collective-permute-done((f32[96,128]{1,0:T(8,128)S(1)}, f32[96,128]{1,0:T(8,128)S(1)}, u32[]{:S(2)}, u32[]{:S(2)}) %collective-permute-start.14) | collective-permute-done | bytes 49184 | tf_op jit(solution)/shard_map/ppermute | solution.py:500
  39.3 0.6 %collective-permute-done.15.refs_5_ = f32[96,128]{1,0:T(8,128)S(1)} collective-permute-done((f32[96,128]{1,0:T(8,128)S(1)}, f32[96,128]{1,0:T(8,128)S(1)}, u32[]{:S(2)}, u32[]{:S(2)}) %collective-permute-start.15) | collective-permute-done | bytes 49184 | tf_op jit(solution)/shard_map/ppermute | solution.py:500
  39.9 1.5 %collective-permute-done.16.refs_6_ = f32[96,128]{1,0:T(8,128)S(1)} collective-permute-done((f32[96,128]{1,0:T(8,128)S(1)}, f32[96,128]{1,0:T(8,128)S(1)}, u32[]{:S(2)}, u32[]{:S(2)}) %collective-permute-start.16) | collective-permute-done | bytes 49184 | tf_op jit(solution)/shard_map/ppermute | solution.py:500
  41.5 0.5 back_across.1
  42.0 0.8 %back_within.1 = (f32[96,256]{1,0:T(8,128)S(1)}, f32[96,256]{1,0:T(8,128)S(1)}) custom-call(f32[96,128]{1,0:T(8,128)S(1)} %collective-permute-done.10.refs_0_, f32[96,128]{1,0:T(8,128)S(1)} %collective-permute-done.11.refs_1_, f32[96,128]{1,0:T(8,128)S(1)} %collective-permute-done.12.refs_2_, f32[96,128]{1,0:T(8,128)S(1)} %collective-permute-done.13.refs_3_, ...), custom_call_target="tpu_custom_call" | custom-call | flops 301989888 | bytes 4784128 | tf_op jit(solution)/shard_map/back_within/pallas_call | solution.py:482
  42.8 0.6 %collective-permute-start.18 = (f32[96,256]{1,0:T(8,128)S(1)}, f32[96,256]{1,0:T(8,128)S(1)}, u32[]{:S(2)}, u32[]{:S(2)}) collective-permute-start(f32[96,256]{1,0:T(8,128)S(1)} %get-tuple-element.92), channel_id=1, source_target_pairs={{0,8},{8,0},{16,24},{24,16},{1,9},{9,1},{17,25},{25,17},{2,10},{10... | collective-permute-start | bytes 294920 | tf_op jit(solution)/shard_map/ppermute | solution.py:500
  43.4 1.5 %collective-permute-start.19 = (f32[96,256]{1,0:T(8,128)S(1)}, f32[96,256]{1,0:T(8,128)S(1)}, u32[]{:S(2)}, u32[]{:S(2)}) collective-permute-start(f32[96,256]{1,0:T(8,128)S(1)} %add.3), channel_id=1, source_target_pairs={{0,16},{8,24},{16,0},{24,8},{1,17},{9,25},{17,1},{25,9},{2,18},{10... | collective-permute-start | bytes 294920 | tf_op jit(solution)/shard_map/ppermute | solution.py:500
  44.9 1.1 %exchange.1 = (f32[3,4,8,256]{3,2,1,0:T(8,128)S(1)}, f32[3,4,8,256]{3,2,1,0:T(8,128)S(1)}) custom-call(f32[3,4,8,256]{3,2,1,0:T(8,128)S(1)} %get-tuple-element.50.refs_0_, f32[3,4,8,256]{3,2,1,0:T(8,128)S(1)} %collective-permute-done.2.refs_1_, f32[3,4,8,256]{3,2,1,0:T(8,128)S(1)} %collective-permute-done.refs_2_, ...), custom_call_target="tpu_custom_call" | custom-call | flops 2457600 | bytes 774272 | tf_op jit(solution)/shard_map/exchange/pallas_call | solution.py:482
  46.1 0.5 back_own.1.refs_0_
  46.5 1.7 %collective-permute-done.19.refs_2_ = f32[96,256]{1,0:T(8,128)S(1)} collective-permute-done((f32[96,256]{1,0:T(8,128)S(1)}, f32[96,256]{1,0:T(8,128)S(1)}, u32[]{:S(2)}, u32[]{:S(2)}) %collective-permute-start.19) | collective-permute-done | bytes 98336 | tf_op jit(solution)/shard_map/ppermute | solution.py:500
  48.2 0.7 %predict.1 = (f32[3,4,8,256]{3,2,1,0:T(8,128)}, f32[3,4,8,256]{3,2,1,0:T(8,128)}) custom-call(f32[96,256]{1,0:T(8,128)S(1)} %back_own.1.refs_0_, f32[96,256]{1,0:T(8,128)S(1)} %collective-permute-done.18.refs_1_, f32[96,256]{1,0:T(8,128)S(1)} %collective-permute-done.19.refs_2_, f32[3,4,8,256]{3,2,1,0:T(8,128)S(1)} %get-tuple-element.96.refs_3_, ...), custom_call_target="tpu_custom_call" | custom-call | flops 491520 | bytes 688128 | tf_op jit(solution)/shard_map/predict/pallas_call | solution.py:482
  (28 shorter events, 1.2 us)
Async XLA Ops:
  1.5 5.8 %collective-permute-start = (f32[3,4,8,256]{3,2,1,0:T(8,128)S(1)}, f32[3,4,8,256]{3,2,1,0:T(8,128)S(1)}, u32[]{:S(2)}, u32[]{:S(2)}) collective-permute-start(f32[3,4,8,256]{3,2,1,0:T(8,128)S(1)} %get-tuple-element.50.refs_0_), channel_id=1, source_target_pairs={{0,16},{8,24},{16,0},{24,8},{1,17},{9,25},{17,1},{25,9},{2,18},{10... | collective-permute-start | bytes 294920 | tf_op jit(solution)/shard_map/ppermute | solution.py:500
  4.5 3.2 %collective-permute-start.2 = (f32[3,4,8,256]{3,2,1,0:T(8,128)S(1)}, f32[3,4,8,256]{3,2,1,0:T(8,128)S(1)}, u32[]{:S(2)}, u32[]{:S(2)}) collective-permute-start(f32[3,4,8,256]{3,2,1,0:T(8,128)S(1)} %get-tuple-element.50.refs_0_), channel_id=1, source_target_pairs={{0,8},{8,0},{16,24},{24,16},{1,9},{9,1},{17,25},{25,17},{2,10},{10... | collective-permute-start | bytes 294920 | tf_op jit(solution)/shard_map/ppermute | solution.py:500
  7.3 1.4 %collective-permute-start.1 = (f32[3,4,8,256]{3,2,1,0:T(8,128)S(1)}, f32[3,4,8,256]{3,2,1,0:T(8,128)S(1)}, u32[]{:S(2)}, u32[]{:S(2)}) collective-permute-start(f32[3,4,8,256]{3,2,1,0:T(8,128)S(1)} %collective-permute-done.refs_2_), channel_id=1, source_target_pairs={{0,8},{8,0},{16,24},{24,16},{1,9},{9,1},{17,25},{25,17},{2,10},{10... | collective-permute-start | bytes 294920 | tf_op jit(solution)/shard_map/ppermute | solution.py:500
  7.7 12.9 %copy-start = (bf16[6,8,64,128]{3,2,1,0:T(8,128)(2,1)S(1)}, bf16[6,8,64,128]{3,2,1,0:T(8,128)(2,1)}, u32[]{:S(2)}) copy-start(bf16[6,8,64,128]{3,2,1,0:T(8,128)(2,1)} %param.15) | copy-start | bytes 2359300
  7.7 12.9 %copy-start.1 = (bf16[64,128]{1,0:T(8,128)(2,1)S(1)}, bf16[64,128]{1,0:T(8,128)(2,1)}, u32[]{:S(2)}) copy-start(bf16[64,128]{1,0:T(8,128)(2,1)} %constant.11.clone.twice_ref) | copy-start | bytes 49156
  9.2 9.7 %collective-permute-start.4 = (f32[96,128]{1,0:T(8,128)S(1)}, f32[96,128]{1,0:T(8,128)S(1)}, u32[]{:S(2)}, u32[]{:S(2)}) collective-permute-start(f32[96,128]{1,0:T(8,128)S(1)} %get-tuple-element.58), channel_id=1, source_target_pairs={{0,6},{1,7},{2,4},{3,5},{4,2},{5,3},{6,0},{7,1},{8,14},{9,15},{10,... | collective-permute-start | bytes 147464 | tf_op jit(solution)/shard_map/ppermute | solution.py:500
  13.0 7.5 %collective-permute-start.5 = (f32[96,128]{1,0:T(8,128)S(1)}, f32[96,128]{1,0:T(8,128)S(1)}, u32[]{:S(2)}, u32[]{:S(2)}) collective-permute-start(f32[96,128]{1,0:T(8,128)S(1)} %get-tuple-element.59), channel_id=1, source_target_pairs={{0,5},{1,4},{2,7},{3,6},{4,1},{5,0},{6,3},{7,2},{8,13},{9,12},{10,... | collective-permute-start | bytes 147464 | tf_op jit(solution)/shard_map/ppermute | solution.py:500
  13.4 11.4 %collective-permute-start.3 = (f32[120,128]{1,0:T(8,128)S(1)}, f32[120,128]{1,0:T(8,128)S(1)}, u32[]{:S(2)}, u32[]{:S(2)}) collective-permute-start(f32[120,128]{1,0:T(8,128)S(1)} %get-tuple-element.57), channel_id=1, source_target_pairs={{0,7},{1,6},{2,5},{3,4},{4,3},{5,2},{6,1},{7,0},{8,15},{9,14},{10,... | collective-permute-start | bytes 184328 | tf_op jit(solution)/shard_map/ppermute | solution.py:500
  15.9 9.0 %collective-permute-start.7 = (f32[120,128]{1,0:T(8,128)S(1)}, f32[120,128]{1,0:T(8,128)S(1)}, u32[]{:S(2)}, u32[]{:S(2)}) collective-permute-start(f32[120,128]{1,0:T(8,128)S(1)} %get-tuple-element.61), channel_id=1, source_target_pairs={{0,3},{1,2},{2,1},{3,0},{4,7},{5,6},{6,5},{7,4},{8,11},{9,10},{10,... | collective-permute-start | bytes 184328 | tf_op jit(solution)/shard_map/ppermute | solution.py:500
  18.4 6.4 %collective-permute-start.9 = (f32[120,128]{1,0:T(8,128)S(1)}, f32[120,128]{1,0:T(8,128)S(1)}, u32[]{:S(2)}, u32[]{:S(2)}) collective-permute-start(f32[120,128]{1,0:T(8,128)S(1)} %get-tuple-element.63), channel_id=1, source_target_pairs={{0,1},{1,0},{2,3},{3,2},{4,5},{5,4},{6,7},{7,6},{8,9},{9,8},{10,11... | collective-permute-start | bytes 184328 | tf_op jit(solution)/shard_map/ppermute | solution.py:500
  18.9 5.4 %collective-permute-start.6 = (f32[96,128]{1,0:T(8,128)S(1)}, f32[96,128]{1,0:T(8,128)S(1)}, u32[]{:S(2)}, u32[]{:S(2)}) collective-permute-start(f32[96,128]{1,0:T(8,128)S(1)} %get-tuple-element.60), channel_id=1, source_target_pairs={{0,4},{1,5},{2,6},{3,7},{4,0},{5,1},{6,2},{7,3},{8,12},{9,13},{10,... | collective-permute-start | bytes 147464 | tf_op jit(solution)/shard_map/ppermute | solution.py:500
  20.6 4.3 %collective-permute-start.8 = (f32[96,128]{1,0:T(8,128)S(1)}, f32[96,128]{1,0:T(8,128)S(1)}, u32[]{:S(2)}, u32[]{:S(2)}) collective-permute-start(f32[96,128]{1,0:T(8,128)S(1)} %get-tuple-element.62), channel_id=1, source_target_pairs={{0,2},{1,3},{2,0},{3,1},{4,6},{5,7},{6,4},{7,5},{8,10},{9,11},{10,... | collective-permute-start | bytes 147464 | tf_op jit(solution)/shard_map/ppermute | solution.py:500
  26.6 7.9 %collective-permute-start.10 = (f32[96,128]{1,0:T(8,128)S(1)}, f32[96,128]{1,0:T(8,128)S(1)}, u32[]{:S(2)}, u32[]{:S(2)}) collective-permute-start(f32[96,128]{1,0:T(8,128)S(1)} %get-tuple-element.75), channel_id=1, source_target_pairs={{0,7},{1,6},{2,5},{3,4},{4,3},{5,2},{6,1},{7,0},{8,15},{9,14},{10,... | collective-permute-start | bytes 147464 | tf_op jit(solution)/shard_map/ppermute | solution.py:500
  29.2 8.2 %collective-permute-start.11 = (f32[96,128]{1,0:T(8,128)S(1)}, f32[96,128]{1,0:T(8,128)S(1)}, u32[]{:S(2)}, u32[]{:S(2)}) collective-permute-start(f32[96,128]{1,0:T(8,128)S(1)} %get-tuple-element.76), channel_id=1, source_target_pairs={{0,6},{1,7},{2,4},{3,5},{4,2},{5,3},{6,0},{7,1},{8,14},{9,15},{10,... | collective-permute-start | bytes 147464 | tf_op jit(solution)/shard_map/ppermute | solution.py:500
  31.5 6.3 %collective-permute-start.12 = (f32[96,128]{1,0:T(8,128)S(1)}, f32[96,128]{1,0:T(8,128)S(1)}, u32[]{:S(2)}, u32[]{:S(2)}) collective-permute-start(f32[96,128]{1,0:T(8,128)S(1)} %get-tuple-element.77), channel_id=1, source_target_pairs={{0,5},{1,4},{2,7},{3,6},{4,1},{5,0},{6,3},{7,2},{8,13},{9,12},{10,... | collective-permute-start | bytes 147464 | tf_op jit(solution)/shard_map/ppermute | solution.py:500
  31.5 6.8 %collective-permute-start.13 = (f32[96,128]{1,0:T(8,128)S(1)}, f32[96,128]{1,0:T(8,128)S(1)}, u32[]{:S(2)}, u32[]{:S(2)}) collective-permute-start(f32[96,128]{1,0:T(8,128)S(1)} %get-tuple-element.78), channel_id=1, source_target_pairs={{0,4},{1,5},{2,6},{3,7},{4,0},{5,1},{6,2},{7,3},{8,12},{9,13},{10,... | collective-permute-start | bytes 147464 | tf_op jit(solution)/shard_map/ppermute | solution.py:500
  34.3 5.0 %collective-permute-start.14 = (f32[96,128]{1,0:T(8,128)S(1)}, f32[96,128]{1,0:T(8,128)S(1)}, u32[]{:S(2)}, u32[]{:S(2)}) collective-permute-start(f32[96,128]{1,0:T(8,128)S(1)} %get-tuple-element.79), channel_id=1, source_target_pairs={{0,3},{1,2},{2,1},{3,0},{4,7},{5,6},{6,5},{7,4},{8,11},{9,10},{10,... | collective-permute-start | bytes 147464 | tf_op jit(solution)/shard_map/ppermute | solution.py:500
  34.5 5.5 %collective-permute-start.15 = (f32[96,128]{1,0:T(8,128)S(1)}, f32[96,128]{1,0:T(8,128)S(1)}, u32[]{:S(2)}, u32[]{:S(2)}) collective-permute-start(f32[96,128]{1,0:T(8,128)S(1)} %get-tuple-element.80), channel_id=1, source_target_pairs={{0,2},{1,3},{2,0},{3,1},{4,6},{5,7},{6,4},{7,5},{8,10},{9,11},{10,... | collective-permute-start | bytes 147464 | tf_op jit(solution)/shard_map/ppermute | solution.py:500
  37.4 4.1 %collective-permute-start.16 = (f32[96,128]{1,0:T(8,128)S(1)}, f32[96,128]{1,0:T(8,128)S(1)}, u32[]{:S(2)}, u32[]{:S(2)}) collective-permute-start(f32[96,128]{1,0:T(8,128)S(1)} %get-tuple-element.81), channel_id=1, source_target_pairs={{0,1},{1,0},{2,3},{3,2},{4,5},{5,4},{6,7},{7,6},{8,9},{9,8},{10,11... | collective-permute-start | bytes 147464 | tf_op jit(solution)/shard_map/ppermute | solution.py:500
  41.5 3.5 %copy-start.2 = (f32[16]{0:T(128)S(1)}, f32[16]{0:T(128)}, u32[]{:S(2)}) copy-start(f32[16]{0:T(128)} %refs_7_.1) | copy-start | bytes 196
  41.5 3.5 %copy-start.3 = (f32[16]{0:T(128)S(1)}, f32[16]{0:T(128)}, u32[]{:S(2)}) copy-start(f32[16]{0:T(128)} %refs_8_.1) | copy-start | bytes 196
  41.9 1.4 %collective-permute-start.17 = (f32[96,256]{1,0:T(8,128)S(1)}, f32[96,256]{1,0:T(8,128)S(1)}, u32[]{:S(2)}, u32[]{:S(2)}) collective-permute-start(f32[96,256]{1,0:T(8,128)S(1)} %back_across.1), channel_id=1, source_target_pairs={{0,8},{8,0},{16,24},{24,16},{1,9},{9,1},{17,25},{25,17},{2,10},{10... | collective-permute-start | bytes 294920 | tf_op jit(solution)/shard_map/ppermute | solution.py:500
  42.8 3.7 %collective-permute-start.18 = (f32[96,256]{1,0:T(8,128)S(1)}, f32[96,256]{1,0:T(8,128)S(1)}, u32[]{:S(2)}, u32[]{:S(2)}) collective-permute-start(f32[96,256]{1,0:T(8,128)S(1)} %get-tuple-element.92), channel_id=1, source_target_pairs={{0,8},{8,0},{16,24},{24,16},{1,9},{9,1},{17,25},{25,17},{2,10},{10... | collective-permute-start | bytes 294920 | tf_op jit(solution)/shard_map/ppermute | solution.py:500
  43.4 4.8 %collective-permute-start.19 = (f32[96,256]{1,0:T(8,128)S(1)}, f32[96,256]{1,0:T(8,128)S(1)}, u32[]{:S(2)}, u32[]{:S(2)}) collective-permute-start(f32[96,256]{1,0:T(8,128)S(1)} %add.3), channel_id=1, source_target_pairs={{0,16},{8,24},{16,0},{24,8},{1,17},{9,25},{17,1},{25,9},{2,18},{10... | collective-permute-start | bytes 294920 | tf_op jit(solution)/shard_map/ppermute | solution.py:500

commit v13 on v12

--- a/solution.py
+++ b/solution.py
@@ -185,6 +185,10 @@
     return [number for number in range(1, devices) if (number & (number + 1)) == 0]
 
 
+def carrying(devices):
+    return meeting(devices) + [devices // 2]
+
+
 def edge_spots(depth, width, lanes, start, field):
     pieces = width // lanes
     return [start + (field * pieces + piece) * depth for piece in range(pieces)]
@@ -229,7 +233,7 @@
     lines, lanes = total.shape[0], first_ref.shape[1]
     for spot, (number, out_ref) in enumerate(zip(order_y, out_refs)):
         out_ref[:lines] = total[:, spot * lanes : (spot + 1) * lanes]
-        if number in meeting(len(order_y)):
+        if number in carrying(len(order_y)):
             up = lax.bitwise_xor(gy, number) > gy
             out_ref[lines:] = jnp.where(up, last_ref[...], first_ref[...])
 
@@ -508,6 +512,10 @@
     return pltpu.with_memory_space_constraint(value, pltpu.VMEM)
 
 
+def chunk_order(devices):
+    return list(range(devices - 1, -1, -1))
+
+
 def after(value, other):
     return lax.optimization_barrier((value, other))[0]
 
@@ -547,7 +555,7 @@
     whole_y = count_y * height
 
     cells = f32(3, depth, height, width)
-    order_x, order_y = list(range(count_x)), list(range(count_y - 1, -1, -1))
+    order_x, order_y = list(range(count_x)), chunk_order(count_y)
     table = line_table(count_x, count_y, width, rows)
     if table is None:
         table = line_table_here(count_x, width, rows, order_y)
@@ -606,7 +614,7 @@
     )
     spectrum = call(
         functools.partial(lines_kernel, late, order_y),
-        [f32(lines + (edge_rows if n in meeting(count_y) else 0), lanes) for n in order_y],
+        [f32(lines + (edge_rows if n in carrying(count_y) else 0), lanes) for n in order_y],
         [vmem] * 6,
         (gathered[-1], early_sums, first, last, ms_rows, held(table)),
         flops=transform_flops * len(late) // count_x,

time: 49.2 us -> 49.7 us (1.010)
  waiting for transfers between devices: 8.87 us -> 9.43 us
    ppermute x20, waiting for transfers between devices: 8.87 us -> 9.43 us  [swapped(): return lax.ppermute(chunk, axis, [(i, i ^ number) for i in range(devices)])]
  transfers between devices with their start and end apart: 20 -> 20, of which waited for: 9 -> 7; matrix products, arithmetic and copies ran while one was open for 0% -> 0% of each run, Pallas kernels for 16% -> 15%
where the time goes in v13:
time: 49.7 us; the launch traced here: 49.5 us
  starting transfers between devices  27.5 us (55%)
  Pallas kernels  11.8 us (24%)
  waiting for transfers between devices  9.43 us (19%)
  between operations  0.75 us (2%)
    ppermute x20, starting transfers between devices, swapped(): return lax.ppermute(chunk, axis, [(i, i ^ number) for i in range(devices)])  27.5 us
    pallas_call x11, Pallas kernels, call(): pl.pallas_call(body, out_shape=out, in_specs=ins, out_specs=[vmem] * len(...  11.8 us
    ppermute x20, waiting for transfers between devices, swapped(): return lax.ppermute(chunk, axis, [(i, i ^ number) for i in range(devices)])  9.43 us
  transfers between devices with their start and end apart: 20, of which 7 were waited for; matrix products, arithmetic and copies ran while one was open for 0% of the time, Pallas kernels for 15%

profile of v13, /device:TPU:0, one launch (start us, length us, event | category | flops | bytes accessed | tf_op | source)
XLA Modules:
  0.0 49.5 jit_solution(5694385709438744624)
XLA Ops:
  0.6 0.9 %pack.1 = (f32[3,4,8,256]{3,2,1,0:T(8,128)S(1)}, f32[24,128]{1,0:T(8,128)S(1)}, f32[24,128]{1,0:T(8,128)S(1)}, f32[16,256]{1,0:T(8,128)S(1)}) custom-call(f32[4,8,256]{2,1,0:T(8,128)} %theta_ref.1, f32[4,8,256]{2,1,0:T(8,128)} %phi_ref.1, s32[4,8,256]{2,1,0:T(8,128)} %labels_ref.1, f32[16]{0:T(128)} %refs_7_.1), custom_call_target="tpu_custom_call" | custom-call | bytes 237632 | tf_op jit(solution)/shard_map/pack/pallas_call | solution.py:486
  1.5 3.0 %collective-permute-start = (f32[3,4,8,256]{3,2,1,0:T(8,128)S(1)}, f32[3,4,8,256]{3,2,1,0:T(8,128)S(1)}, u32[]{:S(2)}, u32[]{:S(2)}) collective-permute-start(f32[3,4,8,256]{3,2,1,0:T(8,128)S(1)} %get-tuple-element.50.refs_0_), channel_id=1, source_target_pairs={{0,16},{8,24},{16,0},{24,8},{1,17},{9,25},{17,1},{25,9},{2,18},{10... | collective-permute-start | bytes 294920 | tf_op jit(solution)/shard_map/ppermute | solution.py:504
  4.5 2.6 %load.1 = (bf16[2,4,256,1024]{3,2,1,0:T(8,128)(2,1)S(1)}, bf16[128,384]{1,0:T(8,128)(2,1)S(1)}, bf16[128,384]{1,0:T(8,128)(2,1)S(1)}) custom-call(bf16[4,8,2,4,256,128]{5,4,3,2,1,0:T(8,128)(2,1)} %constant.8.clone.refs_0_, bf16[8,128,384]{2,1,0:T(8,128)(2,1)} %constant.9.clone.refs_1_, bf16[8,128,384]{2,1,0:T(8,128)(2,1)} %constant.10.clone.refs_2_), custom_call_target="tpu_custom_call" | custom-call | bytes 22740992 | tf_op jit(solution)/shard_map/load/pallas_call | solution.py:486
  7.3 0.4 collective-permute-start.1
  7.7 1.0 %early_lines.1.refs_1_ = f32[96,1024]{1,0:T(8,128)S(1)} custom-call(f32[3,4,8,256]{3,2,1,0:T(8,128)S(1)} %get-tuple-element.50.refs_0_, f32[3,4,8,256]{3,2,1,0:T(8,128)S(1)} %collective-permute-done.2.refs_1_, f32[3,4,8,256]{3,2,1,0:T(8,128)S(1)} %collective-permute-done.refs_2_, f32[16,256]{1,0:T(8,128)S(1)} %get-tuple-element.53.refs_3_.refs_4_, ...), custom_call_target="tpu_custom_call" | custom-call | flops 452984832 | bytes 4898816 | tf_op jit(solution)/shard_map/early_lines/pallas_call | solution.py:486
  8.7 0.5 lines.1
  9.2 3.9 %collective-permute-start.4 = (f32[96,128]{1,0:T(8,128)S(1)}, f32[96,128]{1,0:T(8,128)S(1)}, u32[]{:S(2)}, u32[]{:S(2)}) collective-permute-start(f32[96,128]{1,0:T(8,128)S(1)} %get-tuple-element.58), channel_id=1, source_target_pairs={{0,6},{1,7},{2,4},{3,5},{4,2},{5,3},{6,0},{7,1},{8,14},{9,15},{10,... | collective-permute-start | bytes 147464 | tf_op jit(solution)/shard_map/ppermute | solution.py:504
  13.4 2.4 %collective-permute-start.3 = (f32[120,128]{1,0:T(8,128)S(1)}, f32[120,128]{1,0:T(8,128)S(1)}, u32[]{:S(2)}, u32[]{:S(2)}) collective-permute-start(f32[120,128]{1,0:T(8,128)S(1)} %get-tuple-element.57), channel_id=1, source_target_pairs={{0,7},{1,6},{2,5},{3,4},{4,3},{5,2},{6,1},{7,0},{8,15},{9,14},{10,... | collective-permute-start | bytes 184328 | tf_op jit(solution)/shard_map/ppermute | solution.py:504
  15.9 1.1 %collective-permute-start.6 = (f32[120,128]{1,0:T(8,128)S(1)}, f32[120,128]{1,0:T(8,128)S(1)}, u32[]{:S(2)}, u32[]{:S(2)}) collective-permute-start(f32[120,128]{1,0:T(8,128)S(1)} %get-tuple-element.60), channel_id=1, source_target_pairs={{0,4},{1,5},{2,6},{3,7},{4,0},{5,1},{6,2},{7,3},{8,12},{9,13},{10,... | collective-permute-start | bytes 184328 | tf_op jit(solution)/shard_map/ppermute | solution.py:504
  16.9 1.8 %collective-permute-start.7 = (f32[120,128]{1,0:T(8,128)S(1)}, f32[120,128]{1,0:T(8,128)S(1)}, u32[]{:S(2)}, u32[]{:S(2)}) collective-permute-start(f32[120,128]{1,0:T(8,128)S(1)} %get-tuple-element.61), channel_id=1, source_target_pairs={{0,3},{1,2},{2,1},{3,0},{4,7},{5,6},{6,5},{7,4},{8,11},{9,10},{10,... | collective-permute-start | bytes 184328 | tf_op jit(solution)/shard_map/ppermute | solution.py:504
  18.7 1.1 %collective-permute-start.9 = (f32[120,128]{1,0:T(8,128)S(1)}, f32[120,128]{1,0:T(8,128)S(1)}, u32[]{:S(2)}, u32[]{:S(2)}) collective-permute-start(f32[120,128]{1,0:T(8,128)S(1)} %get-tuple-element.63), channel_id=1, source_target_pairs={{0,1},{1,0},{2,3},{3,2},{4,5},{5,4},{6,7},{7,6},{8,9},{9,8},{10,11... | collective-permute-start | bytes 184328 | tf_op jit(solution)/shard_map/ppermute | solution.py:504
  19.9 1.6 %collective-permute-done.5.refs_2_ = f32[96,128]{1,0:T(8,128)S(1)} collective-permute-done((f32[96,128]{1,0:T(8,128)S(1)}, f32[96,128]{1,0:T(8,128)S(1)}, u32[]{:S(2)}, u32[]{:S(2)}) %collective-permute-start.5) | collective-permute-done | bytes 49184 | tf_op jit(solution)/shard_map/ppermute | solution.py:504
  21.4 1.6 %tensor.1.refs_8_ = bf16[48,128,128]{2,1,0:T(8,128)(2,1)S(1)} custom-call(bf16[48,64,128]{2,1,0:T(8,128)(2,1)S(1)} %bitcast.1, bf16[64,128]{1,0:T(8,128)(2,1)S(1)} %copy-done.1), custom_call_target="tpu_custom_call" | custom-call | flops 100663296 | bytes 2375680 | tf_op jit(solution)/shard_map/tensor/pallas_call | solution.py:486
  23.0 2.5 %collective-permute-done.8.refs_5_ = f32[96,128]{1,0:T(8,128)S(1)} collective-permute-done((f32[96,128]{1,0:T(8,128)S(1)}, f32[96,128]{1,0:T(8,128)S(1)}, u32[]{:S(2)}, u32[]{:S(2)}) %collective-permute-start.8) | collective-permute-done | bytes 49184 | tf_op jit(solution)/shard_map/ppermute | solution.py:504
  25.5 1.7 %waves.1 = (f32[96,128]{1,0:T(8,128)S(1)}, f32[96,128]{1,0:T(8,128)S(1)}, f32[96,128]{1,0:T(8,128)S(1)}, f32[96,128]{1,0:T(8,128)S(1)}, f32[96,128]{1,0:T(8,128)...) custom-call(f32[120,128]{1,0:T(8,128)S(1)} %collective-permute-done.3.refs_0_.refs_6_, ...), custom_call_target="tpu_custom_call" | custom-call | flops 125829120 | bytes 2605056 | tf_op jit(solution)/shard_map/waves/pallas_call | solution.py:486
  27.3 3.0 %collective-permute-start.10 = (f32[96,128]{1,0:T(8,128)S(1)}, f32[96,128]{1,0:T(8,128)S(1)}, u32[]{:S(2)}, u32[]{:S(2)}) collective-permute-start(f32[96,128]{1,0:T(8,128)S(1)} %get-tuple-element.75), channel_id=1, source_target_pairs={{0,7},{1,6},{2,5},{3,4},{4,3},{5,2},{6,1},{7,0},{8,15},{9,14},{10,... | collective-permute-start | bytes 147464 | tf_op jit(solution)/shard_map/ppermute | solution.py:504
  30.2 1.8 %collective-permute-start.11 = (f32[96,128]{1,0:T(8,128)S(1)}, f32[96,128]{1,0:T(8,128)S(1)}, u32[]{:S(2)}, u32[]{:S(2)}) collective-permute-start(f32[96,128]{1,0:T(8,128)S(1)} %get-tuple-element.76), channel_id=1, source_target_pairs={{0,6},{1,7},{2,4},{3,5},{4,2},{5,3},{6,0},{7,1},{8,14},{9,15},{10,... | collective-permute-start | bytes 147464 | tf_op jit(solution)/shard_map/ppermute | solution.py:504
  32.0 2.9 %collective-permute-start.13 = (f32[96,128]{1,0:T(8,128)S(1)}, f32[96,128]{1,0:T(8,128)S(1)}, u32[]{:S(2)}, u32[]{:S(2)}) collective-permute-start(f32[96,128]{1,0:T(8,128)S(1)} %get-tuple-element.78), channel_id=1, source_target_pairs={{0,4},{1,5},{2,6},{3,7},{4,0},{5,1},{6,2},{7,3},{8,12},{9,13},{10,... | collective-permute-start | bytes 147464 | tf_op jit(solution)/shard_map/ppermute | solution.py:504
  35.0 0.5 %collective-permute-start.14 = (f32[96,128]{1,0:T(8,128)S(1)}, f32[96,128]{1,0:T(8,128)S(1)}, u32[]{:S(2)}, u32[]{:S(2)}) collective-permute-start(f32[96,128]{1,0:T(8,128)S(1)} %get-tuple-element.79), channel_id=1, source_target_pairs={{0,3},{1,2},{2,1},{3,0},{4,7},{5,6},{6,5},{7,4},{8,11},{9,10},{10,... | collective-permute-start | bytes 147464 | tf_op jit(solution)/shard_map/ppermute | solution.py:504
  35.5 2.4 %collective-permute-start.15 = (f32[96,128]{1,0:T(8,128)S(1)}, f32[96,128]{1,0:T(8,128)S(1)}, u32[]{:S(2)}, u32[]{:S(2)}) collective-permute-start(f32[96,128]{1,0:T(8,128)S(1)} %get-tuple-element.80), channel_id=1, source_target_pairs={{0,2},{1,3},{2,0},{3,1},{4,6},{5,7},{6,4},{7,5},{8,10},{9,11},{10,... | collective-permute-start | bytes 147464 | tf_op jit(solution)/shard_map/ppermute | solution.py:504
  37.9 0.6 %collective-permute-start.16 = (f32[96,128]{1,0:T(8,128)S(1)}, f32[96,128]{1,0:T(8,128)S(1)}, u32[]{:S(2)}, u32[]{:S(2)}) collective-permute-start(f32[96,128]{1,0:T(8,128)S(1)} %get-tuple-element.81), channel_id=1, source_target_pairs={{0,1},{1,0},{2,3},{3,2},{4,5},{5,4},{6,7},{7,6},{8,9},{9,8},{10,11... | collective-permute-start | bytes 147464 | tf_op jit(solution)/shard_map/ppermute | solution.py:504
  38.5 1.5 %collective-permute-done.14.refs_4_ = f32[96,128]{1,0:T(8,128)S(1)} collective-permute-done((f32[96,128]{1,0:T(8,128)S(1)}, f32[96,128]{1,0:T(8,128)S(1)}, u32[]{:S(2)}, u32[]{:S(2)}) %collective-permute-start.14) | collective-permute-done | bytes 49184 | tf_op jit(solution)/shard_map/ppermute | solution.py:504
  40.0 0.5 %collective-permute-done.15.refs_5_ = f32[96,128]{1,0:T(8,128)S(1)} collective-permute-done((f32[96,128]{1,0:T(8,128)S(1)}, f32[96,128]{1,0:T(8,128)S(1)}, u32[]{:S(2)}, u32[]{:S(2)}) %collective-permute-start.15) | collective-permute-done | bytes 49184 | tf_op jit(solution)/shard_map/ppermute | solution.py:504
  40.5 1.5 %collective-permute-done.16.refs_6_ = f32[96,128]{1,0:T(8,128)S(1)} collective-permute-done((f32[96,128]{1,0:T(8,128)S(1)}, f32[96,128]{1,0:T(8,128)S(1)}, u32[]{:S(2)}, u32[]{:S(2)}) %collective-permute-start.16) | collective-permute-done | bytes 49184 | tf_op jit(solution)/shard_map/ppermute | solution.py:504
  42.0 0.5 back_across.1
  42.5 0.8 %back_within.1 = (f32[96,256]{1,0:T(8,128)S(1)}, f32[96,256]{1,0:T(8,128)S(1)}) custom-call(f32[96,128]{1,0:T(8,128)S(1)} %collective-permute-done.10.refs_0_, f32[96,128]{1,0:T(8,128)S(1)} %collective-permute-done.11.refs_1_, f32[96,128]{1,0:T(8,128)S(1)} %collective-permute-done.12.refs_2_, f32[96,128]{1,0:T(8,128)S(1)} %collective-permute-done.13.refs_3_, ...), custom_call_target="tpu_custom_call" | custom-call | flops 301989888 | bytes 4784128 | tf_op jit(solution)/shard_map/back_within/pallas_call | solution.py:486
  43.3 0.6 %collective-permute-start.18 = (f32[96,256]{1,0:T(8,128)S(1)}, f32[96,256]{1,0:T(8,128)S(1)}, u32[]{:S(2)}, u32[]{:S(2)}) collective-permute-start(f32[96,256]{1,0:T(8,128)S(1)} %get-tuple-element.92), channel_id=1, source_target_pairs={{0,8},{8,0},{16,24},{24,16},{1,9},{9,1},{17,25},{25,17},{2,10},{10... | collective-permute-start | bytes 294920 | tf_op jit(solution)/shard_map/ppermute | solution.py:504
  43.9 1.6 %collective-permute-start.19 = (f32[96,256]{1,0:T(8,128)S(1)}, f32[96,256]{1,0:T(8,128)S(1)}, u32[]{:S(2)}, u32[]{:S(2)}) collective-permute-start(f32[96,256]{1,0:T(8,128)S(1)} %add.3), channel_id=1, source_target_pairs={{0,16},{8,24},{16,0},{24,8},{1,17},{9,25},{17,1},{25,9},{2,18},{10... | collective-permute-start | bytes 294920 | tf_op jit(solution)/shard_map/ppermute | solution.py:504
  45.5 1.1 %exchange.1 = (f32[3,4,8,256]{3,2,1,0:T(8,128)S(1)}, f32[3,4,8,256]{3,2,1,0:T(8,128)S(1)}) custom-call(f32[3,4,8,256]{3,2,1,0:T(8,128)S(1)} %get-tuple-element.50.refs_0_, f32[3,4,8,256]{3,2,1,0:T(8,128)S(1)} %collective-permute-done.2.refs_1_, f32[3,4,8,256]{3,2,1,0:T(8,128)S(1)} %collective-permute-done.refs_2_, ...), custom_call_target="tpu_custom_call" | custom-call | flops 2457600 | bytes 774272 | tf_op jit(solution)/shard_map/exchange/pallas_call | solution.py:486
  46.6 0.5 back_own.1.refs_0_
  47.1 1.7 %collective-permute-done.19.refs_2_ = f32[96,256]{1,0:T(8,128)S(1)} collective-permute-done((f32[96,256]{1,0:T(8,128)S(1)}, f32[96,256]{1,0:T(8,128)S(1)}, u32[]{:S(2)}, u32[]{:S(2)}) %collective-permute-start.19) | collective-permute-done | bytes 98336 | tf_op jit(solution)/shard_map/ppermute | solution.py:504
  48.8 0.7 %predict.1 = (f32[3,4,8,256]{3,2,1,0:T(8,128)}, f32[3,4,8,256]{3,2,1,0:T(8,128)}) custom-call(f32[96,256]{1,0:T(8,128)S(1)} %back_own.1.refs_0_, f32[96,256]{1,0:T(8,128)S(1)} %collective-permute-done.18.refs_1_, f32[96,256]{1,0:T(8,128)S(1)} %collective-permute-done.19.refs_2_, f32[3,4,8,256]{3,2,1,0:T(8,128)S(1)} %get-tuple-element.96.refs_3_, ...), custom_call_target="tpu_custom_call" | custom-call | flops 491520 | bytes 688128 | tf_op jit(solution)/shard_map/predict/pallas_call | solution.py:486
  (28 shorter events, 0.7 us)
Async XLA Ops:
  1.5 5.8 %collective-permute-start = (f32[3,4,8,256]{3,2,1,0:T(8,128)S(1)}, f32[3,4,8,256]{3,2,1,0:T(8,128)S(1)}, u32[]{:S(2)}, u32[]{:S(2)}) collective-permute-start(f32[3,4,8,256]{3,2,1,0:T(8,128)S(1)} %get-tuple-element.50.refs_0_), channel_id=1, source_target_pairs={{0,16},{8,24},{16,0},{24,8},{1,17},{9,25},{17,1},{25,9},{2,18},{10... | collective-permute-start | bytes 294920 | tf_op jit(solution)/shard_map/ppermute | solution.py:504
  4.5 3.2 %collective-permute-start.2 = (f32[3,4,8,256]{3,2,1,0:T(8,128)S(1)}, f32[3,4,8,256]{3,2,1,0:T(8,128)S(1)}, u32[]{:S(2)}, u32[]{:S(2)}) collective-permute-start(f32[3,4,8,256]{3,2,1,0:T(8,128)S(1)} %get-tuple-element.50.refs_0_), channel_id=1, source_target_pairs={{0,8},{8,0},{16,24},{24,16},{1,9},{9,1},{17,25},{25,17},{2,10},{10... | collective-permute-start | bytes 294920 | tf_op jit(solution)/shard_map/ppermute | solution.py:504
  7.3 1.4 %collective-permute-start.1 = (f32[3,4,8,256]{3,2,1,0:T(8,128)S(1)}, f32[3,4,8,256]{3,2,1,0:T(8,128)S(1)}, u32[]{:S(2)}, u32[]{:S(2)}) collective-permute-start(f32[3,4,8,256]{3,2,1,0:T(8,128)S(1)} %collective-permute-done.refs_2_), channel_id=1, source_target_pairs={{0,8},{8,0},{16,24},{24,16},{1,9},{9,1},{17,25},{25,17},{2,10},{10... | collective-permute-start | bytes 294920 | tf_op jit(solution)/shard_map/ppermute | solution.py:504
  7.7 13.7 %copy-start = (bf16[6,8,64,128]{3,2,1,0:T(8,128)(2,1)S(1)}, bf16[6,8,64,128]{3,2,1,0:T(8,128)(2,1)}, u32[]{:S(2)}) copy-start(bf16[6,8,64,128]{3,2,1,0:T(8,128)(2,1)} %param.15) | copy-start | bytes 2359300
  7.7 13.7 %copy-start.1 = (bf16[64,128]{1,0:T(8,128)(2,1)S(1)}, bf16[64,128]{1,0:T(8,128)(2,1)}, u32[]{:S(2)}) copy-start(bf16[64,128]{1,0:T(8,128)(2,1)} %constant.11.clone.twice_ref) | copy-start | bytes 49156
  9.2 9.5 %collective-permute-start.4 = (f32[96,128]{1,0:T(8,128)S(1)}, f32[96,128]{1,0:T(8,128)S(1)}, u32[]{:S(2)}, u32[]{:S(2)}) collective-permute-start(f32[96,128]{1,0:T(8,128)S(1)} %get-tuple-element.58), channel_id=1, source_target_pairs={{0,6},{1,7},{2,4},{3,5},{4,2},{5,3},{6,0},{7,1},{8,14},{9,15},{10,... | collective-permute-start | bytes 147464 | tf_op jit(solution)/shard_map/ppermute | solution.py:504
  13.0 8.4 %collective-permute-start.5 = (f32[96,128]{1,0:T(8,128)S(1)}, f32[96,128]{1,0:T(8,128)S(1)}, u32[]{:S(2)}, u32[]{:S(2)}) collective-permute-start(f32[96,128]{1,0:T(8,128)S(1)} %get-tuple-element.59), channel_id=1, source_target_pairs={{0,5},{1,4},{2,7},{3,6},{4,1},{5,0},{6,3},{7,2},{8,13},{9,12},{10,... | collective-permute-start | bytes 147464 | tf_op jit(solution)/shard_map/ppermute | solution.py:504
  13.4 12.1 %collective-permute-start.3 = (f32[120,128]{1,0:T(8,128)S(1)}, f32[120,128]{1,0:T(8,128)S(1)}, u32[]{:S(2)}, u32[]{:S(2)}) collective-permute-start(f32[120,128]{1,0:T(8,128)S(1)} %get-tuple-element.57), channel_id=1, source_target_pairs={{0,7},{1,6},{2,5},{3,4},{4,3},{5,2},{6,1},{7,0},{8,15},{9,14},{10,... | collective-permute-start | bytes 184328 | tf_op jit(solution)/shard_map/ppermute | solution.py:504
  15.9 9.7 %collective-permute-start.6 = (f32[120,128]{1,0:T(8,128)S(1)}, f32[120,128]{1,0:T(8,128)S(1)}, u32[]{:S(2)}, u32[]{:S(2)}) collective-permute-start(f32[120,128]{1,0:T(8,128)S(1)} %get-tuple-element.60), channel_id=1, source_target_pairs={{0,4},{1,5},{2,6},{3,7},{4,0},{5,1},{6,2},{7,3},{8,12},{9,13},{10,... | collective-permute-start | bytes 184328 | tf_op jit(solution)/shard_map/ppermute | solution.py:504
  16.9 8.6 %collective-permute-start.7 = (f32[120,128]{1,0:T(8,128)S(1)}, f32[120,128]{1,0:T(8,128)S(1)}, u32[]{:S(2)}, u32[]{:S(2)}) collective-permute-start(f32[120,128]{1,0:T(8,128)S(1)} %get-tuple-element.61), channel_id=1, source_target_pairs={{0,3},{1,2},{2,1},{3,0},{4,7},{5,6},{6,5},{7,4},{8,11},{9,10},{10,... | collective-permute-start | bytes 184328 | tf_op jit(solution)/shard_map/ppermute | solution.py:504
  18.7 6.8 %collective-permute-start.9 = (f32[120,128]{1,0:T(8,128)S(1)}, f32[120,128]{1,0:T(8,128)S(1)}, u32[]{:S(2)}, u32[]{:S(2)}) collective-permute-start(f32[120,128]{1,0:T(8,128)S(1)} %get-tuple-element.63), channel_id=1, source_target_pairs={{0,1},{1,0},{2,3},{3,2},{4,5},{5,4},{6,7},{7,6},{8,9},{9,8},{10,11... | collective-permute-start | bytes 184328 | tf_op jit(solution)/shard_map/ppermute | solution.py:504
  21.4 4.1 %collective-permute-start.8 = (f32[96,128]{1,0:T(8,128)S(1)}, f32[96,128]{1,0:T(8,128)S(1)}, u32[]{:S(2)}, u32[]{:S(2)}) collective-permute-start(f32[96,128]{1,0:T(8,128)S(1)} %get-tuple-element.62), channel_id=1, source_target_pairs={{0,2},{1,3},{2,0},{3,1},{4,6},{5,7},{6,4},{7,5},{8,10},{9,11},{10,... | collective-permute-start | bytes 147464 | tf_op jit(solution)/shard_map/ppermute | solution.py:504
  27.3 8.2 %collective-permute-start.10 = (f32[96,128]{1,0:T(8,128)S(1)}, f32[96,128]{1,0:T(8,128)S(1)}, u32[]{:S(2)}, u32[]{:S(2)}) collective-permute-start(f32[96,128]{1,0:T(8,128)S(1)} %get-tuple-element.75), channel_id=1, source_target_pairs={{0,7},{1,6},{2,5},{3,4},{4,3},{5,2},{6,1},{7,0},{8,15},{9,14},{10,... | collective-permute-start | bytes 147464 | tf_op jit(solution)/shard_map/ppermute | solution.py:504
  30.2 7.7 %collective-permute-start.11 = (f32[96,128]{1,0:T(8,128)S(1)}, f32[96,128]{1,0:T(8,128)S(1)}, u32[]{:S(2)}, u32[]{:S(2)}) collective-permute-start(f32[96,128]{1,0:T(8,128)S(1)} %get-tuple-element.76), channel_id=1, source_target_pairs={{0,6},{1,7},{2,4},{3,5},{4,2},{5,3},{6,0},{7,1},{8,14},{9,15},{10,... | collective-permute-start | bytes 147464 | tf_op jit(solution)/shard_map/ppermute | solution.py:504
  32.0 6.4 %collective-permute-start.12 = (f32[96,128]{1,0:T(8,128)S(1)}, f32[96,128]{1,0:T(8,128)S(1)}, u32[]{:S(2)}, u32[]{:S(2)}) collective-permute-start(f32[96,128]{1,0:T(8,128)S(1)} %get-tuple-element.77), channel_id=1, source_target_pairs={{0,5},{1,4},{2,7},{3,6},{4,1},{5,0},{6,3},{7,2},{8,13},{9,12},{10,... | collective-permute-start | bytes 147464 | tf_op jit(solution)/shard_map/ppermute | solution.py:504
  32.0 6.4 %collective-permute-start.13 = (f32[96,128]{1,0:T(8,128)S(1)}, f32[96,128]{1,0:T(8,128)S(1)}, u32[]{:S(2)}, u32[]{:S(2)}) collective-permute-start(f32[96,128]{1,0:T(8,128)S(1)} %get-tuple-element.78), channel_id=1, source_target_pairs={{0,4},{1,5},{2,6},{3,7},{4,0},{5,1},{6,2},{7,3},{8,12},{9,13},{10,... | collective-permute-start | bytes 147464 | tf_op jit(solution)/shard_map/ppermute | solution.py:504
  35.0 5.0 %collective-permute-start.14 = (f32[96,128]{1,0:T(8,128)S(1)}, f32[96,128]{1,0:T(8,128)S(1)}, u32[]{:S(2)}, u32[]{:S(2)}) collective-permute-start(f32[96,128]{1,0:T(8,128)S(1)} %get-tuple-element.79), channel_id=1, source_target_pairs={{0,3},{1,2},{2,1},{3,0},{4,7},{5,6},{6,5},{7,4},{8,11},{9,10},{10,... | collective-permute-start | bytes 147464 | tf_op jit(solution)/shard_map/ppermute | solution.py:504
  35.5 5.0 %collective-permute-start.15 = (f32[96,128]{1,0:T(8,128)S(1)}, f32[96,128]{1,0:T(8,128)S(1)}, u32[]{:S(2)}, u32[]{:S(2)}) collective-permute-start(f32[96,128]{1,0:T(8,128)S(1)} %get-tuple-element.80), channel_id=1, source_target_pairs={{0,2},{1,3},{2,0},{3,1},{4,6},{5,7},{6,4},{7,5},{8,10},{9,11},{10,... | collective-permute-start | bytes 147464 | tf_op jit(solution)/shard_map/ppermute | solution.py:504
  37.9 4.1 %collective-permute-start.16 = (f32[96,128]{1,0:T(8,128)S(1)}, f32[96,128]{1,0:T(8,128)S(1)}, u32[]{:S(2)}, u32[]{:S(2)}) collective-permute-start(f32[96,128]{1,0:T(8,128)S(1)} %get-tuple-element.81), channel_id=1, source_target_pairs={{0,1},{1,0},{2,3},{3,2},{4,5},{5,4},{6,7},{7,6},{8,9},{9,8},{10,11... | collective-permute-start | bytes 147464 | tf_op jit(solution)/shard_map/ppermute | solution.py:504
  42.0 3.5 %copy-start.2 = (f32[16]{0:T(128)S(1)}, f32[16]{0:T(128)}, u32[]{:S(2)}) copy-start(f32[16]{0:T(128)} %refs_7_.1) | copy-start | bytes 196
  42.0 3.5 %copy-start.3 = (f32[16]{0:T(128)S(1)}, f32[16]{0:T(128)}, u32[]{:S(2)}) copy-start(f32[16]{0:T(128)} %refs_8_.1) | copy-start | bytes 196
  42.5 1.4 %collective-permute-start.17 = (f32[96,256]{1,0:T(8,128)S(1)}, f32[96,256]{1,0:T(8,128)S(1)}, u32[]{:S(2)}, u32[]{:S(2)}) collective-permute-start(f32[96,256]{1,0:T(8,128)S(1)} %back_across.1), channel_id=1, source_target_pairs={{0,8},{8,0},{16,24},{24,16},{1,9},{9,1},{17,25},{25,17},{2,10},{10... | collective-permute-start | bytes 294920 | tf_op jit(solution)/shard_map/ppermute | solution.py:504
  43.3 3.7 %collective-permute-start.18 = (f32[96,256]{1,0:T(8,128)S(1)}, f32[96,256]{1,0:T(8,128)S(1)}, u32[]{:S(2)}, u32[]{:S(2)}) collective-permute-start(f32[96,256]{1,0:T(8,128)S(1)} %get-tuple-element.92), channel_id=1, source_target_pairs={{0,8},{8,0},{16,24},{24,16},{1,9},{9,1},{17,25},{25,17},{2,10},{10... | collective-permute-start | bytes 294920 | tf_op jit(solution)/shard_map/ppermute | solution.py:504
  43.9 4.8 %collective-permute-start.19 = (f32[96,256]{1,0:T(8,128)S(1)}, f32[96,256]{1,0:T(8,128)S(1)}, u32[]{:S(2)}, u32[]{:S(2)}) collective-permute-start(f32[96,256]{1,0:T(8,128)S(1)} %add.3), channel_id=1, source_target_pairs={{0,16},{8,24},{16,0},{24,8},{1,17},{9,25},{17,1},{25,9},{2,18},{10... | collective-permute-start | bytes 294920 | tf_op jit(solution)/shard_map/ppermute | solution.py:504
